TPU v7x, 512 devices: a whole 4x8x8 slice. The times are simulated.
512 devices in a mesh: band: 8 (over y_lo, core), dom: 64 (over x, y_hi, z).
Axes of the slice: x: 4, y: 8 (y_hi: 2, y_lo: 4; y = y_hi * 4 + y_lo), z: 8, core: 2. Of those that a mesh axis runs over, the one named last changes fastest.
Arguments:
- states_in: float32 [512, 65536], P('band', 'dom'), may hold values from -6 to 6
- stiffness: float32 [343, 343], replicated, may hold values from -2 to 2, as said below
- cell_scale: float32 [384], P('dom'), may hold values from 0.5 to 2
- potential: float32 [65536], P('dom'), may hold values from 0 to 2
- inv_mass_sqrt: float32 [65536], P('dom'), may hold values from 0.25 to 1.75
- cell_nodes: int32 [384, 343], P('dom'), may hold values from 0 to 1151, as said below
- shared_nodes: int32 [8192], P('dom'), may hold values from 0 to 1023, as said below
Outputs:
- filtered: float32 [512, 65536], P('band', 'dom')
- margin: float32 [512, 512], P('band')
Inputs may be any that keep to these rules, and one draw needn't show every extreme that they name: `stiffness`: symmetric. `cell_nodes`: in the cells of a subdomain, an entry below 1024 is one of its own nodes and an entry l of 1024 or more stands for entry l - 1024 of the next subdomain's (cyclically) shared_nodes list; every value from 0 to 1151 occurs in the subdomain's cells. `shared_nodes`: the 128 entries of each subdomain are distinct.
All inputs are finite; a program needn't handle non-finite values.
Results may differ from a plain program's by a relative error of at most 0.0001.
Values sent between devices are 32-bit elements; how exact they have to be, the bound alone decides.
No kernel may reach another device: no remote copies, remote signals or barrier semaphores. Data moves between devices by JAX's collectives and lax.ppermute only.
A program may use at most 64 MiB of HBM per device.

v0:
```python
import jax
import jax.numpy as jnp
from jax import lax
from jax.sharding import PartitionSpec as P

DEGREE = 3


center_shift = 1.0
half_width = 4.0


def passed_along(x, axis, by):
    peers = lax.axis_size(axis)
    return lax.ppermute(x, axis, [(i, (i + by) % peers) for i in range(peers)])


def per_device(
    states_in, stiffness, cell_scale, potential, inv_mass_sqrt, cell_nodes, shared_nodes
):
    owned = states_in.shape[1]
    shared_count = shared_nodes.shape[0]
    block_rows = states_in.shape[0]

    def operate(vector):
        scaled = vector * inv_mass_sqrt[None, :]
        outgoing = jnp.take(scaled, shared_nodes, axis=1)
        ghosts = passed_along(outgoing, "dom", -1)
        extended = jnp.concatenate([scaled, ghosts], axis=1)
        cellwise = jnp.take(extended, cell_nodes, axis=1)
        product = jnp.einsum(
            "bcj,kj->bck",
            cellwise,
            stiffness,
            precision=lax.Precision.HIGHEST,
            preferred_element_type=jnp.float32,
        )
        product = product * cell_scale[None, :, None]
        summed = (
            jnp.zeros((block_rows, owned + shared_count), jnp.float32)
            .at[:, cell_nodes]
            .add(product)
        )
        returned = passed_along(summed[:, owned:], "dom", 1)
        own_sums = summed[:, :owned].at[:, shared_nodes].add(returned)
        return inv_mass_sqrt[None, :] * own_sums + potential[None, :] * vector

    previous = states_in
    current = (operate(states_in) - center_shift * states_in) / half_width
    for degree_step in range(DEGREE - 1):
        following = 2.0 * (operate(current) - center_shift * current) / half_width - previous
        previous = current
        current = following
    total_nodes = owned * lax.axis_size("dom")
    contract = (((1,), (1,)), ((), ()))
    pieces = lax.all_to_all(current, "band", split_axis=1, concat_axis=0, tiled=True)
    gram_local = lax.dot_general(
        pieces,
        pieces,
        contract,
        precision=lax.Precision.HIGHEST,
        preferred_element_type=jnp.float32,
    )
    summed_gram = lax.psum(gram_local, ("band", "dom"))
    row_block = lax.dynamic_slice_in_dim(
        summed_gram, lax.axis_index("band") * block_rows, block_rows, 0
    )
    return (current, row_block / total_nodes)


def solution(mesh):
    return jax.shard_map(
        per_device,
        mesh=mesh,
        in_specs=(P("band", "dom"), P(), P("dom"), P("dom"), P("dom"), P("dom", None), P("dom")),
        out_specs=(P("band", "dom"), P("band", None)),
        check_vma=False,
    )
```

profile of v0, /device:TPU:1, one launch (start us, length us, event | category | flops | bytes accessed | tf_op | source)
XLA Modules:
  0.0 459.6 jit_solution(5606167754359788286)
XLA Ops:
  11.4 19.0 %collective-permute-start = (f32[64,128]{0,1:T(8,128)S(1)}, f32[64,128]{0,1:T(8,128)S(1)}, u32[]{:S(2)}, u32[]{:S(2)}) collective-permute-start(f32[64,128]{0,1:T(8,128)S(1)} %select_bitcast_fusion.5), channel_id=1, source_target_pairs={{0,63},{1,0},{2,1},{3,2},{4,3},{5,4},{6,5},{7,6},{8,7},{9,8},{10,9... | collective-permute-start | bytes 98312 | tf_op jit(solution)/shard_map/ppermute | solution.py:15
  31.8 3.9 gather_fusion.1
  38.8 14.4 %scatter_custom_fusion = f32[64,1152]{0,1:T(8,128)S(1)} fusion(s32[2058]{0:T(1024)S(1)} %reshape.102, f32[2058,64]{1,0:T(8,128)S(1)} %reshape.153, f32[]{:T(128)} %constant.27.clone.1), kind=kCustom, calls=%fused_computation.37 | custom fusion | flops 131712 | bytes 294916 | tf_op jit(solution)/shard_map/scatter-add | solution.py:42
  53.2 1.9 collective-permute-start.1
  55.2 13.3 %collective-permute-done.1 = f32[64,128]{0,1:T(8,128)S(1)} collective-permute-done((f32[64,128]{0,1:T(8,128)S(1)}, f32[64,128]{0,1:T(8,128)S(1)}, u32[]{:S(2)}, u32[]{:S(2)}) %collective-permute-start.1) | collective-permute-done | bytes 32800 | tf_op jit(solution)/shard_map/ppermute | solution.py:15
  68.6 1.5 scatter_custom_fusion.1
  71.3 2.1 collective-permute-start.2
  73.4 2.9 collective-permute-done.2
  76.3 5.0 %gather_fusion.3 = f32[2058,64]{1,0:T(8,128)} fusion(f32[64,1152]{0,1:T(8,128)S(1)} %pad_maximum_fusion.1, s32[3072]{0:T(1024)S(1)} %pad_clamp_fusion), kind=kCustom, calls=%fused_computation.4.clone | custom fusion | bytes 1061928 | tf_op jit(solution)/shard_map/jit(_take)/gather | solution.py:30
  81.3 1.6 copy.24
  83.4 1.3 fusion.1
  86.1 14.7 %scatter_custom_fusion.2 = f32[64,1152]{0,1:T(8,128)S(1)} fusion(s32[2058]{0:T(1024)S(1)} %reshape.102, f32[2058,64]{1,0:T(8,128)} %reshape.154, f32[]{:T(128)} %constant.27.clone.1), kind=kCustom, calls=%fused_computation.35 | custom fusion | flops 131712 | bytes 295424 | tf_op jit(solution)/shard_map/scatter-add | solution.py:42
  100.8 1.9 collective-permute-start.3
  102.8 11.2 %collective-permute-done.3 = f32[64,128]{0,1:T(8,128)S(1)} collective-permute-done((f32[64,128]{0,1:T(8,128)S(1)}, f32[64,128]{0,1:T(8,128)S(1)}, u32[]{:S(2)}, u32[]{:S(2)}) %collective-permute-start.3) | collective-permute-done | bytes 32800 | tf_op jit(solution)/shard_map/ppermute | solution.py:15
  114.0 1.5 scatter_custom_fusion.3
  116.6 1.9 collective-permute-start.4
  118.6 3.1 collective-permute-done.4
  121.7 5.0 %gather_fusion.5 = f32[2058,64]{1,0:T(8,128)} fusion(f32[64,1152]{0,1:T(8,128)S(1)} %pad_maximum_fusion.2, s32[3072]{0:T(1024)S(1)} %pad_clamp_fusion), kind=kCustom, calls=%fused_computation.5.clone | custom fusion | bytes 1061928 | tf_op jit(solution)/shard_map/jit(_take)/gather | solution.py:30
  126.7 2.4 copy.29
  129.1 1.4 reshape.151
  130.6 1.3 fusion.2
  131.9 1.3 copy.37
  133.2 2.3 reshape.155
  135.6 14.7 %scatter_custom_fusion.4 = f32[64,1152]{0,1:T(8,128)S(1)} fusion(s32[2058]{0:T(1024)S(1)} %reshape.102, f32[2058,64]{1,0:T(8,128)} %reshape.155, f32[]{:T(128)} %constant.27.clone.1), kind=kCustom, calls=%fused_computation.33 | custom fusion | flops 131712 | bytes 295424 | tf_op jit(solution)/shard_map/scatter-add | solution.py:42
  150.3 1.9 collective-permute-start.5
  153.1 10.4 %collective-permute-done.5 = f32[64,128]{0,1:T(8,128)S(1)} collective-permute-done((f32[64,128]{0,1:T(8,128)S(1)}, f32[64,128]{0,1:T(8,128)S(1)}, u32[]{:S(2)}, u32[]{:S(2)}) %collective-permute-start.5) | collective-permute-done | bytes 32800 | tf_op jit(solution)/shard_map/ppermute | solution.py:15
  163.5 3.0 scatter_custom_fusion.5
  166.5 1.5 multiply_subtract_fusion
  168.2 18.5 %all_to_all.19 = f32[64,8,128]{2,0,1:T(8,128)S(1)} all-to-all(f32[64,8,128]{2,0,1:T(8,128)S(1)} %copy.33), channel_id=1, replica_groups=mesh['band'=8,'dom'=64] {'band'}, dimensions={1} | all-to-all | bytes 524288 | tf_op jit(solution)/shard_map/all_to_all | solution.py:56
  186.7 2.0 fusion.21
  189.7 261.5 %all-reduce.2.cloned.1.call-done = f32[512,512]{1,0:T(8,128)} async-done(((f32[512,512]{1,0:T(8,128)}), f32[512,512]{1,0:T(8,128)}) %all-reduce.2.cloned.1.call-update) | async-done | bytes 1048592 | tf_op jit(solution)/shard_map/psum | solution.py:64
  451.2 1.6 dynamic-slice_multiply_fusion
  (54 shorter events, 15.0 us)
Async XLA Ops:
  7.2 29.4 %copy-start = (f32[343,343]{1,0:T(8,128)S(1)}, f32[343,343]{1,0:T(8,128)}, u32[]{:S(2)}) copy-start(f32[343,343]{1,0:T(8,128)} %param.12) | copy-start | bytes 1411792
  7.2 444.0 %all-reduce.2.cloned.1.call-start = ((), (), s32[]{:S(2)}) async-start(), calls=%async_computation.1 | async-start | bytes 2097152 | tf_op jit(solution)/shard_map/psum | solution.py:64
  8.6 21.8 %copy-start.3 = (s32[6,343]{1,0:T(8,128)S(1)}, s32[6,343]{1,0:T(8,128)}, u32[]{:S(2)}) copy-start(s32[6,343]{1,0:T(8,128)} %param.16) | copy-start | bytes 24700
  11.4 20.3 %collective-permute-start = (f32[64,128]{0,1:T(8,128)S(1)}, f32[64,128]{0,1:T(8,128)S(1)}, u32[]{:S(2)}, u32[]{:S(2)}) collective-permute-start(f32[64,128]{0,1:T(8,128)S(1)} %select_bitcast_fusion.5), channel_id=1, source_target_pairs={{0,63},{1,0},{2,1},{3,2},{4,3},{5,4},{6,5},{7,6},{8,7},{9,8},{10,9... | collective-permute-start | bytes 98312 | tf_op jit(solution)/shard_map/ppermute | solution.py:15
  36.4 0.7 copy-start.4
  38.7 16.4 %copy-start.1 = (f32[1024]{0:T(1024)S(1)}, f32[1024]{0:T(1024)}, u32[]{:S(2)}) copy-start(f32[1024]{0:T(1024)} %param.15) | copy-start | bytes 12292
  38.8 31.2 %copy-start.2 = (f32[1024]{0:T(1024)S(1)}, f32[1024]{0:T(1024)}, u32[]{:S(2)}) copy-start(f32[1024]{0:T(1024)} %param.14) | copy-start | bytes 12292
  53.2 15.3 %collective-permute-start.1 = (f32[64,128]{0,1:T(8,128)S(1)}, f32[64,128]{0,1:T(8,128)S(1)}, u32[]{:S(2)}, u32[]{:S(2)}) collective-permute-start(f32[64,128]{0,1:T(8,128)S(1)} %slice.37), channel_id=1, source_target_pairs={{0,1},{1,2},{2,3},{3,4},{4,5},{5,6},{6,7},{7,8},{8,9},{9,10},{10,1... | collective-permute-start | bytes 98312 | tf_op jit(solution)/shard_map/ppermute | solution.py:15
  71.3 5.0 %collective-permute-start.2 = (f32[64,128]{0,1:T(8,128)S(1)}, f32[64,128]{0,1:T(8,128)S(1)}, u32[]{:S(2)}, u32[]{:S(2)}) collective-permute-start(f32[64,128]{0,1:T(8,128)S(1)} %select_bitcast_fusion.4), channel_id=1, source_target_pairs={{0,63},{1,0},{2,1},{3,2},{4,3},{5,4},{6,5},{7,6},{8,7},{9,8},{10,9... | collective-permute-start | bytes 98312 | tf_op jit(solution)/shard_map/ppermute | solution.py:15
  100.8 13.1 %collective-permute-start.3 = (f32[64,128]{0,1:T(8,128)S(1)}, f32[64,128]{0,1:T(8,128)S(1)}, u32[]{:S(2)}, u32[]{:S(2)}) collective-permute-start(f32[64,128]{0,1:T(8,128)S(1)} %slice.39), channel_id=1, source_target_pairs={{0,1},{1,2},{2,3},{3,4},{4,5},{5,6},{6,7},{7,8},{8,9},{9,10},{10,1... | collective-permute-start | bytes 98312 | tf_op jit(solution)/shard_map/ppermute | solution.py:15
  116.6 5.0 %collective-permute-start.4 = (f32[64,128]{0,1:T(8,128)S(1)}, f32[64,128]{0,1:T(8,128)S(1)}, u32[]{:S(2)}, u32[]{:S(2)}) collective-permute-start(f32[64,128]{0,1:T(8,128)S(1)} %select_bitcast_fusion.3), channel_id=1, source_target_pairs={{0,63},{1,0},{2,1},{3,2},{4,3},{5,4},{6,5},{7,6},{8,7},{9,8},{10,9... | collective-permute-start | bytes 98312 | tf_op jit(solution)/shard_map/ppermute | solution.py:15
  150.3 13.2 %collective-permute-start.5 = (f32[64,128]{0,1:T(8,128)S(1)}, f32[64,128]{0,1:T(8,128)S(1)}, u32[]{:S(2)}, u32[]{:S(2)}) collective-permute-start(f32[64,128]{0,1:T(8,128)S(1)} %slice.41), channel_id=1, source_target_pairs={{0,1},{1,2},{2,3},{3,4},{4,5},{5,6},{6,7},{7,8},{8,9},{9,10},{10,1... | collective-permute-start | bytes 98312 | tf_op jit(solution)/shard_map/ppermute | solution.py:15
Sparse Core Ops, SparseCore 0:
  188.9 262.2 all-reduce.1
where the time goes:
time: 460 us
  waiting for transfers between devices  304 us (66%)
  other arithmetic  56.7 us (12%)
  local copies, waits for them, and re-layouts  31.6 us (7%)
  starting transfers between devices  28.8 us (6%)
  blocking collectives  18.5 us (4%)
  between operations  14.5 us (3%)
  matrix products  5.92 us (1%)
    psum x1, waiting for transfers between devices, per_device(): summed_gram = lax.psum(gram_local, ('band', 'dom'))  262 us
    scatter-add x3, other arithmetic, operate(): summed = jnp.zeros((block_rows, owned + shared_count), jnp.float32).at[:,...  43.8 us
    ppermute x6, waiting for transfers between devices, passed_along(): return lax.ppermute(x, axis, [(i, (i + by) % peers) for i in range(peers)])  42.1 us
    ppermute x6, starting transfers between devices, passed_along(): return lax.ppermute(x, axis, [(i, (i + by) % peers) for i in range(peers)])  28.7 us
    gather x9, local copies, waits for them, and re-layouts, operate(): cellwise = jnp.take(extended, cell_nodes, axis=1)  20.4 us
    all_to_all x1, blocking collectives, per_device(): lax.all_to_all(current, 'band', split_axis=1, concat_axis=0, tiled=True)  18.5 us
  transfers between devices with their start and end apart: 7, of which 7 were waited for; matrix products, arithmetic and copies ran while one was open for 0% of the time, Pallas kernels for 0%

commit v1 on v0

v1 whole, which is shorter than its diff:
```python
import functools

import jax
import jax.numpy as jnp
from jax import lax
from jax.experimental import pallas as pl
from jax.experimental.pallas import tpu as pltpu
from jax.sharding import PartitionSpec as P

DEGREE = 3
CENTER = 1.0
HALF_WIDTH = 4.0
LIMIT = 48 * 1024 * 1024

f32 = jnp.float32
bf16 = jnp.bfloat16


def rounded_up(count, to):
    return -(-count // to) * to


def parts(x, count):
    out = []
    for i in range(count):
        piece = x.astype(bf16)
        out.append(piece)
        if i + 1 < count:
            x = x - piece.astype(f32)
    return out


def dot(a, b):
    return jnp.dot(a, b, preferred_element_type=f32)


def dot_t(a, b):
    return lax.dot_general(a, b, (((1,), (1,)), ((), ())), preferred_element_type=f32)


def one_hot(row, count):
    at = lax.broadcasted_iota(jnp.int32, (count, row.shape[1]), 0)
    return jnp.where(at == row, 1.0, 0.0).astype(bf16)


def picked(x, chosen):
    rows = x.shape[0]
    got = dot(jnp.concatenate(parts(x, 3), axis=0), chosen)
    return got[:rows] + got[rows : 2 * rows] + got[2 * rows :]


def placed(x, chosen):
    rows = x.shape[0]
    got = dot_t(jnp.concatenate(parts(x, 3), axis=0), chosen)
    return got[:rows] + got[rows : 2 * rows] + got[2 * rows :]


def start_kernel(states, inv_mass, shared, message):
    rows, owned = states.shape
    chosen = one_hot(shared[...], owned)
    both = jnp.concatenate(
        [states[...], jnp.broadcast_to(inv_mass[...], (8, owned))], axis=0
    )
    message[...] = picked(both, chosen)


def apply_cells(own, ghost, cells, stiff, scale, chosen_all, cells_pad, stiff_pad):
    rows = own.shape[0]
    n_cells, npc = cells.shape
    pad = stiff_pad.shape[0]
    nodes = chosen_all.shape[0]
    cells_pad[...] = jnp.full(cells_pad.shape, -1, jnp.int32)
    cells_pad[:n_cells, :npc] = cells[...]
    stiff_pad[...] = jnp.zeros(stiff_pad.shape, f32)
    stiff_pad[:npc, :npc] = stiff[...]
    for c in range(n_cells):
        chosen_all[:, c * pad : (c + 1) * pad] = one_hot(cells_pad[c : c + 1, :], nodes)
    values = jnp.concatenate([own, ghost], axis=1)
    gathered = dot(jnp.concatenate(parts(values, 2), axis=0), chosen_all[...])
    gathered = gathered.astype(bf16)
    high, low = parts(stiff_pad[...], 2)
    stacked = jnp.concatenate(
        [gathered[:rows, c * pad : (c + 1) * pad] for c in range(n_cells)]
        + [gathered[rows:, c * pad : (c + 1) * pad] for c in range(n_cells)],
        axis=0,
    )
    half = n_cells * rows
    by_high = dot(stacked, high)
    product = by_high[:half] + by_high[half:] + dot(stacked[:half], low)
    product = jnp.concatenate(
        [product[c * rows : (c + 1) * rows] * scale[c] for c in range(n_cells)], axis=1
    )
    summed = dot_t(jnp.concatenate(parts(product, 2), axis=0), chosen_all[...])
    summed = summed[:rows] + summed[rows:]
    return summed[:, : own.shape[1]], summed[:, own.shape[1] :]


def first_kernel(
    states, fetched, inv_mass, potential, cells, stiff, scale, shared,
    partial, down, up, chosen_all, cells_pad, stiff_pad,
):
    rows, owned = states.shape
    current = states[...]
    ghost_inv = fetched[rows : rows + 1, :]
    ghost = fetched[:rows, :]
    own_sum, ghost_sum = apply_cells(
        current * inv_mass[...], ghost * ghost_inv, cells, stiff, scale,
        chosen_all, cells_pad, stiff_pad,
    )
    up[...] = ghost_inv * ghost_sum * (1.0 / HALF_WIDTH)
    here = (inv_mass[...] * own_sum + (potential[...] - CENTER) * current) * (1.0 / HALF_WIDTH)
    partial[...] = here
    down[...] = picked(here, one_hot(shared[...], owned))


def next_kernel(
    last, previous, part, fetched, sent_up, got_down, got_up, inv_mass, potential,
    cells, stiff, scale, shared, *rest,
):
    if last:
        partial, up, chosen_all, cells_pad, stiff_pad = rest
    else:
        current_out, partial, down, up, chosen_all, cells_pad, stiff_pad = rest
    rows, owned = previous.shape
    chosen = one_hot(shared[...], owned)
    current = part[...] + placed(got_up[...], chosen)
    ghost_inv = fetched[rows : rows + 1, :]
    ghost = got_down[...] + sent_up[...]
    own_sum, ghost_sum = apply_cells(
        current * inv_mass[...], ghost * ghost_inv, cells, stiff, scale,
        chosen_all, cells_pad, stiff_pad,
    )
    up[...] = ghost_inv * ghost_sum * (2.0 / HALF_WIDTH)
    here = (inv_mass[...] * own_sum + (potential[...] - CENTER) * current) * (
        2.0 / HALF_WIDTH
    ) - previous[...]
    partial[...] = here
    if not last:
        current_out[...] = current
        down[...] = picked(here, chosen)


def finish_kernel(part, got_up, shared, filtered, at_shared):
    owned = part.shape[1]
    chosen = one_hot(shared[...], owned)
    here = part[...] + placed(got_up[...], chosen)
    filtered[...] = here
    at_shared[...] = picked(here, chosen)


def gram_kernel(total_nodes, filtered, at_shared, gathered, late, out):
    rows = filtered.shape[0]

    def against(a, b):
        a_high, a_low = parts(a, 2)
        b_high, b_low = parts(b, 2)
        by_high = dot_t(jnp.concatenate([a_high, a_low], axis=0), b_high)
        return by_high[:rows] + by_high[rows:] + dot_t(a_high, b_low)

    whole = against(filtered[...], gathered[...]) + against(at_shared[...], late[...])
    out[...] = whole * (1.0 / total_nodes)


def per_device(
    states_in, stiffness, cell_scale, potential, inv_mass_sqrt, cell_nodes, shared_nodes
):
    rows, owned = states_in.shape
    shared_count = shared_nodes.shape[0]
    n_cells, npc = cell_nodes.shape
    nodes = owned + shared_count
    pad = rounded_up(npc, 128)
    n_dom = lax.axis_size("dom")
    n_band = lax.axis_size("band")
    backward = [(i, (i - 1) % n_dom) for i in range(n_dom)]
    forward = [(i, (i + 1) % n_dom) for i in range(n_dom)]

    in_vmem = pl.BlockSpec(memory_space=pltpu.VMEM)
    in_smem = pl.BlockSpec(memory_space=pltpu.SMEM)
    params = pltpu.CompilerParams(vmem_limit_bytes=LIMIT)
    inv_mass = inv_mass_sqrt.reshape(1, owned)
    pot = potential.reshape(1, owned)
    shared = shared_nodes.reshape(1, shared_count)
    block = jax.ShapeDtypeStruct((rows, owned), f32)
    edge = jax.ShapeDtypeStruct((rows, shared_count), f32)
    scratch = [
        pltpu.VMEM((nodes, n_cells * pad), bf16),
        pltpu.VMEM((8, pad), jnp.int32),
        pltpu.VMEM((pad, pad), f32),
    ]

    def call(kernel, out_shape, specs, scratch_shapes=()):
        return pl.pallas_call(
            kernel,
            out_shape=out_shape,
            in_specs=specs,
            out_specs=jax.tree.map(lambda _: in_vmem, out_shape),
            scratch_shapes=scratch_shapes,
            compiler_params=params,
        )

    message = call(
        start_kernel, jax.ShapeDtypeStruct((rows + 8, shared_count), f32), [in_vmem] * 3
    )(states_in, inv_mass, shared)
    fetched = lax.ppermute(message, "dom", backward)
    fixed = (inv_mass, pot, cell_nodes, stiffness, cell_scale, shared)
    fixed_specs = [in_vmem] * 4 + [in_smem, in_vmem]
    partial, down, up = call(
        first_kernel, (block, edge, edge), [in_vmem] * 2 + fixed_specs, scratch
    )(states_in, fetched, *fixed)
    previous = states_in
    for step in range(DEGREE - 1):
        last = step == DEGREE - 2
        got_up = lax.ppermute(up, "dom", forward)
        got_down = lax.ppermute(down, "dom", backward)
        outs = (block, edge) if last else (block, block, edge, edge)
        results = call(
            functools.partial(next_kernel, last), outs, [in_vmem] * 6 + fixed_specs, scratch
        )(previous, partial, fetched, up, got_down, got_up, *fixed)
        if last:
            partial, up = results
        else:
            previous, partial, down, up = results
    gathered = lax.all_gather(partial, "band", axis=0, tiled=True)
    got_up = lax.ppermute(up, "dom", forward)
    filtered, at_shared = call(finish_kernel, (block, edge), [in_vmem] * 3)(
        partial, got_up, shared
    )
    late = lax.all_to_all(
        jnp.broadcast_to(got_up[None], (n_band, rows, shared_count)),
        "band", split_axis=0, concat_axis=0, tiled=True,
    ).reshape(n_band * rows, shared_count)
    gram = call(
        functools.partial(gram_kernel, owned * n_dom),
        jax.ShapeDtypeStruct((rows, n_band * rows), f32),
        [in_vmem] * 4,
    )(filtered, at_shared, gathered, late)
    pieces = lax.all_to_all(gram, "dom", split_axis=0, concat_axis=0, tiled=True)
    pieces = pieces.reshape(n_dom, rows // n_dom, n_band * rows)
    own_rows = jnp.broadcast_to(jnp.sum(pieces, axis=0)[None], pieces.shape)
    margin = lax.all_to_all(
        own_rows.reshape(rows, n_band * rows), "dom", split_axis=0, concat_axis=0, tiled=True
    )
    return filtered, margin


def solution(mesh):
    return jax.shard_map(
        per_device,
        mesh=mesh,
        in_specs=(P("band", "dom"), P(), P("dom"), P("dom"), P("dom"), P("dom", None), P("dom")),
        out_specs=(P("band", "dom"), P("band", None)),
        check_vma=False,
    )
```

time: 460 us -> 181 us (0.39)
  the two profiles are of different devices: /device:TPU:1 before, /device:TPU:2 now
where the time goes in v1:
time: 181 us; the launch traced here: 180 us
  starting transfers between devices  48 us (27%)
  waiting for transfers between devices  45.9 us (25%)
  blocking collectives  43.9 us (24%)
  Pallas kernels  18.9 us (10%)
  between operations  14.2 us (8%)
  local copies, waits for them, and re-layouts  9.52 us (5%)
    all_to_all x1, blocking collectives, per_device(): lax.all_to_all(gram, 'dom', split_axis=0, concat_axis=0, tiled=True)  24.9 us
    ppermute x2, starting transfers between devices, per_device(): got_down = lax.ppermute(down, 'dom', backward)  22.4 us
    ppermute x3, waiting for transfers between devices, per_device(): got_up = lax.ppermute(up, 'dom', forward)  21.6 us
    all_to_all x1, blocking collectives, per_device(): lax.all_to_all(own_rows.reshape(rows, n_band * rows), 'dom', split_axis=0...  19 us
    ppermute x1, starting transfers between devices, per_device(): fetched = lax.ppermute(message, 'dom', backward)  16.2 us
    all_to_all x1, waiting for transfers between devices, per_device(): lax.all_to_all(jnp.broadcast_to(got_up[None], (n_band, rows, shared_count...  11.6 us
    pallas_call x2, Pallas kernels, per_device(): call(functools.partial(next_kernel, last), outs, [in_vmem] * 6 + fixed_sp...  10.6 us
    all_gather x1, waiting for transfers between devices, per_device(): gathered = lax.all_gather(partial, 'band', axis=0, tiled=True)  9.24 us
  transfers between devices with their start and end apart: 8, of which 6 were waited for; matrix products, arithmetic and copies ran while one was open for 0% of the time, Pallas kernels for 1%

profile of v1, /device:TPU:2, one launch (start us, length us, event | category | flops | bytes accessed | tf_op | source)
XLA Modules:
  0.0 180.4 jit_solution(16759879692307620496)
XLA Ops:
  7.2 0.9 copy-done.2
  8.2 0.7 copy-done.6
  8.8 0.7 copy-done.8
  9.5 0.3 shard_map.86
  9.8 16.2 %collective-permute-start = (f32[72,128]{1,0:T(8,128)S(1)}, f32[72,128]{1,0:T(8,128)S(1)}, u32[]{:S(2)}, u32[]{:S(2)}) collective-permute-start(f32[72,128]{1,0:T(8,128)S(1)} %shard_map.86), channel_id=1, source_target_pairs={{0,63},{1,0},{2,1},{3,2},{4,3},{5,4},{6,5},{7,6},{8,7},{9,8},{10,9... | collective-permute-start | bytes 110600 | tf_op jit(solution)/shard_map/ppermute | solution.py:204
  26.0 1.9 %collective-permute-done.fetched = f32[72,128]{1,0:T(8,128)S(1)} collective-permute-done((f32[72,128]{1,0:T(8,128)S(1)}, f32[72,128]{1,0:T(8,128)S(1)}, u32[]{:S(2)}, u32[]{:S(2)}) %collective-permute-start) | collective-permute-done | bytes 36896 | tf_op jit(solution)/shard_map/ppermute | solution.py:204
  27.8 1.0 copy-done
  28.9 0.7 copy-done.5
  29.6 0.7 copy-done.7
  30.3 0.7 copy-done.10
  30.9 5.1 %shard_map.87 = (f32[64,1024]{1,0:T(8,128)S(1)}, f32[64,128]{1,0:T(8,128)S(1)}, f32[64,128]{1,0:T(8,128)S(1)}) custom-call(f32[64,1024]{1,0:T(8,128)S(1)} %copy-done.2, f32[72,128]{1,0:T(8,128)S(1)} %collective-permute-done.fetched, f32[1,1024]{1,0:T(1,128)S(1)} %bitcast.11, f32[1,1024]{1,0:T(1,128)S(1)} %bitcast.14, s32[6,343]{1,0:T(8,128)S(1)} %copy-done.5, ...), custom_call_target="tpu_custom_call" | custom-call | tf_op jit(solution)/shard_map/pallas_call | solution.py:207
  36.1 1.9 %collective-permute-start.2 = (f32[64,128]{1,0:T(8,128)S(1)}, f32[64,128]{1,0:T(8,128)S(1)}, u32[]{:S(2)}, u32[]{:S(2)}) collective-permute-start(f32[64,128]{1,0:T(8,128)S(1)} %get-tuple-element.14.sent_up), channel_id=1, source_target_pairs={{0,1},{1,2},{2,3},{3,4},{4,5},{5,6},{6,7},{7,8},{8,9},{9,10},{10,1... | collective-permute-start | bytes 98312 | tf_op jit(solution)/shard_map/ppermute | solution.py:213
  38.0 11.3 %collective-permute-start.1 = (f32[64,128]{1,0:T(8,128)S(1)}, f32[64,128]{1,0:T(8,128)S(1)}, u32[]{:S(2)}, u32[]{:S(2)}) collective-permute-start(f32[64,128]{1,0:T(8,128)S(1)} %get-tuple-element.15), channel_id=1, source_target_pairs={{0,63},{1,0},{2,1},{3,2},{4,3},{5,4},{6,5},{7,6},{8,7},{9,8},{10,9... | collective-permute-start | bytes 98312 | tf_op jit(solution)/shard_map/ppermute | solution.py:214
  49.3 1.6 collective-permute-done.1.got_down
  50.9 5.2 %shard_map.88 = (f32[64,1024]{1,0:T(8,128)S(1)}, f32[64,1024]{1,0:T(8,128)S(1)}, f32[64,128]{1,0:T(8,128)S(1)}, f32[64,128]{1,0:T(8,128)S(1)}) custom-call(f32[64,1024]{1,0:T(8,128)S(1)} %copy-done.2, f32[64,1024]{1,0:T(8,128)S(1)} %get-tuple-element.13.part, f32[72,128]{1,0:T(8,128)S(1)} %collective-permute-done.fetched, ...), custom_call_target="tpu_custom_call" | custom-call | tf_op jit(solution)/shard_map/pallas_call | solution.py:216
  56.0 11.1 %collective-permute-start.3 = (f32[64,128]{1,0:T(8,128)S(1)}, f32[64,128]{1,0:T(8,128)S(1)}, u32[]{:S(2)}, u32[]{:S(2)}) collective-permute-start(f32[64,128]{1,0:T(8,128)S(1)} %get-tuple-element.19), channel_id=1, source_target_pairs={{0,63},{1,0},{2,1},{3,2},{4,3},{5,4},{6,5},{7,6},{8,7},{9,8},{10,9... | collective-permute-start | bytes 98312 | tf_op jit(solution)/shard_map/ppermute | solution.py:214
  67.2 1.9 %collective-permute-start.4 = (f32[64,128]{1,0:T(8,128)S(1)}, f32[64,128]{1,0:T(8,128)S(1)}, u32[]{:S(2)}, u32[]{:S(2)}) collective-permute-start(f32[64,128]{1,0:T(8,128)S(1)} %get-tuple-element.18.sent_up), channel_id=1, source_target_pairs={{0,1},{1,2},{2,3},{3,4},{4,5},{5,6},{6,7},{7,8},{8,9},{9,10},{10,1... | collective-permute-start | bytes 98312 | tf_op jit(solution)/shard_map/ppermute | solution.py:213
  69.1 10.8 %collective-permute-done.4.got_up = f32[64,128]{1,0:T(8,128)S(1)} collective-permute-done((f32[64,128]{1,0:T(8,128)S(1)}, f32[64,128]{1,0:T(8,128)S(1)}, u32[]{:S(2)}, u32[]{:S(2)}) %collective-permute-start.4) | collective-permute-done | bytes 32800 | tf_op jit(solution)/shard_map/ppermute | solution.py:213
  79.9 5.4 %shard_map.89 = (f32[64,1024]{1,0:T(8,128)}, f32[64,128]{1,0:T(8,128)S(1)}) custom-call(f32[64,1024]{1,0:T(8,128)S(1)} %get-tuple-element.16.previous, f32[64,1024]{1,0:T(8,128)S(1)} %get-tuple-element.17.part, f32[72,128]{1,0:T(8,128)S(1)} %collective-permute-done.fetched, f32[64,128]{1,0:T(8,128)S(1)} %get-tuple-element.18.sent_up, ...), custom_call_target="tpu_custom_call" | custom-call | tf_op jit(solution)/shard_map/pallas_call | solution.py:216
  85.4 1.9 %collective-permute-start.5 = (f32[64,128]{1,0:T(8,128)S(1)}, f32[64,128]{1,0:T(8,128)S(1)}, u32[]{:S(2)}, u32[]{:S(2)}) collective-permute-start(f32[64,128]{1,0:T(8,128)S(1)} %get-tuple-element.21), channel_id=1, source_target_pairs={{0,1},{1,2},{2,3},{3,4},{4,5},{5,6},{6,7},{7,8},{8,9},{9,10},{10,1... | collective-permute-start | bytes 98312 | tf_op jit(solution)/shard_map/ppermute | solution.py:224
  87.3 10.8 %collective-permute-done.5.got_up = f32[64,128]{1,0:T(8,128)S(1)} collective-permute-done((f32[64,128]{1,0:T(8,128)S(1)}, f32[64,128]{1,0:T(8,128)S(1)}, u32[]{:S(2)}, u32[]{:S(2)}) %collective-permute-start.5) | collective-permute-done | bytes 32800 | tf_op jit(solution)/shard_map/ppermute | solution.py:224
  98.1 0.7 broadcast_in_dim.2
  98.8 3.6 %all-to-all-start = ((f32[8,64,128]{2,1,0:T(8,128)}), f32[8,64,128]{2,1,0:T(8,128)S(1)}, u32[]{:S(2)}, u32[]{:S(2)}) async-start(f32[8,64,128]{2,1,0:T(8,128)} %broadcast_in_dim.2), calls=%async_computation | async-start | bytes 524288 | tf_op jit(solution)/shard_map/all_to_all | solution.py:228
  102.4 2.0 %shard_map.90 = (f32[64,1024]{1,0:T(8,128)}, f32[64,128]{1,0:T(8,128)S(1)}) custom-call(f32[64,1024]{1,0:T(8,128)} %get-tuple-element.20.part, f32[64,128]{1,0:T(8,128)S(1)} %collective-permute-done.5.got_up, s32[1,128]{1,0:T(1,128)S(1)} %bitcast.21), custom_call_target="tpu_custom_call" | custom-call | tf_op jit(solution)/shard_map/pallas_call | solution.py:225
  104.4 11.6 %all-to-all-done = f32[8,64,128]{2,1,0:T(8,128)S(1)} async-done(((f32[8,64,128]{2,1,0:T(8,128)}), f32[8,64,128]{2,1,0:T(8,128)S(1)}, u32[]{:S(2)}, u32[]{:S(2)}) %all-to-all-start) | async-done | bytes 262176 | tf_op jit(solution)/shard_map/all_to_all | solution.py:228
  116.0 9.2 %all-gather.2.cloned.1.call-done.gathered = f32[512,1024]{1,0:T(8,128)} async-done(((f32[64,1024]{1,0:T(8,128)}), f32[512,1024]{1,0:T(8,128)}) %all-gather.2.cloned.1.call-update) | async-done | bytes 2097168 | tf_op jit(solution)/shard_map/all_gather | solution.py:223
  125.3 1.6 copy-done.3
  126.9 0.9 copy-done.4
  127.8 0.9 shard_map.91
  128.8 24.9 %all_to_all.23 = f32[64,1,512]{2,1,0:T(1,128)S(1)} all-to-all(f32[64,1,512]{2,1,0:T(1,128)S(1)} %copy.9), channel_id=1, replica_groups=mesh['band'=8,'dom'=64] {'dom'}, dimensions={0} | all-to-all | bytes 262144 | tf_op jit(solution)/shard_map/all_to_all | solution.py:237
  153.9 19.0 %all_to_all.24 = f32[64,1,512]{2,1,0:T(1,128)S(1)} all-to-all(f32[64,1,512]{2,1,0:T(1,128)S(1)} %reshape.37), channel_id=1, replica_groups=mesh['band'=8,'dom'=64] {'dom'}, dimensions={0} | all-to-all | bytes 262144 | tf_op jit(solution)/shard_map/all_to_all | solution.py:240
  172.9 0.7 copy.12
  (20 shorter events, 0.4 us)
Async XLA Ops:
  7.2 118.1 %all-gather.2.cloned.1.call-start = ((), (), s32[]{:S(2)}) async-start(), calls=%async_computation.3 | async-start | bytes 2359296 | tf_op jit(solution)/shard_map/all_gather | solution.py:223
  7.2 1.0 copy-start.2
  8.2 0.7 copy-start.6
  8.8 0.7 copy-start.8
  9.8 18.0 %collective-permute-start = (f32[72,128]{1,0:T(8,128)S(1)}, f32[72,128]{1,0:T(8,128)S(1)}, u32[]{:S(2)}, u32[]{:S(2)}) collective-permute-start(f32[72,128]{1,0:T(8,128)S(1)} %shard_map.86), channel_id=1, source_target_pairs={{0,63},{1,0},{2,1},{3,2},{4,3},{5,4},{6,5},{7,6},{8,7},{9,8},{10,9... | collective-permute-start | bytes 110600 | tf_op jit(solution)/shard_map/ppermute | solution.py:204
  27.8 1.0 copy-start
  28.9 0.7 copy-start.5
  29.6 0.7 copy-start.7
  30.3 0.7 copy-start.10
  30.9 49.0 %copy-start.1 = (f32[343,343]{1,0:T(8,128)S(1)}, f32[343,343]{1,0:T(8,128)}, u32[]{:S(2)}) copy-start(f32[343,343]{1,0:T(8,128)} %stiff.5) | copy-start | bytes 1411792
  30.9 71.5 %copy-start.9 = (s32[128]{0:T(128)S(1)}, s32[128]{0:T(128)}, u32[]{:S(2)}) copy-start(s32[128]{0:T(128)} %param.13) | copy-start | bytes 1540
  36.1 13.2 %collective-permute-start.2 = (f32[64,128]{1,0:T(8,128)S(1)}, f32[64,128]{1,0:T(8,128)S(1)}, u32[]{:S(2)}, u32[]{:S(2)}) collective-permute-start(f32[64,128]{1,0:T(8,128)S(1)} %get-tuple-element.14.sent_up), channel_id=1, source_target_pairs={{0,1},{1,2},{2,3},{3,4},{4,5},{5,6},{6,7},{7,8},{8,9},{9,10},{10,1... | collective-permute-start | bytes 98312 | tf_op jit(solution)/shard_map/ppermute | solution.py:213
  38.0 12.9 %collective-permute-start.1 = (f32[64,128]{1,0:T(8,128)S(1)}, f32[64,128]{1,0:T(8,128)S(1)}, u32[]{:S(2)}, u32[]{:S(2)}) collective-permute-start(f32[64,128]{1,0:T(8,128)S(1)} %get-tuple-element.15), channel_id=1, source_target_pairs={{0,63},{1,0},{2,1},{3,2},{4,3},{5,4},{6,5},{7,6},{8,7},{9,8},{10,9... | collective-permute-start | bytes 98312 | tf_op jit(solution)/shard_map/ppermute | solution.py:214
  56.0 13.1 %collective-permute-start.3 = (f32[64,128]{1,0:T(8,128)S(1)}, f32[64,128]{1,0:T(8,128)S(1)}, u32[]{:S(2)}, u32[]{:S(2)}) collective-permute-start(f32[64,128]{1,0:T(8,128)S(1)} %get-tuple-element.19), channel_id=1, source_target_pairs={{0,63},{1,0},{2,1},{3,2},{4,3},{5,4},{6,5},{7,6},{8,7},{9,8},{10,9... | collective-permute-start | bytes 98312 | tf_op jit(solution)/shard_map/ppermute | solution.py:214
  67.2 12.7 %collective-permute-start.4 = (f32[64,128]{1,0:T(8,128)S(1)}, f32[64,128]{1,0:T(8,128)S(1)}, u32[]{:S(2)}, u32[]{:S(2)}) collective-permute-start(f32[64,128]{1,0:T(8,128)S(1)} %get-tuple-element.18.sent_up), channel_id=1, source_target_pairs={{0,1},{1,2},{2,3},{3,4},{4,5},{5,6},{6,7},{7,8},{8,9},{9,10},{10,1... | collective-permute-start | bytes 98312 | tf_op jit(solution)/shard_map/ppermute | solution.py:213
  85.4 12.7 %collective-permute-start.5 = (f32[64,128]{1,0:T(8,128)S(1)}, f32[64,128]{1,0:T(8,128)S(1)}, u32[]{:S(2)}, u32[]{:S(2)}) collective-permute-start(f32[64,128]{1,0:T(8,128)S(1)} %get-tuple-element.21), channel_id=1, source_target_pairs={{0,1},{1,2},{2,3},{3,4},{4,5},{5,6},{6,7},{7,8},{8,9},{9,10},{10,1... | collective-permute-start | bytes 98312 | tf_op jit(solution)/shard_map/ppermute | solution.py:224
  98.8 17.2 %all-to-all-start = ((f32[8,64,128]{2,1,0:T(8,128)}), f32[8,64,128]{2,1,0:T(8,128)S(1)}, u32[]{:S(2)}, u32[]{:S(2)}) async-start(f32[8,64,128]{2,1,0:T(8,128)} %broadcast_in_dim.2), calls=%async_computation | async-start | bytes 524288 | tf_op jit(solution)/shard_map/all_to_all | solution.py:228
  125.3 1.6 copy-start.3
  126.9 0.9 copy-start.4
Sparse Core Ops, SparseCore 0:
  85.5 39.7 all-gather.1

commit v2 on v1

v2 whole, which is shorter than its diff:
```python
import functools

import jax
import jax.numpy as jnp
from jax import lax
from jax.experimental import pallas as pl
from jax.experimental.pallas import tpu as pltpu
from jax.sharding import Mesh, PartitionSpec as P

DEGREE = 3
CENTER = 1.0
HALF_WIDTH = 4.0
LIMIT = 28 * 1024 * 1024
BAND = ("chip", "core")
DOM = ("x", "half", "z")

f32 = jnp.float32
bf16 = jnp.bfloat16


def rounded_up(count, to):
    return -(-count // to) * to


def parts(x, count):
    out = []
    for i in range(count):
        piece = x.astype(bf16)
        out.append(piece)
        if i + 1 < count:
            x = x - piece.astype(f32)
    return out


def dot(a, b):
    return jnp.dot(a, b, preferred_element_type=f32)


def dot_t(a, b):
    return lax.dot_general(a, b, (((1,), (1,)), ((), ())), preferred_element_type=f32)


def one_hot(row, count):
    at = lax.broadcasted_iota(jnp.int32, (count, row.shape[1]), 0)
    return jnp.where(at == row, 1.0, 0.0).astype(bf16)


def picked(x, chosen):
    rows = x.shape[0]
    got = dot(jnp.concatenate(parts(x, 3), axis=0), chosen)
    return got[:rows] + got[rows : 2 * rows] + got[2 * rows :]


def placed(x, chosen):
    rows = x.shape[0]
    got = dot_t(jnp.concatenate(parts(x, 3), axis=0), chosen)
    return got[:rows] + got[rows : 2 * rows] + got[2 * rows :]


def start_kernel(states, inv_mass, shared, message):
    rows, owned = states.shape
    chosen = one_hot(shared[...], owned)
    both = jnp.concatenate(
        [states[...], jnp.broadcast_to(inv_mass[...], (8, owned))], axis=0
    )
    message[...] = picked(both, chosen)


def prepare_kernel(cells, stiff, shared, chosen_all, high, low, chosen, cells_pad, stiff_pad):
    n_cells, npc = cells.shape
    pad = stiff_pad.shape[0]
    nodes = chosen_all.shape[0]
    cells_pad[...] = jnp.full(cells_pad.shape, -1, jnp.int32)
    cells_pad[:n_cells, :npc] = cells[...]
    stiff_pad[...] = jnp.zeros(stiff_pad.shape, f32)
    stiff_pad[:npc, :npc] = stiff[...]
    for c in range(n_cells):
        chosen_all[:, c * pad : (c + 1) * pad] = one_hot(cells_pad[c : c + 1, :], nodes)
    high[...], low[...] = parts(stiff_pad[...], 2)
    chosen[...] = one_hot(shared[...], chosen.shape[0])


def apply_cells(own, ghost, scale, chosen_all, high, low):
    rows, owned = own.shape
    pad = high.shape[0]
    n_cells = chosen_all.shape[1] // pad
    values = jnp.concatenate([own, ghost], axis=1)
    gathered = dot(jnp.concatenate(parts(values, 2), axis=0), chosen_all[...])
    gathered = gathered.astype(bf16)
    stacked = jnp.concatenate(
        [gathered[:rows, c * pad : (c + 1) * pad] for c in range(n_cells)]
        + [gathered[rows:, c * pad : (c + 1) * pad] for c in range(n_cells)],
        axis=0,
    )
    half = n_cells * rows
    by_high = dot(stacked, high[...])
    product = by_high[:half] + by_high[half:] + dot(stacked[:half], low[...])
    product = jnp.concatenate(
        [product[c * rows : (c + 1) * rows] * scale[c] for c in range(n_cells)], axis=1
    )
    summed = dot_t(jnp.concatenate(parts(product, 2), axis=0), chosen_all[...])
    summed = summed[:rows] + summed[rows:]
    return summed[:, :owned], summed[:, owned:]


def is_even():
    return lax.axis_index("z") % 2 == 0


def send_both(up, down, near, far):
    even = is_even()
    near[...] = jnp.where(even, up, down)
    far[...] = jnp.zeros(far.shape, f32)
    far[: down.shape[0], :] = jnp.where(even, down, up)


def first_kernel(
    states, fetched, inv_mass, potential, scale, chosen_all, high, low, chosen,
    far, near, partial,
):
    rows, owned = states.shape
    current = states[...]
    ghost_inv = fetched[rows : rows + 1, :]
    ghost = fetched[:rows, :]
    own_sum, ghost_sum = apply_cells(
        current * inv_mass[...], ghost * ghost_inv, scale, chosen_all, high, low
    )
    up = ghost_inv * ghost_sum * (1.0 / HALF_WIDTH)
    here = (inv_mass[...] * own_sum + (potential[...] - CENTER) * current) * (1.0 / HALF_WIDTH)
    partial[...] = here
    send_both(up, picked(here, chosen[...]), near, far)


def next_kernel(
    last, previous, part, fetched, sent_near, sent_far, got_near, got_far, inv_mass,
    potential, scale, chosen_all, high, low, chosen, *outs,
):
    rows, owned = previous.shape
    even = is_even()
    got_up = jnp.where(even, got_far[:rows, :], got_near[...])
    got_down = jnp.where(even, got_near[...], got_far[:rows, :])
    sent_up = jnp.where(even, sent_near[...], sent_far[:rows, :])
    current = part[...] + placed(got_up, chosen[...])
    ghost_inv = fetched[rows : rows + 1, :]
    ghost = got_down + sent_up
    own_sum, ghost_sum = apply_cells(
        current * inv_mass[...], ghost * ghost_inv, scale, chosen_all, high, low
    )
    up_now = ghost_inv * ghost_sum * (2.0 / HALF_WIDTH)
    here = (inv_mass[...] * own_sum + (potential[...] - CENTER) * current) * (
        2.0 / HALF_WIDTH
    ) - previous[...]
    if last:
        up, partial = outs
        up[...] = up_now
    else:
        far, near, partial, current_out = outs
        current_out[...] = current
        send_both(up_now, picked(here, chosen[...]), near, far)
    partial[...] = here


def finish_kernel(part, got_up, chosen, filtered):
    filtered[...] = part[...] + placed(got_up[...], chosen[...])


def gram_kernel(total_nodes, filtered, sibling, *rest):
    chips = (len(rest) - 4) // 2 + 1
    blocks, lates = rest[: chips - 1], rest[chips - 1 : 2 * chips - 2]
    chosen, out, g_high, g_low = rest[2 * chips - 2 :]
    rows, owned = filtered.shape
    chip = lax.axis_index("chip")
    core = lax.axis_index("core")

    for s in range(chips):
        base = lax.rem(chip - s + chips, chips) * (2 * rows)
        here = pl.ds(pl.multiple_of(base + core * rows, rows), rows)
        other = pl.ds(pl.multiple_of(base + (1 - core) * rows, rows), rows)
        block = filtered if s == 0 else blocks[s - 1]
        g_high[here, :owned], g_low[here, :owned] = parts(block[...], 2)
        if s == 0:
            g_high[here, owned:] = jnp.zeros((rows, g_high.shape[1] - owned), bf16)
            g_low[here, owned:] = jnp.zeros((rows, g_high.shape[1] - owned), bf16)
        else:
            g_high[here, owned:], g_low[here, owned:] = parts(lates[s - 1][...], 2)
        g_high[other, :] = jnp.zeros((rows, g_high.shape[1]), bf16)
        g_low[other, :] = jnp.zeros((rows, g_high.shape[1]), bf16)
    both = jnp.concatenate([filtered[...], sibling[...]], axis=0)
    both = jnp.concatenate([both, picked(both, chosen[...])], axis=1)
    b_high, b_low = parts(both, 2)
    by_high = dot_t(jnp.concatenate([b_high, b_low], axis=0), g_high[...])
    whole = by_high[: 2 * rows] + by_high[2 * rows :] + dot_t(b_high, g_low[...])
    whole = whole * (1.0 / total_nodes)
    out[pl.ds(pl.multiple_of(core * rows, rows), rows), :] = whole[:rows]
    out[pl.ds(pl.multiple_of((1 - core) * rows, rows), rows), :] = whole[rows:]


def per_device(
    states_in, stiffness, cell_scale, potential, inv_mass_sqrt, cell_nodes, shared_nodes
):
    rows, owned = states_in.shape
    shared_count = shared_nodes.shape[0]
    n_cells, npc = cell_nodes.shape
    nodes = owned + shared_count
    pad = rounded_up(npc, 128)
    n_dom = lax.axis_size(DOM)
    n_band = lax.axis_size(BAND)
    chips = lax.axis_size("chip")
    backward = [(i, (i - 1) % n_dom) for i in range(n_dom)]
    forward = [(i, (i + 1) % n_dom) for i in range(n_dom)]
    near_pairs = [(i, i ^ 1) for i in range(n_dom)]
    far_pairs = [(i, (((i + 1) ^ 1) - 1) % n_dom) for i in range(n_dom)]

    in_vmem = pl.BlockSpec(memory_space=pltpu.VMEM)
    in_smem = pl.BlockSpec(memory_space=pltpu.SMEM)
    params = pltpu.CompilerParams(vmem_limit_bytes=LIMIT)
    inv_mass = inv_mass_sqrt.reshape(1, owned)
    pot = potential.reshape(1, owned)
    shared = shared_nodes.reshape(1, shared_count)
    block = jax.ShapeDtypeStruct((rows, owned), f32)
    edge = jax.ShapeDtypeStruct((rows, shared_count), f32)
    tall = jax.ShapeDtypeStruct((rows + 8, shared_count), f32)

    def call(kernel, out_shape, specs, scratch_shapes=()):
        return pl.pallas_call(
            kernel,
            out_shape=out_shape,
            in_specs=specs,
            out_specs=jax.tree.map(lambda _: in_vmem, out_shape),
            scratch_shapes=scratch_shapes,
            compiler_params=params,
        )

    message = call(
        start_kernel, jax.ShapeDtypeStruct((rows + 8, shared_count), f32), [in_vmem] * 3
    )(states_in, inv_mass, shared)
    fetched = lax.ppermute(message, DOM, backward)
    prepared = call(
        prepare_kernel,
        (
            jax.ShapeDtypeStruct((nodes, n_cells * pad), bf16),
            jax.ShapeDtypeStruct((pad, pad), bf16),
            jax.ShapeDtypeStruct((pad, pad), bf16),
            jax.ShapeDtypeStruct((owned, shared_count), bf16),
        ),
        [in_vmem] * 3,
        [pltpu.VMEM((8, pad), jnp.int32), pltpu.VMEM((pad, pad), f32)],
    )(cell_nodes, stiffness, shared)
    chosen = prepared[3]
    fixed = (inv_mass, pot, cell_scale, *prepared)
    fixed_specs = [in_vmem] * 2 + [in_smem] + [in_vmem] * 4
    far, near, partial = call(
        first_kernel, (tall, edge, block), [in_vmem] * 2 + fixed_specs
    )(states_in, fetched, *fixed)
    previous = states_in
    for step in range(DEGREE - 1):
        last = step == DEGREE - 2
        got_near = lax.ppermute(near, DOM, near_pairs)
        got_far = lax.ppermute(far, DOM, far_pairs)
        outs = (edge, block) if last else (tall, edge, block, block)
        results = call(
            functools.partial(next_kernel, last), outs, [in_vmem] * 7 + fixed_specs
        )(previous, partial, fetched, near, far, got_near, got_far, *fixed)
        if last:
            up, partial = results
        else:
            far, near, partial, previous = results

    def from_chip(x, s):
        return lax.ppermute(x, "chip", [(i, (i + s) % chips) for i in range(chips)])

    got_up = lax.ppermute(up, DOM, forward)
    blocks = [from_chip(partial, s) for s in range(1, chips)]
    filtered = call(finish_kernel, block, [in_vmem] * 3)(partial, got_up, chosen)
    lates = [from_chip(got_up, s) for s in range(1, chips)]
    sibling = lax.ppermute(filtered, "core", [(0, 1), (1, 0)])
    gram = call(
        functools.partial(gram_kernel, owned * n_dom),
        jax.ShapeDtypeStruct((2 * rows, n_band * rows), f32),
        [in_vmem] * (2 + 2 * (chips - 1) + 1),
        [pltpu.VMEM((n_band * rows, nodes), bf16)] * 2,
    )(filtered, sibling, *blocks, *lates, chosen)
    columns = n_band * rows
    flat = n_dom // 2
    pieces = lax.all_to_all(
        gram.reshape(2 * flat, rows // flat, columns), ("core", "x", "z"), 0, 0, tiled=True
    )
    mine = jnp.sum(pieces, axis=0)
    spread = lax.all_to_all(
        jnp.broadcast_to(mine[None], (n_dom, rows // flat, columns)), DOM, 0, 0, tiled=True
    )
    n_x, n_half, n_z = (lax.axis_size(name) for name in DOM)
    margin = jnp.sum(spread.reshape(n_x, n_half, n_z, rows // flat, columns), axis=1)
    return filtered, margin.reshape(rows, columns)


def solution(mesh):
    fine = Mesh(mesh.devices.reshape(4, 2, 4, 2, 8), BAND + DOM)
    return jax.shard_map(
        per_device,
        mesh=fine,
        in_specs=(P(BAND, DOM), P(), P(DOM), P(DOM), P(DOM), P(DOM, None), P(DOM)),
        out_specs=(P(BAND, DOM), P(BAND, None)),
        check_vma=False,
    )
```

time: 181 us -> 161 us (0.89)
  the two profiles are of different devices: /device:TPU:2 before, /device:TPU:8 now
where the time goes in v2:
time: 161 us
  starting transfers between devices  58 us (36%)
  blocking collectives  47.4 us (29%)
  waiting for transfers between devices  26.5 us (16%)
  Pallas kernels  18 us (11%)
  local copies, waits for them, and re-layouts  9.59 us (6%)
    all_to_all x1, blocking collectives, per_device(): lax.all_to_all(jnp.broadcast_to(mine[None], (n_dom, rows // flat, columns...  29.2 us
    all_to_all x1, blocking collectives, per_device(): lax.all_to_all(gram.reshape(2 * flat, rows // flat, columns), ('core', 'x...  18.2 us
    ppermute x1, starting transfers between devices, per_device(): fetched = lax.ppermute(message, DOM, backward)  17.5 us
    ppermute x2, starting transfers between devices, per_device(): got_far = lax.ppermute(far, DOM, far_pairs)  17.5 us
    ppermute x6, starting transfers between devices, from_chip(): return lax.ppermute(x, 'chip', [(i, (i + s) % chips) for i in range(chips)])  15.3 us
    ppermute x6, waiting for transfers between devices, from_chip(): return lax.ppermute(x, 'chip', [(i, (i + s) % chips) for i in range(chips)])  15 us
    unnamed x28, local copies, waits for them, and re-layouts  8.62 us
    pallas_call x2, Pallas kernels, per_device(): call(functools.partial(next_kernel, last), outs, [in_vmem] * 7 + fixed_sp...  8.11 us
  transfers between devices with their start and end apart: 13, of which 6 were waited for; matrix products, arithmetic and copies ran while one was open for 0% of the time, Pallas kernels for 2%

profile of v2, /device:TPU:8, one launch (start us, length us, event | category | flops | bytes accessed | tf_op | source)
XLA Modules:
  0.0 160.6 jit_solution(3225253597686935715)
XLA Ops:
  0.7 0.9 copy-done
  3.2 17.5 %collective-permute-start = (f32[72,128]{1,0:T(8,128)S(1)}, f32[72,128]{1,0:T(8,128)S(1)}, u32[]{:S(2)}, u32[]{:S(2)}) collective-permute-start(f32[72,128]{1,0:T(8,128)S(1)} %shard_map.86), channel_id=1, source_target_pairs={{0,63},{1,0},{2,1},{3,2},{4,3},{5,4},{6,5},{7,6},{8,7},{9,8},{10,9... | collective-permute-start | bytes 110600 | tf_op jit(solution)/shard_map/ppermute | solution.py:237
  20.7 1.0 copy-done.3
  23.1 2.9 %shard_map.87 = (bf16[1152,2304]{1,0:T(8,128)(2,1)S(1)}, bf16[384,384]{1,0:T(8,128)(2,1)S(1)}, bf16[384,384]{1,0:T(8,128)(2,1)S(1)}, bf16[1024,128]{1,0:T(8,128)(2,1)S(1)}) custom-call(s32[6,343]{1,0:T(8,128)S(1)} %copy-done.9, f32[343,343]{1,0:T(8,128)S(1)} %copy-done.3, s32[1,128]{1,0:T(1,128)S(1)} %bitcast.12), custom_call_target="tpu_custom_call" | custom-call | tf_op jit(solution)/shard_map/pallas_call | solution.py:238
  26.1 0.9 copy-done.1
  29.1 4.0 %shard_map.88 = (f32[72,128]{1,0:T(8,128)S(1)}, f32[64,128]{1,0:T(8,128)S(1)}, f32[64,1024]{1,0:T(8,128)S(1)}) custom-call(f32[64,1024]{1,0:T(8,128)S(1)} %copy-done.1, f32[72,128]{1,0:T(8,128)S(1)} %collective-permute-done.fetched, f32[1,1024]{1,0:T(1,128)S(1)} %bitcast.5, f32[1,1024]{1,0:T(1,128)S(1)} %bitcast.8, f32[6]{0:T(128)S(1)} %copy-done.10, ...), custom_call_target="tpu_custom_call" | custom-call | tf_op jit(solution)/shard_map/pallas_call | solution.py:252
  33.1 9.0 %collective-permute-start.2 = (f32[72,128]{1,0:T(8,128)S(1)}, f32[72,128]{1,0:T(8,128)S(1)}, u32[]{:S(2)}, u32[]{:S(2)}) collective-permute-start(f32[72,128]{1,0:T(8,128)S(1)} %get-tuple-element.21.sent_far), channel_id=1, source_target_pairs={{0,63},{1,2},{2,1},{3,4},{4,3},{5,6},{6,5},{7,8},{8,7},{9,10},{10,... | collective-permute-start | bytes 110600 | tf_op jit(solution)/shard_map/ppermute | solution.py:259
  42.1 1.9 %collective-permute-start.1 = (f32[64,128]{1,0:T(8,128)S(1)}, f32[64,128]{1,0:T(8,128)S(1)}, u32[]{:S(2)}, u32[]{:S(2)}) collective-permute-start(f32[64,128]{1,0:T(8,128)S(1)} %get-tuple-element.20.sent_near), channel_id=1, source_target_pairs={{0,1},{1,0},{2,3},{3,2},{4,5},{5,4},{6,7},{7,6},{8,9},{9,8},{10,11... | collective-permute-start | bytes 98312 | tf_op jit(solution)/shard_map/ppermute | solution.py:258
  44.1 3.9 %collective-permute-done.1.got_near = f32[64,128]{1,0:T(8,128)S(1)} collective-permute-done((f32[64,128]{1,0:T(8,128)S(1)}, f32[64,128]{1,0:T(8,128)S(1)}, u32[]{:S(2)}, u32[]{:S(2)}) %collective-permute-start.1) | collective-permute-done | bytes 32800 | tf_op jit(solution)/shard_map/ppermute | solution.py:258
  48.0 4.2 %shard_map.89 = (f32[72,128]{1,0:T(8,128)S(1)}, f32[64,128]{1,0:T(8,128)S(1)}, f32[64,1024]{1,0:T(8,128)S(1)}, f32[64,1024]{1,0:T(8,128)S(1)}) custom-call(f32[64,1024]{1,0:T(8,128)S(1)} %copy-done.1, f32[64,1024]{1,0:T(8,128)S(1)} %get-tuple-element.19.part, f32[72,128]{1,0:T(8,128)S(1)} %collective-permute-done.fetched, ...), custom_call_target="tpu_custom_call" | custom-call | tf_op jit(solution)/shard_map/pallas_call | solution.py:261
  52.2 8.5 %collective-permute-start.4 = (f32[72,128]{1,0:T(8,128)S(1)}, f32[72,128]{1,0:T(8,128)S(1)}, u32[]{:S(2)}, u32[]{:S(2)}) collective-permute-start(f32[72,128]{1,0:T(8,128)S(1)} %get-tuple-element.25.sent_far), channel_id=1, source_target_pairs={{0,63},{1,2},{2,1},{3,4},{4,3},{5,6},{6,5},{7,8},{8,7},{9,10},{10,... | collective-permute-start | bytes 110600 | tf_op jit(solution)/shard_map/ppermute | solution.py:259
  60.7 1.9 %collective-permute-start.3 = (f32[64,128]{1,0:T(8,128)S(1)}, f32[64,128]{1,0:T(8,128)S(1)}, u32[]{:S(2)}, u32[]{:S(2)}) collective-permute-start(f32[64,128]{1,0:T(8,128)S(1)} %get-tuple-element.24.sent_near), channel_id=1, source_target_pairs={{0,1},{1,0},{2,3},{3,2},{4,5},{5,4},{6,7},{7,6},{8,9},{9,8},{10,11... | collective-permute-start | bytes 98312 | tf_op jit(solution)/shard_map/ppermute | solution.py:258
  62.6 3.9 %collective-permute-done.3.got_near = f32[64,128]{1,0:T(8,128)S(1)} collective-permute-done((f32[64,128]{1,0:T(8,128)S(1)}, f32[64,128]{1,0:T(8,128)S(1)}, u32[]{:S(2)}, u32[]{:S(2)}) %collective-permute-start.3) | collective-permute-done | bytes 32800 | tf_op jit(solution)/shard_map/ppermute | solution.py:258
  66.5 3.9 %shard_map.90 = (f32[64,128]{1,0:T(8,128)S(1)}, f32[64,1024]{1,0:T(8,128)S(1)}) custom-call(f32[64,1024]{1,0:T(8,128)S(1)} %get-tuple-element.22.previous, f32[64,1024]{1,0:T(8,128)S(1)} %get-tuple-element.23.part, f32[72,128]{1,0:T(8,128)S(1)} %collective-permute-done.fetched, f32[64,128]{1,0:T(8,128)S(1)} %get-tuple-element.24.sent_near, ...), custom_call_target="tpu_custom_call" | custom-call | tf_op jit(solution)/shard_map/pallas_call | solution.py:261
  70.4 1.9 %collective-permute-start.5 = (f32[64,128]{1,0:T(8,128)S(1)}, f32[64,128]{1,0:T(8,128)S(1)}, u32[]{:S(2)}, u32[]{:S(2)}) collective-permute-start(f32[64,128]{1,0:T(8,128)S(1)} %get-tuple-element.27), channel_id=1, source_target_pairs={{0,1},{1,2},{2,3},{3,4},{4,5},{5,6},{6,7},{7,8},{8,9},{9,10},{10,1... | collective-permute-start | bytes 98312 | tf_op jit(solution)/shard_map/ppermute | solution.py:272
  72.3 2.5 %collective-permute-start.9 = (f32[64,1024]{1,0:T(8,128)S(1)}, f32[64,1024]{1,0:T(8,128)S(1)}, u32[]{:S(2)}, u32[]{:S(2)}) collective-permute-start(f32[64,1024]{1,0:T(8,128)S(1)} %get-tuple-element.26.part), channel_id=1, source_target_pairs={{0,384},{128,0},{256,128},{384,256},{1,385},{129,1},{257,129},{385... | collective-permute-start | bytes 786440 | tf_op jit(solution)/shard_map/ppermute | solution.py:270
  74.9 2.7 %collective-permute-start.8 = (f32[64,1024]{1,0:T(8,128)S(1)}, f32[64,1024]{1,0:T(8,128)S(1)}, u32[]{:S(2)}, u32[]{:S(2)}) collective-permute-start(f32[64,1024]{1,0:T(8,128)S(1)} %get-tuple-element.26.part), channel_id=1, source_target_pairs={{0,256},{128,384},{256,0},{384,128},{1,257},{129,385},{257,1},{385... | collective-permute-start | bytes 786440 | tf_op jit(solution)/shard_map/ppermute | solution.py:270
  77.6 3.6 %collective-permute-start.7 = (f32[64,1024]{1,0:T(8,128)S(1)}, f32[64,1024]{1,0:T(8,128)S(1)}, u32[]{:S(2)}, u32[]{:S(2)}) collective-permute-start(f32[64,1024]{1,0:T(8,128)S(1)} %get-tuple-element.26.part), channel_id=1, source_target_pairs={{0,128},{128,256},{256,384},{384,0},{1,129},{129,257},{257,385},{3... | collective-permute-start | bytes 786440 | tf_op jit(solution)/shard_map/ppermute | solution.py:270
  81.2 3.7 %collective-permute-done.5.got_up = f32[64,128]{1,0:T(8,128)S(1)} collective-permute-done((f32[64,128]{1,0:T(8,128)S(1)}, f32[64,128]{1,0:T(8,128)S(1)}, u32[]{:S(2)}, u32[]{:S(2)}) %collective-permute-start.5) | collective-permute-done | bytes 32800 | tf_op jit(solution)/shard_map/ppermute | solution.py:272
  84.9 1.0 shard_map.91.filtered
  85.9 1.9 %collective-permute-start.6 = (f32[64,1024]{1,0:T(8,128)}, f32[64,1024]{1,0:T(8,128)S(1)}, u32[]{:S(2)}, u32[]{:S(2)}) collective-permute-start(f32[64,1024]{1,0:T(8,128)} %shard_map.91.filtered), channel_id=1, source_target_pairs={{0,64},{64,0},{1,65},{65,1},{2,66},{66,2},{3,67},{67,3},{4,68},{68... | collective-permute-start | bytes 786440 | tf_op jit(solution)/shard_map/ppermute | solution.py:276
  87.8 2.5 %collective-permute-start.12 = (f32[64,128]{1,0:T(8,128)S(1)}, f32[64,128]{1,0:T(8,128)S(1)}, u32[]{:S(2)}, u32[]{:S(2)}) collective-permute-start(f32[64,128]{1,0:T(8,128)S(1)} %collective-permute-done.5.got_up), channel_id=1, source_target_pairs={{0,384},{128,0},{256,128},{384,256},{1,385},{129,1},{257,129},{385... | collective-permute-start | bytes 98312 | tf_op jit(solution)/shard_map/ppermute | solution.py:270
  90.3 6.5 %collective-permute-done.12.rest_5_ = f32[64,128]{1,0:T(8,128)S(1)} collective-permute-done((f32[64,128]{1,0:T(8,128)S(1)}, f32[64,128]{1,0:T(8,128)S(1)}, u32[]{:S(2)}, u32[]{:S(2)}) %collective-permute-start.12) | collective-permute-done | bytes 32800 | tf_op jit(solution)/shard_map/ppermute | solution.py:270
  96.8 1.9 %collective-permute-start.11 = (f32[64,128]{1,0:T(8,128)S(1)}, f32[64,128]{1,0:T(8,128)S(1)}, u32[]{:S(2)}, u32[]{:S(2)}) collective-permute-start(f32[64,128]{1,0:T(8,128)S(1)} %collective-permute-done.5.got_up), channel_id=1, source_target_pairs={{0,256},{128,384},{256,0},{384,128},{1,257},{129,385},{257,1},{385... | collective-permute-start | bytes 98312 | tf_op jit(solution)/shard_map/ppermute | solution.py:270
  98.7 4.8 %collective-permute-done.11.rest_4_ = f32[64,128]{1,0:T(8,128)S(1)} collective-permute-done((f32[64,128]{1,0:T(8,128)S(1)}, f32[64,128]{1,0:T(8,128)S(1)}, u32[]{:S(2)}, u32[]{:S(2)}) %collective-permute-start.11) | collective-permute-done | bytes 32800 | tf_op jit(solution)/shard_map/ppermute | solution.py:270
  103.5 2.1 %collective-permute-start.10 = (f32[64,128]{1,0:T(8,128)S(1)}, f32[64,128]{1,0:T(8,128)S(1)}, u32[]{:S(2)}, u32[]{:S(2)}) collective-permute-start(f32[64,128]{1,0:T(8,128)S(1)} %collective-permute-done.5.got_up), channel_id=1, source_target_pairs={{0,128},{128,256},{256,384},{384,0},{1,129},{129,257},{257,385},{3... | collective-permute-start | bytes 98312 | tf_op jit(solution)/shard_map/ppermute | solution.py:270
  105.6 3.7 %collective-permute-done.10.rest_3_ = f32[64,128]{1,0:T(8,128)S(1)} collective-permute-done((f32[64,128]{1,0:T(8,128)S(1)}, f32[64,128]{1,0:T(8,128)S(1)}, u32[]{:S(2)}, u32[]{:S(2)}) %collective-permute-start.10) | collective-permute-done | bytes 32800 | tf_op jit(solution)/shard_map/ppermute | solution.py:270
  109.3 0.9 copy-done.2
  110.3 1.7 %shard_map.92 = f32[128,512]{1,0:T(8,128)S(1)} custom-call(f32[64,1024]{1,0:T(8,128)S(1)} %copy-done.2, f32[64,1024]{1,0:T(8,128)S(1)} %collective-permute-done.6.sibling, f32[64,1024]{1,0:T(8,128)S(1)} %collective-permute-done.7.rest_0_, f32[64,1024]{1,0:T(8,128)S(1)} %collective-permute-done.8.rest_1_, f32[64,1024]{1,0:T(8,128)S(1)} %collective-permute-done.9.rest_2_, ...), custom_call_target="tpu_custom_call" | custom-call | tf_op jit(solution)/shard_map/pallas_call | solution.py:277
  112.1 18.2 %all_to_all.10 = f32[64,2,512]{2,1,0:T(2,128)S(1)} all-to-all(f32[64,2,512]{2,1,0:T(2,128)S(1)} %reshape.26), channel_id=1, replica_groups=mesh['chip'=4,'core'=2,'x'=4,'half'=2,'z'=8] {'core','x','z'}, dimensions={0} | all-to-all | bytes 524288 | tf_op jit(solution)/shard_map/all_to_all | solution.py:285
  130.4 29.2 %all_to_all.11 = f32[64,2,512]{2,1,0:T(2,128)S(1)} all-to-all(f32[64,2,512]{2,1,0:T(2,128)S(1)} %broadcast_in_dim.2), channel_id=1, replica_groups=mesh['chip'=4,'core'=2,'x'=4,'half'=2,'z'=8] {'x','half','z'}, dimensions={0} | all-to-all | bytes 524288 | tf_op jit(solution)/shard_map/all_to_all | solution.py:289
  159.8 0.7 reshape.28
  (36 shorter events, 5.6 us)
Async XLA Ops:
  0.6 47.3 %copy-start.11 = (f32[6]{0:T(128)S(1)}, f32[6]{0:T(128)}, u32[]{:S(2)}) copy-start(f32[6]{0:T(128)} %scale.5) | copy-start | bytes 76
  0.6 1.0 copy-start
  1.6 0.7 copy-start.4
  2.3 0.7 copy-start.12
  3.2 22.9 %collective-permute-start = (f32[72,128]{1,0:T(8,128)S(1)}, f32[72,128]{1,0:T(8,128)S(1)}, u32[]{:S(2)}, u32[]{:S(2)}) collective-permute-start(f32[72,128]{1,0:T(8,128)S(1)} %shard_map.86), channel_id=1, source_target_pairs={{0,63},{1,0},{2,1},{3,2},{4,3},{5,4},{6,5},{7,6},{8,7},{9,8},{10,9... | collective-permute-start | bytes 110600 | tf_op jit(solution)/shard_map/ppermute | solution.py:237
  20.7 1.0 copy-start.3
  21.8 0.7 copy-start.9
  22.5 0.7 copy-start.13
  26.1 1.0 copy-start.1
  27.1 0.7 copy-start.5
  27.7 0.7 copy-start.7
  28.4 0.7 copy-start.10
  29.1 37.4 %copy-start.6 = (f32[1024]{0:T(1024)S(1)}, f32[1024]{0:T(1024)}, u32[]{:S(2)}) copy-start(f32[1024]{0:T(1024)} %param.11) | copy-start | bytes 12292
  29.1 37.4 %copy-start.8 = (f32[1024]{0:T(1024)S(1)}, f32[1024]{0:T(1024)}, u32[]{:S(2)}) copy-start(f32[1024]{0:T(1024)} %param.10) | copy-start | bytes 12292
  33.1 14.8 %collective-permute-start.2 = (f32[72,128]{1,0:T(8,128)S(1)}, f32[72,128]{1,0:T(8,128)S(1)}, u32[]{:S(2)}, u32[]{:S(2)}) collective-permute-start(f32[72,128]{1,0:T(8,128)S(1)} %get-tuple-element.21.sent_far), channel_id=1, source_target_pairs={{0,63},{1,2},{2,1},{3,4},{4,3},{5,6},{6,5},{7,8},{8,7},{9,10},{10,... | collective-permute-start | bytes 110600 | tf_op jit(solution)/shard_map/ppermute | solution.py:259
  42.1 5.8 %collective-permute-start.1 = (f32[64,128]{1,0:T(8,128)S(1)}, f32[64,128]{1,0:T(8,128)S(1)}, u32[]{:S(2)}, u32[]{:S(2)}) collective-permute-start(f32[64,128]{1,0:T(8,128)S(1)} %get-tuple-element.20.sent_near), channel_id=1, source_target_pairs={{0,1},{1,0},{2,3},{3,2},{4,5},{5,4},{6,7},{7,6},{8,9},{9,8},{10,11... | collective-permute-start | bytes 98312 | tf_op jit(solution)/shard_map/ppermute | solution.py:258
  52.2 14.3 %collective-permute-start.4 = (f32[72,128]{1,0:T(8,128)S(1)}, f32[72,128]{1,0:T(8,128)S(1)}, u32[]{:S(2)}, u32[]{:S(2)}) collective-permute-start(f32[72,128]{1,0:T(8,128)S(1)} %get-tuple-element.25.sent_far), channel_id=1, source_target_pairs={{0,63},{1,2},{2,1},{3,4},{4,3},{5,6},{6,5},{7,8},{8,7},{9,10},{10,... | collective-permute-start | bytes 110600 | tf_op jit(solution)/shard_map/ppermute | solution.py:259
  60.7 5.8 %collective-permute-start.3 = (f32[64,128]{1,0:T(8,128)S(1)}, f32[64,128]{1,0:T(8,128)S(1)}, u32[]{:S(2)}, u32[]{:S(2)}) collective-permute-start(f32[64,128]{1,0:T(8,128)S(1)} %get-tuple-element.24.sent_near), channel_id=1, source_target_pairs={{0,1},{1,0},{2,3},{3,2},{4,5},{5,4},{6,7},{7,6},{8,9},{9,8},{10,11... | collective-permute-start | bytes 98312 | tf_op jit(solution)/shard_map/ppermute | solution.py:258
  70.4 14.5 %collective-permute-start.5 = (f32[64,128]{1,0:T(8,128)S(1)}, f32[64,128]{1,0:T(8,128)S(1)}, u32[]{:S(2)}, u32[]{:S(2)}) collective-permute-start(f32[64,128]{1,0:T(8,128)S(1)} %get-tuple-element.27), channel_id=1, source_target_pairs={{0,1},{1,2},{2,3},{3,4},{4,5},{5,6},{6,7},{7,8},{8,9},{9,10},{10,1... | collective-permute-start | bytes 98312 | tf_op jit(solution)/shard_map/ppermute | solution.py:272
  72.3 37.0 %collective-permute-start.9 = (f32[64,1024]{1,0:T(8,128)S(1)}, f32[64,1024]{1,0:T(8,128)S(1)}, u32[]{:S(2)}, u32[]{:S(2)}) collective-permute-start(f32[64,1024]{1,0:T(8,128)S(1)} %get-tuple-element.26.part), channel_id=1, source_target_pairs={{0,384},{128,0},{256,128},{384,256},{1,385},{129,1},{257,129},{385... | collective-permute-start | bytes 786440 | tf_op jit(solution)/shard_map/ppermute | solution.py:270
  74.9 34.4 %collective-permute-start.8 = (f32[64,1024]{1,0:T(8,128)S(1)}, f32[64,1024]{1,0:T(8,128)S(1)}, u32[]{:S(2)}, u32[]{:S(2)}) collective-permute-start(f32[64,1024]{1,0:T(8,128)S(1)} %get-tuple-element.26.part), channel_id=1, source_target_pairs={{0,256},{128,384},{256,0},{384,128},{1,257},{129,385},{257,1},{385... | collective-permute-start | bytes 786440 | tf_op jit(solution)/shard_map/ppermute | solution.py:270
  77.6 31.7 %collective-permute-start.7 = (f32[64,1024]{1,0:T(8,128)S(1)}, f32[64,1024]{1,0:T(8,128)S(1)}, u32[]{:S(2)}, u32[]{:S(2)}) collective-permute-start(f32[64,1024]{1,0:T(8,128)S(1)} %get-tuple-element.26.part), channel_id=1, source_target_pairs={{0,128},{128,256},{256,384},{384,0},{1,129},{129,257},{257,385},{3... | collective-permute-start | bytes 786440 | tf_op jit(solution)/shard_map/ppermute | solution.py:270
  85.9 23.4 %collective-permute-start.6 = (f32[64,1024]{1,0:T(8,128)}, f32[64,1024]{1,0:T(8,128)S(1)}, u32[]{:S(2)}, u32[]{:S(2)}) collective-permute-start(f32[64,1024]{1,0:T(8,128)} %shard_map.91.filtered), channel_id=1, source_target_pairs={{0,64},{64,0},{1,65},{65,1},{2,66},{66,2},{3,67},{67,3},{4,68},{68... | collective-permute-start | bytes 786440 | tf_op jit(solution)/shard_map/ppermute | solution.py:276
  87.8 9.0 %collective-permute-start.12 = (f32[64,128]{1,0:T(8,128)S(1)}, f32[64,128]{1,0:T(8,128)S(1)}, u32[]{:S(2)}, u32[]{:S(2)}) collective-permute-start(f32[64,128]{1,0:T(8,128)S(1)} %collective-permute-done.5.got_up), channel_id=1, source_target_pairs={{0,384},{128,0},{256,128},{384,256},{1,385},{129,1},{257,129},{385... | collective-permute-start | bytes 98312 | tf_op jit(solution)/shard_map/ppermute | solution.py:270
  96.8 6.7 %collective-permute-start.11 = (f32[64,128]{1,0:T(8,128)S(1)}, f32[64,128]{1,0:T(8,128)S(1)}, u32[]{:S(2)}, u32[]{:S(2)}) collective-permute-start(f32[64,128]{1,0:T(8,128)S(1)} %collective-permute-done.5.got_up), channel_id=1, source_target_pairs={{0,256},{128,384},{256,0},{384,128},{1,257},{129,385},{257,1},{385... | collective-permute-start | bytes 98312 | tf_op jit(solution)/shard_map/ppermute | solution.py:270
  103.5 5.8 %collective-permute-start.10 = (f32[64,128]{1,0:T(8,128)S(1)}, f32[64,128]{1,0:T(8,128)S(1)}, u32[]{:S(2)}, u32[]{:S(2)}) collective-permute-start(f32[64,128]{1,0:T(8,128)S(1)} %collective-permute-done.5.got_up), channel_id=1, source_target_pairs={{0,128},{128,256},{256,384},{384,0},{1,129},{129,257},{257,385},{3... | collective-permute-start | bytes 98312 | tf_op jit(solution)/shard_map/ppermute | solution.py:270
  109.3 1.0 copy-start.2

commit v3 on v2

v3 whole, which is shorter than its diff:
```python
import functools

import jax
import jax.numpy as jnp
from jax import lax
from jax.experimental import pallas as pl
from jax.experimental.pallas import tpu as pltpu
from jax.sharding import Mesh, PartitionSpec as P

DEGREE = 3
CENTER = 1.0
HALF_WIDTH = 4.0
LIMIT = 28 * 1024 * 1024
BAND = ("chip", "core")
DOM = ("x", "half", "z")

f32 = jnp.float32
bf16 = jnp.bfloat16


def rounded_up(count, to):
    return -(-count // to) * to


def parts(x, count):
    out = []
    for i in range(count):
        piece = x.astype(bf16)
        out.append(piece)
        if i + 1 < count:
            x = x - piece.astype(f32)
    return out


def dot(a, b):
    return jnp.dot(a, b, preferred_element_type=f32)


def dot_t(a, b):
    return lax.dot_general(a, b, (((1,), (1,)), ((), ())), preferred_element_type=f32)


def one_hot(row, count):
    at = lax.broadcasted_iota(jnp.int32, (count, row.shape[1]), 0)
    return jnp.where(at == row, 1.0, 0.0).astype(bf16)


def picked(x, chosen):
    rows = x.shape[0]
    got = dot(jnp.concatenate(parts(x, 3), axis=0), chosen)
    return got[:rows] + got[rows : 2 * rows] + got[2 * rows :]


def placed(x, chosen):
    rows = x.shape[0]
    got = dot_t(jnp.concatenate(parts(x, 3), axis=0), chosen)
    return got[:rows] + got[rows : 2 * rows] + got[2 * rows :]


def start_kernel(
    states, inv_mass, shared, potential, cells, stiff,
    message, states_in, inv_in, shared_in, pot_in, cells_in, stiff_in, done,
):
    moves = [
        pltpu.make_async_copy(source, target, done.at[i])
        for i, (source, target) in enumerate(
            [
                (shared, shared_in), (inv_mass, inv_in), (states, states_in),
                (potential, pot_in), (cells, cells_in), (stiff, stiff_in),
            ]
        )
    ]
    for move in moves:
        move.start()
    for move in moves[:3]:
        move.wait()
    owned = states_in.shape[1]
    both = jnp.concatenate(
        [states_in[...], jnp.broadcast_to(inv_in[...], (8, owned))], axis=0
    )
    message[...] = picked(both, one_hot(shared_in[...], owned))
    for move in moves[3:]:
        move.wait()


def prepare_kernel(
    cells, stiff, shared, scale, chosen_all, high, low, chosen, scale_row, cells_pad, stiff_pad
):
    n_cells, npc = cells.shape
    pad = stiff_pad.shape[0]
    nodes = chosen_all.shape[0]
    cells_pad[...] = jnp.full(cells_pad.shape, -1, jnp.int32)
    cells_pad[:n_cells, :npc] = cells[...]
    stiff_pad[...] = jnp.zeros(stiff_pad.shape, f32)
    stiff_pad[:npc, :npc] = stiff[...]
    for c in range(n_cells):
        at = slice(c * pad, (c + 1) * pad)
        chosen_all[:, at] = one_hot(cells_pad[c : c + 1, :], nodes)
        scale_row[:, at] = jnp.full((1, pad), scale[c], f32)
    high[...], low[...] = parts(stiff_pad[...], 2)
    chosen[...] = one_hot(shared[...], chosen.shape[0])


def apply_cells(own, ghost, scale, chosen_all, high, low):
    rows, owned = own.shape
    pad = high.shape[0]
    n_cells = chosen_all.shape[1] // pad
    values = jnp.concatenate([own, ghost], axis=1)
    gathered = dot(jnp.concatenate(parts(values, 2), axis=0), chosen_all[...])
    gathered = gathered.astype(bf16)
    stacked = jnp.concatenate(
        [gathered[:rows, c * pad : (c + 1) * pad] for c in range(n_cells)]
        + [gathered[rows:, c * pad : (c + 1) * pad] for c in range(n_cells)],
        axis=0,
    )
    half = n_cells * rows
    by_high = dot(stacked, high[...])
    product = by_high[:half] + by_high[half:] + dot(stacked[:half], low[...])
    product = jnp.concatenate(
        [product[c * rows : (c + 1) * rows] for c in range(n_cells)], axis=1
    ) * scale[...]
    summed = dot_t(jnp.concatenate(parts(product, 2), axis=0), chosen_all[...])
    summed = summed[:rows] + summed[rows:]
    return summed[:, :owned], summed[:, owned:]


def is_even():
    return lax.axis_index("z") % 2 == 0


def send_both(up, down, near, far):
    even = is_even()
    near[...] = jnp.where(even, up, down)
    far[...] = jnp.zeros(far.shape, f32)
    far[: down.shape[0], :] = jnp.where(even, down, up)


def got_both(near, far):
    rows = near.shape[0]
    even = is_even()
    up = jnp.where(even, far[:rows, :], near[...])
    down = jnp.where(even, near[...], far[:rows, :])
    return up, down


def first_kernel(
    states, fetched, inv_mass, potential, scale, chosen_all, high, low, chosen,
    far, near, partial,
):
    rows, owned = states.shape
    current = states[...]
    ghost_inv = fetched[rows : rows + 1, :]
    ghost = fetched[:rows, :]
    own_sum, ghost_sum = apply_cells(
        current * inv_mass[...], ghost * ghost_inv, scale, chosen_all, high, low
    )
    up = ghost_inv * ghost_sum * (1.0 / HALF_WIDTH)
    here = (inv_mass[...] * own_sum + (potential[...] - CENTER) * current) * (1.0 / HALF_WIDTH)
    partial[:, :owned] = here
    partial[:, owned:] = up
    send_both(up, picked(here, chosen[...]), near, far)


def complete(part, got_near, got_far, chosen):
    owned = chosen.shape[0]
    got_up, got_down = got_both(got_near, got_far)
    return part[:, :owned] + placed(got_up, chosen[...]), part[:, owned:] + got_down


def next_kernel(
    previous, part, fetched, got_near, got_far, inv_mass, potential, scale, chosen_all,
    high, low, chosen, far, near, partial, current_out,
):
    rows, owned = current_out.shape
    current, ghost = complete(part, got_near, got_far, chosen)
    ghost_inv = fetched[rows : rows + 1, :]
    own_sum, ghost_sum = apply_cells(
        current * inv_mass[...], ghost * ghost_inv, scale, chosen_all, high, low
    )
    up = ghost_inv * ghost_sum * (2.0 / HALF_WIDTH)
    here = (inv_mass[...] * own_sum + (potential[...] - CENTER) * current) * (
        2.0 / HALF_WIDTH
    ) - previous[...]
    current_out[...] = current
    partial[:, :owned] = here
    partial[:, owned:] = up
    send_both(up, picked(here, chosen[...]), near, far)


def finish_kernel(part, got_near, got_far, chosen, filtered, left):
    owned = filtered.shape[1]
    current, ghost = complete(part, got_near, got_far, chosen)
    filtered[...] = current
    left[:, :owned] = current
    left[:, owned:] = ghost


def gram_kernel(total_nodes, left, sibling, *rest):
    blocks, (out, g_high, g_low) = rest[:-3], rest[-3:]
    chips = len(blocks)
    rows = left.shape[0]
    chip = lax.axis_index("chip")
    core = lax.axis_index("core")
    for s in range(chips):
        at = pl.ds(pl.multiple_of(lax.rem(chip - s + chips, chips) * rows, rows), rows)
        g_high[at, :], g_low[at, :] = parts(blocks[s][...], 2)
    high, low = parts(jnp.concatenate([left[...], sibling[...]], axis=0), 2)
    by_high = dot_t(jnp.concatenate([high, low], axis=0), g_high[...])
    whole = by_high[: 2 * rows] + by_high[2 * rows :] + dot_t(high, g_low[...])
    whole = whole * (1.0 / total_nodes)
    out[pl.ds(pl.multiple_of(core * rows, rows), rows), :] = whole[:rows]
    out[pl.ds(pl.multiple_of((1 - core) * rows, rows), rows), :] = whole[rows:]


def fold_kernel(rows, pieces, out):
    count = pieces.shape[0] // 2
    copies = out.shape[0]
    sums = []
    for core in range(2):
        total = pieces[core * count]
        for i in range(1, count):
            total = total + pieces[core * count + i]
        sums.append(total)
    chips = pieces.shape[2] // rows
    ordered = jnp.concatenate(
        [sums[core][:, i * rows : (i + 1) * rows] for i in range(chips) for core in range(2)],
        axis=1,
    )
    for i in range(copies):
        out[i] = ordered


def per_device(
    states_in, stiffness, cell_scale, potential, inv_mass_sqrt, cell_nodes, shared_nodes
):
    rows, owned = states_in.shape
    shared_count = shared_nodes.shape[0]
    n_cells, npc = cell_nodes.shape
    nodes = owned + shared_count
    pad = rounded_up(npc, 128)
    n_dom = lax.axis_size(DOM)
    n_band = lax.axis_size(BAND)
    chips = lax.axis_size("chip")
    backward = [(i, (i - 1) % n_dom) for i in range(n_dom)]
    near_pairs = [(i, i ^ 1) for i in range(n_dom)]
    far_pairs = [(i, (((i + 1) ^ 1) - 1) % n_dom) for i in range(n_dom)]

    in_vmem = pl.BlockSpec(memory_space=pltpu.VMEM)
    in_smem = pl.BlockSpec(memory_space=pltpu.SMEM)
    in_hbm = pl.BlockSpec(memory_space=pltpu.HBM)
    params = pltpu.CompilerParams(vmem_limit_bytes=LIMIT)

    def shape_of(*sizes, dtype=f32):
        return jax.ShapeDtypeStruct(sizes, dtype)

    block = shape_of(rows, owned)
    wide = shape_of(rows, nodes)
    edge = shape_of(rows, shared_count)
    tall = shape_of(rows + 8, shared_count)

    def call(kernel, out_shape, specs, scratch_shapes=()):
        return pl.pallas_call(
            kernel,
            out_shape=out_shape,
            in_specs=specs,
            out_specs=jax.tree.map(lambda _: in_vmem, out_shape),
            scratch_shapes=scratch_shapes,
            compiler_params=params,
        )

    message, states, inv_mass, shared, pot, cells, stiff = call(
        start_kernel,
        (
            tall, block, shape_of(1, owned), shape_of(1, shared_count, dtype=jnp.int32),
            shape_of(1, owned), shape_of(n_cells, npc, dtype=jnp.int32), shape_of(npc, npc),
        ),
        [in_hbm] * 6,
        [pltpu.SemaphoreType.DMA((6,))],
    )(
        *(
            pltpu.with_memory_space_constraint(x, pltpu.HBM)
            for x in (
                states_in, inv_mass_sqrt.reshape(1, owned),
                shared_nodes.reshape(1, shared_count), potential.reshape(1, owned),
                cell_nodes, stiffness,
            )
        )
    )
    fetched = lax.ppermute(message, DOM, backward)
    prepared = call(
        prepare_kernel,
        (
            shape_of(nodes, n_cells * pad, dtype=bf16),
            shape_of(pad, pad, dtype=bf16),
            shape_of(pad, pad, dtype=bf16),
            shape_of(owned, shared_count, dtype=bf16),
            shape_of(1, n_cells * pad),
        ),
        [in_vmem] * 3 + [in_smem],
        [pltpu.VMEM((8, pad), jnp.int32), pltpu.VMEM((pad, pad), f32)],
    )(cells, stiff, shared, cell_scale)
    *matrices, chosen, scale_row = prepared
    fixed = (inv_mass, pot, scale_row, *matrices, chosen)

    def swapped(near, far):
        return lax.ppermute(near, DOM, near_pairs), lax.ppermute(far, DOM, far_pairs)

    far, near, partial = call(first_kernel, (tall, edge, wide), [in_vmem] * 9)(
        states, fetched, *fixed
    )
    previous = states
    for _ in range(DEGREE - 1):
        far, near, partial, previous = call(
            next_kernel, (tall, edge, wide, block), [in_vmem] * 12
        )(previous, partial, fetched, *swapped(near, far), *fixed)

    blocks = [partial] + [
        lax.ppermute(partial, "chip", [(i, (i + s) % chips) for i in range(chips)])
        for s in range(1, chips)
    ]
    filtered, left = call(finish_kernel, (block, wide), [in_vmem] * 4)(
        partial, *swapped(near, far), chosen
    )
    sibling = lax.ppermute(left, "core", [(0, 1), (1, 0)])
    gram = call(
        functools.partial(gram_kernel, owned * n_dom),
        shape_of(2 * rows, chips * rows),
        [in_vmem] * (2 + chips),
        [pltpu.VMEM((chips * rows, nodes), bf16)] * 2,
    )(left, sibling, *blocks)

    n_z = lax.axis_size("z")
    n_across = lax.axis_size(("x", "half"))
    each = rows // n_z
    pieces = lax.all_to_all(
        gram.reshape(2 * n_z, each, chips * rows), ("core", "z"), 0, 0, tiled=True
    )
    mine = call(functools.partial(fold_kernel, rows), shape_of(n_across, each, n_band * rows), [in_vmem])(pieces)
    spread = lax.all_to_all(mine, ("x", "half"), 0, 0, tiled=True)
    mine = jnp.sum(spread, axis=0)
    margin = lax.all_to_all(
        jnp.broadcast_to(mine[None], (n_z, *mine.shape)), "z", 0, 0, tiled=True
    )
    return filtered, margin.reshape(rows, n_band * rows)


def solution(mesh):
    fine = Mesh(mesh.devices.reshape(4, 2, 4, 2, 8), BAND + DOM)
    return jax.shard_map(
        per_device,
        mesh=fine,
        in_specs=(P(BAND, DOM), P(), P(DOM), P(DOM), P(DOM), P(DOM, None), P(DOM)),
        out_specs=(P(BAND, DOM), P(BAND, None)),
        check_vma=False,
    )
```

time: 161 us -> 143 us (0.89)
  the two profiles are of different devices: /device:TPU:8 before, /device:TPU:16 now
where the time goes in v3:
time: 143 us; the launch traced here: 142 us
  starting transfers between devices  60.3 us (42%)
  blocking collectives  39.6 us (28%)
  waiting for transfers between devices  22.4 us (16%)
  Pallas kernels  17.8 us (12%)
    ppermute x3, starting transfers between devices, swapped(): lax.ppermute(far, DOM, far_pairs)  26.1 us
    ppermute x1, starting transfers between devices, per_device(): fetched = lax.ppermute(message, DOM, backward)  16.6 us
    all_to_all x1, blocking collectives, per_device(): spread = lax.all_to_all(mine, ('x', 'half'), 0, 0, tiled=True)  15.6 us
    ppermute x3, waiting for transfers between devices, per_device(): lax.ppermute(partial, 'chip', [(i, (i + s) % chips) for i in range(chips)])  14.7 us
    all_to_all x1, blocking collectives, per_device(): lax.all_to_all(jnp.broadcast_to(mine[None], (n_z, *mine.shape)), 'z', 0,...  13 us
    all_to_all x1, blocking collectives, per_device(): lax.all_to_all(gram.reshape(2 * n_z, each, chips * rows), ('core', 'z'),...  11 us
    ppermute x3, starting transfers between devices, per_device(): lax.ppermute(partial, 'chip', [(i, (i + s) % chips) for i in range(chips)])  9.88 us
    pallas_call x2, Pallas kernels, per_device(): call(next_kernel, (tall, edge, wide, block), [in_vmem] * 12)  7.78 us
  transfers between devices with their start and end apart: 11, of which 5 were waited for; matrix products, arithmetic and copies ran while one was open for 0% of the time, Pallas kernels for 3%

profile of v3, /device:TPU:16, one launch (start us, length us, event | category | flops | bytes accessed | tf_op | source)
XLA Modules:
  0.0 142.3 jit_solution(9822834697455276003)
XLA Ops:
  0.6 1.3 shard_map.86
  2.0 16.6 %collective-permute-start = (f32[72,128]{1,0:T(8,128)S(1)}, f32[72,128]{1,0:T(8,128)S(1)}, u32[]{:S(2)}, u32[]{:S(2)}) collective-permute-start(f32[72,128]{1,0:T(8,128)S(1)} %get-tuple-element.27), channel_id=1, source_target_pairs={{0,63},{1,0},{2,1},{3,2},{4,3},{5,4},{6,5},{7,6},{8,7},{9,8},{10,9... | collective-permute-start | bytes 110600 | tf_op jit(solution)/shard_map/ppermute | solution.py:289
  18.6 0.0 copy-start
  18.6 0.6 copy-done
  19.2 3.5 %shard_map.87 = (bf16[1152,2304]{1,0:T(8,128)(2,1)S(1)}, bf16[384,384]{1,0:T(8,128)(2,1)S(1)}, bf16[384,384]{1,0:T(8,128)(2,1)S(1)}, bf16[1024,128]{1,0:T(8,128)(2,1)S(1)}, f32[1,2304]{1,0:T(1,128)S(1)}) custom-call(s32[6,343]{1,0:T(8,128)S(1)} %get-tuple-element.30.cells, f32[343,343]{1,0:T(8,128)S(1)} %get-tuple-element.31.stiff, ...), custom_call_target="tpu_custom_call" | custom-call | tf_op jit(solution)/shard_map/pallas_call | solution.py:290
  22.7 3.5 %shard_map.88 = (f32[72,128]{1,0:T(8,128)S(1)}, f32[64,128]{1,0:T(8,128)S(1)}, f32[64,1152]{1,0:T(8,128)S(1)}) custom-call(f32[64,1024]{1,0:T(8,128)S(1)} %get-tuple-element.26.states.previous, f32[72,128]{1,0:T(8,128)S(1)} %collective-permute-done.fetched, f32[1,1024]{1,0:T(1,128)S(1)} %get-tuple-element.28.inv_mass, ...), custom_call_target="tpu_custom_call" | custom-call | tf_op jit(solution)/shard_map/pallas_call | solution.py:308
  26.2 9.8 %collective-permute-start.2 = (f32[72,128]{1,0:T(8,128)S(1)}, f32[72,128]{1,0:T(8,128)S(1)}, u32[]{:S(2)}, u32[]{:S(2)}) collective-permute-start(f32[72,128]{1,0:T(8,128)S(1)} %get-tuple-element.40), channel_id=1, source_target_pairs={{0,63},{1,2},{2,1},{3,4},{4,3},{5,6},{6,5},{7,8},{8,7},{9,10},{10,... | collective-permute-start | bytes 110600 | tf_op jit(solution)/shard_map/ppermute | solution.py:306
  36.1 1.9 %collective-permute-start.1 = (f32[64,128]{1,0:T(8,128)S(1)}, f32[64,128]{1,0:T(8,128)S(1)}, u32[]{:S(2)}, u32[]{:S(2)}) collective-permute-start(f32[64,128]{1,0:T(8,128)S(1)} %get-tuple-element.39), channel_id=1, source_target_pairs={{0,1},{1,0},{2,3},{3,2},{4,5},{5,4},{6,7},{7,6},{8,9},{9,8},{10,11... | collective-permute-start | bytes 98312 | tf_op jit(solution)/shard_map/ppermute | solution.py:306
  38.0 3.9 %collective-permute-done.1.got_near = f32[64,128]{1,0:T(8,128)S(1)} collective-permute-done((f32[64,128]{1,0:T(8,128)S(1)}, f32[64,128]{1,0:T(8,128)S(1)}, u32[]{:S(2)}, u32[]{:S(2)}) %collective-permute-start.1) | collective-permute-done | bytes 32800 | tf_op jit(solution)/shard_map/ppermute | solution.py:306
  41.9 0.0 collective-permute-done.2.got_far
  41.9 3.7 %shard_map.89 = (f32[72,128]{1,0:T(8,128)S(1)}, f32[64,128]{1,0:T(8,128)S(1)}, f32[64,1152]{1,0:T(8,128)S(1)}, f32[64,1024]{1,0:T(8,128)S(1)}) custom-call(f32[64,1024]{1,0:T(8,128)S(1)} %get-tuple-element.26.states.previous, f32[64,1152]{1,0:T(8,128)S(1)} %get-tuple-element.38.part, f32[72,128]{1,0:T(8,128)S(1)} %collective-permute-done.fetched, ...), custom_call_target="tpu_custom_call" | custom-call | tf_op jit(solution)/shard_map/pallas_call | solution.py:313
  45.6 8.2 %collective-permute-start.4 = (f32[72,128]{1,0:T(8,128)S(1)}, f32[72,128]{1,0:T(8,128)S(1)}, u32[]{:S(2)}, u32[]{:S(2)}) collective-permute-start(f32[72,128]{1,0:T(8,128)S(1)} %get-tuple-element.44), channel_id=1, source_target_pairs={{0,63},{1,2},{2,1},{3,4},{4,3},{5,6},{6,5},{7,8},{8,7},{9,10},{10,... | collective-permute-start | bytes 110600 | tf_op jit(solution)/shard_map/ppermute | solution.py:306
  53.7 1.9 %collective-permute-start.3 = (f32[64,128]{1,0:T(8,128)S(1)}, f32[64,128]{1,0:T(8,128)S(1)}, u32[]{:S(2)}, u32[]{:S(2)}) collective-permute-start(f32[64,128]{1,0:T(8,128)S(1)} %get-tuple-element.43), channel_id=1, source_target_pairs={{0,1},{1,0},{2,3},{3,2},{4,5},{5,4},{6,7},{7,6},{8,9},{9,8},{10,11... | collective-permute-start | bytes 98312 | tf_op jit(solution)/shard_map/ppermute | solution.py:306
  55.7 3.9 %collective-permute-done.3.got_near = f32[64,128]{1,0:T(8,128)S(1)} collective-permute-done((f32[64,128]{1,0:T(8,128)S(1)}, f32[64,128]{1,0:T(8,128)S(1)}, u32[]{:S(2)}, u32[]{:S(2)}) %collective-permute-start.3) | collective-permute-done | bytes 32800 | tf_op jit(solution)/shard_map/ppermute | solution.py:306
  59.5 0.0 collective-permute-done.4.got_far
  59.6 4.1 %shard_map.90 = (f32[72,128]{1,0:T(8,128)S(1)}, f32[64,128]{1,0:T(8,128)S(1)}, f32[64,1152]{1,0:T(8,128)S(1)}, f32[64,1024]{1,0:T(8,128)}) custom-call(f32[64,1024]{1,0:T(8,128)S(1)} %get-tuple-element.41.previous, f32[64,1152]{1,0:T(8,128)S(1)} %get-tuple-element.42.part, f32[72,128]{1,0:T(8,128)S(1)} %collective-permute-done.fetched, ...), custom_call_target="tpu_custom_call" | custom-call | tf_op jit(solution)/shard_map/pallas_call | solution.py:313
  63.7 8.1 %collective-permute-start.6 = (f32[72,128]{1,0:T(8,128)S(1)}, f32[72,128]{1,0:T(8,128)S(1)}, u32[]{:S(2)}, u32[]{:S(2)}) collective-permute-start(f32[72,128]{1,0:T(8,128)S(1)} %get-tuple-element.47), channel_id=1, source_target_pairs={{0,63},{1,2},{2,1},{3,4},{4,3},{5,6},{6,5},{7,8},{8,7},{9,10},{10,... | collective-permute-start | bytes 110600 | tf_op jit(solution)/shard_map/ppermute | solution.py:306
  71.8 1.9 %collective-permute-start.5 = (f32[64,128]{1,0:T(8,128)S(1)}, f32[64,128]{1,0:T(8,128)S(1)}, u32[]{:S(2)}, u32[]{:S(2)}) collective-permute-start(f32[64,128]{1,0:T(8,128)S(1)} %get-tuple-element.46), channel_id=1, source_target_pairs={{0,1},{1,0},{2,3},{3,2},{4,5},{5,4},{6,7},{7,6},{8,9},{9,8},{10,11... | collective-permute-start | bytes 98312 | tf_op jit(solution)/shard_map/ppermute | solution.py:306
  73.7 4.0 %collective-permute-start.10 = (f32[64,1152]{1,0:T(8,128)S(1)}, f32[64,1152]{1,0:T(8,128)S(1)}, u32[]{:S(2)}, u32[]{:S(2)}) collective-permute-start(f32[64,1152]{1,0:T(8,128)S(1)} %get-tuple-element.45.part.rest_0_), channel_id=1, source_target_pairs={{0,384},{128,0},{256,128},{384,256},{1,385},{129,1},{257,129},{385... | collective-permute-start | bytes 884744 | tf_op jit(solution)/shard_map/ppermute | solution.py:318
  77.7 3.0 %collective-permute-start.9 = (f32[64,1152]{1,0:T(8,128)S(1)}, f32[64,1152]{1,0:T(8,128)S(1)}, u32[]{:S(2)}, u32[]{:S(2)}) collective-permute-start(f32[64,1152]{1,0:T(8,128)S(1)} %get-tuple-element.45.part.rest_0_), channel_id=1, source_target_pairs={{0,256},{128,384},{256,0},{384,128},{1,257},{129,385},{257,1},{385... | collective-permute-start | bytes 884744 | tf_op jit(solution)/shard_map/ppermute | solution.py:318
  80.7 2.9 %collective-permute-start.8 = (f32[64,1152]{1,0:T(8,128)S(1)}, f32[64,1152]{1,0:T(8,128)S(1)}, u32[]{:S(2)}, u32[]{:S(2)}) collective-permute-start(f32[64,1152]{1,0:T(8,128)S(1)} %get-tuple-element.45.part.rest_0_), channel_id=1, source_target_pairs={{0,128},{128,256},{256,384},{384,0},{1,129},{129,257},{257,385},{3... | collective-permute-start | bytes 884744 | tf_op jit(solution)/shard_map/ppermute | solution.py:318
  83.7 1.0 shard_map.91
  84.6 1.9 %collective-permute-start.7 = (f32[64,1152]{1,0:T(8,128)S(1)}, f32[64,1152]{1,0:T(8,128)S(1)}, u32[]{:S(2)}, u32[]{:S(2)}) collective-permute-start(f32[64,1152]{1,0:T(8,128)S(1)} %get-tuple-element.49.left), channel_id=1, source_target_pairs={{0,64},{64,0},{1,65},{65,1},{2,66},{66,2},{3,67},{67,3},{4,68},{68... | collective-permute-start | bytes 884744 | tf_op jit(solution)/shard_map/ppermute | solution.py:324
  86.5 9.5 %collective-permute-done.10.rest_3_ = f32[64,1152]{1,0:T(8,128)S(1)} collective-permute-done((f32[64,1152]{1,0:T(8,128)S(1)}, f32[64,1152]{1,0:T(8,128)S(1)}, u32[]{:S(2)}, u32[]{:S(2)}) %collective-permute-start.10) | collective-permute-done | bytes 294944 | tf_op jit(solution)/shard_map/ppermute | solution.py:318
  96.1 3.2 %collective-permute-done.9.rest_2_ = f32[64,1152]{1,0:T(8,128)S(1)} collective-permute-done((f32[64,1152]{1,0:T(8,128)S(1)}, f32[64,1152]{1,0:T(8,128)S(1)}, u32[]{:S(2)}, u32[]{:S(2)}) %collective-permute-start.9) | collective-permute-done | bytes 294944 | tf_op jit(solution)/shard_map/ppermute | solution.py:318
  99.2 2.0 %collective-permute-done.8.rest_1_ = f32[64,1152]{1,0:T(8,128)S(1)} collective-permute-done((f32[64,1152]{1,0:T(8,128)S(1)}, f32[64,1152]{1,0:T(8,128)S(1)}, u32[]{:S(2)}, u32[]{:S(2)}) %collective-permute-start.8) | collective-permute-done | bytes 294944 | tf_op jit(solution)/shard_map/ppermute | solution.py:318
  101.2 0.6 shard_map.92
  101.9 11.0 %all_to_all.15.pieces = f32[16,8,256]{2,1,0:T(8,128)S(1)} all-to-all(f32[16,8,256]{2,1,0:T(8,128)S(1)} %bitcast.5), channel_id=1, replica_groups=mesh['chip'=4,'core'=2,'x'=4,'half'=2,'z'=8] {'core','z'}, dimensions={0} | all-to-all | bytes 262144 | tf_op jit(solution)/shard_map/all_to_all | solution.py:335
  112.9 0.1 shard_map.93
  113.0 15.6 %all_to_all.16 = f32[8,8,512]{2,1,0:T(8,128)S(1)} all-to-all(f32[8,8,512]{2,1,0:T(8,128)S(1)} %shard_map.93), channel_id=1, replica_groups=mesh['chip'=4,'core'=2,'x'=4,'half'=2,'z'=8] {'x','half'}, dimensions={0} | all-to-all | bytes 262144 | tf_op jit(solution)/shard_map/all_to_all | solution.py:339
  128.6 13.0 %all_to_all.17 = f32[8,8,512]{2,1,0:T(8,128)S(1)} all-to-all(f32[8,8,512]{2,1,0:T(8,128)S(1)} %broadcast_in_dim.2), channel_id=1, replica_groups=mesh['chip'=4,'core'=2,'x'=4,'half'=2,'z'=8] {'z'}, dimensions={0} | all-to-all | bytes 262144 | tf_op jit(solution)/shard_map/all_to_all | solution.py:341
  141.6 0.7 copy.10
  (6 shorter events, 0.0 us)
Async XLA Ops:
  2.0 20.8 %collective-permute-start = (f32[72,128]{1,0:T(8,128)S(1)}, f32[72,128]{1,0:T(8,128)S(1)}, u32[]{:S(2)}, u32[]{:S(2)}) collective-permute-start(f32[72,128]{1,0:T(8,128)S(1)} %get-tuple-element.27), channel_id=1, source_target_pairs={{0,63},{1,0},{2,1},{3,2},{4,3},{5,4},{6,5},{7,6},{8,7},{9,8},{10,9... | collective-permute-start | bytes 110600 | tf_op jit(solution)/shard_map/ppermute | solution.py:289
  18.6 0.7 copy-start
  26.2 15.6 %collective-permute-start.2 = (f32[72,128]{1,0:T(8,128)S(1)}, f32[72,128]{1,0:T(8,128)S(1)}, u32[]{:S(2)}, u32[]{:S(2)}) collective-permute-start(f32[72,128]{1,0:T(8,128)S(1)} %get-tuple-element.40), channel_id=1, source_target_pairs={{0,63},{1,2},{2,1},{3,4},{4,3},{5,6},{6,5},{7,8},{8,7},{9,10},{10,... | collective-permute-start | bytes 110600 | tf_op jit(solution)/shard_map/ppermute | solution.py:306
  36.1 5.8 %collective-permute-start.1 = (f32[64,128]{1,0:T(8,128)S(1)}, f32[64,128]{1,0:T(8,128)S(1)}, u32[]{:S(2)}, u32[]{:S(2)}) collective-permute-start(f32[64,128]{1,0:T(8,128)S(1)} %get-tuple-element.39), channel_id=1, source_target_pairs={{0,1},{1,0},{2,3},{3,2},{4,5},{5,4},{6,7},{7,6},{8,9},{9,8},{10,11... | collective-permute-start | bytes 98312 | tf_op jit(solution)/shard_map/ppermute | solution.py:306
  45.6 14.0 %collective-permute-start.4 = (f32[72,128]{1,0:T(8,128)S(1)}, f32[72,128]{1,0:T(8,128)S(1)}, u32[]{:S(2)}, u32[]{:S(2)}) collective-permute-start(f32[72,128]{1,0:T(8,128)S(1)} %get-tuple-element.44), channel_id=1, source_target_pairs={{0,63},{1,2},{2,1},{3,4},{4,3},{5,6},{6,5},{7,8},{8,7},{9,10},{10,... | collective-permute-start | bytes 110600 | tf_op jit(solution)/shard_map/ppermute | solution.py:306
  53.7 5.8 %collective-permute-start.3 = (f32[64,128]{1,0:T(8,128)S(1)}, f32[64,128]{1,0:T(8,128)S(1)}, u32[]{:S(2)}, u32[]{:S(2)}) collective-permute-start(f32[64,128]{1,0:T(8,128)S(1)} %get-tuple-element.43), channel_id=1, source_target_pairs={{0,1},{1,0},{2,3},{3,2},{4,5},{5,4},{6,7},{7,6},{8,9},{9,8},{10,11... | collective-permute-start | bytes 98312 | tf_op jit(solution)/shard_map/ppermute | solution.py:306
  63.7 20.0 %collective-permute-start.6 = (f32[72,128]{1,0:T(8,128)S(1)}, f32[72,128]{1,0:T(8,128)S(1)}, u32[]{:S(2)}, u32[]{:S(2)}) collective-permute-start(f32[72,128]{1,0:T(8,128)S(1)} %get-tuple-element.47), channel_id=1, source_target_pairs={{0,63},{1,2},{2,1},{3,4},{4,3},{5,6},{6,5},{7,8},{8,7},{9,10},{10,... | collective-permute-start | bytes 110600 | tf_op jit(solution)/shard_map/ppermute | solution.py:306
  71.8 11.8 %collective-permute-start.5 = (f32[64,128]{1,0:T(8,128)S(1)}, f32[64,128]{1,0:T(8,128)S(1)}, u32[]{:S(2)}, u32[]{:S(2)}) collective-permute-start(f32[64,128]{1,0:T(8,128)S(1)} %get-tuple-element.46), channel_id=1, source_target_pairs={{0,1},{1,0},{2,3},{3,2},{4,5},{5,4},{6,7},{7,6},{8,9},{9,8},{10,11... | collective-permute-start | bytes 98312 | tf_op jit(solution)/shard_map/ppermute | solution.py:306
  73.7 22.3 %collective-permute-start.10 = (f32[64,1152]{1,0:T(8,128)S(1)}, f32[64,1152]{1,0:T(8,128)S(1)}, u32[]{:S(2)}, u32[]{:S(2)}) collective-permute-start(f32[64,1152]{1,0:T(8,128)S(1)} %get-tuple-element.45.part.rest_0_), channel_id=1, source_target_pairs={{0,384},{128,0},{256,128},{384,256},{1,385},{129,1},{257,129},{385... | collective-permute-start | bytes 884744 | tf_op jit(solution)/shard_map/ppermute | solution.py:318
  77.7 21.5 %collective-permute-start.9 = (f32[64,1152]{1,0:T(8,128)S(1)}, f32[64,1152]{1,0:T(8,128)S(1)}, u32[]{:S(2)}, u32[]{:S(2)}) collective-permute-start(f32[64,1152]{1,0:T(8,128)S(1)} %get-tuple-element.45.part.rest_0_), channel_id=1, source_target_pairs={{0,256},{128,384},{256,0},{384,128},{1,257},{129,385},{257,1},{385... | collective-permute-start | bytes 884744 | tf_op jit(solution)/shard_map/ppermute | solution.py:318
  80.7 20.5 %collective-permute-start.8 = (f32[64,1152]{1,0:T(8,128)S(1)}, f32[64,1152]{1,0:T(8,128)S(1)}, u32[]{:S(2)}, u32[]{:S(2)}) collective-permute-start(f32[64,1152]{1,0:T(8,128)S(1)} %get-tuple-element.45.part.rest_0_), channel_id=1, source_target_pairs={{0,128},{128,256},{256,384},{384,0},{1,129},{129,257},{257,385},{3... | collective-permute-start | bytes 884744 | tf_op jit(solution)/shard_map/ppermute | solution.py:318
  84.6 16.6 %collective-permute-start.7 = (f32[64,1152]{1,0:T(8,128)S(1)}, f32[64,1152]{1,0:T(8,128)S(1)}, u32[]{:S(2)}, u32[]{:S(2)}) collective-permute-start(f32[64,1152]{1,0:T(8,128)S(1)} %get-tuple-element.49.left), channel_id=1, source_target_pairs={{0,64},{64,0},{1,65},{65,1},{2,66},{66,2},{3,67},{67,3},{4,68},{68... | collective-permute-start | bytes 884744 | tf_op jit(solution)/shard_map/ppermute | solution.py:324

commit v4 on v3

--- a/solution.py
+++ b/solution.py
@@ -41,8 +41,8 @@
 
 
 def one_hot(row, count):
-    at = lax.broadcasted_iota(jnp.int32, (count, row.shape[1]), 0)
-    return jnp.where(at == row, 1.0, 0.0).astype(bf16)
+    at = lax.broadcasted_iota(jnp.int16, (count, row.shape[1]), 0)
+    return jnp.where(at == row.astype(jnp.int16), jnp.array(1, bf16), jnp.array(0, bf16))
 
 
 def picked(x, chosen):
@@ -161,9 +161,8 @@
     send_both(up, picked(here, chosen[...]), near, far)
 
 
-def complete(part, got_near, got_far, chosen):
+def complete(part, got_up, got_down, chosen):
     owned = chosen.shape[0]
-    got_up, got_down = got_both(got_near, got_far)
     return part[:, :owned] + placed(got_up, chosen[...]), part[:, owned:] + got_down
 
 
@@ -172,7 +171,7 @@
     high, low, chosen, far, near, partial, current_out,
 ):
     rows, owned = current_out.shape
-    current, ghost = complete(part, got_near, got_far, chosen)
+    current, ghost = complete(part, *got_both(got_near, got_far), chosen)
     ghost_inv = fetched[rows : rows + 1, :]
     own_sum, ghost_sum = apply_cells(
         current * inv_mass[...], ghost * ghost_inv, scale, chosen_all, high, low
@@ -189,7 +188,7 @@
 
 def finish_kernel(part, got_near, got_far, chosen, filtered, left):
     owned = filtered.shape[1]
-    current, ghost = complete(part, got_near, got_far, chosen)
+    current, ghost = complete(part, *got_both(got_near, got_far), chosen)
     filtered[...] = current
     left[:, :owned] = current
     left[:, owned:] = ghost
@@ -197,13 +196,12 @@
 
 def gram_kernel(total_nodes, left, sibling, *rest):
     blocks, (out, g_high, g_low) = rest[:-3], rest[-3:]
-    chips = len(blocks)
     rows = left.shape[0]
     chip = lax.axis_index("chip")
     core = lax.axis_index("core")
-    for s in range(chips):
-        at = pl.ds(pl.multiple_of(lax.rem(chip - s + chips, chips) * rows, rows), rows)
-        g_high[at, :], g_low[at, :] = parts(blocks[s][...], 2)
+    for s, block in enumerate(blocks):
+        at = pl.ds(pl.multiple_of((chip ^ s) * rows, rows), rows)
+        g_high[at, :], g_low[at, :] = parts(block[...], 2)
     high, low = parts(jnp.concatenate([left[...], sibling[...]], axis=0), 2)
     by_high = dot_t(jnp.concatenate([high, low], axis=0), g_high[...])
     whole = by_high[: 2 * rows] + by_high[2 * rows :] + dot_t(high, g_low[...])
@@ -314,10 +312,12 @@
             next_kernel, (tall, edge, wide, block), [in_vmem] * 12
         )(previous, partial, fetched, *swapped(near, far), *fixed)
 
-    blocks = [partial] + [
-        lax.ppermute(partial, "chip", [(i, (i + s) % chips) for i in range(chips)])
-        for s in range(1, chips)
-    ]
+    def from_chip(x, s):
+        return lax.ppermute(x, "chip", [(i, i ^ s) for i in range(chips)])
+
+    second = from_chip(partial, 2)
+    blocks = [partial, from_chip(partial, 1), second, from_chip(second, 1)]
+
     filtered, left = call(finish_kernel, (block, wide), [in_vmem] * 4)(
         partial, *swapped(near, far), chosen
     )

time: 143 us -> 141 us (0.986)
  the two profiles are of different devices: /device:TPU:16 before, /device:TPU:8 now
where the time goes in v4:
time: 141 us
  starting transfers between devices  61.2 us (43%)
  blocking collectives  38.8 us (28%)
  waiting for transfers between devices  22.6 us (16%)
  Pallas kernels  15.9 us (11%)
    ppermute x3, starting transfers between devices, swapped(): lax.ppermute(far, DOM, far_pairs)  28.8 us
    ppermute x1, starting transfers between devices, per_device(): fetched = lax.ppermute(message, DOM, backward)  17.5 us
    all_to_all x1, blocking collectives, per_device(): spread = lax.all_to_all(mine, ('x', 'half'), 0, 0, tiled=True)  15.7 us
    all_to_all x1, blocking collectives, per_device(): lax.all_to_all(jnp.broadcast_to(mine[None], (n_z, *mine.shape)), 'z', 0,...  12.1 us
    all_to_all x1, blocking collectives, per_device(): lax.all_to_all(gram.reshape(2 * n_z, each, chips * rows), ('core', 'z'),...  11.1 us
    ppermute x3, waiting for transfers between devices, from_chip(): return lax.ppermute(x, 'chip', [(i, i ^ s) for i in range(chips)])  9.36 us
    ppermute x3, waiting for transfers between devices, swapped(): lax.ppermute(near, DOM, near_pairs)  8.3 us
    pallas_call x2, Pallas kernels, per_device(): call(next_kernel, (tall, edge, wide, block), [in_vmem] * 12)  7.77 us
  transfers between devices with their start and end apart: 11, of which 6 were waited for; matrix products, arithmetic and copies ran while one was open for 0% of the time, Pallas kernels for 2%

profile of v4, /device:TPU:8, one launch (start us, length us, event | category | flops | bytes accessed | tf_op | source)
XLA Modules:
  0.0 140.7 jit_solution(6877478712041163947)
XLA Ops:
  0.6 1.3 shard_map.86
  2.0 17.5 %collective-permute-start = (f32[72,128]{1,0:T(8,128)S(1)}, f32[72,128]{1,0:T(8,128)S(1)}, u32[]{:S(2)}, u32[]{:S(2)}) collective-permute-start(f32[72,128]{1,0:T(8,128)S(1)} %get-tuple-element.27), channel_id=1, source_target_pairs={{0,63},{1,0},{2,1},{3,2},{4,3},{5,4},{6,5},{7,6},{8,7},{9,8},{10,9... | collective-permute-start | bytes 110600 | tf_op jit(solution)/shard_map/ppermute | solution.py:287
  19.5 0.0 copy-start
  19.5 0.6 copy-done
  20.1 1.6 %shard_map.87 = (bf16[1152,2304]{1,0:T(8,128)(2,1)S(1)}, bf16[384,384]{1,0:T(8,128)(2,1)S(1)}, bf16[384,384]{1,0:T(8,128)(2,1)S(1)}, bf16[1024,128]{1,0:T(8,128)(2,1)S(1)}, f32[1,2304]{1,0:T(1,128)S(1)}) custom-call(s32[6,343]{1,0:T(8,128)S(1)} %get-tuple-element.30.cells, f32[343,343]{1,0:T(8,128)S(1)} %get-tuple-element.31.stiff, ...), custom_call_target="tpu_custom_call" | custom-call | tf_op jit(solution)/shard_map/pallas_call | solution.py:288
  21.7 0.0 collective-permute-done.fetched
  21.7 3.5 %shard_map.88 = (f32[72,128]{1,0:T(8,128)S(1)}, f32[64,128]{1,0:T(8,128)S(1)}, f32[64,1152]{1,0:T(8,128)S(1)}) custom-call(f32[64,1024]{1,0:T(8,128)S(1)} %get-tuple-element.26.states.previous, f32[72,128]{1,0:T(8,128)S(1)} %collective-permute-done.fetched, f32[1,1024]{1,0:T(1,128)S(1)} %get-tuple-element.28.inv_mass, ...), custom_call_target="tpu_custom_call" | custom-call | tf_op jit(solution)/shard_map/pallas_call | solution.py:306
  25.2 12.1 %collective-permute-start.2 = (f32[72,128]{1,0:T(8,128)S(1)}, f32[72,128]{1,0:T(8,128)S(1)}, u32[]{:S(2)}, u32[]{:S(2)}) collective-permute-start(f32[72,128]{1,0:T(8,128)S(1)} %get-tuple-element.40), channel_id=1, source_target_pairs={{0,63},{1,2},{2,1},{3,4},{4,3},{5,6},{6,5},{7,8},{8,7},{9,10},{10,... | collective-permute-start | bytes 110600 | tf_op jit(solution)/shard_map/ppermute | solution.py:304
  37.4 1.9 %collective-permute-start.1 = (f32[64,128]{1,0:T(8,128)S(1)}, f32[64,128]{1,0:T(8,128)S(1)}, u32[]{:S(2)}, u32[]{:S(2)}) collective-permute-start(f32[64,128]{1,0:T(8,128)S(1)} %get-tuple-element.39), channel_id=1, source_target_pairs={{0,1},{1,0},{2,3},{3,2},{4,5},{5,4},{6,7},{7,6},{8,9},{9,8},{10,11... | collective-permute-start | bytes 98312 | tf_op jit(solution)/shard_map/ppermute | solution.py:304
  39.3 3.9 %collective-permute-done.1.got_near = f32[64,128]{1,0:T(8,128)S(1)} collective-permute-done((f32[64,128]{1,0:T(8,128)S(1)}, f32[64,128]{1,0:T(8,128)S(1)}, u32[]{:S(2)}, u32[]{:S(2)}) %collective-permute-start.1) | collective-permute-done | bytes 32800 | tf_op jit(solution)/shard_map/ppermute | solution.py:304
  43.2 3.7 %shard_map.89 = (f32[72,128]{1,0:T(8,128)S(1)}, f32[64,128]{1,0:T(8,128)S(1)}, f32[64,1152]{1,0:T(8,128)S(1)}, f32[64,1024]{1,0:T(8,128)S(1)}) custom-call(f32[64,1024]{1,0:T(8,128)S(1)} %get-tuple-element.26.states.previous, f32[64,1152]{1,0:T(8,128)S(1)} %get-tuple-element.38.part, f32[72,128]{1,0:T(8,128)S(1)} %collective-permute-done.fetched, ...), custom_call_target="tpu_custom_call" | custom-call | tf_op jit(solution)/shard_map/pallas_call | solution.py:311
  46.9 8.5 %collective-permute-start.4 = (f32[72,128]{1,0:T(8,128)S(1)}, f32[72,128]{1,0:T(8,128)S(1)}, u32[]{:S(2)}, u32[]{:S(2)}) collective-permute-start(f32[72,128]{1,0:T(8,128)S(1)} %get-tuple-element.44), channel_id=1, source_target_pairs={{0,63},{1,2},{2,1},{3,4},{4,3},{5,6},{6,5},{7,8},{8,7},{9,10},{10,... | collective-permute-start | bytes 110600 | tf_op jit(solution)/shard_map/ppermute | solution.py:304
  55.4 1.9 %collective-permute-start.3 = (f32[64,128]{1,0:T(8,128)S(1)}, f32[64,128]{1,0:T(8,128)S(1)}, u32[]{:S(2)}, u32[]{:S(2)}) collective-permute-start(f32[64,128]{1,0:T(8,128)S(1)} %get-tuple-element.43), channel_id=1, source_target_pairs={{0,1},{1,0},{2,3},{3,2},{4,5},{5,4},{6,7},{7,6},{8,9},{9,8},{10,11... | collective-permute-start | bytes 98312 | tf_op jit(solution)/shard_map/ppermute | solution.py:304
  57.3 3.9 %collective-permute-done.3.got_near = f32[64,128]{1,0:T(8,128)S(1)} collective-permute-done((f32[64,128]{1,0:T(8,128)S(1)}, f32[64,128]{1,0:T(8,128)S(1)}, u32[]{:S(2)}, u32[]{:S(2)}) %collective-permute-start.3) | collective-permute-done | bytes 32800 | tf_op jit(solution)/shard_map/ppermute | solution.py:304
  61.2 0.1 collective-permute-done.4.got_far
  61.3 4.1 %shard_map.90 = (f32[72,128]{1,0:T(8,128)S(1)}, f32[64,128]{1,0:T(8,128)S(1)}, f32[64,1152]{1,0:T(8,128)S(1)}, f32[64,1024]{1,0:T(8,128)}) custom-call(f32[64,1024]{1,0:T(8,128)S(1)} %get-tuple-element.41.previous, f32[64,1152]{1,0:T(8,128)S(1)} %get-tuple-element.42.part, f32[72,128]{1,0:T(8,128)S(1)} %collective-permute-done.fetched, ...), custom_call_target="tpu_custom_call" | custom-call | tf_op jit(solution)/shard_map/pallas_call | solution.py:311
  65.4 2.0 %collective-permute-start.9 = (f32[64,1152]{1,0:T(8,128)S(1)}, f32[64,1152]{1,0:T(8,128)S(1)}, u32[]{:S(2)}, u32[]{:S(2)}) collective-permute-start(f32[64,1152]{1,0:T(8,128)S(1)} %get-tuple-element.45.part.rest_0_), channel_id=1, source_target_pairs={{0,256},{128,384},{256,0},{384,128},{1,257},{129,385},{257,1},{385... | collective-permute-start | bytes 884744 | tf_op jit(solution)/shard_map/ppermute | solution.py:316
  67.4 8.2 %collective-permute-start.6 = (f32[72,128]{1,0:T(8,128)S(1)}, f32[72,128]{1,0:T(8,128)S(1)}, u32[]{:S(2)}, u32[]{:S(2)}) collective-permute-start(f32[72,128]{1,0:T(8,128)S(1)} %get-tuple-element.47), channel_id=1, source_target_pairs={{0,63},{1,2},{2,1},{3,4},{4,3},{5,6},{6,5},{7,8},{8,7},{9,10},{10,... | collective-permute-start | bytes 110600 | tf_op jit(solution)/shard_map/ppermute | solution.py:304
  75.5 1.9 %collective-permute-start.5 = (f32[64,128]{1,0:T(8,128)S(1)}, f32[64,128]{1,0:T(8,128)S(1)}, u32[]{:S(2)}, u32[]{:S(2)}) collective-permute-start(f32[64,128]{1,0:T(8,128)S(1)} %get-tuple-element.46), channel_id=1, source_target_pairs={{0,1},{1,0},{2,3},{3,2},{4,5},{5,4},{6,7},{7,6},{8,9},{9,8},{10,11... | collective-permute-start | bytes 98312 | tf_op jit(solution)/shard_map/ppermute | solution.py:304
  77.5 3.3 %collective-permute-start.8 = (f32[64,1152]{1,0:T(8,128)S(1)}, f32[64,1152]{1,0:T(8,128)S(1)}, u32[]{:S(2)}, u32[]{:S(2)}) collective-permute-start(f32[64,1152]{1,0:T(8,128)S(1)} %get-tuple-element.45.part.rest_0_), channel_id=1, source_target_pairs={{0,128},{128,0},{256,384},{384,256},{1,129},{129,1},{257,385},{385... | collective-permute-start | bytes 884744 | tf_op jit(solution)/shard_map/ppermute | solution.py:316
  80.8 0.5 collective-permute-done.5.got_near
  81.4 4.8 %collective-permute-done.6.got_far = f32[72,128]{1,0:T(8,128)S(1)} collective-permute-done((f32[72,128]{1,0:T(8,128)S(1)}, f32[72,128]{1,0:T(8,128)S(1)}, u32[]{:S(2)}, u32[]{:S(2)}) %collective-permute-start.6) | collective-permute-done | bytes 36896 | tf_op jit(solution)/shard_map/ppermute | solution.py:304
  86.2 1.0 shard_map.91
  87.2 1.9 %collective-permute-start.7 = (f32[64,1152]{1,0:T(8,128)S(1)}, f32[64,1152]{1,0:T(8,128)S(1)}, u32[]{:S(2)}, u32[]{:S(2)}) collective-permute-start(f32[64,1152]{1,0:T(8,128)S(1)} %get-tuple-element.49.left), channel_id=1, source_target_pairs={{0,64},{64,0},{1,65},{65,1},{2,66},{66,2},{3,67},{67,3},{4,68},{68... | collective-permute-start | bytes 884744 | tf_op jit(solution)/shard_map/ppermute | solution.py:324
  89.1 1.9 %collective-permute-start.10 = (f32[64,1152]{1,0:T(8,128)S(1)}, f32[64,1152]{1,0:T(8,128)S(1)}, u32[]{:S(2)}, u32[]{:S(2)}) collective-permute-start(f32[64,1152]{1,0:T(8,128)S(1)} %collective-permute-done.9.rest_2_), channel_id=1, source_target_pairs={{0,128},{128,0},{256,384},{384,256},{1,129},{129,1},{257,385},{385... | collective-permute-start | bytes 884744 | tf_op jit(solution)/shard_map/ppermute | solution.py:316
  91.0 9.4 %collective-permute-done.10.rest_3_ = f32[64,1152]{1,0:T(8,128)S(1)} collective-permute-done((f32[64,1152]{1,0:T(8,128)S(1)}, f32[64,1152]{1,0:T(8,128)S(1)}, u32[]{:S(2)}, u32[]{:S(2)}) %collective-permute-start.10) | collective-permute-done | bytes 294944 | tf_op jit(solution)/shard_map/ppermute | solution.py:316
  100.4 0.7 shard_map.92
  101.1 11.1 %all_to_all.15.pieces = f32[16,8,256]{2,1,0:T(8,128)S(1)} all-to-all(f32[16,8,256]{2,1,0:T(8,128)S(1)} %bitcast.5), channel_id=1, replica_groups=mesh['chip'=4,'core'=2,'x'=4,'half'=2,'z'=8] {'core','z'}, dimensions={0} | all-to-all | bytes 262144 | tf_op jit(solution)/shard_map/all_to_all | solution.py:335
  112.2 0.1 shard_map.93
  112.3 15.7 %all_to_all.16 = f32[8,8,512]{2,1,0:T(8,128)S(1)} all-to-all(f32[8,8,512]{2,1,0:T(8,128)S(1)} %shard_map.93), channel_id=1, replica_groups=mesh['chip'=4,'core'=2,'x'=4,'half'=2,'z'=8] {'x','half'}, dimensions={0} | all-to-all | bytes 262144 | tf_op jit(solution)/shard_map/all_to_all | solution.py:339
  128.0 12.1 %all_to_all.17 = f32[8,8,512]{2,1,0:T(8,128)S(1)} all-to-all(f32[8,8,512]{2,1,0:T(8,128)S(1)} %broadcast_in_dim.2), channel_id=1, replica_groups=mesh['chip'=4,'core'=2,'x'=4,'half'=2,'z'=8] {'z'}, dimensions={0} | all-to-all | bytes 262144 | tf_op jit(solution)/shard_map/all_to_all | solution.py:341
  140.1 0.7 copy.10
  (6 shorter events, 0.0 us)
Async XLA Ops:
  2.0 19.7 %collective-permute-start = (f32[72,128]{1,0:T(8,128)S(1)}, f32[72,128]{1,0:T(8,128)S(1)}, u32[]{:S(2)}, u32[]{:S(2)}) collective-permute-start(f32[72,128]{1,0:T(8,128)S(1)} %get-tuple-element.27), channel_id=1, source_target_pairs={{0,63},{1,0},{2,1},{3,2},{4,3},{5,4},{6,5},{7,6},{8,7},{9,8},{10,9... | collective-permute-start | bytes 110600 | tf_op jit(solution)/shard_map/ppermute | solution.py:287
  19.5 0.7 copy-start
  25.2 18.0 %collective-permute-start.2 = (f32[72,128]{1,0:T(8,128)S(1)}, f32[72,128]{1,0:T(8,128)S(1)}, u32[]{:S(2)}, u32[]{:S(2)}) collective-permute-start(f32[72,128]{1,0:T(8,128)S(1)} %get-tuple-element.40), channel_id=1, source_target_pairs={{0,63},{1,2},{2,1},{3,4},{4,3},{5,6},{6,5},{7,8},{8,7},{9,10},{10,... | collective-permute-start | bytes 110600 | tf_op jit(solution)/shard_map/ppermute | solution.py:304
  37.4 5.8 %collective-permute-start.1 = (f32[64,128]{1,0:T(8,128)S(1)}, f32[64,128]{1,0:T(8,128)S(1)}, u32[]{:S(2)}, u32[]{:S(2)}) collective-permute-start(f32[64,128]{1,0:T(8,128)S(1)} %get-tuple-element.39), channel_id=1, source_target_pairs={{0,1},{1,0},{2,3},{3,2},{4,5},{5,4},{6,7},{7,6},{8,9},{9,8},{10,11... | collective-permute-start | bytes 98312 | tf_op jit(solution)/shard_map/ppermute | solution.py:304
  46.9 14.4 %collective-permute-start.4 = (f32[72,128]{1,0:T(8,128)S(1)}, f32[72,128]{1,0:T(8,128)S(1)}, u32[]{:S(2)}, u32[]{:S(2)}) collective-permute-start(f32[72,128]{1,0:T(8,128)S(1)} %get-tuple-element.44), channel_id=1, source_target_pairs={{0,63},{1,2},{2,1},{3,4},{4,3},{5,6},{6,5},{7,8},{8,7},{9,10},{10,... | collective-permute-start | bytes 110600 | tf_op jit(solution)/shard_map/ppermute | solution.py:304
  55.4 5.8 %collective-permute-start.3 = (f32[64,128]{1,0:T(8,128)S(1)}, f32[64,128]{1,0:T(8,128)S(1)}, u32[]{:S(2)}, u32[]{:S(2)}) collective-permute-start(f32[64,128]{1,0:T(8,128)S(1)} %get-tuple-element.43), channel_id=1, source_target_pairs={{0,1},{1,0},{2,3},{3,2},{4,5},{5,4},{6,7},{7,6},{8,9},{9,8},{10,11... | collective-permute-start | bytes 98312 | tf_op jit(solution)/shard_map/ppermute | solution.py:304
  65.4 23.7 %collective-permute-start.9 = (f32[64,1152]{1,0:T(8,128)S(1)}, f32[64,1152]{1,0:T(8,128)S(1)}, u32[]{:S(2)}, u32[]{:S(2)}) collective-permute-start(f32[64,1152]{1,0:T(8,128)S(1)} %get-tuple-element.45.part.rest_0_), channel_id=1, source_target_pairs={{0,256},{128,384},{256,0},{384,128},{1,257},{129,385},{257,1},{385... | collective-permute-start | bytes 884744 | tf_op jit(solution)/shard_map/ppermute | solution.py:316
  67.4 18.8 %collective-permute-start.6 = (f32[72,128]{1,0:T(8,128)S(1)}, f32[72,128]{1,0:T(8,128)S(1)}, u32[]{:S(2)}, u32[]{:S(2)}) collective-permute-start(f32[72,128]{1,0:T(8,128)S(1)} %get-tuple-element.47), channel_id=1, source_target_pairs={{0,63},{1,2},{2,1},{3,4},{4,3},{5,6},{6,5},{7,8},{8,7},{9,10},{10,... | collective-permute-start | bytes 110600 | tf_op jit(solution)/shard_map/ppermute | solution.py:304
  75.5 5.8 %collective-permute-start.5 = (f32[64,128]{1,0:T(8,128)S(1)}, f32[64,128]{1,0:T(8,128)S(1)}, u32[]{:S(2)}, u32[]{:S(2)}) collective-permute-start(f32[64,128]{1,0:T(8,128)S(1)} %get-tuple-element.46), channel_id=1, source_target_pairs={{0,1},{1,0},{2,3},{3,2},{4,5},{5,4},{6,7},{7,6},{8,9},{9,8},{10,11... | collective-permute-start | bytes 98312 | tf_op jit(solution)/shard_map/ppermute | solution.py:304
  77.5 13.6 %collective-permute-start.8 = (f32[64,1152]{1,0:T(8,128)S(1)}, f32[64,1152]{1,0:T(8,128)S(1)}, u32[]{:S(2)}, u32[]{:S(2)}) collective-permute-start(f32[64,1152]{1,0:T(8,128)S(1)} %get-tuple-element.45.part.rest_0_), channel_id=1, source_target_pairs={{0,128},{128,0},{256,384},{384,256},{1,129},{129,1},{257,385},{385... | collective-permute-start | bytes 884744 | tf_op jit(solution)/shard_map/ppermute | solution.py:316
  87.2 3.9 %collective-permute-start.7 = (f32[64,1152]{1,0:T(8,128)S(1)}, f32[64,1152]{1,0:T(8,128)S(1)}, u32[]{:S(2)}, u32[]{:S(2)}) collective-permute-start(f32[64,1152]{1,0:T(8,128)S(1)} %get-tuple-element.49.left), channel_id=1, source_target_pairs={{0,64},{64,0},{1,65},{65,1},{2,66},{66,2},{3,67},{67,3},{4,68},{68... | collective-permute-start | bytes 884744 | tf_op jit(solution)/shard_map/ppermute | solution.py:324
  89.1 11.3 %collective-permute-start.10 = (f32[64,1152]{1,0:T(8,128)S(1)}, f32[64,1152]{1,0:T(8,128)S(1)}, u32[]{:S(2)}, u32[]{:S(2)}) collective-permute-start(f32[64,1152]{1,0:T(8,128)S(1)} %collective-permute-done.9.rest_2_), channel_id=1, source_target_pairs={{0,128},{128,0},{256,384},{384,256},{1,129},{129,1},{257,385},{385... | collective-permute-start | bytes 884744 | tf_op jit(solution)/shard_map/ppermute | solution.py:316

commit v5 on v4

--- a/solution.py
+++ b/solution.py
@@ -186,23 +186,39 @@
     send_both(up, picked(here, chosen[...]), near, far)
 
 
-def finish_kernel(part, got_near, got_far, chosen, filtered, left):
+def relay_kernel(block, near, far, out):
+    del near, far
+    out[:8, :128] = block[:8, :128]
+
+
+def late_kernel(got_near, got_far, late):
+    late[...] = jnp.concatenate(got_both(got_near, got_far), axis=1)
+
+
+def halves(late):
+    count = late.shape[1] // 2
+    return late[:, :count], late[:, count:]
+
+
+def finish_kernel(part, late, chosen, filtered, left):
     owned = filtered.shape[1]
-    current, ghost = complete(part, *got_both(got_near, got_far), chosen)
+    current, ghost = complete(part, *halves(late), chosen)
     filtered[...] = current
     left[:, :owned] = current
     left[:, owned:] = ghost
 
 
-def gram_kernel(total_nodes, left, sibling, *rest):
+def gram_kernel(total_nodes, left, sibling, late, chosen, *rest):
     blocks, (out, g_high, g_low) = rest[:-3], rest[-3:]
-    rows = left.shape[0]
+    chips = len(blocks)
+    rows, owned = left.shape[0], chosen.shape[0]
     chip = lax.axis_index("chip")
     core = lax.axis_index("core")
-    for s, block in enumerate(blocks):
+    for s in range(chips):
         at = pl.ds(pl.multiple_of((chip ^ s) * rows, rows), rows)
-        g_high[at, :], g_low[at, :] = parts(block[...], 2)
-    high, low = parts(jnp.concatenate([left[...], sibling[...]], axis=0), 2)
+        g_high[at, :], g_low[at, :] = parts(blocks[s][...], 2)
+    theirs = jnp.concatenate(complete(sibling, *halves(late), chosen), axis=1)
+    high, low = parts(jnp.concatenate([left[...], theirs], axis=0), 2)
     by_high = dot_t(jnp.concatenate([high, low], axis=0), g_high[...])
     whole = by_high[: 2 * rows] + by_high[2 * rows :] + dot_t(high, g_low[...])
     whole = whole * (1.0 / total_nodes)
@@ -256,13 +272,14 @@
     edge = shape_of(rows, shared_count)
     tall = shape_of(rows + 8, shared_count)
 
-    def call(kernel, out_shape, specs, scratch_shapes=()):
+    def call(kernel, out_shape, specs, scratch_shapes=(), aliases={}):
         return pl.pallas_call(
             kernel,
             out_shape=out_shape,
             in_specs=specs,
             out_specs=jax.tree.map(lambda _: in_vmem, out_shape),
             scratch_shapes=scratch_shapes,
+            input_output_aliases=aliases,
             compiler_params=params,
         )
 
@@ -315,19 +332,26 @@
     def from_chip(x, s):
         return lax.ppermute(x, "chip", [(i, i ^ s) for i in range(chips)])
 
+    got_near, got_far = swapped(near, far)
     second = from_chip(partial, 2)
-    blocks = [partial, from_chip(partial, 1), second, from_chip(second, 1)]
-
-    filtered, left = call(finish_kernel, (block, wide), [in_vmem] * 4)(
-        partial, *swapped(near, far), chosen
-    )
-    sibling = lax.ppermute(left, "core", [(0, 1), (1, 0)])
+    relayed = call(relay_kernel, wide, [in_vmem] * 3, aliases={0: 0})(
+        second, got_near, got_far
+    )
+    blocks = [partial, from_chip(partial, 1), relayed, from_chip(relayed, 1)]
+
+    def from_sibling(x):
+        return lax.ppermute(x, "core", [(0, 1), (1, 0)])
+
+    late = call(late_kernel, shape_of(rows, 2 * shared_count), [in_vmem] * 2)(
+        got_near, got_far
+    )
+    filtered, left = call(finish_kernel, (block, wide), [in_vmem] * 3)(partial, late, chosen)
     gram = call(
         functools.partial(gram_kernel, owned * n_dom),
         shape_of(2 * rows, chips * rows),
-        [in_vmem] * (2 + chips),
+        [in_vmem] * (4 + chips),
         [pltpu.VMEM((chips * rows, nodes), bf16)] * 2,
-    )(left, sibling, *blocks)
+    )(left, from_sibling(partial), from_sibling(late), chosen, *blocks)
 
     n_z = lax.axis_size("z")
     n_across = lax.axis_size(("x", "half"))

time: 141 us -> 136 us (0.965)
  the two profiles are of different devices: /device:TPU:8 before, /device:TPU:16 now
where the time goes in v5:
time: 136 us
  starting transfers between devices  63.7 us (47%)
  blocking collectives  39.8 us (29%)
  Pallas kernels  16 us (12%)
  waiting for transfers between devices  14.3 us (11%)
    ppermute x3, starting transfers between devices, swapped(): lax.ppermute(far, DOM, far_pairs)  28.1 us
    ppermute x1, starting transfers between devices, per_device(): fetched = lax.ppermute(message, DOM, backward)  16.6 us
    all_to_all x1, blocking collectives, per_device(): spread = lax.all_to_all(mine, ('x', 'half'), 0, 0, tiled=True)  16.1 us
    all_to_all x1, blocking collectives, per_device(): lax.all_to_all(jnp.broadcast_to(mine[None], (n_z, *mine.shape)), 'z', 0,...  12.1 us
    all_to_all x1, blocking collectives, per_device(): lax.all_to_all(gram.reshape(2 * n_z, each, chips * rows), ('core', 'z'),...  11.7 us
    ppermute x3, starting transfers between devices, from_chip(): return lax.ppermute(x, 'chip', [(i, i ^ s) for i in range(chips)])  9.44 us
    pallas_call x2, Pallas kernels, per_device(): call(next_kernel, (tall, edge, wide, block), [in_vmem] * 12)  7.78 us
    ppermute x3, waiting for transfers between devices, swapped(): lax.ppermute(near, DOM, near_pairs)  7.76 us
  transfers between devices with their start and end apart: 12, of which 5 were waited for; matrix products, arithmetic and copies ran while one was open for 0% of the time, Pallas kernels for 2%

profile of v5, /device:TPU:16, one launch (start us, length us, event | category | flops | bytes accessed | tf_op | source)
XLA Modules:
  0.0 135.9 jit_solution(17240389104483670106)
XLA Ops:
  0.6 1.3 shard_map.86
  2.0 16.6 %collective-permute-start = (f32[72,128]{1,0:T(8,128)S(1)}, f32[72,128]{1,0:T(8,128)S(1)}, u32[]{:S(2)}, u32[]{:S(2)}) collective-permute-start(f32[72,128]{1,0:T(8,128)S(1)} %get-tuple-element.27), channel_id=1, source_target_pairs={{0,63},{1,0},{2,1},{3,2},{4,3},{5,4},{6,5},{7,6},{8,7},{9,8},{10,9... | collective-permute-start | bytes 110600 | tf_op jit(solution)/shard_map/ppermute | solution.py:304
  18.6 0.0 copy-start
  18.6 0.6 copy-done
  19.2 1.6 %shard_map.87 = (bf16[1152,2304]{1,0:T(8,128)(2,1)S(1)}, bf16[384,384]{1,0:T(8,128)(2,1)S(1)}, bf16[384,384]{1,0:T(8,128)(2,1)S(1)}, bf16[1024,128]{1,0:T(8,128)(2,1)S(1)}, f32[1,2304]{1,0:T(1,128)S(1)}) custom-call(s32[6,343]{1,0:T(8,128)S(1)} %get-tuple-element.30.cells, f32[343,343]{1,0:T(8,128)S(1)} %get-tuple-element.31.stiff, ...), custom_call_target="tpu_custom_call" | custom-call | tf_op jit(solution)/shard_map/pallas_call | solution.py:305
  20.8 3.5 %shard_map.88 = (f32[72,128]{1,0:T(8,128)S(1)}, f32[64,128]{1,0:T(8,128)S(1)}, f32[64,1152]{1,0:T(8,128)S(1)}) custom-call(f32[64,1024]{1,0:T(8,128)S(1)} %get-tuple-element.26.states.previous, f32[72,128]{1,0:T(8,128)S(1)} %collective-permute-done.fetched, f32[1,1024]{1,0:T(1,128)S(1)} %get-tuple-element.28.inv_mass, ...), custom_call_target="tpu_custom_call" | custom-call | tf_op jit(solution)/shard_map/pallas_call | solution.py:323
  24.3 11.7 %collective-permute-start.2 = (f32[72,128]{1,0:T(8,128)S(1)}, f32[72,128]{1,0:T(8,128)S(1)}, u32[]{:S(2)}, u32[]{:S(2)}) collective-permute-start(f32[72,128]{1,0:T(8,128)S(1)} %get-tuple-element.40), channel_id=1, source_target_pairs={{0,63},{1,2},{2,1},{3,4},{4,3},{5,6},{6,5},{7,8},{8,7},{9,10},{10,... | collective-permute-start | bytes 110600 | tf_op jit(solution)/shard_map/ppermute | solution.py:321
  36.1 1.9 %collective-permute-start.1 = (f32[64,128]{1,0:T(8,128)S(1)}, f32[64,128]{1,0:T(8,128)S(1)}, u32[]{:S(2)}, u32[]{:S(2)}) collective-permute-start(f32[64,128]{1,0:T(8,128)S(1)} %get-tuple-element.39), channel_id=1, source_target_pairs={{0,1},{1,0},{2,3},{3,2},{4,5},{5,4},{6,7},{7,6},{8,9},{9,8},{10,11... | collective-permute-start | bytes 98312 | tf_op jit(solution)/shard_map/ppermute | solution.py:321
  38.0 3.9 %collective-permute-done.1.got_near = f32[64,128]{1,0:T(8,128)S(1)} collective-permute-done((f32[64,128]{1,0:T(8,128)S(1)}, f32[64,128]{1,0:T(8,128)S(1)}, u32[]{:S(2)}, u32[]{:S(2)}) %collective-permute-start.1) | collective-permute-done | bytes 32800 | tf_op jit(solution)/shard_map/ppermute | solution.py:321
  41.9 0.0 collective-permute-done.2.got_far
  41.9 3.7 %shard_map.89 = (f32[72,128]{1,0:T(8,128)S(1)}, f32[64,128]{1,0:T(8,128)S(1)}, f32[64,1152]{1,0:T(8,128)S(1)}, f32[64,1024]{1,0:T(8,128)S(1)}) custom-call(f32[64,1024]{1,0:T(8,128)S(1)} %get-tuple-element.26.states.previous, f32[64,1152]{1,0:T(8,128)S(1)} %get-tuple-element.38.part, f32[72,128]{1,0:T(8,128)S(1)} %collective-permute-done.fetched, ...), custom_call_target="tpu_custom_call" | custom-call | tf_op jit(solution)/shard_map/pallas_call | solution.py:328
  45.6 8.2 %collective-permute-start.4 = (f32[72,128]{1,0:T(8,128)S(1)}, f32[72,128]{1,0:T(8,128)S(1)}, u32[]{:S(2)}, u32[]{:S(2)}) collective-permute-start(f32[72,128]{1,0:T(8,128)S(1)} %get-tuple-element.44), channel_id=1, source_target_pairs={{0,63},{1,2},{2,1},{3,4},{4,3},{5,6},{6,5},{7,8},{8,7},{9,10},{10,... | collective-permute-start | bytes 110600 | tf_op jit(solution)/shard_map/ppermute | solution.py:321
  53.7 1.9 %collective-permute-start.3 = (f32[64,128]{1,0:T(8,128)S(1)}, f32[64,128]{1,0:T(8,128)S(1)}, u32[]{:S(2)}, u32[]{:S(2)}) collective-permute-start(f32[64,128]{1,0:T(8,128)S(1)} %get-tuple-element.43), channel_id=1, source_target_pairs={{0,1},{1,0},{2,3},{3,2},{4,5},{5,4},{6,7},{7,6},{8,9},{9,8},{10,11... | collective-permute-start | bytes 98312 | tf_op jit(solution)/shard_map/ppermute | solution.py:321
  55.7 3.9 %collective-permute-done.3.got_near = f32[64,128]{1,0:T(8,128)S(1)} collective-permute-done((f32[64,128]{1,0:T(8,128)S(1)}, f32[64,128]{1,0:T(8,128)S(1)}, u32[]{:S(2)}, u32[]{:S(2)}) %collective-permute-start.3) | collective-permute-done | bytes 32800 | tf_op jit(solution)/shard_map/ppermute | solution.py:321
  59.6 4.1 %shard_map.90 = (f32[72,128]{1,0:T(8,128)S(1)}, f32[64,128]{1,0:T(8,128)S(1)}, f32[64,1152]{1,0:T(8,128)S(1)}, f32[64,1024]{1,0:T(8,128)}) custom-call(f32[64,1024]{1,0:T(8,128)S(1)} %get-tuple-element.41.previous, f32[64,1152]{1,0:T(8,128)S(1)} %get-tuple-element.42.part, f32[72,128]{1,0:T(8,128)S(1)} %collective-permute-done.fetched, ...), custom_call_target="tpu_custom_call" | custom-call | tf_op jit(solution)/shard_map/pallas_call | solution.py:328
  63.7 4.0 %collective-permute-start.10 = (f32[64,1152]{1,0:T(8,128)S(1)}, f32[64,1152]{1,0:T(8,128)S(1)}, u32[]{:S(2)}, u32[]{:S(2)}) collective-permute-start(f32[64,1152]{1,0:T(8,128)S(1)} %get-tuple-element.45.part.rest_0_), channel_id=1, source_target_pairs={{0,256},{128,384},{256,0},{384,128},{1,257},{129,385},{257,1},{385... | collective-permute-start | bytes 884744 | tf_op jit(solution)/shard_map/ppermute | solution.py:333
  67.7 8.2 %collective-permute-start.6 = (f32[72,128]{1,0:T(8,128)S(1)}, f32[72,128]{1,0:T(8,128)S(1)}, u32[]{:S(2)}, u32[]{:S(2)}) collective-permute-start(f32[72,128]{1,0:T(8,128)S(1)} %get-tuple-element.47), channel_id=1, source_target_pairs={{0,63},{1,2},{2,1},{3,4},{4,3},{5,6},{6,5},{7,8},{8,7},{9,10},{10,... | collective-permute-start | bytes 110600 | tf_op jit(solution)/shard_map/ppermute | solution.py:321
  75.9 1.9 %collective-permute-start.5 = (f32[64,128]{1,0:T(8,128)S(1)}, f32[64,128]{1,0:T(8,128)S(1)}, u32[]{:S(2)}, u32[]{:S(2)}) collective-permute-start(f32[64,128]{1,0:T(8,128)S(1)} %get-tuple-element.46), channel_id=1, source_target_pairs={{0,1},{1,0},{2,3},{3,2},{4,5},{5,4},{6,7},{7,6},{8,9},{9,8},{10,11... | collective-permute-start | bytes 98312 | tf_op jit(solution)/shard_map/ppermute | solution.py:321
  77.8 3.5 %collective-permute-start.9 = (f32[64,1152]{1,0:T(8,128)S(1)}, f32[64,1152]{1,0:T(8,128)S(1)}, u32[]{:S(2)}, u32[]{:S(2)}) collective-permute-start(f32[64,1152]{1,0:T(8,128)S(1)} %get-tuple-element.45.part.rest_0_), channel_id=1, source_target_pairs={{0,128},{128,0},{256,384},{384,256},{1,129},{129,1},{257,385},{385... | collective-permute-start | bytes 884744 | tf_op jit(solution)/shard_map/ppermute | solution.py:333
  81.3 1.9 %collective-permute-start.7 = (f32[64,1152]{1,0:T(8,128)S(1)}, f32[64,1152]{1,0:T(8,128)S(1)}, u32[]{:S(2)}, u32[]{:S(2)}) collective-permute-start(f32[64,1152]{1,0:T(8,128)S(1)} %get-tuple-element.45.part.rest_0_), channel_id=1, source_target_pairs={{0,64},{64,0},{1,65},{65,1},{2,66},{66,2},{3,67},{67,3},{4,68},{68... | collective-permute-start | bytes 884744 | tf_op jit(solution)/shard_map/ppermute | solution.py:343
  83.2 2.2 %collective-permute-done.6.got_far.far = f32[72,128]{1,0:T(8,128)S(1)} collective-permute-done((f32[72,128]{1,0:T(8,128)S(1)}, f32[72,128]{1,0:T(8,128)S(1)}, u32[]{:S(2)}, u32[]{:S(2)}) %collective-permute-start.6) | collective-permute-done | bytes 36896 | tf_op jit(solution)/shard_map/ppermute | solution.py:321
  85.4 1.9 %collective-permute-start.11 = (f32[64,1152]{1,0:T(8,128)S(1)}, f32[64,1152]{1,0:T(8,128)S(1)}, u32[]{:S(2)}, u32[]{:S(2)}) collective-permute-start(f32[64,1152]{1,0:T(8,128)S(1)} %shard_map.93.rest_2_), channel_id=1, source_target_pairs={{0,128},{128,0},{256,384},{384,256},{1,129},{129,1},{257,385},{385... | collective-permute-start | bytes 884744 | tf_op jit(solution)/shard_map/ppermute | solution.py:333
  87.4 1.9 %collective-permute-start.8 = (f32[64,256]{1,0:T(8,128)S(1)}, f32[64,256]{1,0:T(8,128)S(1)}, u32[]{:S(2)}, u32[]{:S(2)}) collective-permute-start(f32[64,256]{1,0:T(8,128)S(1)} %shard_map.91.late), channel_id=1, source_target_pairs={{0,64},{64,0},{1,65},{65,1},{2,66},{66,2},{3,67},{67,3},{4,68},{68... | collective-permute-start | bytes 196616 | tf_op jit(solution)/shard_map/ppermute | solution.py:343
  89.3 1.0 shard_map.92
  90.3 0.3 collective-permute-done.8.late
  90.5 4.1 %collective-permute-done.11.rest_3_ = f32[64,1152]{1,0:T(8,128)S(1)} collective-permute-done((f32[64,1152]{1,0:T(8,128)S(1)}, f32[64,1152]{1,0:T(8,128)S(1)}, u32[]{:S(2)}, u32[]{:S(2)}) %collective-permute-start.11) | collective-permute-done | bytes 294944 | tf_op jit(solution)/shard_map/ppermute | solution.py:333
  94.6 0.8 shard_map.94
  95.3 11.7 %all_to_all.15.pieces = f32[16,8,256]{2,1,0:T(8,128)S(1)} all-to-all(f32[16,8,256]{2,1,0:T(8,128)S(1)} %bitcast.5), channel_id=1, replica_groups=mesh['chip'=4,'core'=2,'x'=4,'half'=2,'z'=8] {'core','z'}, dimensions={0} | all-to-all | bytes 262144 | tf_op jit(solution)/shard_map/all_to_all | solution.py:359
  107.0 0.1 shard_map.95
  107.1 16.1 %all_to_all.16 = f32[8,8,512]{2,1,0:T(8,128)S(1)} all-to-all(f32[8,8,512]{2,1,0:T(8,128)S(1)} %shard_map.95), channel_id=1, replica_groups=mesh['chip'=4,'core'=2,'x'=4,'half'=2,'z'=8] {'x','half'}, dimensions={0} | all-to-all | bytes 262144 | tf_op jit(solution)/shard_map/all_to_all | solution.py:363
  123.2 12.1 %all_to_all.17 = f32[8,8,512]{2,1,0:T(8,128)S(1)} all-to-all(f32[8,8,512]{2,1,0:T(8,128)S(1)} %broadcast_in_dim.2), channel_id=1, replica_groups=mesh['chip'=4,'core'=2,'x'=4,'half'=2,'z'=8] {'z'}, dimensions={0} | all-to-all | bytes 262144 | tf_op jit(solution)/shard_map/all_to_all | solution.py:365
  135.3 0.7 copy.12
  (10 shorter events, 0.1 us)
Async XLA Ops:
  2.0 18.8 %collective-permute-start = (f32[72,128]{1,0:T(8,128)S(1)}, f32[72,128]{1,0:T(8,128)S(1)}, u32[]{:S(2)}, u32[]{:S(2)}) collective-permute-start(f32[72,128]{1,0:T(8,128)S(1)} %get-tuple-element.27), channel_id=1, source_target_pairs={{0,63},{1,0},{2,1},{3,2},{4,3},{5,4},{6,5},{7,6},{8,7},{9,8},{10,9... | collective-permute-start | bytes 110600 | tf_op jit(solution)/shard_map/ppermute | solution.py:304
  18.6 0.7 copy-start
  24.3 17.6 %collective-permute-start.2 = (f32[72,128]{1,0:T(8,128)S(1)}, f32[72,128]{1,0:T(8,128)S(1)}, u32[]{:S(2)}, u32[]{:S(2)}) collective-permute-start(f32[72,128]{1,0:T(8,128)S(1)} %get-tuple-element.40), channel_id=1, source_target_pairs={{0,63},{1,2},{2,1},{3,4},{4,3},{5,6},{6,5},{7,8},{8,7},{9,10},{10,... | collective-permute-start | bytes 110600 | tf_op jit(solution)/shard_map/ppermute | solution.py:321
  36.1 5.8 %collective-permute-start.1 = (f32[64,128]{1,0:T(8,128)S(1)}, f32[64,128]{1,0:T(8,128)S(1)}, u32[]{:S(2)}, u32[]{:S(2)}) collective-permute-start(f32[64,128]{1,0:T(8,128)S(1)} %get-tuple-element.39), channel_id=1, source_target_pairs={{0,1},{1,0},{2,3},{3,2},{4,5},{5,4},{6,7},{7,6},{8,9},{9,8},{10,11... | collective-permute-start | bytes 98312 | tf_op jit(solution)/shard_map/ppermute | solution.py:321
  45.6 14.0 %collective-permute-start.4 = (f32[72,128]{1,0:T(8,128)S(1)}, f32[72,128]{1,0:T(8,128)S(1)}, u32[]{:S(2)}, u32[]{:S(2)}) collective-permute-start(f32[72,128]{1,0:T(8,128)S(1)} %get-tuple-element.44), channel_id=1, source_target_pairs={{0,63},{1,2},{2,1},{3,4},{4,3},{5,6},{6,5},{7,8},{8,7},{9,10},{10,... | collective-permute-start | bytes 110600 | tf_op jit(solution)/shard_map/ppermute | solution.py:321
  53.7 5.8 %collective-permute-start.3 = (f32[64,128]{1,0:T(8,128)S(1)}, f32[64,128]{1,0:T(8,128)S(1)}, u32[]{:S(2)}, u32[]{:S(2)}) collective-permute-start(f32[64,128]{1,0:T(8,128)S(1)} %get-tuple-element.43), channel_id=1, source_target_pairs={{0,1},{1,0},{2,3},{3,2},{4,5},{5,4},{6,7},{7,6},{8,9},{9,8},{10,11... | collective-permute-start | bytes 98312 | tf_op jit(solution)/shard_map/ppermute | solution.py:321
  63.7 21.8 %collective-permute-start.10 = (f32[64,1152]{1,0:T(8,128)S(1)}, f32[64,1152]{1,0:T(8,128)S(1)}, u32[]{:S(2)}, u32[]{:S(2)}) collective-permute-start(f32[64,1152]{1,0:T(8,128)S(1)} %get-tuple-element.45.part.rest_0_), channel_id=1, source_target_pairs={{0,256},{128,384},{256,0},{384,128},{1,257},{129,385},{257,1},{385... | collective-permute-start | bytes 884744 | tf_op jit(solution)/shard_map/ppermute | solution.py:333
  67.7 17.7 %collective-permute-start.6 = (f32[72,128]{1,0:T(8,128)S(1)}, f32[72,128]{1,0:T(8,128)S(1)}, u32[]{:S(2)}, u32[]{:S(2)}) collective-permute-start(f32[72,128]{1,0:T(8,128)S(1)} %get-tuple-element.47), channel_id=1, source_target_pairs={{0,63},{1,2},{2,1},{3,4},{4,3},{5,6},{6,5},{7,8},{8,7},{9,10},{10,... | collective-permute-start | bytes 110600 | tf_op jit(solution)/shard_map/ppermute | solution.py:321
  75.9 7.4 %collective-permute-start.5 = (f32[64,128]{1,0:T(8,128)S(1)}, f32[64,128]{1,0:T(8,128)S(1)}, u32[]{:S(2)}, u32[]{:S(2)}) collective-permute-start(f32[64,128]{1,0:T(8,128)S(1)} %get-tuple-element.46), channel_id=1, source_target_pairs={{0,1},{1,0},{2,3},{3,2},{4,5},{5,4},{6,7},{7,6},{8,9},{9,8},{10,11... | collective-permute-start | bytes 98312 | tf_op jit(solution)/shard_map/ppermute | solution.py:321
  77.8 12.7 %collective-permute-start.9 = (f32[64,1152]{1,0:T(8,128)S(1)}, f32[64,1152]{1,0:T(8,128)S(1)}, u32[]{:S(2)}, u32[]{:S(2)}) collective-permute-start(f32[64,1152]{1,0:T(8,128)S(1)} %get-tuple-element.45.part.rest_0_), channel_id=1, source_target_pairs={{0,128},{128,0},{256,384},{384,256},{1,129},{129,1},{257,385},{385... | collective-permute-start | bytes 884744 | tf_op jit(solution)/shard_map/ppermute | solution.py:333
  81.3 9.2 %collective-permute-start.7 = (f32[64,1152]{1,0:T(8,128)S(1)}, f32[64,1152]{1,0:T(8,128)S(1)}, u32[]{:S(2)}, u32[]{:S(2)}) collective-permute-start(f32[64,1152]{1,0:T(8,128)S(1)} %get-tuple-element.45.part.rest_0_), channel_id=1, source_target_pairs={{0,64},{64,0},{1,65},{65,1},{2,66},{66,2},{3,67},{67,3},{4,68},{68... | collective-permute-start | bytes 884744 | tf_op jit(solution)/shard_map/ppermute | solution.py:343
  85.4 9.2 %collective-permute-start.11 = (f32[64,1152]{1,0:T(8,128)S(1)}, f32[64,1152]{1,0:T(8,128)S(1)}, u32[]{:S(2)}, u32[]{:S(2)}) collective-permute-start(f32[64,1152]{1,0:T(8,128)S(1)} %shard_map.93.rest_2_), channel_id=1, source_target_pairs={{0,128},{128,0},{256,384},{384,256},{1,129},{129,1},{257,385},{385... | collective-permute-start | bytes 884744 | tf_op jit(solution)/shard_map/ppermute | solution.py:333
  87.4 3.1 %collective-permute-start.8 = (f32[64,256]{1,0:T(8,128)S(1)}, f32[64,256]{1,0:T(8,128)S(1)}, u32[]{:S(2)}, u32[]{:S(2)}) collective-permute-start(f32[64,256]{1,0:T(8,128)S(1)} %shard_map.91.late), channel_id=1, source_target_pairs={{0,64},{64,0},{1,65},{65,1},{2,66},{66,2},{3,67},{67,3},{4,68},{68... | collective-permute-start | bytes 196616 | tf_op jit(solution)/shard_map/ppermute | solution.py:343

commit v6 on v5

--- a/solution.py
+++ b/solution.py
@@ -45,16 +45,19 @@
     return jnp.where(at == row.astype(jnp.int16), jnp.array(1, bf16), jnp.array(0, bf16))
 
 
+def one_hot_rows(column, count):
+    at = lax.broadcasted_iota(jnp.int16, (column.shape[0], count), 1)
+    return jnp.where(at == column.astype(jnp.int16), jnp.array(1, bf16), jnp.array(0, bf16))
+
+
 def picked(x, chosen):
     rows = x.shape[0]
     got = dot(jnp.concatenate(parts(x, 3), axis=0), chosen)
     return got[:rows] + got[rows : 2 * rows] + got[2 * rows :]
 
 
-def placed(x, chosen):
-    rows = x.shape[0]
-    got = dot_t(jnp.concatenate(parts(x, 3), axis=0), chosen)
-    return got[:rows] + got[rows : 2 * rows] + got[2 * rows :]
+def placed(x, chosen_t):
+    return picked(x, chosen_t)
 
 
 def start_kernel(
@@ -84,33 +87,67 @@
 
 
 def prepare_kernel(
-    cells, stiff, shared, scale, chosen_all, high, low, chosen, scale_row, cells_pad, stiff_pad
+    cells, stiff, shared, scale,
+    slots, late_slots, high, low, chosen, chosen_t, scale_row, cells_pad, stiff_pad,
 ):
     n_cells, npc = cells.shape
     pad = stiff_pad.shape[0]
-    nodes = chosen_all.shape[0]
+    nodes = slots.shape[1]
+    owned, shared_count = chosen.shape
     cells_pad[...] = jnp.full(cells_pad.shape, -1, jnp.int32)
     cells_pad[:n_cells, :npc] = cells[...]
+    cells_pad[8:9, :shared_count] = shared[...]
+    columns = jnp.transpose(cells_pad[...])
+    shared_column = columns[:shared_count, 8:9]
+    ghosts = lax.broadcasted_iota(jnp.int16, (shared_count, pad), 0) + jnp.int16(owned)
+    shareds = jnp.broadcast_to(shared_column.astype(jnp.int16), (shared_count, pad))
+    for c in range(n_cells):
+        at = slice(c * pad, (c + 1) * pad)
+        slots[at, :] = one_hot_rows(columns[:, c : c + 1], nodes)
+        row = cells_pad[c : c + 1, :].astype(jnp.int16)
+        for i, names in enumerate((shareds, ghosts)):
+            late_slots[i * shared_count : (i + 1) * shared_count, at] = jnp.where(
+                names == row, jnp.array(1, bf16), jnp.array(0, bf16)
+            )
+        scale_row[:, at] = jnp.full((1, pad), scale[c], f32)
     stiff_pad[...] = jnp.zeros(stiff_pad.shape, f32)
     stiff_pad[:npc, :npc] = stiff[...]
-    for c in range(n_cells):
-        at = slice(c * pad, (c + 1) * pad)
-        chosen_all[:, at] = one_hot(cells_pad[c : c + 1, :], nodes)
-        scale_row[:, at] = jnp.full((1, pad), scale[c], f32)
     high[...], low[...] = parts(stiff_pad[...], 2)
-    chosen[...] = one_hot(shared[...], chosen.shape[0])
-
-
-def apply_cells(own, ghost, scale, chosen_all, high, low):
-    rows, owned = own.shape
+    chosen[...] = one_hot(shared[...], owned)
+    chosen_t[...] = one_hot_rows(shared_column, owned)
+
+
+def twice(x, apply):
+    rows = x.shape[0]
+    got = apply(jnp.concatenate(parts(x, 2), axis=0))
+    return got[:rows] + got[rows:]
+
+
+def first_gather_kernel(states, inv_mass, slots, gathered):
+    owned = states.shape[1]
+    values = states[...] * inv_mass[...]
+    gathered[...] = twice(values, lambda x: dot_t(x, slots[:, :owned]))
+
+
+def gather_kernel(part, fetched, inv_mass, slots, gathered):
+    rows = part.shape[0]
+    owned = inv_mass.shape[1]
+    values = jnp.concatenate(
+        [part[:, :owned] * inv_mass[...], part[:, owned:] * fetched[rows : rows + 1, :]],
+        axis=1,
+    )
+    gathered[...] = twice(values, lambda x: dot_t(x, slots[...]))
+
+
+def apply_cells(gathered, late, late_slots, scale, slots, high, low):
+    rows = gathered.shape[0]
     pad = high.shape[0]
-    n_cells = chosen_all.shape[1] // pad
-    values = jnp.concatenate([own, ghost], axis=1)
-    gathered = dot(jnp.concatenate(parts(values, 2), axis=0), chosen_all[...])
-    gathered = gathered.astype(bf16)
+    n_cells = slots.shape[0] // pad
+    values = gathered[...] + twice(late, lambda x: dot(x, late_slots))
+    v_high, v_low = parts(values, 2)
     stacked = jnp.concatenate(
-        [gathered[:rows, c * pad : (c + 1) * pad] for c in range(n_cells)]
-        + [gathered[rows:, c * pad : (c + 1) * pad] for c in range(n_cells)],
+        [v_high[:, c * pad : (c + 1) * pad] for c in range(n_cells)]
+        + [v_low[:, c * pad : (c + 1) * pad] for c in range(n_cells)],
         axis=0,
     )
     half = n_cells * rows
@@ -119,9 +156,7 @@
     product = jnp.concatenate(
         [product[c * rows : (c + 1) * rows] for c in range(n_cells)], axis=1
     ) * scale[...]
-    summed = dot_t(jnp.concatenate(parts(product, 2), axis=0), chosen_all[...])
-    summed = summed[:rows] + summed[rows:]
-    return summed[:, :owned], summed[:, owned:]
+    return twice(product, lambda x: dot(x, slots[...]))
 
 
 def is_even():
@@ -144,40 +179,43 @@
 
 
 def first_kernel(
-    states, fetched, inv_mass, potential, scale, chosen_all, high, low, chosen,
-    far, near, partial,
+    states, gathered, fetched, inv_mass, potential, scale, slots, late_slots, high, low,
+    chosen, far, near, partial,
 ):
     rows, owned = states.shape
-    current = states[...]
     ghost_inv = fetched[rows : rows + 1, :]
-    ghost = fetched[:rows, :]
-    own_sum, ghost_sum = apply_cells(
-        current * inv_mass[...], ghost * ghost_inv, scale, chosen_all, high, low
-    )
-    up = ghost_inv * ghost_sum * (1.0 / HALF_WIDTH)
-    here = (inv_mass[...] * own_sum + (potential[...] - CENTER) * current) * (1.0 / HALF_WIDTH)
+    shared_count = chosen.shape[1]
+    summed = apply_cells(
+        gathered, fetched[:rows, :] * ghost_inv, late_slots[shared_count:, :], scale, slots,
+        high, low,
+    )
+    up = ghost_inv * summed[:, owned:] * (1.0 / HALF_WIDTH)
+    here = (
+        inv_mass[...] * summed[:, :owned] + (potential[...] - CENTER) * states[...]
+    ) * (1.0 / HALF_WIDTH)
     partial[:, :owned] = here
     partial[:, owned:] = up
     send_both(up, picked(here, chosen[...]), near, far)
 
 
-def complete(part, got_up, got_down, chosen):
-    owned = chosen.shape[0]
-    return part[:, :owned] + placed(got_up, chosen[...]), part[:, owned:] + got_down
+def complete(part, got_up, got_down, chosen_t):
+    owned = chosen_t.shape[1]
+    return part[:, :owned] + placed(got_up, chosen_t[...]), part[:, owned:] + got_down
 
 
 def next_kernel(
-    previous, part, fetched, got_near, got_far, inv_mass, potential, scale, chosen_all,
-    high, low, chosen, far, near, partial, current_out,
+    previous, part, gathered, message, fetched, got_near, got_far, inv_mass, potential, scale,
+    slots, late_slots, high, low, chosen, chosen_t, far, near, partial, current_out,
 ):
     rows, owned = current_out.shape
-    current, ghost = complete(part, *got_both(got_near, got_far), chosen)
+    got_up, got_down = got_both(got_near, got_far)
     ghost_inv = fetched[rows : rows + 1, :]
-    own_sum, ghost_sum = apply_cells(
-        current * inv_mass[...], ghost * ghost_inv, scale, chosen_all, high, low
-    )
-    up = ghost_inv * ghost_sum * (2.0 / HALF_WIDTH)
-    here = (inv_mass[...] * own_sum + (potential[...] - CENTER) * current) * (
+    shared_inv = message[rows : rows + 1, :]
+    late = jnp.concatenate([got_up * shared_inv, got_down * ghost_inv], axis=1)
+    summed = apply_cells(gathered, late, late_slots[...], scale, slots, high, low)
+    current = part[:, :owned] + placed(got_up, chosen_t[...])
+    up = ghost_inv * summed[:, owned:] * (2.0 / HALF_WIDTH)
+    here = (inv_mass[...] * summed[:, :owned] + (potential[...] - CENTER) * current) * (
         2.0 / HALF_WIDTH
     ) - previous[...]
     current_out[...] = current
@@ -200,24 +238,24 @@
     return late[:, :count], late[:, count:]
 
 
-def finish_kernel(part, late, chosen, filtered, left):
+def finish_kernel(part, late, chosen_t, filtered, left):
     owned = filtered.shape[1]
-    current, ghost = complete(part, *halves(late), chosen)
+    current, ghost = complete(part, *halves(late), chosen_t)
     filtered[...] = current
     left[:, :owned] = current
     left[:, owned:] = ghost
 
 
-def gram_kernel(total_nodes, left, sibling, late, chosen, *rest):
+def gram_kernel(total_nodes, left, sibling, late, chosen_t, *rest):
     blocks, (out, g_high, g_low) = rest[:-3], rest[-3:]
     chips = len(blocks)
-    rows, owned = left.shape[0], chosen.shape[0]
+    rows = left.shape[0]
     chip = lax.axis_index("chip")
     core = lax.axis_index("core")
     for s in range(chips):
         at = pl.ds(pl.multiple_of((chip ^ s) * rows, rows), rows)
         g_high[at, :], g_low[at, :] = parts(blocks[s][...], 2)
-    theirs = jnp.concatenate(complete(sibling, *halves(late), chosen), axis=1)
+    theirs = jnp.concatenate(complete(sibling, *halves(late), chosen_t), axis=1)
     high, low = parts(jnp.concatenate([left[...], theirs], axis=0), 2)
     by_high = dot_t(jnp.concatenate([high, low], axis=0), g_high[...])
     whole = by_high[: 2 * rows] + by_high[2 * rows :] + dot_t(high, g_low[...])
@@ -302,32 +340,39 @@
         )
     )
     fetched = lax.ppermute(message, DOM, backward)
-    prepared = call(
+    slot_count = n_cells * pad
+    slots, late_slots, high, low, chosen, chosen_t, scale = call(
         prepare_kernel,
         (
-            shape_of(nodes, n_cells * pad, dtype=bf16),
+            shape_of(slot_count, nodes, dtype=bf16),
+            shape_of(2 * shared_count, slot_count, dtype=bf16),
             shape_of(pad, pad, dtype=bf16),
             shape_of(pad, pad, dtype=bf16),
             shape_of(owned, shared_count, dtype=bf16),
-            shape_of(1, n_cells * pad),
+            shape_of(shared_count, owned, dtype=bf16),
+            shape_of(1, slot_count),
         ),
         [in_vmem] * 3 + [in_smem],
-        [pltpu.VMEM((8, pad), jnp.int32), pltpu.VMEM((pad, pad), f32)],
+        [pltpu.VMEM((16, pad), jnp.int32), pltpu.VMEM((pad, pad), f32)],
     )(cells, stiff, shared, cell_scale)
-    *matrices, chosen, scale_row = prepared
-    fixed = (inv_mass, pot, scale_row, *matrices, chosen)
+    fixed = (inv_mass, pot, scale, slots, late_slots, high, low, chosen)
+    by_slot = shape_of(rows, slot_count)
 
     def swapped(near, far):
         return lax.ppermute(near, DOM, near_pairs), lax.ppermute(far, DOM, far_pairs)
 
-    far, near, partial = call(first_kernel, (tall, edge, wide), [in_vmem] * 9)(
-        states, fetched, *fixed
+    gathered = call(first_gather_kernel, by_slot, [in_vmem] * 3)(states, inv_mass, slots)
+    far, near, partial = call(first_kernel, (tall, edge, wide), [in_vmem] * 11)(
+        states, gathered, fetched, *fixed
     )
     previous = states
     for _ in range(DEGREE - 1):
+        gathered = call(gather_kernel, by_slot, [in_vmem] * 4)(
+            partial, fetched, inv_mass, slots
+        )
         far, near, partial, previous = call(
-            next_kernel, (tall, edge, wide, block), [in_vmem] * 12
-        )(previous, partial, fetched, *swapped(near, far), *fixed)
+            next_kernel, (tall, edge, wide, block), [in_vmem] * 16
+        )(previous, partial, gathered, message, fetched, *swapped(near, far), *fixed, chosen_t)
 
     def from_chip(x, s):
         return lax.ppermute(x, "chip", [(i, i ^ s) for i in range(chips)])
@@ -345,13 +390,13 @@
     late = call(late_kernel, shape_of(rows, 2 * shared_count), [in_vmem] * 2)(
         got_near, got_far
     )
-    filtered, left = call(finish_kernel, (block, wide), [in_vmem] * 3)(partial, late, chosen)
+    filtered, left = call(finish_kernel, (block, wide), [in_vmem] * 3)(partial, late, chosen_t)
     gram = call(
         functools.partial(gram_kernel, owned * n_dom),
         shape_of(2 * rows, chips * rows),
         [in_vmem] * (4 + chips),
         [pltpu.VMEM((chips * rows, nodes), bf16)] * 2,
-    )(left, from_sibling(partial), from_sibling(late), chosen, *blocks)
+    )(left, from_sibling(partial), from_sibling(late), chosen_t, *blocks)
 
     n_z = lax.axis_size("z")
     n_across = lax.axis_size(("x", "half"))

time: 136 us -> 132 us (0.971)
  waiting for transfers between devices: 14.3 us -> 11.1 us
  starting transfers between devices: 63.7 us -> 62.1 us
    ppermute x3, waiting for transfers between devices: 7.76 us -> 4.63 us  [swapped(): lax.ppermute(near, DOM, near_pairs)]
    ppermute x3, starting transfers between devices: 28.1 us -> 26.5 us  [swapped(): lax.ppermute(far, DOM, far_pairs)]
    pallas_call x5 -> x8, Pallas kernels: 13.8 us -> 14 us  [the longest x2 4.81 us: per_device(): call(next_kernel, (tall, edge, wide, block), [in_vmem] * 16)]
  transfers between devices with their start and end apart: 12 -> 12, of which waited for: 5 -> 5; matrix products, arithmetic and copies ran while one was open for 0% -> 0% of each run, Pallas kernels for 2% -> 5%
where the time goes in v6:
time: 132 us
  starting transfers between devices  62.1 us (47%)
  blocking collectives  40 us (30%)
  Pallas kernels  16.2 us (12%)
  waiting for transfers between devices  11.1 us (8%)
  local copies, waits for them, and re-layouts  1.32 us (1%)
    ppermute x3, starting transfers between devices, swapped(): lax.ppermute(far, DOM, far_pairs)  26.5 us
    ppermute x1, starting transfers between devices, per_device(): fetched = lax.ppermute(message, DOM, backward)  16.6 us
    all_to_all x1, blocking collectives, per_device(): spread = lax.all_to_all(mine, ('x', 'half'), 0, 0, tiled=True)  16.2 us
    all_to_all x1, blocking collectives, per_device(): lax.all_to_all(jnp.broadcast_to(mine[None], (n_z, *mine.shape)), 'z', 0,...  12.1 us
    all_to_all x1, blocking collectives, per_device(): lax.all_to_all(gram.reshape(2 * n_z, each, chips * rows), ('core', 'z'),...  11.7 us
    ppermute x3, starting transfers between devices, from_chip(): return lax.ppermute(x, 'chip', [(i, i ^ s) for i in range(chips)])  9.43 us
    ppermute x3, starting transfers between devices, swapped(): lax.ppermute(near, DOM, near_pairs)  5.76 us
    pallas_call x2, Pallas kernels, per_device(): call(next_kernel, (tall, edge, wide, block), [in_vmem] * 16)  4.81 us
  transfers between devices with their start and end apart: 12, of which 5 were waited for; matrix products, arithmetic and copies ran while one was open for 0% of the time, Pallas kernels for 5%

profile of v6, /device:TPU:16, one launch (start us, length us, event | category | flops | bytes accessed | tf_op | source)
XLA Modules:
  0.0 131.6 jit_solution(9544738709478469671)
XLA Ops:
  0.6 1.3 %shard_map.86 = (f32[72,128]{1,0:T(8,128)S(1)}, f32[64,1024]{1,0:T(8,128)S(1)}, f32[1,1024]{1,0:T(1,128)S(1)}, s32[1,128]{1,0:T(1,128)S(1)}, f32[1,1024]{1,0:T(1...) custom-call(f32[64,1024]{1,0:T(8,128)} %states.1, f32[1,1024]{1,0:T(1,128)} %bitcast.7, s32[1,128]{1,0:T(1,128)} %bitcast.9, ...), custom_call_target="tpu_custom_call" | custom-call | tf_op jit(solution)/shard_map/pallas_call | solution.py:324
  2.0 16.6 %collective-permute-start = (f32[72,128]{1,0:T(8,128)S(1)}, f32[72,128]{1,0:T(8,128)S(1)}, u32[]{:S(2)}, u32[]{:S(2)}) collective-permute-start(f32[72,128]{1,0:T(8,128)S(1)} %get-tuple-element.34.message), channel_id=1, source_target_pairs={{0,63},{1,0},{2,1},{3,2},{4,3},{5,4},{6,5},{7,6},{8,7},{9,8},{10,9... | collective-permute-start | bytes 110600 | tf_op jit(solution)/shard_map/ppermute | solution.py:342
  18.6 0.6 copy-done
  19.2 1.5 %shard_map.87 = (bf16[2304,1152]{1,0:T(8,128)(2,1)S(1)}, bf16[256,2304]{1,0:T(8,128)(2,1)S(1)}, bf16[384,384]{1,0:T(8,128)(2,1)S(1)}, bf16[384,384]{1,0:T(8,128)...) custom-call(s32[6,343]{1,0:T(8,128)S(1)} %get-tuple-element.30.cells, ...), custom_call_target="tpu_custom_call" | custom-call | tf_op jit(solution)/shard_map/pallas_call | solution.py:344
  20.8 1.6 %shard_map.88.gathered = f32[64,2304]{1,0:T(8,128)S(1)} custom-call(f32[64,1024]{1,0:T(8,128)S(1)} %get-tuple-element.28.states.previous, f32[1,1024]{1,0:T(1,128)S(1)} %get-tuple-element.29.inv_mass, bf16[2304,1152]{1,0:T(8,128)(2,1)S(1)} %get-tuple-element.33.slots), custom_call_target="tpu_custom_call" | custom-call | tf_op jit(solution)/shard_map/pallas_call | solution.py:364
  22.4 2.0 %shard_map.89 = (f32[72,128]{1,0:T(8,128)S(1)}, f32[64,128]{1,0:T(8,128)S(1)}, f32[64,1152]{1,0:T(8,128)S(1)}) custom-call(f32[64,1024]{1,0:T(8,128)S(1)} %get-tuple-element.28.states.previous, f32[64,2304]{1,0:T(8,128)S(1)} %shard_map.88.gathered, f32[72,128]{1,0:T(8,128)S(1)} %collective-permute-done.fetched, f32[1,1024]{1,0:T(1,128)S(1)} %get-tuple-element.29.inv_mass, ...), custom_call_target="tpu_custom_call" | custom-call | tf_op jit(solution)/shard_map/pallas_call | solution.py:365
  24.4 10.1 %collective-permute-start.2 = (f32[72,128]{1,0:T(8,128)S(1)}, f32[72,128]{1,0:T(8,128)S(1)}, u32[]{:S(2)}, u32[]{:S(2)}) collective-permute-start(f32[72,128]{1,0:T(8,128)S(1)} %get-tuple-element.43), channel_id=1, source_target_pairs={{0,63},{1,2},{2,1},{3,4},{4,3},{5,6},{6,5},{7,8},{8,7},{9,10},{10,... | collective-permute-start | bytes 110600 | tf_op jit(solution)/shard_map/ppermute | solution.py:362
  34.5 1.9 %collective-permute-start.1 = (f32[64,128]{1,0:T(8,128)S(1)}, f32[64,128]{1,0:T(8,128)S(1)}, u32[]{:S(2)}, u32[]{:S(2)}) collective-permute-start(f32[64,128]{1,0:T(8,128)S(1)} %get-tuple-element.42), channel_id=1, source_target_pairs={{0,1},{1,0},{2,3},{3,2},{4,5},{5,4},{6,7},{7,6},{8,9},{9,8},{10,11... | collective-permute-start | bytes 98312 | tf_op jit(solution)/shard_map/ppermute | solution.py:362
  36.5 1.6 %shard_map.90.gathered = f32[64,2304]{1,0:T(8,128)S(1)} custom-call(f32[64,1152]{1,0:T(8,128)S(1)} %get-tuple-element.41.part, f32[72,128]{1,0:T(8,128)S(1)} %collective-permute-done.fetched, f32[1,1024]{1,0:T(1,128)S(1)} %get-tuple-element.29.inv_mass, bf16[2304,1152]{1,0:T(8,128)(2,1)S(1)} %get-tuple-element.33.slots), custom_call_target="tpu_custom_call" | custom-call | tf_op jit(solution)/shard_map/pallas_call | solution.py:370
  38.0 2.3 %collective-permute-done.1.got_near = f32[64,128]{1,0:T(8,128)S(1)} collective-permute-done((f32[64,128]{1,0:T(8,128)S(1)}, f32[64,128]{1,0:T(8,128)S(1)}, u32[]{:S(2)}, u32[]{:S(2)}) %collective-permute-start.1) | collective-permute-done | bytes 32800 | tf_op jit(solution)/shard_map/ppermute | solution.py:362
  40.3 2.1 %shard_map.91 = (f32[72,128]{1,0:T(8,128)S(1)}, f32[64,128]{1,0:T(8,128)S(1)}, f32[64,1152]{1,0:T(8,128)S(1)}, f32[64,1024]{1,0:T(8,128)S(1)}) custom-call(f32[64,1024]{1,0:T(8,128)S(1)} %get-tuple-element.28.states.previous, f32[64,1152]{1,0:T(8,128)S(1)} %get-tuple-element.41.part, f32[64,2304]{1,0:T(8,128)S(1)} %shard_map.90.gathered, ...), custom_call_target="tpu_custom_call" | custom-call | tf_op jit(solution)/shard_map/pallas_call | solution.py:373
  42.5 8.2 %collective-permute-start.4 = (f32[72,128]{1,0:T(8,128)S(1)}, f32[72,128]{1,0:T(8,128)S(1)}, u32[]{:S(2)}, u32[]{:S(2)}) collective-permute-start(f32[72,128]{1,0:T(8,128)S(1)} %get-tuple-element.48), channel_id=1, source_target_pairs={{0,63},{1,2},{2,1},{3,4},{4,3},{5,6},{6,5},{7,8},{8,7},{9,10},{10,... | collective-permute-start | bytes 110600 | tf_op jit(solution)/shard_map/ppermute | solution.py:362
  50.6 1.9 %collective-permute-start.3 = (f32[64,128]{1,0:T(8,128)S(1)}, f32[64,128]{1,0:T(8,128)S(1)}, u32[]{:S(2)}, u32[]{:S(2)}) collective-permute-start(f32[64,128]{1,0:T(8,128)S(1)} %get-tuple-element.47), channel_id=1, source_target_pairs={{0,1},{1,0},{2,3},{3,2},{4,5},{5,4},{6,7},{7,6},{8,9},{9,8},{10,11... | collective-permute-start | bytes 98312 | tf_op jit(solution)/shard_map/ppermute | solution.py:362
  52.6 1.6 %shard_map.92.gathered = f32[64,2304]{1,0:T(8,128)S(1)} custom-call(f32[64,1152]{1,0:T(8,128)S(1)} %get-tuple-element.46.part, f32[72,128]{1,0:T(8,128)S(1)} %collective-permute-done.fetched, f32[1,1024]{1,0:T(1,128)S(1)} %get-tuple-element.29.inv_mass, bf16[2304,1152]{1,0:T(8,128)(2,1)S(1)} %get-tuple-element.33.slots), custom_call_target="tpu_custom_call" | custom-call | tf_op jit(solution)/shard_map/pallas_call | solution.py:370
  54.1 2.3 %collective-permute-done.3.got_near = f32[64,128]{1,0:T(8,128)S(1)} collective-permute-done((f32[64,128]{1,0:T(8,128)S(1)}, f32[64,128]{1,0:T(8,128)S(1)}, u32[]{:S(2)}, u32[]{:S(2)}) %collective-permute-start.3) | collective-permute-done | bytes 32800 | tf_op jit(solution)/shard_map/ppermute | solution.py:362
  56.5 2.7 %shard_map.93 = (f32[72,128]{1,0:T(8,128)S(1)}, f32[64,128]{1,0:T(8,128)S(1)}, f32[64,1152]{1,0:T(8,128)S(1)}, f32[64,1024]{1,0:T(8,128)}) custom-call(f32[64,1024]{1,0:T(8,128)S(1)} %get-tuple-element.45.previous, f32[64,1152]{1,0:T(8,128)S(1)} %get-tuple-element.46.part, f32[64,2304]{1,0:T(8,128)S(1)} %shard_map.92.gathered, ...), custom_call_target="tpu_custom_call" | custom-call | tf_op jit(solution)/shard_map/pallas_call | solution.py:373
  59.1 4.0 %collective-permute-start.10 = (f32[64,1152]{1,0:T(8,128)S(1)}, f32[64,1152]{1,0:T(8,128)S(1)}, u32[]{:S(2)}, u32[]{:S(2)}) collective-permute-start(f32[64,1152]{1,0:T(8,128)S(1)} %get-tuple-element.49.part.rest_0_), channel_id=1, source_target_pairs={{0,256},{128,384},{256,0},{384,128},{1,257},{129,385},{257,1},{385... | collective-permute-start | bytes 884744 | tf_op jit(solution)/shard_map/ppermute | solution.py:378
  63.2 8.2 %collective-permute-start.6 = (f32[72,128]{1,0:T(8,128)S(1)}, f32[72,128]{1,0:T(8,128)S(1)}, u32[]{:S(2)}, u32[]{:S(2)}) collective-permute-start(f32[72,128]{1,0:T(8,128)S(1)} %get-tuple-element.51), channel_id=1, source_target_pairs={{0,63},{1,2},{2,1},{3,4},{4,3},{5,6},{6,5},{7,8},{8,7},{9,10},{10,... | collective-permute-start | bytes 110600 | tf_op jit(solution)/shard_map/ppermute | solution.py:362
  71.3 1.9 %collective-permute-start.5 = (f32[64,128]{1,0:T(8,128)S(1)}, f32[64,128]{1,0:T(8,128)S(1)}, u32[]{:S(2)}, u32[]{:S(2)}) collective-permute-start(f32[64,128]{1,0:T(8,128)S(1)} %get-tuple-element.50), channel_id=1, source_target_pairs={{0,1},{1,0},{2,3},{3,2},{4,5},{5,4},{6,7},{7,6},{8,9},{9,8},{10,11... | collective-permute-start | bytes 98312 | tf_op jit(solution)/shard_map/ppermute | solution.py:362
  73.3 3.5 %collective-permute-start.9 = (f32[64,1152]{1,0:T(8,128)S(1)}, f32[64,1152]{1,0:T(8,128)S(1)}, u32[]{:S(2)}, u32[]{:S(2)}) collective-permute-start(f32[64,1152]{1,0:T(8,128)S(1)} %get-tuple-element.49.part.rest_0_), channel_id=1, source_target_pairs={{0,128},{128,0},{256,384},{384,256},{1,129},{129,1},{257,385},{385... | collective-permute-start | bytes 884744 | tf_op jit(solution)/shard_map/ppermute | solution.py:378
  76.8 1.9 %collective-permute-start.7 = (f32[64,1152]{1,0:T(8,128)S(1)}, f32[64,1152]{1,0:T(8,128)S(1)}, u32[]{:S(2)}, u32[]{:S(2)}) collective-permute-start(f32[64,1152]{1,0:T(8,128)S(1)} %get-tuple-element.49.part.rest_0_), channel_id=1, source_target_pairs={{0,64},{64,0},{1,65},{65,1},{2,66},{66,2},{3,67},{67,3},{4,68},{68... | collective-permute-start | bytes 884744 | tf_op jit(solution)/shard_map/ppermute | solution.py:388
  78.7 2.4 %collective-permute-done.6.got_far.far = f32[72,128]{1,0:T(8,128)S(1)} collective-permute-done((f32[72,128]{1,0:T(8,128)S(1)}, f32[72,128]{1,0:T(8,128)S(1)}, u32[]{:S(2)}, u32[]{:S(2)}) %collective-permute-start.6) | collective-permute-done | bytes 36896 | tf_op jit(solution)/shard_map/ppermute | solution.py:362
  81.1 1.9 %collective-permute-start.11 = (f32[64,1152]{1,0:T(8,128)S(1)}, f32[64,1152]{1,0:T(8,128)S(1)}, u32[]{:S(2)}, u32[]{:S(2)}) collective-permute-start(f32[64,1152]{1,0:T(8,128)S(1)} %shard_map.96.rest_2_), channel_id=1, source_target_pairs={{0,128},{128,0},{256,384},{384,256},{1,129},{129,1},{257,385},{385... | collective-permute-start | bytes 884744 | tf_op jit(solution)/shard_map/ppermute | solution.py:378
  83.0 1.9 %collective-permute-start.8 = (f32[64,256]{1,0:T(8,128)S(1)}, f32[64,256]{1,0:T(8,128)S(1)}, u32[]{:S(2)}, u32[]{:S(2)}) collective-permute-start(f32[64,256]{1,0:T(8,128)S(1)} %shard_map.94.late), channel_id=1, source_target_pairs={{0,64},{64,0},{1,65},{65,1},{2,66},{66,2},{3,67},{67,3},{4,68},{68... | collective-permute-start | bytes 196616 | tf_op jit(solution)/shard_map/ppermute | solution.py:388
  85.0 1.0 shard_map.95
  85.9 0.3 collective-permute-done.8.late
  86.2 3.8 %collective-permute-done.11.rest_3_ = f32[64,1152]{1,0:T(8,128)S(1)} collective-permute-done((f32[64,1152]{1,0:T(8,128)S(1)}, f32[64,1152]{1,0:T(8,128)S(1)}, u32[]{:S(2)}, u32[]{:S(2)}) %collective-permute-start.11) | collective-permute-done | bytes 294944 | tf_op jit(solution)/shard_map/ppermute | solution.py:378
  90.0 0.8 shard_map.97
  90.8 11.7 %all_to_all.15.pieces = f32[16,8,256]{2,1,0:T(8,128)S(1)} all-to-all(f32[16,8,256]{2,1,0:T(8,128)S(1)} %bitcast.5), channel_id=1, replica_groups=mesh['chip'=4,'core'=2,'x'=4,'half'=2,'z'=8] {'core','z'}, dimensions={0} | all-to-all | bytes 262144 | tf_op jit(solution)/shard_map/all_to_all | solution.py:404
  102.6 16.2 %all_to_all.16 = f32[8,8,512]{2,1,0:T(8,128)S(1)} all-to-all(f32[8,8,512]{2,1,0:T(8,128)S(1)} %shard_map.98), channel_id=1, replica_groups=mesh['chip'=4,'core'=2,'x'=4,'half'=2,'z'=8] {'x','half'}, dimensions={0} | all-to-all | bytes 262144 | tf_op jit(solution)/shard_map/all_to_all | solution.py:408
  118.8 12.1 %all_to_all.17 = f32[8,8,512]{2,1,0:T(8,128)S(1)} all-to-all(f32[8,8,512]{2,1,0:T(8,128)S(1)} %broadcast_in_dim.2), channel_id=1, replica_groups=mesh['chip'=4,'core'=2,'x'=4,'half'=2,'z'=8] {'z'}, dimensions={0} | all-to-all | bytes 262144 | tf_op jit(solution)/shard_map/all_to_all | solution.py:410
  130.9 0.7 copy.12
  (13 shorter events, 0.2 us)
Async XLA Ops:
  2.0 20.4 %collective-permute-start = (f32[72,128]{1,0:T(8,128)S(1)}, f32[72,128]{1,0:T(8,128)S(1)}, u32[]{:S(2)}, u32[]{:S(2)}) collective-permute-start(f32[72,128]{1,0:T(8,128)S(1)} %get-tuple-element.34.message), channel_id=1, source_target_pairs={{0,63},{1,0},{2,1},{3,2},{4,3},{5,4},{6,5},{7,6},{8,7},{9,8},{10,9... | collective-permute-start | bytes 110600 | tf_op jit(solution)/shard_map/ppermute | solution.py:342
  18.6 0.7 copy-start
  24.4 16.0 %collective-permute-start.2 = (f32[72,128]{1,0:T(8,128)S(1)}, f32[72,128]{1,0:T(8,128)S(1)}, u32[]{:S(2)}, u32[]{:S(2)}) collective-permute-start(f32[72,128]{1,0:T(8,128)S(1)} %get-tuple-element.43), channel_id=1, source_target_pairs={{0,63},{1,2},{2,1},{3,4},{4,3},{5,6},{6,5},{7,8},{8,7},{9,10},{10,... | collective-permute-start | bytes 110600 | tf_op jit(solution)/shard_map/ppermute | solution.py:362
  34.5 5.8 %collective-permute-start.1 = (f32[64,128]{1,0:T(8,128)S(1)}, f32[64,128]{1,0:T(8,128)S(1)}, u32[]{:S(2)}, u32[]{:S(2)}) collective-permute-start(f32[64,128]{1,0:T(8,128)S(1)} %get-tuple-element.42), channel_id=1, source_target_pairs={{0,1},{1,0},{2,3},{3,2},{4,5},{5,4},{6,7},{7,6},{8,9},{9,8},{10,11... | collective-permute-start | bytes 98312 | tf_op jit(solution)/shard_map/ppermute | solution.py:362
  42.5 14.0 %collective-permute-start.4 = (f32[72,128]{1,0:T(8,128)S(1)}, f32[72,128]{1,0:T(8,128)S(1)}, u32[]{:S(2)}, u32[]{:S(2)}) collective-permute-start(f32[72,128]{1,0:T(8,128)S(1)} %get-tuple-element.48), channel_id=1, source_target_pairs={{0,63},{1,2},{2,1},{3,4},{4,3},{5,6},{6,5},{7,8},{8,7},{9,10},{10,... | collective-permute-start | bytes 110600 | tf_op jit(solution)/shard_map/ppermute | solution.py:362
  50.6 5.8 %collective-permute-start.3 = (f32[64,128]{1,0:T(8,128)S(1)}, f32[64,128]{1,0:T(8,128)S(1)}, u32[]{:S(2)}, u32[]{:S(2)}) collective-permute-start(f32[64,128]{1,0:T(8,128)S(1)} %get-tuple-element.47), channel_id=1, source_target_pairs={{0,1},{1,0},{2,3},{3,2},{4,5},{5,4},{6,7},{7,6},{8,9},{9,8},{10,11... | collective-permute-start | bytes 98312 | tf_op jit(solution)/shard_map/ppermute | solution.py:362
  59.1 22.0 %collective-permute-start.10 = (f32[64,1152]{1,0:T(8,128)S(1)}, f32[64,1152]{1,0:T(8,128)S(1)}, u32[]{:S(2)}, u32[]{:S(2)}) collective-permute-start(f32[64,1152]{1,0:T(8,128)S(1)} %get-tuple-element.49.part.rest_0_), channel_id=1, source_target_pairs={{0,256},{128,384},{256,0},{384,128},{1,257},{129,385},{257,1},{385... | collective-permute-start | bytes 884744 | tf_op jit(solution)/shard_map/ppermute | solution.py:378
  63.2 17.9 %collective-permute-start.6 = (f32[72,128]{1,0:T(8,128)S(1)}, f32[72,128]{1,0:T(8,128)S(1)}, u32[]{:S(2)}, u32[]{:S(2)}) collective-permute-start(f32[72,128]{1,0:T(8,128)S(1)} %get-tuple-element.51), channel_id=1, source_target_pairs={{0,63},{1,2},{2,1},{3,4},{4,3},{5,6},{6,5},{7,8},{8,7},{9,10},{10,... | collective-permute-start | bytes 110600 | tf_op jit(solution)/shard_map/ppermute | solution.py:362
  71.3 7.4 %collective-permute-start.5 = (f32[64,128]{1,0:T(8,128)S(1)}, f32[64,128]{1,0:T(8,128)S(1)}, u32[]{:S(2)}, u32[]{:S(2)}) collective-permute-start(f32[64,128]{1,0:T(8,128)S(1)} %get-tuple-element.50), channel_id=1, source_target_pairs={{0,1},{1,0},{2,3},{3,2},{4,5},{5,4},{6,7},{7,6},{8,9},{9,8},{10,11... | collective-permute-start | bytes 98312 | tf_op jit(solution)/shard_map/ppermute | solution.py:362
  73.3 12.9 %collective-permute-start.9 = (f32[64,1152]{1,0:T(8,128)S(1)}, f32[64,1152]{1,0:T(8,128)S(1)}, u32[]{:S(2)}, u32[]{:S(2)}) collective-permute-start(f32[64,1152]{1,0:T(8,128)S(1)} %get-tuple-element.49.part.rest_0_), channel_id=1, source_target_pairs={{0,128},{128,0},{256,384},{384,256},{1,129},{129,1},{257,385},{385... | collective-permute-start | bytes 884744 | tf_op jit(solution)/shard_map/ppermute | solution.py:378
  76.8 9.4 %collective-permute-start.7 = (f32[64,1152]{1,0:T(8,128)S(1)}, f32[64,1152]{1,0:T(8,128)S(1)}, u32[]{:S(2)}, u32[]{:S(2)}) collective-permute-start(f32[64,1152]{1,0:T(8,128)S(1)} %get-tuple-element.49.part.rest_0_), channel_id=1, source_target_pairs={{0,64},{64,0},{1,65},{65,1},{2,66},{66,2},{3,67},{67,3},{4,68},{68... | collective-permute-start | bytes 884744 | tf_op jit(solution)/shard_map/ppermute | solution.py:388
  81.1 8.9 %collective-permute-start.11 = (f32[64,1152]{1,0:T(8,128)S(1)}, f32[64,1152]{1,0:T(8,128)S(1)}, u32[]{:S(2)}, u32[]{:S(2)}) collective-permute-start(f32[64,1152]{1,0:T(8,128)S(1)} %shard_map.96.rest_2_), channel_id=1, source_target_pairs={{0,128},{128,0},{256,384},{384,256},{1,129},{129,1},{257,385},{385... | collective-permute-start | bytes 884744 | tf_op jit(solution)/shard_map/ppermute | solution.py:378
  83.0 3.1 %collective-permute-start.8 = (f32[64,256]{1,0:T(8,128)S(1)}, f32[64,256]{1,0:T(8,128)S(1)}, u32[]{:S(2)}, u32[]{:S(2)}) collective-permute-start(f32[64,256]{1,0:T(8,128)S(1)} %shard_map.94.late), channel_id=1, source_target_pairs={{0,64},{64,0},{1,65},{65,1},{2,66},{66,2},{3,67},{67,3},{4,68},{68... | collective-permute-start | bytes 196616 | tf_op jit(solution)/shard_map/ppermute | solution.py:388

commit v7 on v6

--- a/solution.py
+++ b/solution.py
@@ -11,6 +11,7 @@
 CENTER = 1.0
 HALF_WIDTH = 4.0
 LIMIT = 28 * 1024 * 1024
+LATE = 8
 BAND = ("chip", "core")
 DOM = ("x", "half", "z")
 
@@ -205,9 +206,9 @@
 
 def next_kernel(
     previous, part, gathered, message, fetched, got_near, got_far, inv_mass, potential, scale,
-    slots, late_slots, high, low, chosen, chosen_t, far, near, partial, current_out,
+    slots, late_slots, high, low, chosen, chosen_t, far, near, partial, *current_out,
 ):
-    rows, owned = current_out.shape
+    rows, owned = previous.shape
     got_up, got_down = got_both(got_near, got_far)
     ghost_inv = fetched[rows : rows + 1, :]
     shared_inv = message[rows : rows + 1, :]
@@ -218,29 +219,33 @@
     here = (inv_mass[...] * summed[:, :owned] + (potential[...] - CENTER) * current) * (
         2.0 / HALF_WIDTH
     ) - previous[...]
-    current_out[...] = current
+    for out in current_out:
+        out[...] = current
     partial[:, :owned] = here
     partial[:, owned:] = up
     send_both(up, picked(here, chosen[...]), near, far)
 
 
-def relay_kernel(block, near, far, out):
-    del near, far
+def relay_kernel(block, near, out):
+    del near
     out[:8, :128] = block[:8, :128]
 
 
 def late_kernel(got_near, got_far, late):
-    late[...] = jnp.concatenate(got_both(got_near, got_far), axis=1)
-
-
-def halves(late):
-    count = late.shape[1] // 2
-    return late[:, :count], late[:, count:]
+    up, down = got_both(got_near, got_far)
+    count = up.shape[1]
+    late[:, :count] = up
+    late[:, count : 2 * count] = down
+    late[:, 2 * count :] = jnp.zeros((up.shape[0], late.shape[1] - 2 * count), f32)
+
+
+def halves(late, count):
+    return late[:, :count], late[:, count : 2 * count]
 
 
 def finish_kernel(part, late, chosen_t, filtered, left):
     owned = filtered.shape[1]
-    current, ghost = complete(part, *halves(late), chosen_t)
+    current, ghost = complete(part, *halves(late, chosen_t.shape[0]), chosen_t)
     filtered[...] = current
     left[:, :owned] = current
     left[:, owned:] = ghost
@@ -255,7 +260,7 @@
     for s in range(chips):
         at = pl.ds(pl.multiple_of((chip ^ s) * rows, rows), rows)
         g_high[at, :], g_low[at, :] = parts(blocks[s][...], 2)
-    theirs = jnp.concatenate(complete(sibling, *halves(late), chosen_t), axis=1)
+    theirs = jnp.concatenate(complete(sibling, *halves(late, chosen_t.shape[0]), chosen_t), axis=1)
     high, low = parts(jnp.concatenate([left[...], theirs], axis=0), 2)
     by_high = dot_t(jnp.concatenate([high, low], axis=0), g_high[...])
     whole = by_high[: 2 * rows] + by_high[2 * rows :] + dot_t(high, g_low[...])
@@ -365,29 +370,28 @@
     far, near, partial = call(first_kernel, (tall, edge, wide), [in_vmem] * 11)(
         states, gathered, fetched, *fixed
     )
-    previous = states
-    for _ in range(DEGREE - 1):
+    previous = [states]
+    for step in range(DEGREE - 1):
         gathered = call(gather_kernel, by_slot, [in_vmem] * 4)(
             partial, fetched, inv_mass, slots
         )
-        far, near, partial, previous = call(
-            next_kernel, (tall, edge, wide, block), [in_vmem] * 16
-        )(previous, partial, gathered, message, fetched, *swapped(near, far), *fixed, chosen_t)
+        currents = [block] * (step < DEGREE - 2)
+        far, near, partial, *previous = call(
+            next_kernel, (tall, edge, wide, *currents), [in_vmem] * 16
+        )(*previous, partial, gathered, message, fetched, *swapped(near, far), *fixed, chosen_t)
 
     def from_chip(x, s):
         return lax.ppermute(x, "chip", [(i, i ^ s) for i in range(chips)])
 
     got_near, got_far = swapped(near, far)
     second = from_chip(partial, 2)
-    relayed = call(relay_kernel, wide, [in_vmem] * 3, aliases={0: 0})(
-        second, got_near, got_far
-    )
+    relayed = call(relay_kernel, wide, [in_vmem] * 2, aliases={0: 0})(second, got_near)
     blocks = [partial, from_chip(partial, 1), relayed, from_chip(relayed, 1)]
 
     def from_sibling(x):
         return lax.ppermute(x, "core", [(0, 1), (1, 0)])
 
-    late = call(late_kernel, shape_of(rows, 2 * shared_count), [in_vmem] * 2)(
+    late = call(late_kernel, shape_of(rows, LATE * shared_count), [in_vmem] * 2)(
         got_near, got_far
     )
     filtered, left = call(finish_kernel, (block, wide), [in_vmem] * 3)(partial, late, chosen_t)

time: 132 us -> 130 us (0.985)
  the two profiles are of different devices: /device:TPU:16 before, /device:TPU:2 now
where the time goes in v7:
time: 130 us
  starting transfers between devices  57.4 us (44%)
  blocking collectives  43.7 us (34%)
  Pallas kernels  15.7 us (12%)
  waiting for transfers between devices  10.8 us (8%)
  local copies, waits for them, and re-layouts  1.32 us (1%)
    ppermute x3, starting transfers between devices, swapped(): lax.ppermute(far, DOM, far_pairs)  23.2 us
    all_to_all x1, blocking collectives, per_device(): spread = lax.all_to_all(mine, ('x', 'half'), 0, 0, tiled=True)  20.5 us
    ppermute x1, starting transfers between devices, per_device(): fetched = lax.ppermute(message, DOM, backward)  16.2 us
    all_to_all x1, blocking collectives, per_device(): lax.all_to_all(jnp.broadcast_to(mine[None], (n_z, *mine.shape)), 'z', 0,...  12.1 us
    all_to_all x1, blocking collectives, per_device(): lax.all_to_all(gram.reshape(2 * n_z, each, chips * rows), ('core', 'z'),...  11.1 us
    ppermute x3, starting transfers between devices, from_chip(): return lax.ppermute(x, 'chip', [(i, i ^ s) for i in range(chips)])  8.22 us
    ppermute x3, waiting for transfers between devices, from_chip(): return lax.ppermute(x, 'chip', [(i, i ^ s) for i in range(chips)])  6.18 us
    ppermute x3, starting transfers between devices, swapped(): lax.ppermute(near, DOM, near_pairs)  5.76 us
  transfers between devices with their start and end apart: 12, of which 4 were waited for; matrix products, arithmetic and copies ran while one was open for 0% of the time, Pallas kernels for 6%

profile of v7, /device:TPU:2, one launch (start us, length us, event | category | flops | bytes accessed | tf_op | source)
XLA Modules:
  0.0 129.7 jit_solution(18350791067858526838)
XLA Ops:
  0.6 1.3 %shard_map.86 = (f32[72,128]{1,0:T(8,128)S(1)}, f32[64,1024]{1,0:T(8,128)S(1)}, f32[1,1024]{1,0:T(1,128)S(1)}, s32[1,128]{1,0:T(1,128)S(1)}, f32[1,1024]{1,0:T(1...) custom-call(f32[64,1024]{1,0:T(8,128)} %states.1, f32[1,1024]{1,0:T(1,128)} %bitcast.7, s32[1,128]{1,0:T(1,128)} %bitcast.9, ...), custom_call_target="tpu_custom_call" | custom-call | tf_op jit(solution)/shard_map/pallas_call | solution.py:329
  2.0 16.2 %collective-permute-start = (f32[72,128]{1,0:T(8,128)S(1)}, f32[72,128]{1,0:T(8,128)S(1)}, u32[]{:S(2)}, u32[]{:S(2)}) collective-permute-start(f32[72,128]{1,0:T(8,128)S(1)} %get-tuple-element.34.message), channel_id=1, source_target_pairs={{0,63},{1,0},{2,1},{3,2},{4,3},{5,4},{6,5},{7,6},{8,7},{9,8},{10,9... | collective-permute-start | bytes 110600 | tf_op jit(solution)/shard_map/ppermute | solution.py:347
  18.2 0.6 copy-done
  18.8 1.5 %shard_map.87 = (bf16[2304,1152]{1,0:T(8,128)(2,1)S(1)}, bf16[256,2304]{1,0:T(8,128)(2,1)S(1)}, bf16[384,384]{1,0:T(8,128)(2,1)S(1)}, bf16[384,384]{1,0:T(8,128)...) custom-call(s32[6,343]{1,0:T(8,128)S(1)} %get-tuple-element.30.cells, ...), custom_call_target="tpu_custom_call" | custom-call | tf_op jit(solution)/shard_map/pallas_call | solution.py:349
  20.4 1.6 %shard_map.88.gathered = f32[64,2304]{1,0:T(8,128)S(1)} custom-call(f32[64,1024]{1,0:T(8,128)S(1)} %get-tuple-element.28.states.previous, f32[1,1024]{1,0:T(1,128)S(1)} %get-tuple-element.29.inv_mass, bf16[2304,1152]{1,0:T(8,128)(2,1)S(1)} %get-tuple-element.33.slots), custom_call_target="tpu_custom_call" | custom-call | tf_op jit(solution)/shard_map/pallas_call | solution.py:369
  22.0 2.0 %shard_map.89 = (f32[72,128]{1,0:T(8,128)S(1)}, f32[64,128]{1,0:T(8,128)S(1)}, f32[64,1152]{1,0:T(8,128)S(1)}) custom-call(f32[64,1024]{1,0:T(8,128)S(1)} %get-tuple-element.28.states.previous, f32[64,2304]{1,0:T(8,128)S(1)} %shard_map.88.gathered, f32[72,128]{1,0:T(8,128)S(1)} %collective-permute-done.fetched, f32[1,1024]{1,0:T(1,128)S(1)} %get-tuple-element.29.inv_mass, ...), custom_call_target="tpu_custom_call" | custom-call | tf_op jit(solution)/shard_map/pallas_call | solution.py:370
  24.0 9.3 %collective-permute-start.2 = (f32[72,128]{1,0:T(8,128)S(1)}, f32[72,128]{1,0:T(8,128)S(1)}, u32[]{:S(2)}, u32[]{:S(2)}) collective-permute-start(f32[72,128]{1,0:T(8,128)S(1)} %get-tuple-element.43), channel_id=1, source_target_pairs={{0,63},{1,2},{2,1},{3,4},{4,3},{5,6},{6,5},{7,8},{8,7},{9,10},{10,... | collective-permute-start | bytes 110600 | tf_op jit(solution)/shard_map/ppermute | solution.py:367
  33.2 1.9 %collective-permute-start.1 = (f32[64,128]{1,0:T(8,128)S(1)}, f32[64,128]{1,0:T(8,128)S(1)}, u32[]{:S(2)}, u32[]{:S(2)}) collective-permute-start(f32[64,128]{1,0:T(8,128)S(1)} %get-tuple-element.42), channel_id=1, source_target_pairs={{0,1},{1,0},{2,3},{3,2},{4,5},{5,4},{6,7},{7,6},{8,9},{9,8},{10,11... | collective-permute-start | bytes 98312 | tf_op jit(solution)/shard_map/ppermute | solution.py:367
  35.2 1.6 %shard_map.90.gathered = f32[64,2304]{1,0:T(8,128)S(1)} custom-call(f32[64,1152]{1,0:T(8,128)S(1)} %get-tuple-element.41.part, f32[72,128]{1,0:T(8,128)S(1)} %collective-permute-done.fetched, f32[1,1024]{1,0:T(1,128)S(1)} %get-tuple-element.29.inv_mass, bf16[2304,1152]{1,0:T(8,128)(2,1)S(1)} %get-tuple-element.33.slots), custom_call_target="tpu_custom_call" | custom-call | tf_op jit(solution)/shard_map/pallas_call | solution.py:375
  36.7 2.3 %collective-permute-done.1.got_near = f32[64,128]{1,0:T(8,128)S(1)} collective-permute-done((f32[64,128]{1,0:T(8,128)S(1)}, f32[64,128]{1,0:T(8,128)S(1)}, u32[]{:S(2)}, u32[]{:S(2)}) %collective-permute-start.1) | collective-permute-done | bytes 32800 | tf_op jit(solution)/shard_map/ppermute | solution.py:367
  39.1 2.1 %shard_map.91 = (f32[72,128]{1,0:T(8,128)S(1)}, f32[64,128]{1,0:T(8,128)S(1)}, f32[64,1152]{1,0:T(8,128)S(1)}, f32[64,1024]{1,0:T(8,128)S(1)}) custom-call(f32[64,1024]{1,0:T(8,128)S(1)} %get-tuple-element.28.states.previous, f32[64,1152]{1,0:T(8,128)S(1)} %get-tuple-element.41.part, f32[64,2304]{1,0:T(8,128)S(1)} %shard_map.90.gathered, ...), custom_call_target="tpu_custom_call" | custom-call | tf_op jit(solution)/shard_map/pallas_call | solution.py:379
  41.2 6.9 %collective-permute-start.4 = (f32[72,128]{1,0:T(8,128)S(1)}, f32[72,128]{1,0:T(8,128)S(1)}, u32[]{:S(2)}, u32[]{:S(2)}) collective-permute-start(f32[72,128]{1,0:T(8,128)S(1)} %get-tuple-element.48), channel_id=1, source_target_pairs={{0,63},{1,2},{2,1},{3,4},{4,3},{5,6},{6,5},{7,8},{8,7},{9,10},{10,... | collective-permute-start | bytes 110600 | tf_op jit(solution)/shard_map/ppermute | solution.py:367
  48.2 1.9 %collective-permute-start.3 = (f32[64,128]{1,0:T(8,128)S(1)}, f32[64,128]{1,0:T(8,128)S(1)}, u32[]{:S(2)}, u32[]{:S(2)}) collective-permute-start(f32[64,128]{1,0:T(8,128)S(1)} %get-tuple-element.47), channel_id=1, source_target_pairs={{0,1},{1,0},{2,3},{3,2},{4,5},{5,4},{6,7},{7,6},{8,9},{9,8},{10,11... | collective-permute-start | bytes 98312 | tf_op jit(solution)/shard_map/ppermute | solution.py:367
  50.1 1.6 %shard_map.92.gathered = f32[64,2304]{1,0:T(8,128)S(1)} custom-call(f32[64,1152]{1,0:T(8,128)S(1)} %get-tuple-element.46.part, f32[72,128]{1,0:T(8,128)S(1)} %collective-permute-done.fetched, f32[1,1024]{1,0:T(1,128)S(1)} %get-tuple-element.29.inv_mass, bf16[2304,1152]{1,0:T(8,128)(2,1)S(1)} %get-tuple-element.33.slots), custom_call_target="tpu_custom_call" | custom-call | tf_op jit(solution)/shard_map/pallas_call | solution.py:375
  51.6 2.3 %collective-permute-done.3.got_near = f32[64,128]{1,0:T(8,128)S(1)} collective-permute-done((f32[64,128]{1,0:T(8,128)S(1)}, f32[64,128]{1,0:T(8,128)S(1)}, u32[]{:S(2)}, u32[]{:S(2)}) %collective-permute-start.3) | collective-permute-done | bytes 32800 | tf_op jit(solution)/shard_map/ppermute | solution.py:367
  54.0 2.1 %shard_map.93 = (f32[72,128]{1,0:T(8,128)S(1)}, f32[64,128]{1,0:T(8,128)S(1)}, f32[64,1152]{1,0:T(8,128)S(1)}) custom-call(f32[64,1024]{1,0:T(8,128)S(1)} %get-tuple-element.45.previous, f32[64,1152]{1,0:T(8,128)S(1)} %get-tuple-element.46.part, f32[64,2304]{1,0:T(8,128)S(1)} %shard_map.92.gathered, f32[72,128]{1,0:T(8,128)S(1)} %get-tuple-element.34.message, ...), custom_call_target="tpu_custom_call" | custom-call | tf_op jit(solution)/shard_map/pallas_call | solution.py:379
  56.1 2.4 %collective-permute-start.10 = (f32[64,1152]{1,0:T(8,128)S(1)}, f32[64,1152]{1,0:T(8,128)S(1)}, u32[]{:S(2)}, u32[]{:S(2)}) collective-permute-start(f32[64,1152]{1,0:T(8,128)S(1)} %get-tuple-element.49.part.rest_0_), channel_id=1, source_target_pairs={{0,256},{128,384},{256,0},{384,128},{1,257},{129,385},{257,1},{385... | collective-permute-start | bytes 884744 | tf_op jit(solution)/shard_map/ppermute | solution.py:384
  58.5 1.9 %collective-permute-start.5 = (f32[64,128]{1,0:T(8,128)S(1)}, f32[64,128]{1,0:T(8,128)S(1)}, u32[]{:S(2)}, u32[]{:S(2)}) collective-permute-start(f32[64,128]{1,0:T(8,128)S(1)} %get-tuple-element.50), channel_id=1, source_target_pairs={{0,1},{1,0},{2,3},{3,2},{4,5},{5,4},{6,7},{7,6},{8,9},{9,8},{10,11... | collective-permute-start | bytes 98312 | tf_op jit(solution)/shard_map/ppermute | solution.py:367
  60.4 6.9 %collective-permute-start.6 = (f32[72,128]{1,0:T(8,128)S(1)}, f32[72,128]{1,0:T(8,128)S(1)}, u32[]{:S(2)}, u32[]{:S(2)}) collective-permute-start(f32[72,128]{1,0:T(8,128)S(1)} %get-tuple-element.51), channel_id=1, source_target_pairs={{0,63},{1,2},{2,1},{3,4},{4,3},{5,6},{6,5},{7,8},{8,7},{9,10},{10,... | collective-permute-start | bytes 110600 | tf_op jit(solution)/shard_map/ppermute | solution.py:367
  67.4 3.1 %collective-permute-start.9 = (f32[64,1152]{1,0:T(8,128)S(1)}, f32[64,1152]{1,0:T(8,128)S(1)}, u32[]{:S(2)}, u32[]{:S(2)}) collective-permute-start(f32[64,1152]{1,0:T(8,128)S(1)} %get-tuple-element.49.part.rest_0_), channel_id=1, source_target_pairs={{0,128},{128,0},{256,384},{384,256},{1,129},{129,1},{257,385},{385... | collective-permute-start | bytes 884744 | tf_op jit(solution)/shard_map/ppermute | solution.py:384
  70.5 1.9 %collective-permute-start.7 = (f32[64,1152]{1,0:T(8,128)S(1)}, f32[64,1152]{1,0:T(8,128)S(1)}, u32[]{:S(2)}, u32[]{:S(2)}) collective-permute-start(f32[64,1152]{1,0:T(8,128)S(1)} %get-tuple-element.49.part.rest_0_), channel_id=1, source_target_pairs={{0,64},{64,0},{1,65},{65,1},{2,66},{66,2},{3,67},{67,3},{4,68},{68... | collective-permute-start | bytes 884744 | tf_op jit(solution)/shard_map/ppermute | solution.py:392
  72.4 2.8 %collective-permute-start.11 = (f32[64,1152]{1,0:T(8,128)S(1)}, f32[64,1152]{1,0:T(8,128)S(1)}, u32[]{:S(2)}, u32[]{:S(2)}) collective-permute-start(f32[64,1152]{1,0:T(8,128)S(1)} %shard_map.96.rest_2_), channel_id=1, source_target_pairs={{0,128},{128,0},{256,384},{384,256},{1,129},{129,1},{257,385},{385... | collective-permute-start | bytes 884744 | tf_op jit(solution)/shard_map/ppermute | solution.py:384
  75.2 2.1 %collective-permute-start.8 = (f32[64,1024]{1,0:T(8,128)S(1)}, f32[64,1024]{1,0:T(8,128)S(1)}, u32[]{:S(2)}, u32[]{:S(2)}) collective-permute-start(f32[64,1024]{1,0:T(8,128)S(1)} %shard_map.94.late), channel_id=1, source_target_pairs={{0,64},{64,0},{1,65},{65,1},{2,66},{66,2},{3,67},{67,3},{4,68},{68... | collective-permute-start | bytes 786440 | tf_op jit(solution)/shard_map/ppermute | solution.py:392
  77.4 1.0 shard_map.95
  78.3 0.6 collective-permute-done.9.rest_1_
  78.9 5.6 %collective-permute-done.11.rest_3_ = f32[64,1152]{1,0:T(8,128)S(1)} collective-permute-done((f32[64,1152]{1,0:T(8,128)S(1)}, f32[64,1152]{1,0:T(8,128)S(1)}, u32[]{:S(2)}, u32[]{:S(2)}) %collective-permute-start.11) | collective-permute-done | bytes 294944 | tf_op jit(solution)/shard_map/ppermute | solution.py:384
  84.5 0.8 shard_map.97
  85.3 11.1 %all_to_all.15.pieces = f32[16,8,256]{2,1,0:T(8,128)S(1)} all-to-all(f32[16,8,256]{2,1,0:T(8,128)S(1)} %bitcast.5), channel_id=1, replica_groups=mesh['chip'=4,'core'=2,'x'=4,'half'=2,'z'=8] {'core','z'}, dimensions={0} | all-to-all | bytes 262144 | tf_op jit(solution)/shard_map/all_to_all | solution.py:408
  96.3 0.1 shard_map.98
  96.4 20.5 %all_to_all.16 = f32[8,8,512]{2,1,0:T(8,128)S(1)} all-to-all(f32[8,8,512]{2,1,0:T(8,128)S(1)} %shard_map.98), channel_id=1, replica_groups=mesh['chip'=4,'core'=2,'x'=4,'half'=2,'z'=8] {'x','half'}, dimensions={0} | all-to-all | bytes 262144 | tf_op jit(solution)/shard_map/all_to_all | solution.py:412
  117.0 12.1 %all_to_all.17 = f32[8,8,512]{2,1,0:T(8,128)S(1)} all-to-all(f32[8,8,512]{2,1,0:T(8,128)S(1)} %broadcast_in_dim.2), channel_id=1, replica_groups=mesh['chip'=4,'core'=2,'x'=4,'half'=2,'z'=8] {'z'}, dimensions={0} | all-to-all | bytes 262144 | tf_op jit(solution)/shard_map/all_to_all | solution.py:414
  129.1 0.7 copy.12
  (13 shorter events, 0.1 us)
Async XLA Ops:
  2.0 20.0 %collective-permute-start = (f32[72,128]{1,0:T(8,128)S(1)}, f32[72,128]{1,0:T(8,128)S(1)}, u32[]{:S(2)}, u32[]{:S(2)}) collective-permute-start(f32[72,128]{1,0:T(8,128)S(1)} %get-tuple-element.34.message), channel_id=1, source_target_pairs={{0,63},{1,0},{2,1},{3,2},{4,3},{5,4},{6,5},{7,6},{8,7},{9,8},{10,9... | collective-permute-start | bytes 110600 | tf_op jit(solution)/shard_map/ppermute | solution.py:347
  18.1 0.7 copy-start
  24.0 15.1 %collective-permute-start.2 = (f32[72,128]{1,0:T(8,128)S(1)}, f32[72,128]{1,0:T(8,128)S(1)}, u32[]{:S(2)}, u32[]{:S(2)}) collective-permute-start(f32[72,128]{1,0:T(8,128)S(1)} %get-tuple-element.43), channel_id=1, source_target_pairs={{0,63},{1,2},{2,1},{3,4},{4,3},{5,6},{6,5},{7,8},{8,7},{9,10},{10,... | collective-permute-start | bytes 110600 | tf_op jit(solution)/shard_map/ppermute | solution.py:367
  33.2 5.8 %collective-permute-start.1 = (f32[64,128]{1,0:T(8,128)S(1)}, f32[64,128]{1,0:T(8,128)S(1)}, u32[]{:S(2)}, u32[]{:S(2)}) collective-permute-start(f32[64,128]{1,0:T(8,128)S(1)} %get-tuple-element.42), channel_id=1, source_target_pairs={{0,1},{1,0},{2,3},{3,2},{4,5},{5,4},{6,7},{7,6},{8,9},{9,8},{10,11... | collective-permute-start | bytes 98312 | tf_op jit(solution)/shard_map/ppermute | solution.py:367
  41.2 12.8 %collective-permute-start.4 = (f32[72,128]{1,0:T(8,128)S(1)}, f32[72,128]{1,0:T(8,128)S(1)}, u32[]{:S(2)}, u32[]{:S(2)}) collective-permute-start(f32[72,128]{1,0:T(8,128)S(1)} %get-tuple-element.48), channel_id=1, source_target_pairs={{0,63},{1,2},{2,1},{3,4},{4,3},{5,6},{6,5},{7,8},{8,7},{9,10},{10,... | collective-permute-start | bytes 110600 | tf_op jit(solution)/shard_map/ppermute | solution.py:367
  48.2 5.8 %collective-permute-start.3 = (f32[64,128]{1,0:T(8,128)S(1)}, f32[64,128]{1,0:T(8,128)S(1)}, u32[]{:S(2)}, u32[]{:S(2)}) collective-permute-start(f32[64,128]{1,0:T(8,128)S(1)} %get-tuple-element.47), channel_id=1, source_target_pairs={{0,1},{1,0},{2,3},{3,2},{4,5},{5,4},{6,7},{7,6},{8,9},{9,8},{10,11... | collective-permute-start | bytes 98312 | tf_op jit(solution)/shard_map/ppermute | solution.py:367
  56.1 16.3 %collective-permute-start.10 = (f32[64,1152]{1,0:T(8,128)S(1)}, f32[64,1152]{1,0:T(8,128)S(1)}, u32[]{:S(2)}, u32[]{:S(2)}) collective-permute-start(f32[64,1152]{1,0:T(8,128)S(1)} %get-tuple-element.49.part.rest_0_), channel_id=1, source_target_pairs={{0,256},{128,384},{256,0},{384,128},{1,257},{129,385},{257,1},{385... | collective-permute-start | bytes 884744 | tf_op jit(solution)/shard_map/ppermute | solution.py:384
  58.5 13.9 %collective-permute-start.5 = (f32[64,128]{1,0:T(8,128)S(1)}, f32[64,128]{1,0:T(8,128)S(1)}, u32[]{:S(2)}, u32[]{:S(2)}) collective-permute-start(f32[64,128]{1,0:T(8,128)S(1)} %get-tuple-element.50), channel_id=1, source_target_pairs={{0,1},{1,0},{2,3},{3,2},{4,5},{5,4},{6,7},{7,6},{8,9},{9,8},{10,11... | collective-permute-start | bytes 98312 | tf_op jit(solution)/shard_map/ppermute | solution.py:367
  60.4 14.8 %collective-permute-start.6 = (f32[72,128]{1,0:T(8,128)S(1)}, f32[72,128]{1,0:T(8,128)S(1)}, u32[]{:S(2)}, u32[]{:S(2)}) collective-permute-start(f32[72,128]{1,0:T(8,128)S(1)} %get-tuple-element.51), channel_id=1, source_target_pairs={{0,63},{1,2},{2,1},{3,4},{4,3},{5,6},{6,5},{7,8},{8,7},{9,10},{10,... | collective-permute-start | bytes 110600 | tf_op jit(solution)/shard_map/ppermute | solution.py:367
  67.4 11.5 %collective-permute-start.9 = (f32[64,1152]{1,0:T(8,128)S(1)}, f32[64,1152]{1,0:T(8,128)S(1)}, u32[]{:S(2)}, u32[]{:S(2)}) collective-permute-start(f32[64,1152]{1,0:T(8,128)S(1)} %get-tuple-element.49.part.rest_0_), channel_id=1, source_target_pairs={{0,128},{128,0},{256,384},{384,256},{1,129},{129,1},{257,385},{385... | collective-permute-start | bytes 884744 | tf_op jit(solution)/shard_map/ppermute | solution.py:384
  70.5 8.4 %collective-permute-start.7 = (f32[64,1152]{1,0:T(8,128)S(1)}, f32[64,1152]{1,0:T(8,128)S(1)}, u32[]{:S(2)}, u32[]{:S(2)}) collective-permute-start(f32[64,1152]{1,0:T(8,128)S(1)} %get-tuple-element.49.part.rest_0_), channel_id=1, source_target_pairs={{0,64},{64,0},{1,65},{65,1},{2,66},{66,2},{3,67},{67,3},{4,68},{68... | collective-permute-start | bytes 884744 | tf_op jit(solution)/shard_map/ppermute | solution.py:392
  72.4 12.1 %collective-permute-start.11 = (f32[64,1152]{1,0:T(8,128)S(1)}, f32[64,1152]{1,0:T(8,128)S(1)}, u32[]{:S(2)}, u32[]{:S(2)}) collective-permute-start(f32[64,1152]{1,0:T(8,128)S(1)} %shard_map.96.rest_2_), channel_id=1, source_target_pairs={{0,128},{128,0},{256,384},{384,256},{1,129},{129,1},{257,385},{385... | collective-permute-start | bytes 884744 | tf_op jit(solution)/shard_map/ppermute | solution.py:384
  75.2 3.7 %collective-permute-start.8 = (f32[64,1024]{1,0:T(8,128)S(1)}, f32[64,1024]{1,0:T(8,128)S(1)}, u32[]{:S(2)}, u32[]{:S(2)}) collective-permute-start(f32[64,1024]{1,0:T(8,128)S(1)} %shard_map.94.late), channel_id=1, source_target_pairs={{0,64},{64,0},{1,65},{65,1},{2,66},{66,2},{3,67},{67,3},{4,68},{68... | collective-permute-start | bytes 786440 | tf_op jit(solution)/shard_map/ppermute | solution.py:392

commit v8 on v7

--- a/solution.py
+++ b/solution.py
@@ -226,8 +226,8 @@
     send_both(up, picked(here, chosen[...]), near, far)
 
 
-def relay_kernel(block, near, out):
-    del near
+def relay_kernel(block, beside, near, out):
+    del beside, near
     out[:8, :128] = block[:8, :128]
 
 
@@ -385,8 +385,11 @@
 
     got_near, got_far = swapped(near, far)
     second = from_chip(partial, 2)
-    relayed = call(relay_kernel, wide, [in_vmem] * 2, aliases={0: 0})(second, got_near)
-    blocks = [partial, from_chip(partial, 1), relayed, from_chip(relayed, 1)]
+    beside = from_chip(partial, 1)
+    relayed = call(relay_kernel, wide, [in_vmem] * 3, aliases={0: 0})(
+        second, beside, got_near
+    )
+    blocks = [partial, beside, relayed, from_chip(relayed, 1)]
 
     def from_sibling(x):
         return lax.ppermute(x, "core", [(0, 1), (1, 0)])

time: 130 us -> 130 us (level)
  the two profiles are of different devices: /device:TPU:2 before, /device:TPU:16 now
where the time goes in v8:
time: 130 us; the launch traced here: 129 us
  starting transfers between devices  62.6 us (48%)
  blocking collectives  38.1 us (29%)
  Pallas kernels  15.7 us (12%)
  waiting for transfers between devices  10.6 us (8%)
  local copies, waits for them, and re-layouts  1.32 us (1%)
    ppermute x3, starting transfers between devices, swapped(): lax.ppermute(far, DOM, far_pairs)  26.4 us
    ppermute x1, starting transfers between devices, per_device(): fetched = lax.ppermute(message, DOM, backward)  16.6 us
    all_to_all x1, blocking collectives, per_device(): spread = lax.all_to_all(mine, ('x', 'half'), 0, 0, tiled=True)  14.9 us
    all_to_all x1, blocking collectives, per_device(): lax.all_to_all(jnp.broadcast_to(mine[None], (n_z, *mine.shape)), 'z', 0,...  12.1 us
    all_to_all x1, blocking collectives, per_device(): lax.all_to_all(gram.reshape(2 * n_z, each, chips * rows), ('core', 'z'),...  11.1 us
    ppermute x3, starting transfers between devices, from_chip(): return lax.ppermute(x, 'chip', [(i, i ^ s) for i in range(chips)])  9.9 us
    ppermute x3, starting transfers between devices, swapped(): lax.ppermute(near, DOM, near_pairs)  5.76 us
    ppermute x3, waiting for transfers between devices, swapped(): lax.ppermute(near, DOM, near_pairs)  4.63 us
  transfers between devices with their start and end apart: 12, of which 5 were waited for; matrix products, arithmetic and copies ran while one was open for 0% of the time, Pallas kernels for 6%

profile of v8, /device:TPU:16, one launch (start us, length us, event | category | flops | bytes accessed | tf_op | source)
XLA Modules:
  0.0 129.1 jit_solution(1144053073786288850)
XLA Ops:
  0.6 1.3 %shard_map.86 = (f32[72,128]{1,0:T(8,128)S(1)}, f32[64,1024]{1,0:T(8,128)S(1)}, f32[1,1024]{1,0:T(1,128)S(1)}, s32[1,128]{1,0:T(1,128)S(1)}, f32[1,1024]{1,0:T(1...) custom-call(f32[64,1024]{1,0:T(8,128)} %states.1, f32[1,1024]{1,0:T(1,128)} %bitcast.7, s32[1,128]{1,0:T(1,128)} %bitcast.9, ...), custom_call_target="tpu_custom_call" | custom-call | tf_op jit(solution)/shard_map/pallas_call | solution.py:329
  2.0 16.6 %collective-permute-start = (f32[72,128]{1,0:T(8,128)S(1)}, f32[72,128]{1,0:T(8,128)S(1)}, u32[]{:S(2)}, u32[]{:S(2)}) collective-permute-start(f32[72,128]{1,0:T(8,128)S(1)} %get-tuple-element.34.message), channel_id=1, source_target_pairs={{0,63},{1,0},{2,1},{3,2},{4,3},{5,4},{6,5},{7,6},{8,7},{9,8},{10,9... | collective-permute-start | bytes 110600 | tf_op jit(solution)/shard_map/ppermute | solution.py:347
  18.6 0.6 copy-done
  19.2 1.5 %shard_map.87 = (bf16[2304,1152]{1,0:T(8,128)(2,1)S(1)}, bf16[256,2304]{1,0:T(8,128)(2,1)S(1)}, bf16[384,384]{1,0:T(8,128)(2,1)S(1)}, bf16[384,384]{1,0:T(8,128)...) custom-call(s32[6,343]{1,0:T(8,128)S(1)} %get-tuple-element.30.cells, ...), custom_call_target="tpu_custom_call" | custom-call | tf_op jit(solution)/shard_map/pallas_call | solution.py:349
  20.8 1.6 %shard_map.88.gathered = f32[64,2304]{1,0:T(8,128)S(1)} custom-call(f32[64,1024]{1,0:T(8,128)S(1)} %get-tuple-element.28.states.previous, f32[1,1024]{1,0:T(1,128)S(1)} %get-tuple-element.29.inv_mass, bf16[2304,1152]{1,0:T(8,128)(2,1)S(1)} %get-tuple-element.33.slots), custom_call_target="tpu_custom_call" | custom-call | tf_op jit(solution)/shard_map/pallas_call | solution.py:369
  22.4 2.0 %shard_map.89 = (f32[72,128]{1,0:T(8,128)S(1)}, f32[64,128]{1,0:T(8,128)S(1)}, f32[64,1152]{1,0:T(8,128)S(1)}) custom-call(f32[64,1024]{1,0:T(8,128)S(1)} %get-tuple-element.28.states.previous, f32[64,2304]{1,0:T(8,128)S(1)} %shard_map.88.gathered, f32[72,128]{1,0:T(8,128)S(1)} %collective-permute-done.fetched, f32[1,1024]{1,0:T(1,128)S(1)} %get-tuple-element.29.inv_mass, ...), custom_call_target="tpu_custom_call" | custom-call | tf_op jit(solution)/shard_map/pallas_call | solution.py:370
  24.4 10.1 %collective-permute-start.2 = (f32[72,128]{1,0:T(8,128)S(1)}, f32[72,128]{1,0:T(8,128)S(1)}, u32[]{:S(2)}, u32[]{:S(2)}) collective-permute-start(f32[72,128]{1,0:T(8,128)S(1)} %get-tuple-element.43), channel_id=1, source_target_pairs={{0,63},{1,2},{2,1},{3,4},{4,3},{5,6},{6,5},{7,8},{8,7},{9,10},{10,... | collective-permute-start | bytes 110600 | tf_op jit(solution)/shard_map/ppermute | solution.py:367
  34.5 1.9 %collective-permute-start.1 = (f32[64,128]{1,0:T(8,128)S(1)}, f32[64,128]{1,0:T(8,128)S(1)}, u32[]{:S(2)}, u32[]{:S(2)}) collective-permute-start(f32[64,128]{1,0:T(8,128)S(1)} %get-tuple-element.42), channel_id=1, source_target_pairs={{0,1},{1,0},{2,3},{3,2},{4,5},{5,4},{6,7},{7,6},{8,9},{9,8},{10,11... | collective-permute-start | bytes 98312 | tf_op jit(solution)/shard_map/ppermute | solution.py:367
  36.5 1.6 %shard_map.90.gathered = f32[64,2304]{1,0:T(8,128)S(1)} custom-call(f32[64,1152]{1,0:T(8,128)S(1)} %get-tuple-element.41.part, f32[72,128]{1,0:T(8,128)S(1)} %collective-permute-done.fetched, f32[1,1024]{1,0:T(1,128)S(1)} %get-tuple-element.29.inv_mass, bf16[2304,1152]{1,0:T(8,128)(2,1)S(1)} %get-tuple-element.33.slots), custom_call_target="tpu_custom_call" | custom-call | tf_op jit(solution)/shard_map/pallas_call | solution.py:375
  38.0 2.3 %collective-permute-done.1.got_near = f32[64,128]{1,0:T(8,128)S(1)} collective-permute-done((f32[64,128]{1,0:T(8,128)S(1)}, f32[64,128]{1,0:T(8,128)S(1)}, u32[]{:S(2)}, u32[]{:S(2)}) %collective-permute-start.1) | collective-permute-done | bytes 32800 | tf_op jit(solution)/shard_map/ppermute | solution.py:367
  40.3 2.1 %shard_map.91 = (f32[72,128]{1,0:T(8,128)S(1)}, f32[64,128]{1,0:T(8,128)S(1)}, f32[64,1152]{1,0:T(8,128)S(1)}, f32[64,1024]{1,0:T(8,128)S(1)}) custom-call(f32[64,1024]{1,0:T(8,128)S(1)} %get-tuple-element.28.states.previous, f32[64,1152]{1,0:T(8,128)S(1)} %get-tuple-element.41.part, f32[64,2304]{1,0:T(8,128)S(1)} %shard_map.90.gathered, ...), custom_call_target="tpu_custom_call" | custom-call | tf_op jit(solution)/shard_map/pallas_call | solution.py:379
  42.5 8.2 %collective-permute-start.4 = (f32[72,128]{1,0:T(8,128)S(1)}, f32[72,128]{1,0:T(8,128)S(1)}, u32[]{:S(2)}, u32[]{:S(2)}) collective-permute-start(f32[72,128]{1,0:T(8,128)S(1)} %get-tuple-element.48), channel_id=1, source_target_pairs={{0,63},{1,2},{2,1},{3,4},{4,3},{5,6},{6,5},{7,8},{8,7},{9,10},{10,... | collective-permute-start | bytes 110600 | tf_op jit(solution)/shard_map/ppermute | solution.py:367
  50.6 1.9 %collective-permute-start.3 = (f32[64,128]{1,0:T(8,128)S(1)}, f32[64,128]{1,0:T(8,128)S(1)}, u32[]{:S(2)}, u32[]{:S(2)}) collective-permute-start(f32[64,128]{1,0:T(8,128)S(1)} %get-tuple-element.47), channel_id=1, source_target_pairs={{0,1},{1,0},{2,3},{3,2},{4,5},{5,4},{6,7},{7,6},{8,9},{9,8},{10,11... | collective-permute-start | bytes 98312 | tf_op jit(solution)/shard_map/ppermute | solution.py:367
  52.6 1.6 %shard_map.92.gathered = f32[64,2304]{1,0:T(8,128)S(1)} custom-call(f32[64,1152]{1,0:T(8,128)S(1)} %get-tuple-element.46.part, f32[72,128]{1,0:T(8,128)S(1)} %collective-permute-done.fetched, f32[1,1024]{1,0:T(1,128)S(1)} %get-tuple-element.29.inv_mass, bf16[2304,1152]{1,0:T(8,128)(2,1)S(1)} %get-tuple-element.33.slots), custom_call_target="tpu_custom_call" | custom-call | tf_op jit(solution)/shard_map/pallas_call | solution.py:375
  54.1 2.3 %collective-permute-done.3.got_near = f32[64,128]{1,0:T(8,128)S(1)} collective-permute-done((f32[64,128]{1,0:T(8,128)S(1)}, f32[64,128]{1,0:T(8,128)S(1)}, u32[]{:S(2)}, u32[]{:S(2)}) %collective-permute-start.3) | collective-permute-done | bytes 32800 | tf_op jit(solution)/shard_map/ppermute | solution.py:367
  56.5 2.1 %shard_map.93 = (f32[72,128]{1,0:T(8,128)S(1)}, f32[64,128]{1,0:T(8,128)S(1)}, f32[64,1152]{1,0:T(8,128)S(1)}) custom-call(f32[64,1024]{1,0:T(8,128)S(1)} %get-tuple-element.45.previous, f32[64,1152]{1,0:T(8,128)S(1)} %get-tuple-element.46.part, f32[64,2304]{1,0:T(8,128)S(1)} %shard_map.92.gathered, f32[72,128]{1,0:T(8,128)S(1)} %get-tuple-element.34.message, ...), custom_call_target="tpu_custom_call" | custom-call | tf_op jit(solution)/shard_map/pallas_call | solution.py:379
  58.6 4.0 %collective-permute-start.10 = (f32[64,1152]{1,0:T(8,128)S(1)}, f32[64,1152]{1,0:T(8,128)S(1)}, u32[]{:S(2)}, u32[]{:S(2)}) collective-permute-start(f32[64,1152]{1,0:T(8,128)S(1)} %get-tuple-element.49.part.rest_0_), channel_id=1, source_target_pairs={{0,256},{128,384},{256,0},{384,128},{1,257},{129,385},{257,1},{385... | collective-permute-start | bytes 884744 | tf_op jit(solution)/shard_map/ppermute | solution.py:384
  62.6 3.5 %collective-permute-start.9 = (f32[64,1152]{1,0:T(8,128)S(1)}, f32[64,1152]{1,0:T(8,128)S(1)}, u32[]{:S(2)}, u32[]{:S(2)}) collective-permute-start(f32[64,1152]{1,0:T(8,128)S(1)} %get-tuple-element.49.part.rest_0_), channel_id=1, source_target_pairs={{0,128},{128,0},{256,384},{384,256},{1,129},{129,1},{257,385},{385... | collective-permute-start | bytes 884744 | tf_op jit(solution)/shard_map/ppermute | solution.py:384
  66.1 1.9 %collective-permute-start.5 = (f32[64,128]{1,0:T(8,128)S(1)}, f32[64,128]{1,0:T(8,128)S(1)}, u32[]{:S(2)}, u32[]{:S(2)}) collective-permute-start(f32[64,128]{1,0:T(8,128)S(1)} %get-tuple-element.50), channel_id=1, source_target_pairs={{0,1},{1,0},{2,3},{3,2},{4,5},{5,4},{6,7},{7,6},{8,9},{9,8},{10,11... | collective-permute-start | bytes 98312 | tf_op jit(solution)/shard_map/ppermute | solution.py:367
  68.0 8.1 %collective-permute-start.6 = (f32[72,128]{1,0:T(8,128)S(1)}, f32[72,128]{1,0:T(8,128)S(1)}, u32[]{:S(2)}, u32[]{:S(2)}) collective-permute-start(f32[72,128]{1,0:T(8,128)S(1)} %get-tuple-element.51), channel_id=1, source_target_pairs={{0,63},{1,2},{2,1},{3,4},{4,3},{5,6},{6,5},{7,8},{8,7},{9,10},{10,... | collective-permute-start | bytes 110600 | tf_op jit(solution)/shard_map/ppermute | solution.py:367
  76.2 1.9 %collective-permute-start.7 = (f32[64,1152]{1,0:T(8,128)S(1)}, f32[64,1152]{1,0:T(8,128)S(1)}, u32[]{:S(2)}, u32[]{:S(2)}) collective-permute-start(f32[64,1152]{1,0:T(8,128)S(1)} %get-tuple-element.49.part.rest_0_), channel_id=1, source_target_pairs={{0,64},{64,0},{1,65},{65,1},{2,66},{66,2},{3,67},{67,3},{4,68},{68... | collective-permute-start | bytes 884744 | tf_op jit(solution)/shard_map/ppermute | solution.py:395
  78.2 2.4 %collective-permute-start.11 = (f32[64,1152]{1,0:T(8,128)S(1)}, f32[64,1152]{1,0:T(8,128)S(1)}, u32[]{:S(2)}, u32[]{:S(2)}) collective-permute-start(f32[64,1152]{1,0:T(8,128)S(1)} %shard_map.96.rest_2_), channel_id=1, source_target_pairs={{0,128},{128,0},{256,384},{384,256},{1,129},{129,1},{257,385},{385... | collective-permute-start | bytes 884744 | tf_op jit(solution)/shard_map/ppermute | solution.py:384
  80.6 2.4 %collective-permute-done.6.got_far = f32[72,128]{1,0:T(8,128)S(1)} collective-permute-done((f32[72,128]{1,0:T(8,128)S(1)}, f32[72,128]{1,0:T(8,128)S(1)}, u32[]{:S(2)}, u32[]{:S(2)}) %collective-permute-start.6) | collective-permute-done | bytes 36896 | tf_op jit(solution)/shard_map/ppermute | solution.py:367
  83.0 1.9 %collective-permute-start.8 = (f32[64,1024]{1,0:T(8,128)S(1)}, f32[64,1024]{1,0:T(8,128)S(1)}, u32[]{:S(2)}, u32[]{:S(2)}) collective-permute-start(f32[64,1024]{1,0:T(8,128)S(1)} %shard_map.94.late), channel_id=1, source_target_pairs={{0,64},{64,0},{1,65},{65,1},{2,66},{66,2},{3,67},{67,3},{4,68},{68... | collective-permute-start | bytes 786440 | tf_op jit(solution)/shard_map/ppermute | solution.py:395
  84.9 1.0 shard_map.95
  85.9 0.5 collective-permute-done.8.late
  86.4 3.0 %collective-permute-done.11.rest_3_ = f32[64,1152]{1,0:T(8,128)S(1)} collective-permute-done((f32[64,1152]{1,0:T(8,128)S(1)}, f32[64,1152]{1,0:T(8,128)S(1)}, u32[]{:S(2)}, u32[]{:S(2)}) %collective-permute-start.11) | collective-permute-done | bytes 294944 | tf_op jit(solution)/shard_map/ppermute | solution.py:384
  89.5 0.8 shard_map.97
  90.3 11.1 %all_to_all.15.pieces = f32[16,8,256]{2,1,0:T(8,128)S(1)} all-to-all(f32[16,8,256]{2,1,0:T(8,128)S(1)} %bitcast.5), channel_id=1, replica_groups=mesh['chip'=4,'core'=2,'x'=4,'half'=2,'z'=8] {'core','z'}, dimensions={0} | all-to-all | bytes 262144 | tf_op jit(solution)/shard_map/all_to_all | solution.py:411
  101.4 14.9 %all_to_all.16 = f32[8,8,512]{2,1,0:T(8,128)S(1)} all-to-all(f32[8,8,512]{2,1,0:T(8,128)S(1)} %shard_map.98), channel_id=1, replica_groups=mesh['chip'=4,'core'=2,'x'=4,'half'=2,'z'=8] {'x','half'}, dimensions={0} | all-to-all | bytes 262144 | tf_op jit(solution)/shard_map/all_to_all | solution.py:415
  116.4 12.1 %all_to_all.17 = f32[8,8,512]{2,1,0:T(8,128)S(1)} all-to-all(f32[8,8,512]{2,1,0:T(8,128)S(1)} %broadcast_in_dim.2), channel_id=1, replica_groups=mesh['chip'=4,'core'=2,'x'=4,'half'=2,'z'=8] {'z'}, dimensions={0} | all-to-all | bytes 262144 | tf_op jit(solution)/shard_map/all_to_all | solution.py:417
  128.5 0.7 copy.12
  (13 shorter events, 0.2 us)
Async XLA Ops:
  2.0 20.4 %collective-permute-start = (f32[72,128]{1,0:T(8,128)S(1)}, f32[72,128]{1,0:T(8,128)S(1)}, u32[]{:S(2)}, u32[]{:S(2)}) collective-permute-start(f32[72,128]{1,0:T(8,128)S(1)} %get-tuple-element.34.message), channel_id=1, source_target_pairs={{0,63},{1,0},{2,1},{3,2},{4,3},{5,4},{6,5},{7,6},{8,7},{9,8},{10,9... | collective-permute-start | bytes 110600 | tf_op jit(solution)/shard_map/ppermute | solution.py:347
  18.6 0.7 copy-start
  24.4 16.0 %collective-permute-start.2 = (f32[72,128]{1,0:T(8,128)S(1)}, f32[72,128]{1,0:T(8,128)S(1)}, u32[]{:S(2)}, u32[]{:S(2)}) collective-permute-start(f32[72,128]{1,0:T(8,128)S(1)} %get-tuple-element.43), channel_id=1, source_target_pairs={{0,63},{1,2},{2,1},{3,4},{4,3},{5,6},{6,5},{7,8},{8,7},{9,10},{10,... | collective-permute-start | bytes 110600 | tf_op jit(solution)/shard_map/ppermute | solution.py:367
  34.5 5.8 %collective-permute-start.1 = (f32[64,128]{1,0:T(8,128)S(1)}, f32[64,128]{1,0:T(8,128)S(1)}, u32[]{:S(2)}, u32[]{:S(2)}) collective-permute-start(f32[64,128]{1,0:T(8,128)S(1)} %get-tuple-element.42), channel_id=1, source_target_pairs={{0,1},{1,0},{2,3},{3,2},{4,5},{5,4},{6,7},{7,6},{8,9},{9,8},{10,11... | collective-permute-start | bytes 98312 | tf_op jit(solution)/shard_map/ppermute | solution.py:367
  42.5 14.0 %collective-permute-start.4 = (f32[72,128]{1,0:T(8,128)S(1)}, f32[72,128]{1,0:T(8,128)S(1)}, u32[]{:S(2)}, u32[]{:S(2)}) collective-permute-start(f32[72,128]{1,0:T(8,128)S(1)} %get-tuple-element.48), channel_id=1, source_target_pairs={{0,63},{1,2},{2,1},{3,4},{4,3},{5,6},{6,5},{7,8},{8,7},{9,10},{10,... | collective-permute-start | bytes 110600 | tf_op jit(solution)/shard_map/ppermute | solution.py:367
  50.6 5.8 %collective-permute-start.3 = (f32[64,128]{1,0:T(8,128)S(1)}, f32[64,128]{1,0:T(8,128)S(1)}, u32[]{:S(2)}, u32[]{:S(2)}) collective-permute-start(f32[64,128]{1,0:T(8,128)S(1)} %get-tuple-element.47), channel_id=1, source_target_pairs={{0,1},{1,0},{2,3},{3,2},{4,5},{5,4},{6,7},{7,6},{8,9},{9,8},{10,11... | collective-permute-start | bytes 98312 | tf_op jit(solution)/shard_map/ppermute | solution.py:367
  58.6 19.5 %collective-permute-start.10 = (f32[64,1152]{1,0:T(8,128)S(1)}, f32[64,1152]{1,0:T(8,128)S(1)}, u32[]{:S(2)}, u32[]{:S(2)}) collective-permute-start(f32[64,1152]{1,0:T(8,128)S(1)} %get-tuple-element.49.part.rest_0_), channel_id=1, source_target_pairs={{0,256},{128,384},{256,0},{384,128},{1,257},{129,385},{257,1},{385... | collective-permute-start | bytes 884744 | tf_op jit(solution)/shard_map/ppermute | solution.py:384
  62.6 15.5 %collective-permute-start.9 = (f32[64,1152]{1,0:T(8,128)S(1)}, f32[64,1152]{1,0:T(8,128)S(1)}, u32[]{:S(2)}, u32[]{:S(2)}) collective-permute-start(f32[64,1152]{1,0:T(8,128)S(1)} %get-tuple-element.49.part.rest_0_), channel_id=1, source_target_pairs={{0,128},{128,0},{256,384},{384,256},{1,129},{129,1},{257,385},{385... | collective-permute-start | bytes 884744 | tf_op jit(solution)/shard_map/ppermute | solution.py:384
  66.1 12.0 %collective-permute-start.5 = (f32[64,128]{1,0:T(8,128)S(1)}, f32[64,128]{1,0:T(8,128)S(1)}, u32[]{:S(2)}, u32[]{:S(2)}) collective-permute-start(f32[64,128]{1,0:T(8,128)S(1)} %get-tuple-element.50), channel_id=1, source_target_pairs={{0,1},{1,0},{2,3},{3,2},{4,5},{5,4},{6,7},{7,6},{8,9},{9,8},{10,11... | collective-permute-start | bytes 98312 | tf_op jit(solution)/shard_map/ppermute | solution.py:367
  68.0 14.9 %collective-permute-start.6 = (f32[72,128]{1,0:T(8,128)S(1)}, f32[72,128]{1,0:T(8,128)S(1)}, u32[]{:S(2)}, u32[]{:S(2)}) collective-permute-start(f32[72,128]{1,0:T(8,128)S(1)} %get-tuple-element.51), channel_id=1, source_target_pairs={{0,63},{1,2},{2,1},{3,4},{4,3},{5,6},{6,5},{7,8},{8,7},{9,10},{10,... | collective-permute-start | bytes 110600 | tf_op jit(solution)/shard_map/ppermute | solution.py:367
  76.2 9.7 %collective-permute-start.7 = (f32[64,1152]{1,0:T(8,128)S(1)}, f32[64,1152]{1,0:T(8,128)S(1)}, u32[]{:S(2)}, u32[]{:S(2)}) collective-permute-start(f32[64,1152]{1,0:T(8,128)S(1)} %get-tuple-element.49.part.rest_0_), channel_id=1, source_target_pairs={{0,64},{64,0},{1,65},{65,1},{2,66},{66,2},{3,67},{67,3},{4,68},{68... | collective-permute-start | bytes 884744 | tf_op jit(solution)/shard_map/ppermute | solution.py:395
  78.2 11.3 %collective-permute-start.11 = (f32[64,1152]{1,0:T(8,128)S(1)}, f32[64,1152]{1,0:T(8,128)S(1)}, u32[]{:S(2)}, u32[]{:S(2)}) collective-permute-start(f32[64,1152]{1,0:T(8,128)S(1)} %shard_map.96.rest_2_), channel_id=1, source_target_pairs={{0,128},{128,0},{256,384},{384,256},{1,129},{129,1},{257,385},{385... | collective-permute-start | bytes 884744 | tf_op jit(solution)/shard_map/ppermute | solution.py:384
  83.0 3.4 %collective-permute-start.8 = (f32[64,1024]{1,0:T(8,128)S(1)}, f32[64,1024]{1,0:T(8,128)S(1)}, u32[]{:S(2)}, u32[]{:S(2)}) collective-permute-start(f32[64,1024]{1,0:T(8,128)S(1)} %shard_map.94.late), channel_id=1, source_target_pairs={{0,64},{64,0},{1,65},{65,1},{2,66},{66,2},{3,67},{67,3},{4,68},{68... | collective-permute-start | bytes 786440 | tf_op jit(solution)/shard_map/ppermute | solution.py:395

commit v9 on v8

--- a/solution.py
+++ b/solution.py
@@ -199,14 +199,15 @@
     send_both(up, picked(here, chosen[...]), near, far)
 
 
-def complete(part, got_up, got_down, chosen_t):
-    owned = chosen_t.shape[1]
-    return part[:, :owned] + placed(got_up, chosen_t[...]), part[:, owned:] + got_down
+def complete(part, late, chosen_t):
+    count, owned = chosen_t.shape
+    own = part[:, :owned] + placed(late[:, :count], chosen_t[...])
+    return own, late[:, count : 2 * count]
 
 
 def next_kernel(
-    previous, part, gathered, message, fetched, got_near, got_far, inv_mass, potential, scale,
-    slots, late_slots, high, low, chosen, chosen_t, far, near, partial, *current_out,
+    last, previous, part, gathered, message, fetched, got_near, got_far, inv_mass, potential, scale,
+    slots, late_slots, high, low, chosen, chosen_t, far, near, partial, again,
 ):
     rows, owned = previous.shape
     got_up, got_down = got_both(got_near, got_far)
@@ -219,33 +220,29 @@
     here = (inv_mass[...] * summed[:, :owned] + (potential[...] - CENTER) * current) * (
         2.0 / HALF_WIDTH
     ) - previous[...]
-    for out in current_out:
-        out[...] = current
     partial[:, :owned] = here
     partial[:, owned:] = up
+    again[...] = here if last else current
     send_both(up, picked(here, chosen[...]), near, far)
 
 
-def relay_kernel(block, beside, near, out):
+def relay_kernel(beside, block, own, near, block_out, own_out):
     del beside, near
-    out[:8, :128] = block[:8, :128]
-
-
-def late_kernel(got_near, got_far, late):
+    block_out[:8, :128] = block[:8, :128]
+    own_out[:8, :128] = own[:8, :128]
+
+
+def late_kernel(part, got_near, got_far, late):
     up, down = got_both(got_near, got_far)
     count = up.shape[1]
     late[:, :count] = up
-    late[:, count : 2 * count] = down
+    late[:, count : 2 * count] = part[:, part.shape[1] - count :] + down
     late[:, 2 * count :] = jnp.zeros((up.shape[0], late.shape[1] - 2 * count), f32)
-
-
-def halves(late, count):
-    return late[:, :count], late[:, count : 2 * count]
 
 
 def finish_kernel(part, late, chosen_t, filtered, left):
     owned = filtered.shape[1]
-    current, ghost = complete(part, *halves(late, chosen_t.shape[0]), chosen_t)
+    current, ghost = complete(part, late, chosen_t)
     filtered[...] = current
     left[:, :owned] = current
     left[:, owned:] = ghost
@@ -260,7 +257,7 @@
     for s in range(chips):
         at = pl.ds(pl.multiple_of((chip ^ s) * rows, rows), rows)
         g_high[at, :], g_low[at, :] = parts(blocks[s][...], 2)
-    theirs = jnp.concatenate(complete(sibling, *halves(late, chosen_t.shape[0]), chosen_t), axis=1)
+    theirs = jnp.concatenate(complete(sibling, late, chosen_t), axis=1)
     high, low = parts(jnp.concatenate([left[...], theirs], axis=0), 2)
     by_high = dot_t(jnp.concatenate([high, low], axis=0), g_high[...])
     whole = by_high[: 2 * rows] + by_high[2 * rows :] + dot_t(high, g_low[...])
@@ -370,15 +367,16 @@
     far, near, partial = call(first_kernel, (tall, edge, wide), [in_vmem] * 11)(
         states, gathered, fetched, *fixed
     )
-    previous = [states]
+    previous = states
     for step in range(DEGREE - 1):
         gathered = call(gather_kernel, by_slot, [in_vmem] * 4)(
             partial, fetched, inv_mass, slots
         )
-        currents = [block] * (step < DEGREE - 2)
-        far, near, partial, *previous = call(
-            next_kernel, (tall, edge, wide, *currents), [in_vmem] * 16
-        )(*previous, partial, gathered, message, fetched, *swapped(near, far), *fixed, chosen_t)
+        far, near, partial, previous = call(
+            functools.partial(next_kernel, step == DEGREE - 2),
+            (tall, edge, wide, block),
+            [in_vmem] * 16,
+        )(previous, partial, gathered, message, fetched, *swapped(near, far), *fixed, chosen_t)
 
     def from_chip(x, s):
         return lax.ppermute(x, "chip", [(i, i ^ s) for i in range(chips)])
@@ -386,16 +384,16 @@
     got_near, got_far = swapped(near, far)
     second = from_chip(partial, 2)
     beside = from_chip(partial, 1)
-    relayed = call(relay_kernel, wide, [in_vmem] * 3, aliases={0: 0})(
-        second, beside, got_near
+    relayed, own = call(relay_kernel, (wide, block), [in_vmem] * 4, aliases={1: 0, 2: 1})(
+        beside, second, previous, got_near
     )
     blocks = [partial, beside, relayed, from_chip(relayed, 1)]
 
     def from_sibling(x):
         return lax.ppermute(x, "core", [(0, 1), (1, 0)])
 
-    late = call(late_kernel, shape_of(rows, LATE * shared_count), [in_vmem] * 2)(
-        got_near, got_far
+    late = call(late_kernel, shape_of(rows, LATE * shared_count), [in_vmem] * 3)(
+        partial, got_near, got_far
     )
     filtered, left = call(finish_kernel, (block, wide), [in_vmem] * 3)(partial, late, chosen_t)
     gram = call(
@@ -403,7 +401,7 @@
         shape_of(2 * rows, chips * rows),
         [in_vmem] * (4 + chips),
         [pltpu.VMEM((chips * rows, nodes), bf16)] * 2,
-    )(left, from_sibling(partial), from_sibling(late), chosen_t, *blocks)
+    )(left, from_sibling(own), from_sibling(late), chosen_t, *blocks)
 
     n_z = lax.axis_size("z")
     n_across = lax.axis_size(("x", "half"))

time: 130 us -> 130 us (level)
  waiting for transfers between devices: 10.6 us -> 8.39 us
  blocking collectives: 38.1 us -> 39.9 us
    ppermute x3, waiting for transfers between devices: 3.04 us -> 0.01 us  [from_chip(): return lax.ppermute(x, 'chip', [(i, i ^ s) for i in range(chips)])]
    all_to_all x1, blocking collectives: 14.9 us -> 16.8 us  [per_device(): spread = lax.all_to_all(mine, ('x', 'half'), 0, 0, tiled=True)]
  transfers between devices with their start and end apart: 12 -> 12, of which waited for: 5 -> 4; matrix products, arithmetic and copies ran while one was open for 0% -> 0% of each run, Pallas kernels for 6% -> 6%
where the time goes in v9:
time: 130 us
  starting transfers between devices  63.7 us (49%)
  blocking collectives  39.9 us (31%)
  Pallas kernels  15.7 us (12%)
  waiting for transfers between devices  8.39 us (6%)
  local copies, waits for them, and re-layouts  1.32 us (1%)
    ppermute x3, starting transfers between devices, swapped(): lax.ppermute(far, DOM, far_pairs)  26.5 us
    all_to_all x1, blocking collectives, per_device(): spread = lax.all_to_all(mine, ('x', 'half'), 0, 0, tiled=True)  16.8 us
    ppermute x1, starting transfers between devices, per_device(): fetched = lax.ppermute(message, DOM, backward)  16.6 us
    all_to_all x1, blocking collectives, per_device(): lax.all_to_all(jnp.broadcast_to(mine[None], (n_z, *mine.shape)), 'z', 0,...  12.1 us
    all_to_all x1, blocking collectives, per_device(): lax.all_to_all(gram.reshape(2 * n_z, each, chips * rows), ('core', 'z'),...  11.1 us
    ppermute x3, starting transfers between devices, from_chip(): return lax.ppermute(x, 'chip', [(i, i ^ s) for i in range(chips)])  10.6 us
    ppermute x3, starting transfers between devices, swapped(): lax.ppermute(near, DOM, near_pairs)  5.76 us
    ppermute x3, waiting for transfers between devices, swapped(): lax.ppermute(near, DOM, near_pairs)  4.63 us
  transfers between devices with their start and end apart: 12, of which 4 were waited for; matrix products, arithmetic and copies ran while one was open for 0% of the time, Pallas kernels for 6%

profile of v9, /device:TPU:16, one launch (start us, length us, event | category | flops | bytes accessed | tf_op | source)
XLA Modules:
  0.0 129.9 jit_solution(14759093227801667951)
XLA Ops:
  0.6 1.3 %shard_map.86 = (f32[72,128]{1,0:T(8,128)S(1)}, f32[64,1024]{1,0:T(8,128)S(1)}, f32[1,1024]{1,0:T(1,128)S(1)}, s32[1,128]{1,0:T(1,128)S(1)}, f32[1,1024]{1,0:T(1...) custom-call(f32[64,1024]{1,0:T(8,128)} %states.1, f32[1,1024]{1,0:T(1,128)} %bitcast.7, s32[1,128]{1,0:T(1,128)} %bitcast.9, ...), custom_call_target="tpu_custom_call" | custom-call | tf_op jit(solution)/shard_map/pallas_call | solution.py:326
  2.0 16.6 %collective-permute-start = (f32[72,128]{1,0:T(8,128)S(1)}, f32[72,128]{1,0:T(8,128)S(1)}, u32[]{:S(2)}, u32[]{:S(2)}) collective-permute-start(f32[72,128]{1,0:T(8,128)S(1)} %get-tuple-element.37.message), channel_id=1, source_target_pairs={{0,63},{1,0},{2,1},{3,2},{4,3},{5,4},{6,5},{7,6},{8,7},{9,8},{10,9... | collective-permute-start | bytes 110600 | tf_op jit(solution)/shard_map/ppermute | solution.py:344
  18.6 0.6 copy-done
  19.2 1.5 %shard_map.87 = (bf16[2304,1152]{1,0:T(8,128)(2,1)S(1)}, bf16[256,2304]{1,0:T(8,128)(2,1)S(1)}, bf16[384,384]{1,0:T(8,128)(2,1)S(1)}, bf16[384,384]{1,0:T(8,128)...) custom-call(s32[6,343]{1,0:T(8,128)S(1)} %get-tuple-element.33.cells, ...), custom_call_target="tpu_custom_call" | custom-call | tf_op jit(solution)/shard_map/pallas_call | solution.py:346
  20.8 1.6 %shard_map.88.gathered = f32[64,2304]{1,0:T(8,128)S(1)} custom-call(f32[64,1024]{1,0:T(8,128)S(1)} %get-tuple-element.31.states.previous, f32[1,1024]{1,0:T(1,128)S(1)} %get-tuple-element.32.inv_mass, bf16[2304,1152]{1,0:T(8,128)(2,1)S(1)} %get-tuple-element.36.slots), custom_call_target="tpu_custom_call" | custom-call | tf_op jit(solution)/shard_map/pallas_call | solution.py:366
  22.4 2.0 %shard_map.89 = (f32[72,128]{1,0:T(8,128)S(1)}, f32[64,128]{1,0:T(8,128)S(1)}, f32[64,1152]{1,0:T(8,128)S(1)}) custom-call(f32[64,1024]{1,0:T(8,128)S(1)} %get-tuple-element.31.states.previous, f32[64,2304]{1,0:T(8,128)S(1)} %shard_map.88.gathered, f32[72,128]{1,0:T(8,128)S(1)} %collective-permute-done.fetched, f32[1,1024]{1,0:T(1,128)S(1)} %get-tuple-element.32.inv_mass, ...), custom_call_target="tpu_custom_call" | custom-call | tf_op jit(solution)/shard_map/pallas_call | solution.py:367
  24.4 10.1 %collective-permute-start.2 = (f32[72,128]{1,0:T(8,128)S(1)}, f32[72,128]{1,0:T(8,128)S(1)}, u32[]{:S(2)}, u32[]{:S(2)}) collective-permute-start(f32[72,128]{1,0:T(8,128)S(1)} %get-tuple-element.46), channel_id=1, source_target_pairs={{0,63},{1,2},{2,1},{3,4},{4,3},{5,6},{6,5},{7,8},{8,7},{9,10},{10,... | collective-permute-start | bytes 110600 | tf_op jit(solution)/shard_map/ppermute | solution.py:364
  34.5 1.9 %collective-permute-start.1 = (f32[64,128]{1,0:T(8,128)S(1)}, f32[64,128]{1,0:T(8,128)S(1)}, u32[]{:S(2)}, u32[]{:S(2)}) collective-permute-start(f32[64,128]{1,0:T(8,128)S(1)} %get-tuple-element.45), channel_id=1, source_target_pairs={{0,1},{1,0},{2,3},{3,2},{4,5},{5,4},{6,7},{7,6},{8,9},{9,8},{10,11... | collective-permute-start | bytes 98312 | tf_op jit(solution)/shard_map/ppermute | solution.py:364
  36.5 1.6 %shard_map.90.gathered = f32[64,2304]{1,0:T(8,128)S(1)} custom-call(f32[64,1152]{1,0:T(8,128)S(1)} %get-tuple-element.44.part, f32[72,128]{1,0:T(8,128)S(1)} %collective-permute-done.fetched, f32[1,1024]{1,0:T(1,128)S(1)} %get-tuple-element.32.inv_mass, bf16[2304,1152]{1,0:T(8,128)(2,1)S(1)} %get-tuple-element.36.slots), custom_call_target="tpu_custom_call" | custom-call | tf_op jit(solution)/shard_map/pallas_call | solution.py:372
  38.0 2.3 %collective-permute-done.1.got_near = f32[64,128]{1,0:T(8,128)S(1)} collective-permute-done((f32[64,128]{1,0:T(8,128)S(1)}, f32[64,128]{1,0:T(8,128)S(1)}, u32[]{:S(2)}, u32[]{:S(2)}) %collective-permute-start.1) | collective-permute-done | bytes 32800 | tf_op jit(solution)/shard_map/ppermute | solution.py:364
  40.3 2.1 %shard_map.91 = (f32[72,128]{1,0:T(8,128)S(1)}, f32[64,128]{1,0:T(8,128)S(1)}, f32[64,1152]{1,0:T(8,128)S(1)}, f32[64,1024]{1,0:T(8,128)S(1)}) custom-call(f32[64,1024]{1,0:T(8,128)S(1)} %get-tuple-element.31.states.previous, f32[64,1152]{1,0:T(8,128)S(1)} %get-tuple-element.44.part, f32[64,2304]{1,0:T(8,128)S(1)} %shard_map.90.gathered, ...), custom_call_target="tpu_custom_call" | custom-call | tf_op jit(solution)/shard_map/pallas_call | solution.py:375
  42.5 8.2 %collective-permute-start.4 = (f32[72,128]{1,0:T(8,128)S(1)}, f32[72,128]{1,0:T(8,128)S(1)}, u32[]{:S(2)}, u32[]{:S(2)}) collective-permute-start(f32[72,128]{1,0:T(8,128)S(1)} %get-tuple-element.51), channel_id=1, source_target_pairs={{0,63},{1,2},{2,1},{3,4},{4,3},{5,6},{6,5},{7,8},{8,7},{9,10},{10,... | collective-permute-start | bytes 110600 | tf_op jit(solution)/shard_map/ppermute | solution.py:364
  50.6 1.9 %collective-permute-start.3 = (f32[64,128]{1,0:T(8,128)S(1)}, f32[64,128]{1,0:T(8,128)S(1)}, u32[]{:S(2)}, u32[]{:S(2)}) collective-permute-start(f32[64,128]{1,0:T(8,128)S(1)} %get-tuple-element.50), channel_id=1, source_target_pairs={{0,1},{1,0},{2,3},{3,2},{4,5},{5,4},{6,7},{7,6},{8,9},{9,8},{10,11... | collective-permute-start | bytes 98312 | tf_op jit(solution)/shard_map/ppermute | solution.py:364
  52.6 1.6 %shard_map.92.gathered = f32[64,2304]{1,0:T(8,128)S(1)} custom-call(f32[64,1152]{1,0:T(8,128)S(1)} %get-tuple-element.49.part, f32[72,128]{1,0:T(8,128)S(1)} %collective-permute-done.fetched, f32[1,1024]{1,0:T(1,128)S(1)} %get-tuple-element.32.inv_mass, bf16[2304,1152]{1,0:T(8,128)(2,1)S(1)} %get-tuple-element.36.slots), custom_call_target="tpu_custom_call" | custom-call | tf_op jit(solution)/shard_map/pallas_call | solution.py:372
  54.1 2.3 %collective-permute-done.3.got_near = f32[64,128]{1,0:T(8,128)S(1)} collective-permute-done((f32[64,128]{1,0:T(8,128)S(1)}, f32[64,128]{1,0:T(8,128)S(1)}, u32[]{:S(2)}, u32[]{:S(2)}) %collective-permute-start.3) | collective-permute-done | bytes 32800 | tf_op jit(solution)/shard_map/ppermute | solution.py:364
  56.5 2.1 %shard_map.93 = (f32[72,128]{1,0:T(8,128)S(1)}, f32[64,128]{1,0:T(8,128)S(1)}, f32[64,1152]{1,0:T(8,128)S(1)}, f32[64,1024]{1,0:T(8,128)S(1)}) custom-call(f32[64,1024]{1,0:T(8,128)S(1)} %get-tuple-element.48.previous, f32[64,1152]{1,0:T(8,128)S(1)} %get-tuple-element.49.part, f32[64,2304]{1,0:T(8,128)S(1)} %shard_map.92.gathered, ...), custom_call_target="tpu_custom_call" | custom-call | tf_op jit(solution)/shard_map/pallas_call | solution.py:375
  58.6 4.0 %collective-permute-start.8 = (f32[64,1152]{1,0:T(8,128)S(1)}, f32[64,1152]{1,0:T(8,128)S(1)}, u32[]{:S(2)}, u32[]{:S(2)}) collective-permute-start(f32[64,1152]{1,0:T(8,128)S(1)} %get-tuple-element.52.part.rest_0_), channel_id=1, source_target_pairs={{0,256},{128,384},{256,0},{384,128},{1,257},{129,385},{257,1},{385... | collective-permute-start | bytes 884744 | tf_op jit(solution)/shard_map/ppermute | solution.py:382
  62.6 3.5 %collective-permute-start.7 = (f32[64,1152]{1,0:T(8,128)S(1)}, f32[64,1152]{1,0:T(8,128)S(1)}, u32[]{:S(2)}, u32[]{:S(2)}) collective-permute-start(f32[64,1152]{1,0:T(8,128)S(1)} %get-tuple-element.52.part.rest_0_), channel_id=1, source_target_pairs={{0,128},{128,0},{256,384},{384,256},{1,129},{129,1},{257,385},{385... | collective-permute-start | bytes 884744 | tf_op jit(solution)/shard_map/ppermute | solution.py:382
  66.1 1.9 %collective-permute-start.5 = (f32[64,128]{1,0:T(8,128)S(1)}, f32[64,128]{1,0:T(8,128)S(1)}, u32[]{:S(2)}, u32[]{:S(2)}) collective-permute-start(f32[64,128]{1,0:T(8,128)S(1)} %get-tuple-element.53), channel_id=1, source_target_pairs={{0,1},{1,0},{2,3},{3,2},{4,5},{5,4},{6,7},{7,6},{8,9},{9,8},{10,11... | collective-permute-start | bytes 98312 | tf_op jit(solution)/shard_map/ppermute | solution.py:364
  68.0 8.1 %collective-permute-start.6 = (f32[72,128]{1,0:T(8,128)S(1)}, f32[72,128]{1,0:T(8,128)S(1)}, u32[]{:S(2)}, u32[]{:S(2)}) collective-permute-start(f32[72,128]{1,0:T(8,128)S(1)} %get-tuple-element.54), channel_id=1, source_target_pairs={{0,63},{1,2},{2,1},{3,4},{4,3},{5,6},{6,5},{7,8},{8,7},{9,10},{10,... | collective-permute-start | bytes 110600 | tf_op jit(solution)/shard_map/ppermute | solution.py:364
  76.2 3.1 %collective-permute-start.11 = (f32[64,1152]{1,0:T(8,128)S(1)}, f32[64,1152]{1,0:T(8,128)S(1)}, u32[]{:S(2)}, u32[]{:S(2)}) collective-permute-start(f32[64,1152]{1,0:T(8,128)S(1)} %get-tuple-element.59.rest_2_), channel_id=1, source_target_pairs={{0,128},{128,0},{256,384},{384,256},{1,129},{129,1},{257,385},{385... | collective-permute-start | bytes 884744 | tf_op jit(solution)/shard_map/ppermute | solution.py:382
  79.3 3.6 %collective-permute-done.6.got_far = f32[72,128]{1,0:T(8,128)S(1)} collective-permute-done((f32[72,128]{1,0:T(8,128)S(1)}, f32[72,128]{1,0:T(8,128)S(1)}, u32[]{:S(2)}, u32[]{:S(2)}) %collective-permute-start.6) | collective-permute-done | bytes 36896 | tf_op jit(solution)/shard_map/ppermute | solution.py:364
  82.9 1.9 %collective-permute-start.10 = (f32[64,1024]{1,0:T(8,128)S(1)}, f32[64,1024]{1,0:T(8,128)S(1)}, u32[]{:S(2)}, u32[]{:S(2)}) collective-permute-start(f32[64,1024]{1,0:T(8,128)S(1)} %shard_map.94.late), channel_id=1, source_target_pairs={{0,64},{64,0},{1,65},{65,1},{2,66},{66,2},{3,67},{67,3},{4,68},{68... | collective-permute-start | bytes 786440 | tf_op jit(solution)/shard_map/ppermute | solution.py:393
  84.8 2.4 %collective-permute-start.9 = (f32[64,1024]{1,0:T(8,128)S(1)}, f32[64,1024]{1,0:T(8,128)S(1)}, u32[]{:S(2)}, u32[]{:S(2)}) collective-permute-start(f32[64,1024]{1,0:T(8,128)S(1)} %get-tuple-element.58), channel_id=1, source_target_pairs={{0,64},{64,0},{1,65},{65,1},{2,66},{66,2},{3,67},{67,3},{4,68},{68... | collective-permute-start | bytes 786440 | tf_op jit(solution)/shard_map/ppermute | solution.py:393
  87.2 1.0 shard_map.95
  88.2 0.2 collective-permute-done.9.sibling
  88.4 0.8 shard_map.97
  89.2 11.1 %all_to_all.15.pieces = f32[16,8,256]{2,1,0:T(8,128)S(1)} all-to-all(f32[16,8,256]{2,1,0:T(8,128)S(1)} %bitcast.5), channel_id=1, replica_groups=mesh['chip'=4,'core'=2,'x'=4,'half'=2,'z'=8] {'core','z'}, dimensions={0} | all-to-all | bytes 262144 | tf_op jit(solution)/shard_map/all_to_all | solution.py:409
  100.2 0.1 shard_map.98
  100.3 16.8 %all_to_all.16 = f32[8,8,512]{2,1,0:T(8,128)S(1)} all-to-all(f32[8,8,512]{2,1,0:T(8,128)S(1)} %shard_map.98), channel_id=1, replica_groups=mesh['chip'=4,'core'=2,'x'=4,'half'=2,'z'=8] {'x','half'}, dimensions={0} | all-to-all | bytes 262144 | tf_op jit(solution)/shard_map/all_to_all | solution.py:413
  117.1 12.1 %all_to_all.17 = f32[8,8,512]{2,1,0:T(8,128)S(1)} all-to-all(f32[8,8,512]{2,1,0:T(8,128)S(1)} %broadcast_in_dim.2), channel_id=1, replica_groups=mesh['chip'=4,'core'=2,'x'=4,'half'=2,'z'=8] {'z'}, dimensions={0} | all-to-all | bytes 262144 | tf_op jit(solution)/shard_map/all_to_all | solution.py:415
  129.2 0.7 copy.14
  (13 shorter events, 0.1 us)
Async XLA Ops:
  2.0 20.4 %collective-permute-start = (f32[72,128]{1,0:T(8,128)S(1)}, f32[72,128]{1,0:T(8,128)S(1)}, u32[]{:S(2)}, u32[]{:S(2)}) collective-permute-start(f32[72,128]{1,0:T(8,128)S(1)} %get-tuple-element.37.message), channel_id=1, source_target_pairs={{0,63},{1,0},{2,1},{3,2},{4,3},{5,4},{6,5},{7,6},{8,7},{9,8},{10,9... | collective-permute-start | bytes 110600 | tf_op jit(solution)/shard_map/ppermute | solution.py:344
  18.6 0.7 copy-start
  24.4 16.0 %collective-permute-start.2 = (f32[72,128]{1,0:T(8,128)S(1)}, f32[72,128]{1,0:T(8,128)S(1)}, u32[]{:S(2)}, u32[]{:S(2)}) collective-permute-start(f32[72,128]{1,0:T(8,128)S(1)} %get-tuple-element.46), channel_id=1, source_target_pairs={{0,63},{1,2},{2,1},{3,4},{4,3},{5,6},{6,5},{7,8},{8,7},{9,10},{10,... | collective-permute-start | bytes 110600 | tf_op jit(solution)/shard_map/ppermute | solution.py:364
  34.5 5.8 %collective-permute-start.1 = (f32[64,128]{1,0:T(8,128)S(1)}, f32[64,128]{1,0:T(8,128)S(1)}, u32[]{:S(2)}, u32[]{:S(2)}) collective-permute-start(f32[64,128]{1,0:T(8,128)S(1)} %get-tuple-element.45), channel_id=1, source_target_pairs={{0,1},{1,0},{2,3},{3,2},{4,5},{5,4},{6,7},{7,6},{8,9},{9,8},{10,11... | collective-permute-start | bytes 98312 | tf_op jit(solution)/shard_map/ppermute | solution.py:364
  42.5 14.0 %collective-permute-start.4 = (f32[72,128]{1,0:T(8,128)S(1)}, f32[72,128]{1,0:T(8,128)S(1)}, u32[]{:S(2)}, u32[]{:S(2)}) collective-permute-start(f32[72,128]{1,0:T(8,128)S(1)} %get-tuple-element.51), channel_id=1, source_target_pairs={{0,63},{1,2},{2,1},{3,4},{4,3},{5,6},{6,5},{7,8},{8,7},{9,10},{10,... | collective-permute-start | bytes 110600 | tf_op jit(solution)/shard_map/ppermute | solution.py:364
  50.6 5.8 %collective-permute-start.3 = (f32[64,128]{1,0:T(8,128)S(1)}, f32[64,128]{1,0:T(8,128)S(1)}, u32[]{:S(2)}, u32[]{:S(2)}) collective-permute-start(f32[64,128]{1,0:T(8,128)S(1)} %get-tuple-element.50), channel_id=1, source_target_pairs={{0,1},{1,0},{2,3},{3,2},{4,5},{5,4},{6,7},{7,6},{8,9},{9,8},{10,11... | collective-permute-start | bytes 98312 | tf_op jit(solution)/shard_map/ppermute | solution.py:364
  58.6 17.6 %collective-permute-start.8 = (f32[64,1152]{1,0:T(8,128)S(1)}, f32[64,1152]{1,0:T(8,128)S(1)}, u32[]{:S(2)}, u32[]{:S(2)}) collective-permute-start(f32[64,1152]{1,0:T(8,128)S(1)} %get-tuple-element.52.part.rest_0_), channel_id=1, source_target_pairs={{0,256},{128,384},{256,0},{384,128},{1,257},{129,385},{257,1},{385... | collective-permute-start | bytes 884744 | tf_op jit(solution)/shard_map/ppermute | solution.py:382
  62.6 13.6 %collective-permute-start.7 = (f32[64,1152]{1,0:T(8,128)S(1)}, f32[64,1152]{1,0:T(8,128)S(1)}, u32[]{:S(2)}, u32[]{:S(2)}) collective-permute-start(f32[64,1152]{1,0:T(8,128)S(1)} %get-tuple-element.52.part.rest_0_), channel_id=1, source_target_pairs={{0,128},{128,0},{256,384},{384,256},{1,129},{129,1},{257,385},{385... | collective-permute-start | bytes 884744 | tf_op jit(solution)/shard_map/ppermute | solution.py:382
  66.1 10.1 %collective-permute-start.5 = (f32[64,128]{1,0:T(8,128)S(1)}, f32[64,128]{1,0:T(8,128)S(1)}, u32[]{:S(2)}, u32[]{:S(2)}) collective-permute-start(f32[64,128]{1,0:T(8,128)S(1)} %get-tuple-element.53), channel_id=1, source_target_pairs={{0,1},{1,0},{2,3},{3,2},{4,5},{5,4},{6,7},{7,6},{8,9},{9,8},{10,11... | collective-permute-start | bytes 98312 | tf_op jit(solution)/shard_map/ppermute | solution.py:364
  68.0 14.8 %collective-permute-start.6 = (f32[72,128]{1,0:T(8,128)S(1)}, f32[72,128]{1,0:T(8,128)S(1)}, u32[]{:S(2)}, u32[]{:S(2)}) collective-permute-start(f32[72,128]{1,0:T(8,128)S(1)} %get-tuple-element.54), channel_id=1, source_target_pairs={{0,63},{1,2},{2,1},{3,4},{4,3},{5,6},{6,5},{7,8},{8,7},{9,10},{10,... | collective-permute-start | bytes 110600 | tf_op jit(solution)/shard_map/ppermute | solution.py:364
  76.2 12.1 %collective-permute-start.11 = (f32[64,1152]{1,0:T(8,128)S(1)}, f32[64,1152]{1,0:T(8,128)S(1)}, u32[]{:S(2)}, u32[]{:S(2)}) collective-permute-start(f32[64,1152]{1,0:T(8,128)S(1)} %get-tuple-element.59.rest_2_), channel_id=1, source_target_pairs={{0,128},{128,0},{256,384},{384,256},{1,129},{129,1},{257,385},{385... | collective-permute-start | bytes 884744 | tf_op jit(solution)/shard_map/ppermute | solution.py:382
  82.9 5.3 %collective-permute-start.10 = (f32[64,1024]{1,0:T(8,128)S(1)}, f32[64,1024]{1,0:T(8,128)S(1)}, u32[]{:S(2)}, u32[]{:S(2)}) collective-permute-start(f32[64,1024]{1,0:T(8,128)S(1)} %shard_map.94.late), channel_id=1, source_target_pairs={{0,64},{64,0},{1,65},{65,1},{2,66},{66,2},{3,67},{67,3},{4,68},{68... | collective-permute-start | bytes 786440 | tf_op jit(solution)/shard_map/ppermute | solution.py:393
  84.8 3.6 %collective-permute-start.9 = (f32[64,1024]{1,0:T(8,128)S(1)}, f32[64,1024]{1,0:T(8,128)S(1)}, u32[]{:S(2)}, u32[]{:S(2)}) collective-permute-start(f32[64,1024]{1,0:T(8,128)S(1)} %get-tuple-element.58), channel_id=1, source_target_pairs={{0,64},{64,0},{1,65},{65,1},{2,66},{66,2},{3,67},{67,3},{4,68},{68... | collective-permute-start | bytes 786440 | tf_op jit(solution)/shard_map/ppermute | solution.py:393

commit v10 on v9

--- a/solution.py
+++ b/solution.py
@@ -76,25 +76,30 @@
     ]
     for move in moves:
         move.start()
-    for move in moves[:3]:
+    for move in moves[:4]:
         move.wait()
     owned = states_in.shape[1]
     both = jnp.concatenate(
-        [states_in[...], jnp.broadcast_to(inv_in[...], (8, owned))], axis=0
+        [
+            states_in[...],
+            jnp.broadcast_to(inv_in[...], (4, owned)),
+            jnp.broadcast_to(pot_in[...], (4, owned)),
+        ],
+        axis=0,
     )
     message[...] = picked(both, one_hot(shared_in[...], owned))
-    for move in moves[3:]:
+    for move in moves[4:]:
         move.wait()
 
 
 def prepare_kernel(
     cells, stiff, shared, scale,
-    slots, late_slots, high, low, chosen, chosen_t, scale_row, cells_pad, stiff_pad,
+    slots, late_slots, high, low, chosen_t, scale_row, cells_pad, stiff_pad,
 ):
     n_cells, npc = cells.shape
     pad = stiff_pad.shape[0]
     nodes = slots.shape[1]
-    owned, shared_count = chosen.shape
+    shared_count, owned = chosen_t.shape
     cells_pad[...] = jnp.full(cells_pad.shape, -1, jnp.int32)
     cells_pad[:n_cells, :npc] = cells[...]
     cells_pad[8:9, :shared_count] = shared[...]
@@ -114,7 +119,6 @@
     stiff_pad[...] = jnp.zeros(stiff_pad.shape, f32)
     stiff_pad[:npc, :npc] = stiff[...]
     high[...], low[...] = parts(stiff_pad[...], 2)
-    chosen[...] = one_hot(shared[...], owned)
     chosen_t[...] = one_hot_rows(shared_column, owned)
 
 
@@ -140,10 +144,10 @@
     gathered[...] = twice(values, lambda x: dot_t(x, slots[...]))
 
 
-def apply_cells(gathered, late, late_slots, scale, slots, high, low):
+def cell_products(gathered, late, late_slots, scale, high, low):
     rows = gathered.shape[0]
     pad = high.shape[0]
-    n_cells = slots.shape[0] // pad
+    n_cells = gathered.shape[1] // pad
     values = gathered[...] + twice(late, lambda x: dot(x, late_slots))
     v_high, v_low = parts(values, 2)
     stacked = jnp.concatenate(
@@ -157,7 +161,12 @@
     product = jnp.concatenate(
         [product[c * rows : (c + 1) * rows] for c in range(n_cells)], axis=1
     ) * scale[...]
-    return twice(product, lambda x: dot(x, slots[...]))
+    return jnp.concatenate(parts(product, 2), axis=0)
+
+
+def folded(got):
+    rows = got.shape[0] // 2
+    return got[:rows] + got[rows:]
 
 
 def is_even():
@@ -179,24 +188,93 @@
     return up, down
 
 
-def first_kernel(
-    states, gathered, fetched, inv_mass, potential, scale, slots, late_slots, high, low,
-    chosen, far, near, partial,
-):
+def first_edge_kernel(
+    gathered, message, fetched, scale, late_slots, high, low, far, near, products, down_out
+):
+    rows, count = down_out.shape
+    ghost_inv = fetched[rows : rows + 1, :]
+    shared_inv = message[rows : rows + 1, :]
+    shared_pot = message[rows + 4 : rows + 5, :]
+    late = fetched[:rows, :] * ghost_inv
+    product = cell_products(gathered, late, late_slots[count:, :], scale, high, low)
+    products[...] = product
+    summed = folded(dot_t(product, late_slots[...]))
+    up = ghost_inv * summed[:, count:] * (1.0 / HALF_WIDTH)
+    down = (
+        shared_inv * summed[:, :count] + (shared_pot - CENTER) * message[:rows, :]
+    ) * (1.0 / HALF_WIDTH)
+    down_out[...] = down
+    send_both(up, down, near, far)
+
+
+def first_body_kernel(products, states, fetched, inv_mass, potential, slots, partial):
     rows, owned = states.shape
-    ghost_inv = fetched[rows : rows + 1, :]
-    shared_count = chosen.shape[1]
-    summed = apply_cells(
-        gathered, fetched[:rows, :] * ghost_inv, late_slots[shared_count:, :], scale, slots,
-        high, low,
-    )
-    up = ghost_inv * summed[:, owned:] * (1.0 / HALF_WIDTH)
-    here = (
+    summed = folded(dot(products[...], slots[...]))
+    partial[:, :owned] = (
         inv_mass[...] * summed[:, :owned] + (potential[...] - CENTER) * states[...]
     ) * (1.0 / HALF_WIDTH)
+    partial[:, owned:] = fetched[rows : rows + 1, :] * summed[:, owned:] * (1.0 / HALF_WIDTH)
+
+
+def next_edges(
+    gathered, message, fetched, got_near, got_far, down_before, shared_before, scale,
+    late_slots, high, low, far, near,
+):
+    rows, count = near.shape
+    got_up, got_down = got_both(got_near, got_far)
+    ghost_inv = fetched[rows : rows + 1, :]
+    shared_inv = message[rows : rows + 1, :]
+    shared_pot = message[rows + 4 : rows + 5, :]
+    late = jnp.concatenate([got_up * shared_inv, got_down * ghost_inv], axis=1)
+    product = cell_products(gathered, late, late_slots[...], scale, high, low)
+    summed = folded(dot_t(product, late_slots[...]))
+    shared_now = down_before[...] + got_up
+    up = ghost_inv * summed[:, count:] * (2.0 / HALF_WIDTH)
+    down = (shared_inv * summed[:, :count] + (shared_pot - CENTER) * shared_now) * (
+        2.0 / HALF_WIDTH
+    ) - shared_before[:rows, :]
+    send_both(up, down, near, far)
+    return product, down, shared_now
+
+
+def next_edge_kernel(*refs):
+    products, down_out, shared_out = refs[-3:]
+    products[...], down_out[...], shared_out[...] = next_edges(*refs[:-3])
+
+
+def next_body(
+    products, previous, part, fetched, got_near, got_far, inv_mass, potential, slots,
+    chosen_t, partial,
+):
+    rows, owned = previous.shape
+    got_up, _ = got_both(got_near, got_far)
+    summed = folded(dot(products, slots[...]))
+    current = part[:, :owned] + placed(got_up, chosen_t[...])
+    here = (inv_mass[...] * summed[:, :owned] + (potential[...] - CENTER) * current) * (
+        2.0 / HALF_WIDTH
+    ) - previous[...]
     partial[:, :owned] = here
-    partial[:, owned:] = up
-    send_both(up, picked(here, chosen[...]), near, far)
+    partial[:, owned:] = fetched[rows : rows + 1, :] * summed[:, owned:] * (2.0 / HALF_WIDTH)
+    return here, current
+
+
+def next_body_kernel(products, *refs):
+    _, refs[-1][...] = next_body(products[...], *refs[:-1])
+
+
+def last_kernel(
+    gathered, message, fetched, got_near, got_far, down_before, shared_before, scale,
+    late_slots, high, low, previous, part, inv_mass, potential, slots, chosen_t,
+    far, near, partial, again,
+):
+    products, _, _ = next_edges(
+        gathered, message, fetched, got_near, got_far, down_before, shared_before, scale,
+        late_slots, high, low, far, near,
+    )
+    again[...], _ = next_body(
+        products, previous, part, fetched, got_near, got_far, inv_mass, potential, slots,
+        chosen_t, partial,
+    )
 
 
 def complete(part, late, chosen_t):
@@ -343,40 +421,52 @@
     )
     fetched = lax.ppermute(message, DOM, backward)
     slot_count = n_cells * pad
-    slots, late_slots, high, low, chosen, chosen_t, scale = call(
+    slots, late_slots, high, low, chosen_t, scale = call(
         prepare_kernel,
         (
             shape_of(slot_count, nodes, dtype=bf16),
             shape_of(2 * shared_count, slot_count, dtype=bf16),
             shape_of(pad, pad, dtype=bf16),
             shape_of(pad, pad, dtype=bf16),
-            shape_of(owned, shared_count, dtype=bf16),
             shape_of(shared_count, owned, dtype=bf16),
             shape_of(1, slot_count),
         ),
         [in_vmem] * 3 + [in_smem],
         [pltpu.VMEM((16, pad), jnp.int32), pltpu.VMEM((pad, pad), f32)],
     )(cells, stiff, shared, cell_scale)
-    fixed = (inv_mass, pot, scale, slots, late_slots, high, low, chosen)
+    fixed = (scale, late_slots, high, low)
     by_slot = shape_of(rows, slot_count)
 
     def swapped(near, far):
         return lax.ppermute(near, DOM, near_pairs), lax.ppermute(far, DOM, far_pairs)
 
     gathered = call(first_gather_kernel, by_slot, [in_vmem] * 3)(states, inv_mass, slots)
-    far, near, partial = call(first_kernel, (tall, edge, wide), [in_vmem] * 11)(
-        states, gathered, fetched, *fixed
-    )
-    previous = states
+    stacked = shape_of(2 * rows, slot_count, dtype=bf16)
+    far, near, products, down = call(
+        first_edge_kernel, (tall, edge, stacked, edge), [in_vmem] * 7
+    )(gathered, message, fetched, *fixed)
+    partial = call(first_body_kernel, wide, [in_vmem] * 6)(
+        products, states, fetched, inv_mass, pot, slots
+    )
+    previous, shared_now = states, message
     for step in range(DEGREE - 1):
         gathered = call(gather_kernel, by_slot, [in_vmem] * 4)(
             partial, fetched, inv_mass, slots
         )
-        far, near, partial, previous = call(
-            functools.partial(next_kernel, step == DEGREE - 2),
-            (tall, edge, wide, block),
-            [in_vmem] * 16,
-        )(previous, partial, gathered, message, fetched, *swapped(near, far), *fixed, chosen_t)
+        got = swapped(near, far)
+        edges = (gathered, message, fetched, *got, down, shared_now, *fixed)
+        body = (inv_mass, pot, slots, chosen_t)
+        if step == DEGREE - 2:
+            far, near, partial, own = call(
+                last_kernel, (tall, edge, wide, block), [in_vmem] * 17
+            )(*edges, previous, partial, *body)
+        else:
+            far, near, products, down, shared_now = call(
+                next_edge_kernel, (tall, edge, stacked, edge, edge), [in_vmem] * 11
+            )(*edges)
+            partial, previous = call(next_body_kernel, (wide, block), [in_vmem] * 10)(
+                products, previous, partial, fetched, *got, *body
+            )
 
     def from_chip(x, s):
         return lax.ppermute(x, "chip", [(i, i ^ s) for i in range(chips)])
@@ -385,7 +475,7 @@
     second = from_chip(partial, 2)
     beside = from_chip(partial, 1)
     relayed, own = call(relay_kernel, (wide, block), [in_vmem] * 4, aliases={1: 0, 2: 1})(
-        beside, second, previous, got_near
+        beside, second, own, got_near
     )
     blocks = [partial, beside, relayed, from_chip(relayed, 1)]
 

time: 130 us -> 130 us (level)
  the two profiles are of different devices: /device:TPU:16 before, /device:TPU:8 now
where the time goes in v10:
time: 130 us
  starting transfers between devices  62.8 us (48%)
  blocking collectives  40.7 us (31%)
  Pallas kernels  17.4 us (13%)
  waiting for transfers between devices  6.49 us (5%)
  local copies, waits for them, and re-layouts  1.32 us (1%)
    ppermute x3, starting transfers between devices, swapped(): lax.ppermute(far, DOM, far_pairs)  26.5 us
    ppermute x1, starting transfers between devices, per_device(): fetched = lax.ppermute(message, DOM, backward)  17.5 us
    all_to_all x1, blocking collectives, per_device(): spread = lax.all_to_all(mine, ('x', 'half'), 0, 0, tiled=True)  17 us
    all_to_all x1, blocking collectives, per_device(): lax.all_to_all(jnp.broadcast_to(mine[None], (n_z, *mine.shape)), 'z', 0,...  12.6 us
    all_to_all x1, blocking collectives, per_device(): lax.all_to_all(gram.reshape(2 * n_z, each, chips * rows), ('core', 'z'),...  11.1 us
    ppermute x3, starting transfers between devices, from_chip(): return lax.ppermute(x, 'chip', [(i, i ^ s) for i in range(chips)])  7.91 us
    ppermute x3, starting transfers between devices, swapped(): lax.ppermute(near, DOM, near_pairs)  6.58 us
    ppermute x2, starting transfers between devices, from_sibling(): return lax.ppermute(x, 'core', [(0, 1), (1, 0)])  4.33 us
  transfers between devices with their start and end apart: 12, of which 5 were waited for; matrix products, arithmetic and copies ran while one was open for 0% of the time, Pallas kernels for 7%

profile of v10, /device:TPU:8, one launch (start us, length us, event | category | flops | bytes accessed | tf_op | source)
XLA Modules:
  0.0 129.6 jit_solution(9691085297499553555)
XLA Ops:
  0.6 1.3 %shard_map.86 = (f32[72,128]{1,0:T(8,128)S(1)}, f32[64,1024]{1,0:T(8,128)S(1)}, f32[1,1024]{1,0:T(1,128)S(1)}, s32[1,128]{1,0:T(1,128)S(1)}, f32[1,1024]{1,0:T(1...) custom-call(f32[64,1024]{1,0:T(8,128)} %states.1, f32[1,1024]{1,0:T(1,128)} %bitcast.7, s32[1,128]{1,0:T(1,128)} %bitcast.9, ...), custom_call_target="tpu_custom_call" | custom-call | tf_op jit(solution)/shard_map/pallas_call | solution.py:404
  2.0 17.5 %collective-permute-start = (f32[72,128]{1,0:T(8,128)S(1)}, f32[72,128]{1,0:T(8,128)S(1)}, u32[]{:S(2)}, u32[]{:S(2)}) collective-permute-start(f32[72,128]{1,0:T(8,128)S(1)} %get-tuple-element.40.message.refs_1_.refs_6_), channel_id=1, source_target_pairs={{0,63},{1,0},{2,1},{3,2},{4,3},{5,4},{6,5},{7,6},{8,7},{9,8},{10,9... | collective-permute-start | bytes 110600 | tf_op jit(solution)/shard_map/ppermute | solution.py:422
  19.5 0.6 copy-done
  20.1 1.5 %shard_map.87 = (bf16[2304,1152]{1,0:T(8,128)(2,1)S(1)}, bf16[256,2304]{1,0:T(8,128)(2,1)S(1)}, bf16[384,384]{1,0:T(8,128)(2,1)S(1)}, bf16[384,384]{1,0:T(8,128)...) custom-call(s32[6,343]{1,0:T(8,128)S(1)} %get-tuple-element.36.cells, ...), custom_call_target="tpu_custom_call" | custom-call | tf_op jit(solution)/shard_map/pallas_call | solution.py:424
  21.7 1.6 %shard_map.88.gathered = f32[64,2304]{1,0:T(8,128)S(1)} custom-call(f32[64,1024]{1,0:T(8,128)S(1)} %get-tuple-element.34.states.refs_0_, f32[1,1024]{1,0:T(1,128)S(1)} %get-tuple-element.35.inv_mass.refs_5_, bf16[2304,1152]{1,0:T(8,128)(2,1)S(1)} %get-tuple-element.39.slots.refs_7_), custom_call_target="tpu_custom_call" | custom-call | tf_op jit(solution)/shard_map/pallas_call | solution.py:443
  23.3 1.8 %shard_map.89 = (f32[72,128]{1,0:T(8,128)S(1)}, f32[64,128]{1,0:T(8,128)S(1)}, bf16[128,2304]{1,0:T(8,128)(2,1)S(1)}, f32[64,128]{1,0:T(8,128)S(1)}) custom-call(f32[64,2304]{1,0:T(8,128)S(1)} %shard_map.88.gathered, f32[72,128]{1,0:T(8,128)S(1)} %get-tuple-element.40.message.refs_1_.refs_6_, f32[72,128]{1,0:T(8,128)S(1)} %collective-permute-done.fetched.refs_2_, ...), custom_call_target="tpu_custom_call" | custom-call | tf_op jit(solution)/shard_map/pallas_call | solution.py:445
  25.1 10.5 %collective-permute-start.2 = (f32[72,128]{1,0:T(8,128)S(1)}, f32[72,128]{1,0:T(8,128)S(1)}, u32[]{:S(2)}, u32[]{:S(2)}) collective-permute-start(f32[72,128]{1,0:T(8,128)S(1)} %get-tuple-element.48), channel_id=1, source_target_pairs={{0,63},{1,2},{2,1},{3,4},{4,3},{5,6},{6,5},{7,8},{8,7},{9,10},{10,... | collective-permute-start | bytes 110600 | tf_op jit(solution)/shard_map/ppermute | solution.py:441
  35.6 1.9 %collective-permute-start.1 = (f32[64,128]{1,0:T(8,128)S(1)}, f32[64,128]{1,0:T(8,128)S(1)}, u32[]{:S(2)}, u32[]{:S(2)}) collective-permute-start(f32[64,128]{1,0:T(8,128)S(1)} %get-tuple-element.47), channel_id=1, source_target_pairs={{0,1},{1,0},{2,3},{3,2},{4,5},{5,4},{6,7},{7,6},{8,9},{9,8},{10,11... | collective-permute-start | bytes 98312 | tf_op jit(solution)/shard_map/ppermute | solution.py:441
  37.6 1.0 shard_map.90.part.refs_1_
  38.5 1.6 %shard_map.91.refs_0_ = f32[64,2304]{1,0:T(8,128)S(1)} custom-call(f32[64,1152]{1,0:T(8,128)S(1)} %shard_map.90.part.refs_1_, f32[72,128]{1,0:T(8,128)S(1)} %collective-permute-done.fetched.refs_2_, f32[1,1024]{1,0:T(1,128)S(1)} %get-tuple-element.35.inv_mass.refs_5_, bf16[2304,1152]{1,0:T(8,128)(2,1)S(1)} %get-tuple-element.39.slots.refs_7_), custom_call_target="tpu_custom_call" | custom-call | tf_op jit(solution)/shard_map/pallas_call | solution.py:453
  40.1 1.3 %collective-permute-done.1.refs_3_ = f32[64,128]{1,0:T(8,128)S(1)} collective-permute-done((f32[64,128]{1,0:T(8,128)S(1)}, f32[64,128]{1,0:T(8,128)S(1)}, u32[]{:S(2)}, u32[]{:S(2)}) %collective-permute-start.1) | collective-permute-done | bytes 32800 | tf_op jit(solution)/shard_map/ppermute | solution.py:441
  41.4 1.8 %shard_map.92 = (f32[72,128]{1,0:T(8,128)S(1)}, f32[64,128]{1,0:T(8,128)S(1)}, bf16[128,2304]{1,0:T(8,128)(2,1)S(1)}, f32[64,128]{1,0:T(8,128)S(1)}, f32[64,128]{1,0:T(8,128)S(1)}) custom-call(f32[64,2304]{1,0:T(8,128)S(1)} %shard_map.91.refs_0_, f32[72,128]{1,0:T(8,128)S(1)} %get-tuple-element.40.message.refs_1_.refs_6_, ...), custom_call_target="tpu_custom_call" | custom-call | tf_op jit(solution)/shard_map/pallas_call | solution.py:464
  43.3 8.5 %collective-permute-start.4 = (f32[72,128]{1,0:T(8,128)S(1)}, f32[72,128]{1,0:T(8,128)S(1)}, u32[]{:S(2)}, u32[]{:S(2)}) collective-permute-start(f32[72,128]{1,0:T(8,128)S(1)} %get-tuple-element.54), channel_id=1, source_target_pairs={{0,63},{1,2},{2,1},{3,4},{4,3},{5,6},{6,5},{7,8},{8,7},{9,10},{10,... | collective-permute-start | bytes 110600 | tf_op jit(solution)/shard_map/ppermute | solution.py:441
  51.7 1.9 %collective-permute-start.3 = (f32[64,128]{1,0:T(8,128)S(1)}, f32[64,128]{1,0:T(8,128)S(1)}, u32[]{:S(2)}, u32[]{:S(2)}) collective-permute-start(f32[64,128]{1,0:T(8,128)S(1)} %get-tuple-element.53), channel_id=1, source_target_pairs={{0,1},{1,0},{2,3},{3,2},{4,5},{5,4},{6,7},{7,6},{8,9},{9,8},{10,11... | collective-permute-start | bytes 98312 | tf_op jit(solution)/shard_map/ppermute | solution.py:441
  53.7 1.1 shard_map.93
  54.8 1.6 %shard_map.94.gathered = f32[64,2304]{1,0:T(8,128)S(1)} custom-call(f32[64,1152]{1,0:T(8,128)S(1)} %get-tuple-element.52.part, f32[72,128]{1,0:T(8,128)S(1)} %collective-permute-done.fetched.refs_2_, f32[1,1024]{1,0:T(1,128)S(1)} %get-tuple-element.35.inv_mass.refs_5_, bf16[2304,1152]{1,0:T(8,128)(2,1)S(1)} %get-tuple-element.39.slots.refs_7_), custom_call_target="tpu_custom_call" | custom-call | tf_op jit(solution)/shard_map/pallas_call | solution.py:453
  56.3 1.2 collective-permute-done.3.got_near
  57.6 2.3 %shard_map.95 = (f32[72,128]{1,0:T(8,128)S(1)}, f32[64,128]{1,0:T(8,128)S(1)}, f32[64,1152]{1,0:T(8,128)S(1)}, f32[64,1024]{1,0:T(8,128)S(1)}) custom-call(f32[64,2304]{1,0:T(8,128)S(1)} %shard_map.94.gathered, f32[72,128]{1,0:T(8,128)S(1)} %get-tuple-element.40.message.refs_1_.refs_6_, f32[72,128]{1,0:T(8,128)S(1)} %collective-permute-done.fetched.refs_2_, ...), custom_call_target="tpu_custom_call" | custom-call | tf_op jit(solution)/shard_map/pallas_call | solution.py:460
  59.9 2.0 %collective-permute-start.8 = (f32[64,1152]{1,0:T(8,128)S(1)}, f32[64,1152]{1,0:T(8,128)S(1)}, u32[]{:S(2)}, u32[]{:S(2)}) collective-permute-start(f32[64,1152]{1,0:T(8,128)S(1)} %get-tuple-element.58.part.rest_0_), channel_id=1, source_target_pairs={{0,256},{128,384},{256,0},{384,128},{1,257},{129,385},{257,1},{385... | collective-permute-start | bytes 884744 | tf_op jit(solution)/shard_map/ppermute | solution.py:472
  62.0 3.1 %collective-permute-start.7 = (f32[64,1152]{1,0:T(8,128)S(1)}, f32[64,1152]{1,0:T(8,128)S(1)}, u32[]{:S(2)}, u32[]{:S(2)}) collective-permute-start(f32[64,1152]{1,0:T(8,128)S(1)} %get-tuple-element.58.part.rest_0_), channel_id=1, source_target_pairs={{0,128},{128,0},{256,384},{384,256},{1,129},{129,1},{257,385},{385... | collective-permute-start | bytes 884744 | tf_op jit(solution)/shard_map/ppermute | solution.py:472
  65.1 2.7 %collective-permute-start.5 = (f32[64,128]{1,0:T(8,128)S(1)}, f32[64,128]{1,0:T(8,128)S(1)}, u32[]{:S(2)}, u32[]{:S(2)}) collective-permute-start(f32[64,128]{1,0:T(8,128)S(1)} %get-tuple-element.59), channel_id=1, source_target_pairs={{0,1},{1,0},{2,3},{3,2},{4,5},{5,4},{6,7},{7,6},{8,9},{9,8},{10,11... | collective-permute-start | bytes 98312 | tf_op jit(solution)/shard_map/ppermute | solution.py:441
  67.8 7.5 %collective-permute-start.6 = (f32[72,128]{1,0:T(8,128)S(1)}, f32[72,128]{1,0:T(8,128)S(1)}, u32[]{:S(2)}, u32[]{:S(2)}) collective-permute-start(f32[72,128]{1,0:T(8,128)S(1)} %get-tuple-element.60), channel_id=1, source_target_pairs={{0,63},{1,2},{2,1},{3,4},{4,3},{5,6},{6,5},{7,8},{8,7},{9,10},{10,... | collective-permute-start | bytes 110600 | tf_op jit(solution)/shard_map/ppermute | solution.py:441
  75.4 2.7 %collective-permute-start.11 = (f32[64,1152]{1,0:T(8,128)S(1)}, f32[64,1152]{1,0:T(8,128)S(1)}, u32[]{:S(2)}, u32[]{:S(2)}) collective-permute-start(f32[64,1152]{1,0:T(8,128)S(1)} %get-tuple-element.65.rest_2_), channel_id=1, source_target_pairs={{0,128},{128,0},{256,384},{384,256},{1,129},{129,1},{257,385},{385... | collective-permute-start | bytes 884744 | tf_op jit(solution)/shard_map/ppermute | solution.py:472
  78.1 3.7 %collective-permute-done.6.got_far = f32[72,128]{1,0:T(8,128)S(1)} collective-permute-done((f32[72,128]{1,0:T(8,128)S(1)}, f32[72,128]{1,0:T(8,128)S(1)}, u32[]{:S(2)}, u32[]{:S(2)}) %collective-permute-start.6) | collective-permute-done | bytes 36896 | tf_op jit(solution)/shard_map/ppermute | solution.py:441
  81.9 1.9 %collective-permute-start.10 = (f32[64,1024]{1,0:T(8,128)S(1)}, f32[64,1024]{1,0:T(8,128)S(1)}, u32[]{:S(2)}, u32[]{:S(2)}) collective-permute-start(f32[64,1024]{1,0:T(8,128)S(1)} %shard_map.96.late), channel_id=1, source_target_pairs={{0,64},{64,0},{1,65},{65,1},{2,66},{66,2},{3,67},{67,3},{4,68},{68... | collective-permute-start | bytes 786440 | tf_op jit(solution)/shard_map/ppermute | solution.py:483
  83.8 2.4 %collective-permute-start.9 = (f32[64,1024]{1,0:T(8,128)S(1)}, f32[64,1024]{1,0:T(8,128)S(1)}, u32[]{:S(2)}, u32[]{:S(2)}) collective-permute-start(f32[64,1024]{1,0:T(8,128)S(1)} %get-tuple-element.64), channel_id=1, source_target_pairs={{0,64},{64,0},{1,65},{65,1},{2,66},{66,2},{3,67},{67,3},{4,68},{68... | collective-permute-start | bytes 786440 | tf_op jit(solution)/shard_map/ppermute | solution.py:483
  86.2 1.0 shard_map.97
  87.3 0.8 shard_map.99
  88.1 11.1 %all_to_all.15.pieces = f32[16,8,256]{2,1,0:T(8,128)S(1)} all-to-all(f32[16,8,256]{2,1,0:T(8,128)S(1)} %bitcast.5), channel_id=1, replica_groups=mesh['chip'=4,'core'=2,'x'=4,'half'=2,'z'=8] {'core','z'}, dimensions={0} | all-to-all | bytes 262144 | tf_op jit(solution)/shard_map/all_to_all | solution.py:499
  99.3 17.0 %all_to_all.16 = f32[8,8,512]{2,1,0:T(8,128)S(1)} all-to-all(f32[8,8,512]{2,1,0:T(8,128)S(1)} %shard_map.100), channel_id=1, replica_groups=mesh['chip'=4,'core'=2,'x'=4,'half'=2,'z'=8] {'x','half'}, dimensions={0} | all-to-all | bytes 262144 | tf_op jit(solution)/shard_map/all_to_all | solution.py:503
  116.3 12.6 %all_to_all.17 = f32[8,8,512]{2,1,0:T(8,128)S(1)} all-to-all(f32[8,8,512]{2,1,0:T(8,128)S(1)} %broadcast_in_dim.2), channel_id=1, replica_groups=mesh['chip'=4,'core'=2,'x'=4,'half'=2,'z'=8] {'z'}, dimensions={0} | all-to-all | bytes 262144 | tf_op jit(solution)/shard_map/all_to_all | solution.py:505
  128.9 0.7 copy.14
  (15 shorter events, 0.4 us)
Async XLA Ops:
  2.0 21.3 %collective-permute-start = (f32[72,128]{1,0:T(8,128)S(1)}, f32[72,128]{1,0:T(8,128)S(1)}, u32[]{:S(2)}, u32[]{:S(2)}) collective-permute-start(f32[72,128]{1,0:T(8,128)S(1)} %get-tuple-element.40.message.refs_1_.refs_6_), channel_id=1, source_target_pairs={{0,63},{1,0},{2,1},{3,2},{4,3},{5,4},{6,5},{7,6},{8,7},{9,8},{10,9... | collective-permute-start | bytes 110600 | tf_op jit(solution)/shard_map/ppermute | solution.py:422
  19.5 0.7 copy-start
  25.1 16.4 %collective-permute-start.2 = (f32[72,128]{1,0:T(8,128)S(1)}, f32[72,128]{1,0:T(8,128)S(1)}, u32[]{:S(2)}, u32[]{:S(2)}) collective-permute-start(f32[72,128]{1,0:T(8,128)S(1)} %get-tuple-element.48), channel_id=1, source_target_pairs={{0,63},{1,2},{2,1},{3,4},{4,3},{5,6},{6,5},{7,8},{8,7},{9,10},{10,... | collective-permute-start | bytes 110600 | tf_op jit(solution)/shard_map/ppermute | solution.py:441
  35.6 5.8 %collective-permute-start.1 = (f32[64,128]{1,0:T(8,128)S(1)}, f32[64,128]{1,0:T(8,128)S(1)}, u32[]{:S(2)}, u32[]{:S(2)}) collective-permute-start(f32[64,128]{1,0:T(8,128)S(1)} %get-tuple-element.47), channel_id=1, source_target_pairs={{0,1},{1,0},{2,3},{3,2},{4,5},{5,4},{6,7},{7,6},{8,9},{9,8},{10,11... | collective-permute-start | bytes 98312 | tf_op jit(solution)/shard_map/ppermute | solution.py:441
  43.3 14.4 %collective-permute-start.4 = (f32[72,128]{1,0:T(8,128)S(1)}, f32[72,128]{1,0:T(8,128)S(1)}, u32[]{:S(2)}, u32[]{:S(2)}) collective-permute-start(f32[72,128]{1,0:T(8,128)S(1)} %get-tuple-element.54), channel_id=1, source_target_pairs={{0,63},{1,2},{2,1},{3,4},{4,3},{5,6},{6,5},{7,8},{8,7},{9,10},{10,... | collective-permute-start | bytes 110600 | tf_op jit(solution)/shard_map/ppermute | solution.py:441
  51.7 5.8 %collective-permute-start.3 = (f32[64,128]{1,0:T(8,128)S(1)}, f32[64,128]{1,0:T(8,128)S(1)}, u32[]{:S(2)}, u32[]{:S(2)}) collective-permute-start(f32[64,128]{1,0:T(8,128)S(1)} %get-tuple-element.53), channel_id=1, source_target_pairs={{0,1},{1,0},{2,3},{3,2},{4,5},{5,4},{6,7},{7,6},{8,9},{9,8},{10,11... | collective-permute-start | bytes 98312 | tf_op jit(solution)/shard_map/ppermute | solution.py:441
  59.9 15.4 %collective-permute-start.8 = (f32[64,1152]{1,0:T(8,128)S(1)}, f32[64,1152]{1,0:T(8,128)S(1)}, u32[]{:S(2)}, u32[]{:S(2)}) collective-permute-start(f32[64,1152]{1,0:T(8,128)S(1)} %get-tuple-element.58.part.rest_0_), channel_id=1, source_target_pairs={{0,256},{128,384},{256,0},{384,128},{1,257},{129,385},{257,1},{385... | collective-permute-start | bytes 884744 | tf_op jit(solution)/shard_map/ppermute | solution.py:472
  62.0 13.4 %collective-permute-start.7 = (f32[64,1152]{1,0:T(8,128)S(1)}, f32[64,1152]{1,0:T(8,128)S(1)}, u32[]{:S(2)}, u32[]{:S(2)}) collective-permute-start(f32[64,1152]{1,0:T(8,128)S(1)} %get-tuple-element.58.part.rest_0_), channel_id=1, source_target_pairs={{0,128},{128,0},{256,384},{384,256},{1,129},{129,1},{257,385},{385... | collective-permute-start | bytes 884744 | tf_op jit(solution)/shard_map/ppermute | solution.py:472
  65.1 10.3 %collective-permute-start.5 = (f32[64,128]{1,0:T(8,128)S(1)}, f32[64,128]{1,0:T(8,128)S(1)}, u32[]{:S(2)}, u32[]{:S(2)}) collective-permute-start(f32[64,128]{1,0:T(8,128)S(1)} %get-tuple-element.59), channel_id=1, source_target_pairs={{0,1},{1,0},{2,3},{3,2},{4,5},{5,4},{6,7},{7,6},{8,9},{9,8},{10,11... | collective-permute-start | bytes 98312 | tf_op jit(solution)/shard_map/ppermute | solution.py:441
  67.8 14.0 %collective-permute-start.6 = (f32[72,128]{1,0:T(8,128)S(1)}, f32[72,128]{1,0:T(8,128)S(1)}, u32[]{:S(2)}, u32[]{:S(2)}) collective-permute-start(f32[72,128]{1,0:T(8,128)S(1)} %get-tuple-element.60), channel_id=1, source_target_pairs={{0,63},{1,2},{2,1},{3,4},{4,3},{5,6},{6,5},{7,8},{8,7},{9,10},{10,... | collective-permute-start | bytes 110600 | tf_op jit(solution)/shard_map/ppermute | solution.py:441
  75.4 11.9 %collective-permute-start.11 = (f32[64,1152]{1,0:T(8,128)S(1)}, f32[64,1152]{1,0:T(8,128)S(1)}, u32[]{:S(2)}, u32[]{:S(2)}) collective-permute-start(f32[64,1152]{1,0:T(8,128)S(1)} %get-tuple-element.65.rest_2_), channel_id=1, source_target_pairs={{0,128},{128,0},{256,384},{384,256},{1,129},{129,1},{257,385},{385... | collective-permute-start | bytes 884744 | tf_op jit(solution)/shard_map/ppermute | solution.py:472
  81.9 5.3 %collective-permute-start.10 = (f32[64,1024]{1,0:T(8,128)S(1)}, f32[64,1024]{1,0:T(8,128)S(1)}, u32[]{:S(2)}, u32[]{:S(2)}) collective-permute-start(f32[64,1024]{1,0:T(8,128)S(1)} %shard_map.96.late), channel_id=1, source_target_pairs={{0,64},{64,0},{1,65},{65,1},{2,66},{66,2},{3,67},{67,3},{4,68},{68... | collective-permute-start | bytes 786440 | tf_op jit(solution)/shard_map/ppermute | solution.py:483
  83.8 3.6 %collective-permute-start.9 = (f32[64,1024]{1,0:T(8,128)S(1)}, f32[64,1024]{1,0:T(8,128)S(1)}, u32[]{:S(2)}, u32[]{:S(2)}) collective-permute-start(f32[64,1024]{1,0:T(8,128)S(1)} %get-tuple-element.64), channel_id=1, source_target_pairs={{0,64},{64,0},{1,65},{65,1},{2,66},{66,2},{3,67},{67,3},{4,68},{68... | collective-permute-start | bytes 786440 | tf_op jit(solution)/shard_map/ppermute | solution.py:483

commit v11 on v10

--- a/solution.py
+++ b/solution.py
@@ -12,6 +12,7 @@
 HALF_WIDTH = 4.0
 LIMIT = 28 * 1024 * 1024
 LATE = 8
+EXTRA = 4
 BAND = ("chip", "core")
 DOM = ("x", "half", "z")
 
@@ -271,10 +272,14 @@
         gathered, message, fetched, got_near, got_far, down_before, shared_before, scale,
         late_slots, high, low, far, near,
     )
-    again[...], _ = next_body(
+    here, _ = next_body(
         products, previous, part, fetched, got_near, got_far, inv_mass, potential, slots,
         chosen_t, partial,
     )
+    rows, owned = here.shape
+    for i in range(rows // 8):
+        again[:, i * owned : (i + 1) * owned] = here[8 * i : 8 * (i + 1), :]
+    again[:, rows // 8 * owned :] = jnp.zeros((8, again.shape[1] - rows // 8 * owned), f32)
 
 
 def complete(part, late, chosen_t):
@@ -335,7 +340,10 @@
     for s in range(chips):
         at = pl.ds(pl.multiple_of((chip ^ s) * rows, rows), rows)
         g_high[at, :], g_low[at, :] = parts(blocks[s][...], 2)
-    theirs = jnp.concatenate(complete(sibling, late, chosen_t), axis=1)
+    owned = chosen_t.shape[1]
+    rows_of = [sibling[:, i * owned : (i + 1) * owned] for i in range(rows // 8)]
+    theirs = complete(jnp.concatenate(rows_of, axis=0), late, chosen_t)
+    theirs = jnp.concatenate(theirs, axis=1)
     high, low = parts(jnp.concatenate([left[...], theirs], axis=0), 2)
     by_high = dot_t(jnp.concatenate([high, low], axis=0), g_high[...])
     whole = by_high[: 2 * rows] + by_high[2 * rows :] + dot_t(high, g_low[...])
@@ -389,6 +397,7 @@
     wide = shape_of(rows, nodes)
     edge = shape_of(rows, shared_count)
     tall = shape_of(rows + 8, shared_count)
+    beside_rows = shape_of(8, rows // 8 * owned + EXTRA * 128)
 
     def call(kernel, out_shape, specs, scratch_shapes=(), aliases={}):
         return pl.pallas_call(
@@ -458,7 +467,7 @@
         body = (inv_mass, pot, slots, chosen_t)
         if step == DEGREE - 2:
             far, near, partial, own = call(
-                last_kernel, (tall, edge, wide, block), [in_vmem] * 17
+                last_kernel, (tall, edge, wide, beside_rows), [in_vmem] * 17
             )(*edges, previous, partial, *body)
         else:
             far, near, products, down, shared_now = call(
@@ -474,7 +483,7 @@
     got_near, got_far = swapped(near, far)
     second = from_chip(partial, 2)
     beside = from_chip(partial, 1)
-    relayed, own = call(relay_kernel, (wide, block), [in_vmem] * 4, aliases={1: 0, 2: 1})(
+    relayed, own = call(relay_kernel, (wide, beside_rows), [in_vmem] * 4, aliases={1: 0, 2: 1})(
         beside, second, own, got_near
     )
     blocks = [partial, beside, relayed, from_chip(relayed, 1)]

time: 130 us -> 128 us (0.985)
  the two profiles are of different devices: /device:TPU:8 before, /device:TPU:16 now
where the time goes in v11:
time: 128 us; the launch traced here: 127 us
  starting transfers between devices  63.3 us (49%)
  blocking collectives  39.9 us (31%)
  Pallas kernels  17.4 us (14%)
  waiting for transfers between devices  4.74 us (4%)
  local copies, waits for them, and re-layouts  1.32 us (1%)
    ppermute x3, starting transfers between devices, swapped(): lax.ppermute(far, DOM, far_pairs)  25.8 us
    all_to_all x1, blocking collectives, per_device(): spread = lax.all_to_all(mine, ('x', 'half'), 0, 0, tiled=True)  16.8 us
    ppermute x1, starting transfers between devices, per_device(): fetched = lax.ppermute(message, DOM, backward)  16.6 us
    all_to_all x1, blocking collectives, per_device(): lax.all_to_all(jnp.broadcast_to(mine[None], (n_z, *mine.shape)), 'z', 0,...  12.1 us
    all_to_all x1, blocking collectives, per_device(): lax.all_to_all(gram.reshape(2 * n_z, each, chips * rows), ('core', 'z'),...  11.1 us
    ppermute x3, starting transfers between devices, from_chip(): return lax.ppermute(x, 'chip', [(i, i ^ s) for i in range(chips)])  10.5 us
    ppermute x3, starting transfers between devices, swapped(): lax.ppermute(near, DOM, near_pairs)  6.51 us
    ppermute x2, starting transfers between devices, from_sibling(): return lax.ppermute(x, 'core', [(0, 1), (1, 0)])  3.84 us
  transfers between devices with their start and end apart: 12, of which 4 were waited for; matrix products, arithmetic and copies ran while one was open for 0% of the time, Pallas kernels for 7%

profile of v11, /device:TPU:16, one launch (start us, length us, event | category | flops | bytes accessed | tf_op | source)
XLA Modules:
  0.0 127.5 jit_solution(9594552452358045605)
XLA Ops:
  0.6 1.3 %shard_map.86 = (f32[72,128]{1,0:T(8,128)S(1)}, f32[64,1024]{1,0:T(8,128)S(1)}, f32[1,1024]{1,0:T(1,128)S(1)}, s32[1,128]{1,0:T(1,128)S(1)}, f32[1,1024]{1,0:T(1...) custom-call(f32[64,1024]{1,0:T(8,128)} %states.1, f32[1,1024]{1,0:T(1,128)} %bitcast.7, s32[1,128]{1,0:T(1,128)} %bitcast.9, ...), custom_call_target="tpu_custom_call" | custom-call | tf_op jit(solution)/shard_map/pallas_call | solution.py:413
  2.0 16.6 %collective-permute-start = (f32[72,128]{1,0:T(8,128)S(1)}, f32[72,128]{1,0:T(8,128)S(1)}, u32[]{:S(2)}, u32[]{:S(2)}) collective-permute-start(f32[72,128]{1,0:T(8,128)S(1)} %get-tuple-element.40.message.refs_1_.refs_6_), channel_id=1, source_target_pairs={{0,63},{1,0},{2,1},{3,2},{4,3},{5,4},{6,5},{7,6},{8,7},{9,8},{10,9... | collective-permute-start | bytes 110600 | tf_op jit(solution)/shard_map/ppermute | solution.py:431
  18.6 0.6 copy-done
  19.2 1.5 %shard_map.87 = (bf16[2304,1152]{1,0:T(8,128)(2,1)S(1)}, bf16[256,2304]{1,0:T(8,128)(2,1)S(1)}, bf16[384,384]{1,0:T(8,128)(2,1)S(1)}, bf16[384,384]{1,0:T(8,128)...) custom-call(s32[6,343]{1,0:T(8,128)S(1)} %get-tuple-element.36.cells, ...), custom_call_target="tpu_custom_call" | custom-call | tf_op jit(solution)/shard_map/pallas_call | solution.py:433
  20.8 1.6 %shard_map.88.gathered = f32[64,2304]{1,0:T(8,128)S(1)} custom-call(f32[64,1024]{1,0:T(8,128)S(1)} %get-tuple-element.34.states.refs_0_, f32[1,1024]{1,0:T(1,128)S(1)} %get-tuple-element.35.inv_mass.refs_5_, bf16[2304,1152]{1,0:T(8,128)(2,1)S(1)} %get-tuple-element.39.slots.refs_7_), custom_call_target="tpu_custom_call" | custom-call | tf_op jit(solution)/shard_map/pallas_call | solution.py:452
  22.4 1.8 %shard_map.89 = (f32[72,128]{1,0:T(8,128)S(1)}, f32[64,128]{1,0:T(8,128)S(1)}, bf16[128,2304]{1,0:T(8,128)(2,1)S(1)}, f32[64,128]{1,0:T(8,128)S(1)}) custom-call(f32[64,2304]{1,0:T(8,128)S(1)} %shard_map.88.gathered, f32[72,128]{1,0:T(8,128)S(1)} %get-tuple-element.40.message.refs_1_.refs_6_, f32[72,128]{1,0:T(8,128)S(1)} %collective-permute-done.fetched.refs_2_, ...), custom_call_target="tpu_custom_call" | custom-call | tf_op jit(solution)/shard_map/pallas_call | solution.py:454
  24.2 10.1 %collective-permute-start.2 = (f32[72,128]{1,0:T(8,128)S(1)}, f32[72,128]{1,0:T(8,128)S(1)}, u32[]{:S(2)}, u32[]{:S(2)}) collective-permute-start(f32[72,128]{1,0:T(8,128)S(1)} %get-tuple-element.48), channel_id=1, source_target_pairs={{0,63},{1,2},{2,1},{3,4},{4,3},{5,6},{6,5},{7,8},{8,7},{9,10},{10,... | collective-permute-start | bytes 110600 | tf_op jit(solution)/shard_map/ppermute | solution.py:450
  34.3 1.9 %collective-permute-start.1 = (f32[64,128]{1,0:T(8,128)S(1)}, f32[64,128]{1,0:T(8,128)S(1)}, u32[]{:S(2)}, u32[]{:S(2)}) collective-permute-start(f32[64,128]{1,0:T(8,128)S(1)} %get-tuple-element.47), channel_id=1, source_target_pairs={{0,1},{1,0},{2,3},{3,2},{4,5},{5,4},{6,7},{7,6},{8,9},{9,8},{10,11... | collective-permute-start | bytes 98312 | tf_op jit(solution)/shard_map/ppermute | solution.py:450
  36.3 1.0 shard_map.90.part.refs_1_
  37.3 1.6 %shard_map.91.refs_0_ = f32[64,2304]{1,0:T(8,128)S(1)} custom-call(f32[64,1152]{1,0:T(8,128)S(1)} %shard_map.90.part.refs_1_, f32[72,128]{1,0:T(8,128)S(1)} %collective-permute-done.fetched.refs_2_, f32[1,1024]{1,0:T(1,128)S(1)} %get-tuple-element.35.inv_mass.refs_5_, bf16[2304,1152]{1,0:T(8,128)(2,1)S(1)} %get-tuple-element.39.slots.refs_7_), custom_call_target="tpu_custom_call" | custom-call | tf_op jit(solution)/shard_map/pallas_call | solution.py:462
  38.8 1.3 %collective-permute-done.1.refs_3_ = f32[64,128]{1,0:T(8,128)S(1)} collective-permute-done((f32[64,128]{1,0:T(8,128)S(1)}, f32[64,128]{1,0:T(8,128)S(1)}, u32[]{:S(2)}, u32[]{:S(2)}) %collective-permute-start.1) | collective-permute-done | bytes 32800 | tf_op jit(solution)/shard_map/ppermute | solution.py:450
  40.1 1.8 %shard_map.92 = (f32[72,128]{1,0:T(8,128)S(1)}, f32[64,128]{1,0:T(8,128)S(1)}, bf16[128,2304]{1,0:T(8,128)(2,1)S(1)}, f32[64,128]{1,0:T(8,128)S(1)}, f32[64,128]{1,0:T(8,128)S(1)}) custom-call(f32[64,2304]{1,0:T(8,128)S(1)} %shard_map.91.refs_0_, f32[72,128]{1,0:T(8,128)S(1)} %get-tuple-element.40.message.refs_1_.refs_6_, ...), custom_call_target="tpu_custom_call" | custom-call | tf_op jit(solution)/shard_map/pallas_call | solution.py:473
  42.0 8.2 %collective-permute-start.4 = (f32[72,128]{1,0:T(8,128)S(1)}, f32[72,128]{1,0:T(8,128)S(1)}, u32[]{:S(2)}, u32[]{:S(2)}) collective-permute-start(f32[72,128]{1,0:T(8,128)S(1)} %get-tuple-element.54), channel_id=1, source_target_pairs={{0,63},{1,2},{2,1},{3,4},{4,3},{5,6},{6,5},{7,8},{8,7},{9,10},{10,... | collective-permute-start | bytes 110600 | tf_op jit(solution)/shard_map/ppermute | solution.py:450
  50.1 1.9 %collective-permute-start.3 = (f32[64,128]{1,0:T(8,128)S(1)}, f32[64,128]{1,0:T(8,128)S(1)}, u32[]{:S(2)}, u32[]{:S(2)}) collective-permute-start(f32[64,128]{1,0:T(8,128)S(1)} %get-tuple-element.53), channel_id=1, source_target_pairs={{0,1},{1,0},{2,3},{3,2},{4,5},{5,4},{6,7},{7,6},{8,9},{9,8},{10,11... | collective-permute-start | bytes 98312 | tf_op jit(solution)/shard_map/ppermute | solution.py:450
  52.1 1.1 shard_map.93
  53.1 1.6 %shard_map.94.gathered = f32[64,2304]{1,0:T(8,128)S(1)} custom-call(f32[64,1152]{1,0:T(8,128)S(1)} %get-tuple-element.52.part, f32[72,128]{1,0:T(8,128)S(1)} %collective-permute-done.fetched.refs_2_, f32[1,1024]{1,0:T(1,128)S(1)} %get-tuple-element.35.inv_mass.refs_5_, bf16[2304,1152]{1,0:T(8,128)(2,1)S(1)} %get-tuple-element.39.slots.refs_7_), custom_call_target="tpu_custom_call" | custom-call | tf_op jit(solution)/shard_map/pallas_call | solution.py:462
  54.7 1.2 collective-permute-done.3.got_near
  55.9 2.3 %shard_map.95 = (f32[72,128]{1,0:T(8,128)S(1)}, f32[64,128]{1,0:T(8,128)S(1)}, f32[64,1152]{1,0:T(8,128)S(1)}, f32[8,8704]{1,0:T(8,128)S(1)}) custom-call(f32[64,2304]{1,0:T(8,128)S(1)} %shard_map.94.gathered, f32[72,128]{1,0:T(8,128)S(1)} %get-tuple-element.40.message.refs_1_.refs_6_, f32[72,128]{1,0:T(8,128)S(1)} %collective-permute-done.fetched.refs_2_, ...), custom_call_target="tpu_custom_call" | custom-call | tf_op jit(solution)/shard_map/pallas_call | solution.py:469
  58.2 4.0 %collective-permute-start.8 = (f32[64,1152]{1,0:T(8,128)S(1)}, f32[64,1152]{1,0:T(8,128)S(1)}, u32[]{:S(2)}, u32[]{:S(2)}) collective-permute-start(f32[64,1152]{1,0:T(8,128)S(1)} %get-tuple-element.58.part.rest_0_), channel_id=1, source_target_pairs={{0,256},{128,384},{256,0},{384,128},{1,257},{129,385},{257,1},{385... | collective-permute-start | bytes 884744 | tf_op jit(solution)/shard_map/ppermute | solution.py:481
  62.3 3.4 %collective-permute-start.7 = (f32[64,1152]{1,0:T(8,128)S(1)}, f32[64,1152]{1,0:T(8,128)S(1)}, u32[]{:S(2)}, u32[]{:S(2)}) collective-permute-start(f32[64,1152]{1,0:T(8,128)S(1)} %get-tuple-element.58.part.rest_0_), channel_id=1, source_target_pairs={{0,128},{128,0},{256,384},{384,256},{1,129},{129,1},{257,385},{385... | collective-permute-start | bytes 884744 | tf_op jit(solution)/shard_map/ppermute | solution.py:481
  65.7 2.7 %collective-permute-start.5 = (f32[64,128]{1,0:T(8,128)S(1)}, f32[64,128]{1,0:T(8,128)S(1)}, u32[]{:S(2)}, u32[]{:S(2)}) collective-permute-start(f32[64,128]{1,0:T(8,128)S(1)} %get-tuple-element.59), channel_id=1, source_target_pairs={{0,1},{1,0},{2,3},{3,2},{4,5},{5,4},{6,7},{7,6},{8,9},{9,8},{10,11... | collective-permute-start | bytes 98312 | tf_op jit(solution)/shard_map/ppermute | solution.py:450
  68.3 7.5 %collective-permute-start.6 = (f32[72,128]{1,0:T(8,128)S(1)}, f32[72,128]{1,0:T(8,128)S(1)}, u32[]{:S(2)}, u32[]{:S(2)}) collective-permute-start(f32[72,128]{1,0:T(8,128)S(1)} %get-tuple-element.60), channel_id=1, source_target_pairs={{0,63},{1,2},{2,1},{3,4},{4,3},{5,6},{6,5},{7,8},{8,7},{9,10},{10,... | collective-permute-start | bytes 110600 | tf_op jit(solution)/shard_map/ppermute | solution.py:450
  75.9 3.1 %collective-permute-start.11 = (f32[64,1152]{1,0:T(8,128)S(1)}, f32[64,1152]{1,0:T(8,128)S(1)}, u32[]{:S(2)}, u32[]{:S(2)}) collective-permute-start(f32[64,1152]{1,0:T(8,128)S(1)} %get-tuple-element.65.rest_2_), channel_id=1, source_target_pairs={{0,128},{128,0},{256,384},{384,256},{1,129},{129,1},{257,385},{385... | collective-permute-start | bytes 884744 | tf_op jit(solution)/shard_map/ppermute | solution.py:481
  79.0 1.9 %collective-permute-start.9 = (f32[8,8704]{1,0:T(8,128)S(1)}, f32[8,8704]{1,0:T(8,128)S(1)}, u32[]{:S(2)}, u32[]{:S(2)}) collective-permute-start(f32[8,8704]{1,0:T(8,128)S(1)} %get-tuple-element.64), channel_id=1, source_target_pairs={{0,64},{64,0},{1,65},{65,1},{2,66},{66,2},{3,67},{67,3},{4,68},{68... | collective-permute-start | bytes 835592 | tf_op jit(solution)/shard_map/ppermute | solution.py:492
  80.9 1.6 %collective-permute-done.6.got_far = f32[72,128]{1,0:T(8,128)S(1)} collective-permute-done((f32[72,128]{1,0:T(8,128)S(1)}, f32[72,128]{1,0:T(8,128)S(1)}, u32[]{:S(2)}, u32[]{:S(2)}) %collective-permute-start.6) | collective-permute-done | bytes 36896 | tf_op jit(solution)/shard_map/ppermute | solution.py:450
  82.6 1.9 %collective-permute-start.10 = (f32[64,1024]{1,0:T(8,128)S(1)}, f32[64,1024]{1,0:T(8,128)S(1)}, u32[]{:S(2)}, u32[]{:S(2)}) collective-permute-start(f32[64,1024]{1,0:T(8,128)S(1)} %shard_map.96.late), channel_id=1, source_target_pairs={{0,64},{64,0},{1,65},{65,1},{2,66},{66,2},{3,67},{67,3},{4,68},{68... | collective-permute-start | bytes 786440 | tf_op jit(solution)/shard_map/ppermute | solution.py:492
  84.5 1.0 shard_map.97
  86.0 0.8 shard_map.99
  86.8 11.1 %all_to_all.15.pieces = f32[16,8,256]{2,1,0:T(8,128)S(1)} all-to-all(f32[16,8,256]{2,1,0:T(8,128)S(1)} %bitcast.5), channel_id=1, replica_groups=mesh['chip'=4,'core'=2,'x'=4,'half'=2,'z'=8] {'core','z'}, dimensions={0} | all-to-all | bytes 262144 | tf_op jit(solution)/shard_map/all_to_all | solution.py:508
  97.9 16.8 %all_to_all.16 = f32[8,8,512]{2,1,0:T(8,128)S(1)} all-to-all(f32[8,8,512]{2,1,0:T(8,128)S(1)} %shard_map.100), channel_id=1, replica_groups=mesh['chip'=4,'core'=2,'x'=4,'half'=2,'z'=8] {'x','half'}, dimensions={0} | all-to-all | bytes 262144 | tf_op jit(solution)/shard_map/all_to_all | solution.py:512
  114.7 12.1 %all_to_all.17 = f32[8,8,512]{2,1,0:T(8,128)S(1)} all-to-all(f32[8,8,512]{2,1,0:T(8,128)S(1)} %broadcast_in_dim.2), channel_id=1, replica_groups=mesh['chip'=4,'core'=2,'x'=4,'half'=2,'z'=8] {'z'}, dimensions={0} | all-to-all | bytes 262144 | tf_op jit(solution)/shard_map/all_to_all | solution.py:514
  126.8 0.7 copy.14
  (15 shorter events, 0.7 us)
Async XLA Ops:
  2.0 20.4 %collective-permute-start = (f32[72,128]{1,0:T(8,128)S(1)}, f32[72,128]{1,0:T(8,128)S(1)}, u32[]{:S(2)}, u32[]{:S(2)}) collective-permute-start(f32[72,128]{1,0:T(8,128)S(1)} %get-tuple-element.40.message.refs_1_.refs_6_), channel_id=1, source_target_pairs={{0,63},{1,0},{2,1},{3,2},{4,3},{5,4},{6,5},{7,6},{8,7},{9,8},{10,9... | collective-permute-start | bytes 110600 | tf_op jit(solution)/shard_map/ppermute | solution.py:431
  18.6 0.7 copy-start
  24.2 16.0 %collective-permute-start.2 = (f32[72,128]{1,0:T(8,128)S(1)}, f32[72,128]{1,0:T(8,128)S(1)}, u32[]{:S(2)}, u32[]{:S(2)}) collective-permute-start(f32[72,128]{1,0:T(8,128)S(1)} %get-tuple-element.48), channel_id=1, source_target_pairs={{0,63},{1,2},{2,1},{3,4},{4,3},{5,6},{6,5},{7,8},{8,7},{9,10},{10,... | collective-permute-start | bytes 110600 | tf_op jit(solution)/shard_map/ppermute | solution.py:450
  34.3 5.8 %collective-permute-start.1 = (f32[64,128]{1,0:T(8,128)S(1)}, f32[64,128]{1,0:T(8,128)S(1)}, u32[]{:S(2)}, u32[]{:S(2)}) collective-permute-start(f32[64,128]{1,0:T(8,128)S(1)} %get-tuple-element.47), channel_id=1, source_target_pairs={{0,1},{1,0},{2,3},{3,2},{4,5},{5,4},{6,7},{7,6},{8,9},{9,8},{10,11... | collective-permute-start | bytes 98312 | tf_op jit(solution)/shard_map/ppermute | solution.py:450
  42.0 14.0 %collective-permute-start.4 = (f32[72,128]{1,0:T(8,128)S(1)}, f32[72,128]{1,0:T(8,128)S(1)}, u32[]{:S(2)}, u32[]{:S(2)}) collective-permute-start(f32[72,128]{1,0:T(8,128)S(1)} %get-tuple-element.54), channel_id=1, source_target_pairs={{0,63},{1,2},{2,1},{3,4},{4,3},{5,6},{6,5},{7,8},{8,7},{9,10},{10,... | collective-permute-start | bytes 110600 | tf_op jit(solution)/shard_map/ppermute | solution.py:450
  50.1 5.8 %collective-permute-start.3 = (f32[64,128]{1,0:T(8,128)S(1)}, f32[64,128]{1,0:T(8,128)S(1)}, u32[]{:S(2)}, u32[]{:S(2)}) collective-permute-start(f32[64,128]{1,0:T(8,128)S(1)} %get-tuple-element.53), channel_id=1, source_target_pairs={{0,1},{1,0},{2,3},{3,2},{4,5},{5,4},{6,7},{7,6},{8,9},{9,8},{10,11... | collective-permute-start | bytes 98312 | tf_op jit(solution)/shard_map/ppermute | solution.py:450
  58.2 17.6 %collective-permute-start.8 = (f32[64,1152]{1,0:T(8,128)S(1)}, f32[64,1152]{1,0:T(8,128)S(1)}, u32[]{:S(2)}, u32[]{:S(2)}) collective-permute-start(f32[64,1152]{1,0:T(8,128)S(1)} %get-tuple-element.58.part.rest_0_), channel_id=1, source_target_pairs={{0,256},{128,384},{256,0},{384,128},{1,257},{129,385},{257,1},{385... | collective-permute-start | bytes 884744 | tf_op jit(solution)/shard_map/ppermute | solution.py:481
  62.3 13.6 %collective-permute-start.7 = (f32[64,1152]{1,0:T(8,128)S(1)}, f32[64,1152]{1,0:T(8,128)S(1)}, u32[]{:S(2)}, u32[]{:S(2)}) collective-permute-start(f32[64,1152]{1,0:T(8,128)S(1)} %get-tuple-element.58.part.rest_0_), channel_id=1, source_target_pairs={{0,128},{128,0},{256,384},{384,256},{1,129},{129,1},{257,385},{385... | collective-permute-start | bytes 884744 | tf_op jit(solution)/shard_map/ppermute | solution.py:481
  65.7 10.2 %collective-permute-start.5 = (f32[64,128]{1,0:T(8,128)S(1)}, f32[64,128]{1,0:T(8,128)S(1)}, u32[]{:S(2)}, u32[]{:S(2)}) collective-permute-start(f32[64,128]{1,0:T(8,128)S(1)} %get-tuple-element.59), channel_id=1, source_target_pairs={{0,1},{1,0},{2,3},{3,2},{4,5},{5,4},{6,7},{7,6},{8,9},{9,8},{10,11... | collective-permute-start | bytes 98312 | tf_op jit(solution)/shard_map/ppermute | solution.py:450
  68.3 14.2 %collective-permute-start.6 = (f32[72,128]{1,0:T(8,128)S(1)}, f32[72,128]{1,0:T(8,128)S(1)}, u32[]{:S(2)}, u32[]{:S(2)}) collective-permute-start(f32[72,128]{1,0:T(8,128)S(1)} %get-tuple-element.60), channel_id=1, source_target_pairs={{0,63},{1,2},{2,1},{3,4},{4,3},{5,6},{6,5},{7,8},{8,7},{9,10},{10,... | collective-permute-start | bytes 110600 | tf_op jit(solution)/shard_map/ppermute | solution.py:450
  75.9 10.1 %collective-permute-start.11 = (f32[64,1152]{1,0:T(8,128)S(1)}, f32[64,1152]{1,0:T(8,128)S(1)}, u32[]{:S(2)}, u32[]{:S(2)}) collective-permute-start(f32[64,1152]{1,0:T(8,128)S(1)} %get-tuple-element.65.rest_2_), channel_id=1, source_target_pairs={{0,128},{128,0},{256,384},{384,256},{1,129},{129,1},{257,385},{385... | collective-permute-start | bytes 884744 | tf_op jit(solution)/shard_map/ppermute | solution.py:481
  79.0 7.0 %collective-permute-start.9 = (f32[8,8704]{1,0:T(8,128)S(1)}, f32[8,8704]{1,0:T(8,128)S(1)}, u32[]{:S(2)}, u32[]{:S(2)}) collective-permute-start(f32[8,8704]{1,0:T(8,128)S(1)} %get-tuple-element.64), channel_id=1, source_target_pairs={{0,64},{64,0},{1,65},{65,1},{2,66},{66,2},{3,67},{67,3},{4,68},{68... | collective-permute-start | bytes 835592 | tf_op jit(solution)/shard_map/ppermute | solution.py:492
  82.6 3.4 %collective-permute-start.10 = (f32[64,1024]{1,0:T(8,128)S(1)}, f32[64,1024]{1,0:T(8,128)S(1)}, u32[]{:S(2)}, u32[]{:S(2)}) collective-permute-start(f32[64,1024]{1,0:T(8,128)S(1)} %shard_map.96.late), channel_id=1, source_target_pairs={{0,64},{64,0},{1,65},{65,1},{2,66},{66,2},{3,67},{67,3},{4,68},{68... | collective-permute-start | bytes 786440 | tf_op jit(solution)/shard_map/ppermute | solution.py:492

commit v12 on v11

--- a/solution.py
+++ b/solution.py
@@ -95,7 +95,7 @@
 
 def prepare_kernel(
     cells, stiff, shared, scale,
-    slots, late_slots, high, low, chosen_t, scale_row, cells_pad, stiff_pad,
+    slots, late_slots, late_columns, high, low, chosen_t, scale_row, cells_pad, stiff_pad,
 ):
     n_cells, npc = cells.shape
     pad = stiff_pad.shape[0]
@@ -111,6 +111,12 @@
     for c in range(n_cells):
         at = slice(c * pad, (c + 1) * pad)
         slots[at, :] = one_hot_rows(columns[:, c : c + 1], nodes)
+        late_columns[at, :shared_count] = jnp.where(
+            columns[:, c : c + 1].astype(jnp.int16) == shared[...].astype(jnp.int16),
+            jnp.array(1, bf16),
+            jnp.array(0, bf16),
+        )
+        late_columns[at, shared_count:] = slots[at, owned:]
         row = cells_pad[c : c + 1, :].astype(jnp.int16)
         for i, names in enumerate((shareds, ghosts)):
             late_slots[i * shared_count : (i + 1) * shared_count, at] = jnp.where(
@@ -190,7 +196,7 @@
 
 
 def first_edge_kernel(
-    gathered, message, fetched, scale, late_slots, high, low, far, near, products, down_out
+    gathered, message, fetched, scale, late_slots, late_columns, high, low, far, near, products, down_out
 ):
     rows, count = down_out.shape
     ghost_inv = fetched[rows : rows + 1, :]
@@ -199,7 +205,7 @@
     late = fetched[:rows, :] * ghost_inv
     product = cell_products(gathered, late, late_slots[count:, :], scale, high, low)
     products[...] = product
-    summed = folded(dot_t(product, late_slots[...]))
+    summed = folded(dot(product, late_columns[...]))
     up = ghost_inv * summed[:, count:] * (1.0 / HALF_WIDTH)
     down = (
         shared_inv * summed[:, :count] + (shared_pot - CENTER) * message[:rows, :]
@@ -219,7 +225,7 @@
 
 def next_edges(
     gathered, message, fetched, got_near, got_far, down_before, shared_before, scale,
-    late_slots, high, low, far, near,
+    late_slots, late_columns, high, low, far, near,
 ):
     rows, count = near.shape
     got_up, got_down = got_both(got_near, got_far)
@@ -228,7 +234,7 @@
     shared_pot = message[rows + 4 : rows + 5, :]
     late = jnp.concatenate([got_up * shared_inv, got_down * ghost_inv], axis=1)
     product = cell_products(gathered, late, late_slots[...], scale, high, low)
-    summed = folded(dot_t(product, late_slots[...]))
+    summed = folded(dot(product, late_columns[...]))
     shared_now = down_before[...] + got_up
     up = ghost_inv * summed[:, count:] * (2.0 / HALF_WIDTH)
     down = (shared_inv * summed[:, :count] + (shared_pot - CENTER) * shared_now) * (
@@ -265,12 +271,12 @@
 
 def last_kernel(
     gathered, message, fetched, got_near, got_far, down_before, shared_before, scale,
-    late_slots, high, low, previous, part, inv_mass, potential, slots, chosen_t,
+    late_slots, late_columns, high, low, previous, part, inv_mass, potential, slots, chosen_t,
     far, near, partial, again,
 ):
     products, _, _ = next_edges(
         gathered, message, fetched, got_near, got_far, down_before, shared_before, scale,
-        late_slots, high, low, far, near,
+        late_slots, late_columns, high, low, far, near,
     )
     here, _ = next_body(
         products, previous, part, fetched, got_near, got_far, inv_mass, potential, slots,
@@ -286,27 +292,6 @@
     count, owned = chosen_t.shape
     own = part[:, :owned] + placed(late[:, :count], chosen_t[...])
     return own, late[:, count : 2 * count]
-
-
-def next_kernel(
-    last, previous, part, gathered, message, fetched, got_near, got_far, inv_mass, potential, scale,
-    slots, late_slots, high, low, chosen, chosen_t, far, near, partial, again,
-):
-    rows, owned = previous.shape
-    got_up, got_down = got_both(got_near, got_far)
-    ghost_inv = fetched[rows : rows + 1, :]
-    shared_inv = message[rows : rows + 1, :]
-    late = jnp.concatenate([got_up * shared_inv, got_down * ghost_inv], axis=1)
-    summed = apply_cells(gathered, late, late_slots[...], scale, slots, high, low)
-    current = part[:, :owned] + placed(got_up, chosen_t[...])
-    up = ghost_inv * summed[:, owned:] * (2.0 / HALF_WIDTH)
-    here = (inv_mass[...] * summed[:, :owned] + (potential[...] - CENTER) * current) * (
-        2.0 / HALF_WIDTH
-    ) - previous[...]
-    partial[:, :owned] = here
-    partial[:, owned:] = up
-    again[...] = here if last else current
-    send_both(up, picked(here, chosen[...]), near, far)
 
 
 def relay_kernel(beside, block, own, near, block_out, own_out):
@@ -430,11 +415,12 @@
     )
     fetched = lax.ppermute(message, DOM, backward)
     slot_count = n_cells * pad
-    slots, late_slots, high, low, chosen_t, scale = call(
+    slots, late_slots, late_columns, high, low, chosen_t, scale = call(
         prepare_kernel,
         (
             shape_of(slot_count, nodes, dtype=bf16),
             shape_of(2 * shared_count, slot_count, dtype=bf16),
+            shape_of(slot_count, 2 * shared_count, dtype=bf16),
             shape_of(pad, pad, dtype=bf16),
             shape_of(pad, pad, dtype=bf16),
             shape_of(shared_count, owned, dtype=bf16),
@@ -443,7 +429,7 @@
         [in_vmem] * 3 + [in_smem],
         [pltpu.VMEM((16, pad), jnp.int32), pltpu.VMEM((pad, pad), f32)],
     )(cells, stiff, shared, cell_scale)
-    fixed = (scale, late_slots, high, low)
+    fixed = (scale, late_slots, late_columns, high, low)
     by_slot = shape_of(rows, slot_count)
 
     def swapped(near, far):
@@ -452,7 +438,7 @@
     gathered = call(first_gather_kernel, by_slot, [in_vmem] * 3)(states, inv_mass, slots)
     stacked = shape_of(2 * rows, slot_count, dtype=bf16)
     far, near, products, down = call(
-        first_edge_kernel, (tall, edge, stacked, edge), [in_vmem] * 7
+        first_edge_kernel, (tall, edge, stacked, edge), [in_vmem] * 8
     )(gathered, message, fetched, *fixed)
     partial = call(first_body_kernel, wide, [in_vmem] * 6)(
         products, states, fetched, inv_mass, pot, slots
@@ -467,11 +453,11 @@
         body = (inv_mass, pot, slots, chosen_t)
         if step == DEGREE - 2:
             far, near, partial, own = call(
-                last_kernel, (tall, edge, wide, beside_rows), [in_vmem] * 17
+                last_kernel, (tall, edge, wide, beside_rows), [in_vmem] * 18
             )(*edges, previous, partial, *body)
         else:
             far, near, products, down, shared_now = call(
-                next_edge_kernel, (tall, edge, stacked, edge, edge), [in_vmem] * 11
+                next_edge_kernel, (tall, edge, stacked, edge, edge), [in_vmem] * 12
             )(*edges)
             partial, previous = call(next_body_kernel, (wide, block), [in_vmem] * 10)(
                 products, previous, partial, fetched, *got, *body

time: 128 us -> 127 us (level)
  transfers between devices with their start and end apart: 12 -> 12, of which waited for: 4 -> 4; matrix products, arithmetic and copies ran while one was open for 0% -> 0% of each run, Pallas kernels for 7% -> 8%
where the time goes in v12:
time: 127 us
  starting transfers between devices  62.9 us (50%)
  blocking collectives  39.9 us (31%)
  Pallas kernels  16.8 us (13%)
  waiting for transfers between devices  4.75 us (4%)
  local copies, waits for them, and re-layouts  1.32 us (1%)
    ppermute x3, starting transfers between devices, swapped(): lax.ppermute(far, DOM, far_pairs)  25.5 us
    all_to_all x1, blocking collectives, per_device(): spread = lax.all_to_all(mine, ('x', 'half'), 0, 0, tiled=True)  16.8 us
    ppermute x1, starting transfers between devices, per_device(): fetched = lax.ppermute(message, DOM, backward)  16.6 us
    all_to_all x1, blocking collectives, per_device(): lax.all_to_all(jnp.broadcast_to(mine[None], (n_z, *mine.shape)), 'z', 0,...  12.1 us
    all_to_all x1, blocking collectives, per_device(): lax.all_to_all(gram.reshape(2 * n_z, each, chips * rows), ('core', 'z'),...  11.1 us
    ppermute x3, starting transfers between devices, from_chip(): return lax.ppermute(x, 'chip', [(i, i ^ s) for i in range(chips)])  10.6 us
    ppermute x3, starting transfers between devices, swapped(): lax.ppermute(near, DOM, near_pairs)  6.41 us
    ppermute x2, starting transfers between devices, from_sibling(): return lax.ppermute(x, 'core', [(0, 1), (1, 0)])  3.84 us
  transfers between devices with their start and end apart: 12, of which 4 were waited for; matrix products, arithmetic and copies ran while one was open for 0% of the time, Pallas kernels for 8%

profile of v12, /device:TPU:16, one launch (start us, length us, event | category | flops | bytes accessed | tf_op | source)
XLA Modules:
  0.0 126.5 jit_solution(17261898967734052434)
XLA Ops:
  0.6 1.3 %shard_map.86 = (f32[72,128]{1,0:T(8,128)S(1)}, f32[64,1024]{1,0:T(8,128)S(1)}, f32[1,1024]{1,0:T(1,128)S(1)}, s32[1,128]{1,0:T(1,128)S(1)}, f32[1,1024]{1,0:T(1...) custom-call(f32[64,1024]{1,0:T(8,128)} %states.1, f32[1,1024]{1,0:T(1,128)} %bitcast.7, s32[1,128]{1,0:T(1,128)} %bitcast.9, ...), custom_call_target="tpu_custom_call" | custom-call | tf_op jit(solution)/shard_map/pallas_call | solution.py:398
  2.0 16.6 %collective-permute-start = (f32[72,128]{1,0:T(8,128)S(1)}, f32[72,128]{1,0:T(8,128)S(1)}, u32[]{:S(2)}, u32[]{:S(2)}) collective-permute-start(f32[72,128]{1,0:T(8,128)S(1)} %get-tuple-element.41.message.refs_1_.refs_6_), channel_id=1, source_target_pairs={{0,63},{1,0},{2,1},{3,2},{4,3},{5,4},{6,5},{7,6},{8,7},{9,8},{10,9... | collective-permute-start | bytes 110600 | tf_op jit(solution)/shard_map/ppermute | solution.py:416
  18.6 0.6 copy-done
  19.2 1.9 %shard_map.87 = (bf16[2304,1152]{1,0:T(8,128)(2,1)S(1)}, bf16[256,2304]{1,0:T(8,128)(2,1)S(1)}, bf16[2304,256]{1,0:T(8,128)(2,1)S(1)}, bf16[384,384]{1,0:T(8,128...) custom-call(s32[6,343]{1,0:T(8,128)S(1)} %get-tuple-element.37.cells, ...), custom_call_target="tpu_custom_call" | custom-call | tf_op jit(solution)/shard_map/pallas_call | solution.py:418
  21.1 1.6 %shard_map.88.gathered = f32[64,2304]{1,0:T(8,128)S(1)} custom-call(f32[64,1024]{1,0:T(8,128)S(1)} %get-tuple-element.35.states.refs_0_, f32[1,1024]{1,0:T(1,128)S(1)} %get-tuple-element.36.inv_mass.refs_5_, bf16[2304,1152]{1,0:T(8,128)(2,1)S(1)} %get-tuple-element.40.slots.refs_7_), custom_call_target="tpu_custom_call" | custom-call | tf_op jit(solution)/shard_map/pallas_call | solution.py:438
  22.7 1.4 %shard_map.89 = (f32[72,128]{1,0:T(8,128)S(1)}, f32[64,128]{1,0:T(8,128)S(1)}, bf16[128,2304]{1,0:T(8,128)(2,1)S(1)}, f32[64,128]{1,0:T(8,128)S(1)}) custom-call(f32[64,2304]{1,0:T(8,128)S(1)} %shard_map.88.gathered, f32[72,128]{1,0:T(8,128)S(1)} %get-tuple-element.41.message.refs_1_.refs_6_, f32[72,128]{1,0:T(8,128)S(1)} %collective-permute-done.fetched.refs_2_, ...), custom_call_target="tpu_custom_call" | custom-call | tf_op jit(solution)/shard_map/pallas_call | solution.py:440
  24.1 9.8 %collective-permute-start.2 = (f32[72,128]{1,0:T(8,128)S(1)}, f32[72,128]{1,0:T(8,128)S(1)}, u32[]{:S(2)}, u32[]{:S(2)}) collective-permute-start(f32[72,128]{1,0:T(8,128)S(1)} %get-tuple-element.50), channel_id=1, source_target_pairs={{0,63},{1,2},{2,1},{3,4},{4,3},{5,6},{6,5},{7,8},{8,7},{9,10},{10,... | collective-permute-start | bytes 110600 | tf_op jit(solution)/shard_map/ppermute | solution.py:436
  34.0 1.9 %collective-permute-start.1 = (f32[64,128]{1,0:T(8,128)S(1)}, f32[64,128]{1,0:T(8,128)S(1)}, u32[]{:S(2)}, u32[]{:S(2)}) collective-permute-start(f32[64,128]{1,0:T(8,128)S(1)} %get-tuple-element.49), channel_id=1, source_target_pairs={{0,1},{1,0},{2,3},{3,2},{4,5},{5,4},{6,7},{7,6},{8,9},{9,8},{10,11... | collective-permute-start | bytes 98312 | tf_op jit(solution)/shard_map/ppermute | solution.py:436
  35.9 1.0 shard_map.90.part.refs_1_
  36.9 1.6 %shard_map.91.refs_0_ = f32[64,2304]{1,0:T(8,128)S(1)} custom-call(f32[64,1152]{1,0:T(8,128)S(1)} %shard_map.90.part.refs_1_, f32[72,128]{1,0:T(8,128)S(1)} %collective-permute-done.fetched.refs_2_, f32[1,1024]{1,0:T(1,128)S(1)} %get-tuple-element.36.inv_mass.refs_5_, bf16[2304,1152]{1,0:T(8,128)(2,1)S(1)} %get-tuple-element.40.slots.refs_7_), custom_call_target="tpu_custom_call" | custom-call | tf_op jit(solution)/shard_map/pallas_call | solution.py:448
  38.4 1.3 %collective-permute-done.1.refs_3_ = f32[64,128]{1,0:T(8,128)S(1)} collective-permute-done((f32[64,128]{1,0:T(8,128)S(1)}, f32[64,128]{1,0:T(8,128)S(1)}, u32[]{:S(2)}, u32[]{:S(2)}) %collective-permute-start.1) | collective-permute-done | bytes 32800 | tf_op jit(solution)/shard_map/ppermute | solution.py:436
  39.8 1.4 %shard_map.92 = (f32[72,128]{1,0:T(8,128)S(1)}, f32[64,128]{1,0:T(8,128)S(1)}, bf16[128,2304]{1,0:T(8,128)(2,1)S(1)}, f32[64,128]{1,0:T(8,128)S(1)}, f32[64,128]{1,0:T(8,128)S(1)}) custom-call(f32[64,2304]{1,0:T(8,128)S(1)} %shard_map.91.refs_0_, f32[72,128]{1,0:T(8,128)S(1)} %get-tuple-element.41.message.refs_1_.refs_6_, ...), custom_call_target="tpu_custom_call" | custom-call | tf_op jit(solution)/shard_map/pallas_call | solution.py:459
  41.2 8.2 %collective-permute-start.4 = (f32[72,128]{1,0:T(8,128)S(1)}, f32[72,128]{1,0:T(8,128)S(1)}, u32[]{:S(2)}, u32[]{:S(2)}) collective-permute-start(f32[72,128]{1,0:T(8,128)S(1)} %get-tuple-element.56), channel_id=1, source_target_pairs={{0,63},{1,2},{2,1},{3,4},{4,3},{5,6},{6,5},{7,8},{8,7},{9,10},{10,... | collective-permute-start | bytes 110600 | tf_op jit(solution)/shard_map/ppermute | solution.py:436
  49.4 1.9 %collective-permute-start.3 = (f32[64,128]{1,0:T(8,128)S(1)}, f32[64,128]{1,0:T(8,128)S(1)}, u32[]{:S(2)}, u32[]{:S(2)}) collective-permute-start(f32[64,128]{1,0:T(8,128)S(1)} %get-tuple-element.55), channel_id=1, source_target_pairs={{0,1},{1,0},{2,3},{3,2},{4,5},{5,4},{6,7},{7,6},{8,9},{9,8},{10,11... | collective-permute-start | bytes 98312 | tf_op jit(solution)/shard_map/ppermute | solution.py:436
  51.3 1.1 shard_map.93
  52.4 1.6 %shard_map.94.gathered = f32[64,2304]{1,0:T(8,128)S(1)} custom-call(f32[64,1152]{1,0:T(8,128)S(1)} %get-tuple-element.54.part, f32[72,128]{1,0:T(8,128)S(1)} %collective-permute-done.fetched.refs_2_, f32[1,1024]{1,0:T(1,128)S(1)} %get-tuple-element.36.inv_mass.refs_5_, bf16[2304,1152]{1,0:T(8,128)(2,1)S(1)} %get-tuple-element.40.slots.refs_7_), custom_call_target="tpu_custom_call" | custom-call | tf_op jit(solution)/shard_map/pallas_call | solution.py:448
  54.0 1.2 collective-permute-done.3.got_near
  55.2 2.1 %shard_map.95 = (f32[72,128]{1,0:T(8,128)S(1)}, f32[64,128]{1,0:T(8,128)S(1)}, f32[64,1152]{1,0:T(8,128)S(1)}, f32[8,8704]{1,0:T(8,128)S(1)}) custom-call(f32[64,2304]{1,0:T(8,128)S(1)} %shard_map.94.gathered, f32[72,128]{1,0:T(8,128)S(1)} %get-tuple-element.41.message.refs_1_.refs_6_, f32[72,128]{1,0:T(8,128)S(1)} %collective-permute-done.fetched.refs_2_, ...), custom_call_target="tpu_custom_call" | custom-call | tf_op jit(solution)/shard_map/pallas_call | solution.py:455
  57.3 4.0 %collective-permute-start.8 = (f32[64,1152]{1,0:T(8,128)S(1)}, f32[64,1152]{1,0:T(8,128)S(1)}, u32[]{:S(2)}, u32[]{:S(2)}) collective-permute-start(f32[64,1152]{1,0:T(8,128)S(1)} %get-tuple-element.60.part.rest_0_), channel_id=1, source_target_pairs={{0,256},{128,384},{256,0},{384,128},{1,257},{129,385},{257,1},{385... | collective-permute-start | bytes 884744 | tf_op jit(solution)/shard_map/ppermute | solution.py:467
  61.4 3.5 %collective-permute-start.7 = (f32[64,1152]{1,0:T(8,128)S(1)}, f32[64,1152]{1,0:T(8,128)S(1)}, u32[]{:S(2)}, u32[]{:S(2)}) collective-permute-start(f32[64,1152]{1,0:T(8,128)S(1)} %get-tuple-element.60.part.rest_0_), channel_id=1, source_target_pairs={{0,128},{128,0},{256,384},{384,256},{1,129},{129,1},{257,385},{385... | collective-permute-start | bytes 884744 | tf_op jit(solution)/shard_map/ppermute | solution.py:467
  64.8 2.6 %collective-permute-start.5 = (f32[64,128]{1,0:T(8,128)S(1)}, f32[64,128]{1,0:T(8,128)S(1)}, u32[]{:S(2)}, u32[]{:S(2)}) collective-permute-start(f32[64,128]{1,0:T(8,128)S(1)} %get-tuple-element.61), channel_id=1, source_target_pairs={{0,1},{1,0},{2,3},{3,2},{4,5},{5,4},{6,7},{7,6},{8,9},{9,8},{10,11... | collective-permute-start | bytes 98312 | tf_op jit(solution)/shard_map/ppermute | solution.py:436
  67.4 7.5 %collective-permute-start.6 = (f32[72,128]{1,0:T(8,128)S(1)}, f32[72,128]{1,0:T(8,128)S(1)}, u32[]{:S(2)}, u32[]{:S(2)}) collective-permute-start(f32[72,128]{1,0:T(8,128)S(1)} %get-tuple-element.62), channel_id=1, source_target_pairs={{0,63},{1,2},{2,1},{3,4},{4,3},{5,6},{6,5},{7,8},{8,7},{9,10},{10,... | collective-permute-start | bytes 110600 | tf_op jit(solution)/shard_map/ppermute | solution.py:436
  75.0 3.1 %collective-permute-start.11 = (f32[64,1152]{1,0:T(8,128)S(1)}, f32[64,1152]{1,0:T(8,128)S(1)}, u32[]{:S(2)}, u32[]{:S(2)}) collective-permute-start(f32[64,1152]{1,0:T(8,128)S(1)} %get-tuple-element.67.rest_2_), channel_id=1, source_target_pairs={{0,128},{128,0},{256,384},{384,256},{1,129},{129,1},{257,385},{385... | collective-permute-start | bytes 884744 | tf_op jit(solution)/shard_map/ppermute | solution.py:467
  78.0 1.9 %collective-permute-start.9 = (f32[8,8704]{1,0:T(8,128)S(1)}, f32[8,8704]{1,0:T(8,128)S(1)}, u32[]{:S(2)}, u32[]{:S(2)}) collective-permute-start(f32[8,8704]{1,0:T(8,128)S(1)} %get-tuple-element.66), channel_id=1, source_target_pairs={{0,64},{64,0},{1,65},{65,1},{2,66},{66,2},{3,67},{67,3},{4,68},{68... | collective-permute-start | bytes 835592 | tf_op jit(solution)/shard_map/ppermute | solution.py:478
  80.0 1.6 %collective-permute-done.6.got_far = f32[72,128]{1,0:T(8,128)S(1)} collective-permute-done((f32[72,128]{1,0:T(8,128)S(1)}, f32[72,128]{1,0:T(8,128)S(1)}, u32[]{:S(2)}, u32[]{:S(2)}) %collective-permute-start.6) | collective-permute-done | bytes 36896 | tf_op jit(solution)/shard_map/ppermute | solution.py:436
  81.6 1.9 %collective-permute-start.10 = (f32[64,1024]{1,0:T(8,128)S(1)}, f32[64,1024]{1,0:T(8,128)S(1)}, u32[]{:S(2)}, u32[]{:S(2)}) collective-permute-start(f32[64,1024]{1,0:T(8,128)S(1)} %shard_map.96.late), channel_id=1, source_target_pairs={{0,64},{64,0},{1,65},{65,1},{2,66},{66,2},{3,67},{67,3},{4,68},{68... | collective-permute-start | bytes 786440 | tf_op jit(solution)/shard_map/ppermute | solution.py:478
  83.6 1.0 shard_map.97
  85.1 0.8 shard_map.99
  85.9 11.1 %all_to_all.15.pieces = f32[16,8,256]{2,1,0:T(8,128)S(1)} all-to-all(f32[16,8,256]{2,1,0:T(8,128)S(1)} %bitcast.5), channel_id=1, replica_groups=mesh['chip'=4,'core'=2,'x'=4,'half'=2,'z'=8] {'core','z'}, dimensions={0} | all-to-all | bytes 262144 | tf_op jit(solution)/shard_map/all_to_all | solution.py:494
  97.0 16.8 %all_to_all.16 = f32[8,8,512]{2,1,0:T(8,128)S(1)} all-to-all(f32[8,8,512]{2,1,0:T(8,128)S(1)} %shard_map.100), channel_id=1, replica_groups=mesh['chip'=4,'core'=2,'x'=4,'half'=2,'z'=8] {'x','half'}, dimensions={0} | all-to-all | bytes 262144 | tf_op jit(solution)/shard_map/all_to_all | solution.py:498
  113.8 12.1 %all_to_all.17 = f32[8,8,512]{2,1,0:T(8,128)S(1)} all-to-all(f32[8,8,512]{2,1,0:T(8,128)S(1)} %broadcast_in_dim.2), channel_id=1, replica_groups=mesh['chip'=4,'core'=2,'x'=4,'half'=2,'z'=8] {'z'}, dimensions={0} | all-to-all | bytes 262144 | tf_op jit(solution)/shard_map/all_to_all | solution.py:500
  125.9 0.7 copy.14
  (15 shorter events, 0.7 us)
Async XLA Ops:
  2.0 20.8 %collective-permute-start = (f32[72,128]{1,0:T(8,128)S(1)}, f32[72,128]{1,0:T(8,128)S(1)}, u32[]{:S(2)}, u32[]{:S(2)}) collective-permute-start(f32[72,128]{1,0:T(8,128)S(1)} %get-tuple-element.41.message.refs_1_.refs_6_), channel_id=1, source_target_pairs={{0,63},{1,0},{2,1},{3,2},{4,3},{5,4},{6,5},{7,6},{8,7},{9,8},{10,9... | collective-permute-start | bytes 110600 | tf_op jit(solution)/shard_map/ppermute | solution.py:416
  18.6 0.7 copy-start
  24.1 15.6 %collective-permute-start.2 = (f32[72,128]{1,0:T(8,128)S(1)}, f32[72,128]{1,0:T(8,128)S(1)}, u32[]{:S(2)}, u32[]{:S(2)}) collective-permute-start(f32[72,128]{1,0:T(8,128)S(1)} %get-tuple-element.50), channel_id=1, source_target_pairs={{0,63},{1,2},{2,1},{3,4},{4,3},{5,6},{6,5},{7,8},{8,7},{9,10},{10,... | collective-permute-start | bytes 110600 | tf_op jit(solution)/shard_map/ppermute | solution.py:436
  34.0 5.8 %collective-permute-start.1 = (f32[64,128]{1,0:T(8,128)S(1)}, f32[64,128]{1,0:T(8,128)S(1)}, u32[]{:S(2)}, u32[]{:S(2)}) collective-permute-start(f32[64,128]{1,0:T(8,128)S(1)} %get-tuple-element.49), channel_id=1, source_target_pairs={{0,1},{1,0},{2,3},{3,2},{4,5},{5,4},{6,7},{7,6},{8,9},{9,8},{10,11... | collective-permute-start | bytes 98312 | tf_op jit(solution)/shard_map/ppermute | solution.py:436
  41.2 14.0 %collective-permute-start.4 = (f32[72,128]{1,0:T(8,128)S(1)}, f32[72,128]{1,0:T(8,128)S(1)}, u32[]{:S(2)}, u32[]{:S(2)}) collective-permute-start(f32[72,128]{1,0:T(8,128)S(1)} %get-tuple-element.56), channel_id=1, source_target_pairs={{0,63},{1,2},{2,1},{3,4},{4,3},{5,6},{6,5},{7,8},{8,7},{9,10},{10,... | collective-permute-start | bytes 110600 | tf_op jit(solution)/shard_map/ppermute | solution.py:436
  49.4 5.8 %collective-permute-start.3 = (f32[64,128]{1,0:T(8,128)S(1)}, f32[64,128]{1,0:T(8,128)S(1)}, u32[]{:S(2)}, u32[]{:S(2)}) collective-permute-start(f32[64,128]{1,0:T(8,128)S(1)} %get-tuple-element.55), channel_id=1, source_target_pairs={{0,1},{1,0},{2,3},{3,2},{4,5},{5,4},{6,7},{7,6},{8,9},{9,8},{10,11... | collective-permute-start | bytes 98312 | tf_op jit(solution)/shard_map/ppermute | solution.py:436
  57.3 17.6 %collective-permute-start.8 = (f32[64,1152]{1,0:T(8,128)S(1)}, f32[64,1152]{1,0:T(8,128)S(1)}, u32[]{:S(2)}, u32[]{:S(2)}) collective-permute-start(f32[64,1152]{1,0:T(8,128)S(1)} %get-tuple-element.60.part.rest_0_), channel_id=1, source_target_pairs={{0,256},{128,384},{256,0},{384,128},{1,257},{129,385},{257,1},{385... | collective-permute-start | bytes 884744 | tf_op jit(solution)/shard_map/ppermute | solution.py:467
  61.4 13.6 %collective-permute-start.7 = (f32[64,1152]{1,0:T(8,128)S(1)}, f32[64,1152]{1,0:T(8,128)S(1)}, u32[]{:S(2)}, u32[]{:S(2)}) collective-permute-start(f32[64,1152]{1,0:T(8,128)S(1)} %get-tuple-element.60.part.rest_0_), channel_id=1, source_target_pairs={{0,128},{128,0},{256,384},{384,256},{1,129},{129,1},{257,385},{385... | collective-permute-start | bytes 884744 | tf_op jit(solution)/shard_map/ppermute | solution.py:467
  64.8 10.1 %collective-permute-start.5 = (f32[64,128]{1,0:T(8,128)S(1)}, f32[64,128]{1,0:T(8,128)S(1)}, u32[]{:S(2)}, u32[]{:S(2)}) collective-permute-start(f32[64,128]{1,0:T(8,128)S(1)} %get-tuple-element.61), channel_id=1, source_target_pairs={{0,1},{1,0},{2,3},{3,2},{4,5},{5,4},{6,7},{7,6},{8,9},{9,8},{10,11... | collective-permute-start | bytes 98312 | tf_op jit(solution)/shard_map/ppermute | solution.py:436
  67.4 14.2 %collective-permute-start.6 = (f32[72,128]{1,0:T(8,128)S(1)}, f32[72,128]{1,0:T(8,128)S(1)}, u32[]{:S(2)}, u32[]{:S(2)}) collective-permute-start(f32[72,128]{1,0:T(8,128)S(1)} %get-tuple-element.62), channel_id=1, source_target_pairs={{0,63},{1,2},{2,1},{3,4},{4,3},{5,6},{6,5},{7,8},{8,7},{9,10},{10,... | collective-permute-start | bytes 110600 | tf_op jit(solution)/shard_map/ppermute | solution.py:436
  75.0 10.1 %collective-permute-start.11 = (f32[64,1152]{1,0:T(8,128)S(1)}, f32[64,1152]{1,0:T(8,128)S(1)}, u32[]{:S(2)}, u32[]{:S(2)}) collective-permute-start(f32[64,1152]{1,0:T(8,128)S(1)} %get-tuple-element.67.rest_2_), channel_id=1, source_target_pairs={{0,128},{128,0},{256,384},{384,256},{1,129},{129,1},{257,385},{385... | collective-permute-start | bytes 884744 | tf_op jit(solution)/shard_map/ppermute | solution.py:467
  78.0 7.0 %collective-permute-start.9 = (f32[8,8704]{1,0:T(8,128)S(1)}, f32[8,8704]{1,0:T(8,128)S(1)}, u32[]{:S(2)}, u32[]{:S(2)}) collective-permute-start(f32[8,8704]{1,0:T(8,128)S(1)} %get-tuple-element.66), channel_id=1, source_target_pairs={{0,64},{64,0},{1,65},{65,1},{2,66},{66,2},{3,67},{67,3},{4,68},{68... | collective-permute-start | bytes 835592 | tf_op jit(solution)/shard_map/ppermute | solution.py:478
  81.6 3.4 %collective-permute-start.10 = (f32[64,1024]{1,0:T(8,128)S(1)}, f32[64,1024]{1,0:T(8,128)S(1)}, u32[]{:S(2)}, u32[]{:S(2)}) collective-permute-start(f32[64,1024]{1,0:T(8,128)S(1)} %shard_map.96.late), channel_id=1, source_target_pairs={{0,64},{64,0},{1,65},{65,1},{2,66},{66,2},{3,67},{67,3},{4,68},{68... | collective-permute-start | bytes 786440 | tf_op jit(solution)/shard_map/ppermute | solution.py:478

commit v13 on v12

--- a/solution.py
+++ b/solution.py
@@ -294,8 +294,8 @@
     return own, late[:, count : 2 * count]
 
 
-def relay_kernel(beside, block, own, near, block_out, own_out):
-    del beside, near
+def relay_kernel(beside, block, own, block_out, own_out):
+    del beside
     block_out[:8, :128] = block[:8, :128]
     own_out[:8, :128] = own[:8, :128]
 
@@ -469,8 +469,8 @@
     got_near, got_far = swapped(near, far)
     second = from_chip(partial, 2)
     beside = from_chip(partial, 1)
-    relayed, own = call(relay_kernel, (wide, beside_rows), [in_vmem] * 4, aliases={1: 0, 2: 1})(
-        beside, second, own, got_near
+    relayed, own = call(relay_kernel, (wide, beside_rows), [in_vmem] * 3, aliases={1: 0, 2: 1})(
+        beside, second, own
     )
     blocks = [partial, beside, relayed, from_chip(relayed, 1)]
 

time: 127 us -> 127 us (level)
  no operation moved by 1% of the time
where the time goes in v13:
time: 127 us
  starting transfers between devices  63.3 us (50%)
  blocking collectives  40 us (31%)
  Pallas kernels  16.8 us (13%)
  waiting for transfers between devices  4.35 us (3%)
  local copies, waits for them, and re-layouts  1.32 us (1%)
    ppermute x3, starting transfers between devices, swapped(): lax.ppermute(far, DOM, far_pairs)  26.1 us
    all_to_all x1, blocking collectives, per_device(): spread = lax.all_to_all(mine, ('x', 'half'), 0, 0, tiled=True)  16.9 us
    ppermute x1, starting transfers between devices, per_device(): fetched = lax.ppermute(message, DOM, backward)  16.6 us
    all_to_all x1, blocking collectives, per_device(): lax.all_to_all(jnp.broadcast_to(mine[None], (n_z, *mine.shape)), 'z', 0,...  12.1 us
    all_to_all x1, blocking collectives, per_device(): lax.all_to_all(gram.reshape(2 * n_z, each, chips * rows), ('core', 'z'),...  11.1 us
    ppermute x3, starting transfers between devices, from_chip(): return lax.ppermute(x, 'chip', [(i, i ^ s) for i in range(chips)])  11 us
    ppermute x3, starting transfers between devices, swapped(): lax.ppermute(near, DOM, near_pairs)  5.76 us
    ppermute x2, starting transfers between devices, from_sibling(): return lax.ppermute(x, 'core', [(0, 1), (1, 0)])  3.84 us
  transfers between devices with their start and end apart: 12, of which 4 were waited for; matrix products, arithmetic and copies ran while one was open for 0% of the time, Pallas kernels for 8%

profile of v13, /device:TPU:16, one launch (start us, length us, event | category | flops | bytes accessed | tf_op | source)
XLA Modules:
  0.0 126.7 jit_solution(2731093680065468978)
XLA Ops:
  0.6 1.3 %shard_map.86 = (f32[72,128]{1,0:T(8,128)S(1)}, f32[64,1024]{1,0:T(8,128)S(1)}, f32[1,1024]{1,0:T(1,128)S(1)}, s32[1,128]{1,0:T(1,128)S(1)}, f32[1,1024]{1,0:T(1...) custom-call(f32[64,1024]{1,0:T(8,128)} %states.1, f32[1,1024]{1,0:T(1,128)} %bitcast.7, s32[1,128]{1,0:T(1,128)} %bitcast.9, ...), custom_call_target="tpu_custom_call" | custom-call | tf_op jit(solution)/shard_map/pallas_call | solution.py:398
  2.0 16.6 %collective-permute-start = (f32[72,128]{1,0:T(8,128)S(1)}, f32[72,128]{1,0:T(8,128)S(1)}, u32[]{:S(2)}, u32[]{:S(2)}) collective-permute-start(f32[72,128]{1,0:T(8,128)S(1)} %get-tuple-element.41.message.refs_1_.refs_6_), channel_id=1, source_target_pairs={{0,63},{1,0},{2,1},{3,2},{4,3},{5,4},{6,5},{7,6},{8,7},{9,8},{10,9... | collective-permute-start | bytes 110600 | tf_op jit(solution)/shard_map/ppermute | solution.py:416
  18.6 0.6 copy-done
  19.2 1.9 %shard_map.87 = (bf16[2304,1152]{1,0:T(8,128)(2,1)S(1)}, bf16[256,2304]{1,0:T(8,128)(2,1)S(1)}, bf16[2304,256]{1,0:T(8,128)(2,1)S(1)}, bf16[384,384]{1,0:T(8,128...) custom-call(s32[6,343]{1,0:T(8,128)S(1)} %get-tuple-element.37.cells, ...), custom_call_target="tpu_custom_call" | custom-call | tf_op jit(solution)/shard_map/pallas_call | solution.py:418
  21.1 1.6 %shard_map.88.gathered = f32[64,2304]{1,0:T(8,128)S(1)} custom-call(f32[64,1024]{1,0:T(8,128)S(1)} %get-tuple-element.35.states.refs_0_, f32[1,1024]{1,0:T(1,128)S(1)} %get-tuple-element.36.inv_mass.refs_5_, bf16[2304,1152]{1,0:T(8,128)(2,1)S(1)} %get-tuple-element.40.slots.refs_7_), custom_call_target="tpu_custom_call" | custom-call | tf_op jit(solution)/shard_map/pallas_call | solution.py:438
  22.7 1.4 %shard_map.89 = (f32[72,128]{1,0:T(8,128)S(1)}, f32[64,128]{1,0:T(8,128)S(1)}, bf16[128,2304]{1,0:T(8,128)(2,1)S(1)}, f32[64,128]{1,0:T(8,128)S(1)}) custom-call(f32[64,2304]{1,0:T(8,128)S(1)} %shard_map.88.gathered, f32[72,128]{1,0:T(8,128)S(1)} %get-tuple-element.41.message.refs_1_.refs_6_, f32[72,128]{1,0:T(8,128)S(1)} %collective-permute-done.fetched.refs_2_, ...), custom_call_target="tpu_custom_call" | custom-call | tf_op jit(solution)/shard_map/pallas_call | solution.py:440
  24.1 9.8 %collective-permute-start.2 = (f32[72,128]{1,0:T(8,128)S(1)}, f32[72,128]{1,0:T(8,128)S(1)}, u32[]{:S(2)}, u32[]{:S(2)}) collective-permute-start(f32[72,128]{1,0:T(8,128)S(1)} %get-tuple-element.50), channel_id=1, source_target_pairs={{0,63},{1,2},{2,1},{3,4},{4,3},{5,6},{6,5},{7,8},{8,7},{9,10},{10,... | collective-permute-start | bytes 110600 | tf_op jit(solution)/shard_map/ppermute | solution.py:436
  34.0 1.9 %collective-permute-start.1 = (f32[64,128]{1,0:T(8,128)S(1)}, f32[64,128]{1,0:T(8,128)S(1)}, u32[]{:S(2)}, u32[]{:S(2)}) collective-permute-start(f32[64,128]{1,0:T(8,128)S(1)} %get-tuple-element.49), channel_id=1, source_target_pairs={{0,1},{1,0},{2,3},{3,2},{4,5},{5,4},{6,7},{7,6},{8,9},{9,8},{10,11... | collective-permute-start | bytes 98312 | tf_op jit(solution)/shard_map/ppermute | solution.py:436
  35.9 1.0 shard_map.90.part.refs_1_
  36.9 1.6 %shard_map.91.refs_0_ = f32[64,2304]{1,0:T(8,128)S(1)} custom-call(f32[64,1152]{1,0:T(8,128)S(1)} %shard_map.90.part.refs_1_, f32[72,128]{1,0:T(8,128)S(1)} %collective-permute-done.fetched.refs_2_, f32[1,1024]{1,0:T(1,128)S(1)} %get-tuple-element.36.inv_mass.refs_5_, bf16[2304,1152]{1,0:T(8,128)(2,1)S(1)} %get-tuple-element.40.slots.refs_7_), custom_call_target="tpu_custom_call" | custom-call | tf_op jit(solution)/shard_map/pallas_call | solution.py:448
  38.4 1.3 %collective-permute-done.1.refs_3_ = f32[64,128]{1,0:T(8,128)S(1)} collective-permute-done((f32[64,128]{1,0:T(8,128)S(1)}, f32[64,128]{1,0:T(8,128)S(1)}, u32[]{:S(2)}, u32[]{:S(2)}) %collective-permute-start.1) | collective-permute-done | bytes 32800 | tf_op jit(solution)/shard_map/ppermute | solution.py:436
  39.8 1.4 %shard_map.92 = (f32[72,128]{1,0:T(8,128)S(1)}, f32[64,128]{1,0:T(8,128)S(1)}, bf16[128,2304]{1,0:T(8,128)(2,1)S(1)}, f32[64,128]{1,0:T(8,128)S(1)}, f32[64,128]{1,0:T(8,128)S(1)}) custom-call(f32[64,2304]{1,0:T(8,128)S(1)} %shard_map.91.refs_0_, f32[72,128]{1,0:T(8,128)S(1)} %get-tuple-element.41.message.refs_1_.refs_6_, ...), custom_call_target="tpu_custom_call" | custom-call | tf_op jit(solution)/shard_map/pallas_call | solution.py:459
  41.2 8.2 %collective-permute-start.4 = (f32[72,128]{1,0:T(8,128)S(1)}, f32[72,128]{1,0:T(8,128)S(1)}, u32[]{:S(2)}, u32[]{:S(2)}) collective-permute-start(f32[72,128]{1,0:T(8,128)S(1)} %get-tuple-element.56), channel_id=1, source_target_pairs={{0,63},{1,2},{2,1},{3,4},{4,3},{5,6},{6,5},{7,8},{8,7},{9,10},{10,... | collective-permute-start | bytes 110600 | tf_op jit(solution)/shard_map/ppermute | solution.py:436
  49.4 1.9 %collective-permute-start.3 = (f32[64,128]{1,0:T(8,128)S(1)}, f32[64,128]{1,0:T(8,128)S(1)}, u32[]{:S(2)}, u32[]{:S(2)}) collective-permute-start(f32[64,128]{1,0:T(8,128)S(1)} %get-tuple-element.55), channel_id=1, source_target_pairs={{0,1},{1,0},{2,3},{3,2},{4,5},{5,4},{6,7},{7,6},{8,9},{9,8},{10,11... | collective-permute-start | bytes 98312 | tf_op jit(solution)/shard_map/ppermute | solution.py:436
  51.3 1.1 shard_map.93
  52.4 1.6 %shard_map.94.gathered = f32[64,2304]{1,0:T(8,128)S(1)} custom-call(f32[64,1152]{1,0:T(8,128)S(1)} %get-tuple-element.54.part, f32[72,128]{1,0:T(8,128)S(1)} %collective-permute-done.fetched.refs_2_, f32[1,1024]{1,0:T(1,128)S(1)} %get-tuple-element.36.inv_mass.refs_5_, bf16[2304,1152]{1,0:T(8,128)(2,1)S(1)} %get-tuple-element.40.slots.refs_7_), custom_call_target="tpu_custom_call" | custom-call | tf_op jit(solution)/shard_map/pallas_call | solution.py:448
  54.0 1.2 collective-permute-done.3.got_near
  55.2 2.1 %shard_map.95 = (f32[72,128]{1,0:T(8,128)S(1)}, f32[64,128]{1,0:T(8,128)S(1)}, f32[64,1152]{1,0:T(8,128)S(1)}, f32[8,8704]{1,0:T(8,128)S(1)}) custom-call(f32[64,2304]{1,0:T(8,128)S(1)} %shard_map.94.gathered, f32[72,128]{1,0:T(8,128)S(1)} %get-tuple-element.41.message.refs_1_.refs_6_, f32[72,128]{1,0:T(8,128)S(1)} %collective-permute-done.fetched.refs_2_, ...), custom_call_target="tpu_custom_call" | custom-call | tf_op jit(solution)/shard_map/pallas_call | solution.py:455
  57.3 4.0 %collective-permute-start.8 = (f32[64,1152]{1,0:T(8,128)S(1)}, f32[64,1152]{1,0:T(8,128)S(1)}, u32[]{:S(2)}, u32[]{:S(2)}) collective-permute-start(f32[64,1152]{1,0:T(8,128)S(1)} %get-tuple-element.60.part.rest_0_), channel_id=1, source_target_pairs={{0,256},{128,384},{256,0},{384,128},{1,257},{129,385},{257,1},{385... | collective-permute-start | bytes 884744 | tf_op jit(solution)/shard_map/ppermute | solution.py:467
  61.4 3.5 %collective-permute-start.7 = (f32[64,1152]{1,0:T(8,128)S(1)}, f32[64,1152]{1,0:T(8,128)S(1)}, u32[]{:S(2)}, u32[]{:S(2)}) collective-permute-start(f32[64,1152]{1,0:T(8,128)S(1)} %get-tuple-element.60.part.rest_0_), channel_id=1, source_target_pairs={{0,128},{128,0},{256,384},{384,256},{1,129},{129,1},{257,385},{385... | collective-permute-start | bytes 884744 | tf_op jit(solution)/shard_map/ppermute | solution.py:467
  64.8 8.1 %collective-permute-start.6 = (f32[72,128]{1,0:T(8,128)S(1)}, f32[72,128]{1,0:T(8,128)S(1)}, u32[]{:S(2)}, u32[]{:S(2)}) collective-permute-start(f32[72,128]{1,0:T(8,128)S(1)} %get-tuple-element.62), channel_id=1, source_target_pairs={{0,63},{1,2},{2,1},{3,4},{4,3},{5,6},{6,5},{7,8},{8,7},{9,10},{10,... | collective-permute-start | bytes 110600 | tf_op jit(solution)/shard_map/ppermute | solution.py:436
  73.0 1.9 %collective-permute-start.5 = (f32[64,128]{1,0:T(8,128)S(1)}, f32[64,128]{1,0:T(8,128)S(1)}, u32[]{:S(2)}, u32[]{:S(2)}) collective-permute-start(f32[64,128]{1,0:T(8,128)S(1)} %get-tuple-element.61), channel_id=1, source_target_pairs={{0,1},{1,0},{2,3},{3,2},{4,5},{5,4},{6,7},{7,6},{8,9},{9,8},{10,11... | collective-permute-start | bytes 98312 | tf_op jit(solution)/shard_map/ppermute | solution.py:436
  75.0 3.5 %collective-permute-start.11 = (f32[64,1152]{1,0:T(8,128)S(1)}, f32[64,1152]{1,0:T(8,128)S(1)}, u32[]{:S(2)}, u32[]{:S(2)}) collective-permute-start(f32[64,1152]{1,0:T(8,128)S(1)} %get-tuple-element.67.rest_2_), channel_id=1, source_target_pairs={{0,128},{128,0},{256,384},{384,256},{1,129},{129,1},{257,385},{385... | collective-permute-start | bytes 884744 | tf_op jit(solution)/shard_map/ppermute | solution.py:467
  78.4 1.9 %collective-permute-start.9 = (f32[8,8704]{1,0:T(8,128)S(1)}, f32[8,8704]{1,0:T(8,128)S(1)}, u32[]{:S(2)}, u32[]{:S(2)}) collective-permute-start(f32[8,8704]{1,0:T(8,128)S(1)} %get-tuple-element.66), channel_id=1, source_target_pairs={{0,64},{64,0},{1,65},{65,1},{2,66},{66,2},{3,67},{67,3},{4,68},{68... | collective-permute-start | bytes 835592 | tf_op jit(solution)/shard_map/ppermute | solution.py:478
  80.4 1.2 collective-permute-done.6.got_far
  81.6 1.9 %collective-permute-start.10 = (f32[64,1024]{1,0:T(8,128)S(1)}, f32[64,1024]{1,0:T(8,128)S(1)}, u32[]{:S(2)}, u32[]{:S(2)}) collective-permute-start(f32[64,1024]{1,0:T(8,128)S(1)} %shard_map.96.late), channel_id=1, source_target_pairs={{0,64},{64,0},{1,65},{65,1},{2,66},{66,2},{3,67},{67,3},{4,68},{68... | collective-permute-start | bytes 786440 | tf_op jit(solution)/shard_map/ppermute | solution.py:478
  83.6 1.0 shard_map.97
  85.1 0.8 shard_map.99
  85.9 11.1 %all_to_all.15.pieces = f32[16,8,256]{2,1,0:T(8,128)S(1)} all-to-all(f32[16,8,256]{2,1,0:T(8,128)S(1)} %bitcast.5), channel_id=1, replica_groups=mesh['chip'=4,'core'=2,'x'=4,'half'=2,'z'=8] {'core','z'}, dimensions={0} | all-to-all | bytes 262144 | tf_op jit(solution)/shard_map/all_to_all | solution.py:494
  97.0 16.9 %all_to_all.16 = f32[8,8,512]{2,1,0:T(8,128)S(1)} all-to-all(f32[8,8,512]{2,1,0:T(8,128)S(1)} %shard_map.100), channel_id=1, replica_groups=mesh['chip'=4,'core'=2,'x'=4,'half'=2,'z'=8] {'x','half'}, dimensions={0} | all-to-all | bytes 262144 | tf_op jit(solution)/shard_map/all_to_all | solution.py:498
  113.9 12.1 %all_to_all.17 = f32[8,8,512]{2,1,0:T(8,128)S(1)} all-to-all(f32[8,8,512]{2,1,0:T(8,128)S(1)} %broadcast_in_dim.2), channel_id=1, replica_groups=mesh['chip'=4,'core'=2,'x'=4,'half'=2,'z'=8] {'z'}, dimensions={0} | all-to-all | bytes 262144 | tf_op jit(solution)/shard_map/all_to_all | solution.py:500
  126.0 0.7 copy.14
  (15 shorter events, 0.7 us)
Async XLA Ops:
  2.0 20.8 %collective-permute-start = (f32[72,128]{1,0:T(8,128)S(1)}, f32[72,128]{1,0:T(8,128)S(1)}, u32[]{:S(2)}, u32[]{:S(2)}) collective-permute-start(f32[72,128]{1,0:T(8,128)S(1)} %get-tuple-element.41.message.refs_1_.refs_6_), channel_id=1, source_target_pairs={{0,63},{1,0},{2,1},{3,2},{4,3},{5,4},{6,5},{7,6},{8,7},{9,8},{10,9... | collective-permute-start | bytes 110600 | tf_op jit(solution)/shard_map/ppermute | solution.py:416
  18.6 0.7 copy-start
  24.1 15.6 %collective-permute-start.2 = (f32[72,128]{1,0:T(8,128)S(1)}, f32[72,128]{1,0:T(8,128)S(1)}, u32[]{:S(2)}, u32[]{:S(2)}) collective-permute-start(f32[72,128]{1,0:T(8,128)S(1)} %get-tuple-element.50), channel_id=1, source_target_pairs={{0,63},{1,2},{2,1},{3,4},{4,3},{5,6},{6,5},{7,8},{8,7},{9,10},{10,... | collective-permute-start | bytes 110600 | tf_op jit(solution)/shard_map/ppermute | solution.py:436
  34.0 5.8 %collective-permute-start.1 = (f32[64,128]{1,0:T(8,128)S(1)}, f32[64,128]{1,0:T(8,128)S(1)}, u32[]{:S(2)}, u32[]{:S(2)}) collective-permute-start(f32[64,128]{1,0:T(8,128)S(1)} %get-tuple-element.49), channel_id=1, source_target_pairs={{0,1},{1,0},{2,3},{3,2},{4,5},{5,4},{6,7},{7,6},{8,9},{9,8},{10,11... | collective-permute-start | bytes 98312 | tf_op jit(solution)/shard_map/ppermute | solution.py:436
  41.2 14.0 %collective-permute-start.4 = (f32[72,128]{1,0:T(8,128)S(1)}, f32[72,128]{1,0:T(8,128)S(1)}, u32[]{:S(2)}, u32[]{:S(2)}) collective-permute-start(f32[72,128]{1,0:T(8,128)S(1)} %get-tuple-element.56), channel_id=1, source_target_pairs={{0,63},{1,2},{2,1},{3,4},{4,3},{5,6},{6,5},{7,8},{8,7},{9,10},{10,... | collective-permute-start | bytes 110600 | tf_op jit(solution)/shard_map/ppermute | solution.py:436
  49.4 5.8 %collective-permute-start.3 = (f32[64,128]{1,0:T(8,128)S(1)}, f32[64,128]{1,0:T(8,128)S(1)}, u32[]{:S(2)}, u32[]{:S(2)}) collective-permute-start(f32[64,128]{1,0:T(8,128)S(1)} %get-tuple-element.55), channel_id=1, source_target_pairs={{0,1},{1,0},{2,3},{3,2},{4,5},{5,4},{6,7},{7,6},{8,9},{9,8},{10,11... | collective-permute-start | bytes 98312 | tf_op jit(solution)/shard_map/ppermute | solution.py:436
  57.3 17.6 %collective-permute-start.8 = (f32[64,1152]{1,0:T(8,128)S(1)}, f32[64,1152]{1,0:T(8,128)S(1)}, u32[]{:S(2)}, u32[]{:S(2)}) collective-permute-start(f32[64,1152]{1,0:T(8,128)S(1)} %get-tuple-element.60.part.rest_0_), channel_id=1, source_target_pairs={{0,256},{128,384},{256,0},{384,128},{1,257},{129,385},{257,1},{385... | collective-permute-start | bytes 884744 | tf_op jit(solution)/shard_map/ppermute | solution.py:467
  61.4 13.6 %collective-permute-start.7 = (f32[64,1152]{1,0:T(8,128)S(1)}, f32[64,1152]{1,0:T(8,128)S(1)}, u32[]{:S(2)}, u32[]{:S(2)}) collective-permute-start(f32[64,1152]{1,0:T(8,128)S(1)} %get-tuple-element.60.part.rest_0_), channel_id=1, source_target_pairs={{0,128},{128,0},{256,384},{384,256},{1,129},{129,1},{257,385},{385... | collective-permute-start | bytes 884744 | tf_op jit(solution)/shard_map/ppermute | solution.py:467
  64.8 16.8 %collective-permute-start.6 = (f32[72,128]{1,0:T(8,128)S(1)}, f32[72,128]{1,0:T(8,128)S(1)}, u32[]{:S(2)}, u32[]{:S(2)}) collective-permute-start(f32[72,128]{1,0:T(8,128)S(1)} %get-tuple-element.62), channel_id=1, source_target_pairs={{0,63},{1,2},{2,1},{3,4},{4,3},{5,6},{6,5},{7,8},{8,7},{9,10},{10,... | collective-permute-start | bytes 110600 | tf_op jit(solution)/shard_map/ppermute | solution.py:436
  73.0 7.4 %collective-permute-start.5 = (f32[64,128]{1,0:T(8,128)S(1)}, f32[64,128]{1,0:T(8,128)S(1)}, u32[]{:S(2)}, u32[]{:S(2)}) collective-permute-start(f32[64,128]{1,0:T(8,128)S(1)} %get-tuple-element.61), channel_id=1, source_target_pairs={{0,1},{1,0},{2,3},{3,2},{4,5},{5,4},{6,7},{7,6},{8,9},{9,8},{10,11... | collective-permute-start | bytes 98312 | tf_op jit(solution)/shard_map/ppermute | solution.py:436
  75.0 10.1 %collective-permute-start.11 = (f32[64,1152]{1,0:T(8,128)S(1)}, f32[64,1152]{1,0:T(8,128)S(1)}, u32[]{:S(2)}, u32[]{:S(2)}) collective-permute-start(f32[64,1152]{1,0:T(8,128)S(1)} %get-tuple-element.67.rest_2_), channel_id=1, source_target_pairs={{0,128},{128,0},{256,384},{384,256},{1,129},{129,1},{257,385},{385... | collective-permute-start | bytes 884744 | tf_op jit(solution)/shard_map/ppermute | solution.py:467
  78.4 6.6 %collective-permute-start.9 = (f32[8,8704]{1,0:T(8,128)S(1)}, f32[8,8704]{1,0:T(8,128)S(1)}, u32[]{:S(2)}, u32[]{:S(2)}) collective-permute-start(f32[8,8704]{1,0:T(8,128)S(1)} %get-tuple-element.66), channel_id=1, source_target_pairs={{0,64},{64,0},{1,65},{65,1},{2,66},{66,2},{3,67},{67,3},{4,68},{68... | collective-permute-start | bytes 835592 | tf_op jit(solution)/shard_map/ppermute | solution.py:478
  81.6 3.4 %collective-permute-start.10 = (f32[64,1024]{1,0:T(8,128)S(1)}, f32[64,1024]{1,0:T(8,128)S(1)}, u32[]{:S(2)}, u32[]{:S(2)}) collective-permute-start(f32[64,1024]{1,0:T(8,128)S(1)} %shard_map.96.late), channel_id=1, source_target_pairs={{0,64},{64,0},{1,65},{65,1},{2,66},{66,2},{3,67},{67,3},{4,68},{68... | collective-permute-start | bytes 786440 | tf_op jit(solution)/shard_map/ppermute | solution.py:478
